TPU v7x, 32 devices: a whole 2x2x4 slice. The times are simulated.
32 devices in a mesh: gz: 2 (over core), gy: 16 (over z, y, x).
Axes of the slice: x: 2, y: 2, z: 4, core: 2. Of those that a mesh axis runs over, the one named last changes fastest.
Arguments:
- data: bfloat16 [2, 64, 2048, 128], P('gz', 'gy'), may hold values from -6 to 6
- band_offset: int32 [4096], replicated, may hold values from -1 to 0
- interp_weight: float32 [2, 4096], replicated, may hold values from 0.3 to 1
Outputs:
- volume: float32 [2, 2048, 4096], P('gz', 'gy')
- residual: float32 [2, 64, 2048, 128], P('gz', 'gy')
All inputs are finite; a program needn't handle non-finite values.
Results may differ from a plain program's by a relative error of at most 0.0003.
Values sent between devices are 32-bit elements; how exact they have to be, the bound alone decides.
No kernel may reach another device: no remote copies, remote signals or barrier semaphores. Data moves between devices by JAX's collectives and lax.ppermute only.
A program may use at most 192 MiB of HBM per device.

v0:
```python
import jax
import jax.numpy as jnp
from jax import lax
from jax.sharding import PartitionSpec as P

NX = 4096
NY = 2048
XB = 64
YB = 64
ITERS = 2
XA = 64
YA = 32


PENALTY = 0.5
TV_WEIGHT = 0.25
PRECISE = lax.Precision.HIGHEST


def with_halo(block, sides, width):
    for axis, dim in sides:
        count = lax.axis_size(axis)
        forward = [(i, i + 1) for i in range(count - 1)]
        backward = [(target, source) for source, target in forward]
        low = lax.ppermute(
            lax.slice_in_dim(block, block.shape[dim] - width, None, axis=dim), axis, forward
        )
        high = lax.ppermute(lax.slice_in_dim(block, 0, width, axis=dim), axis, backward)
        block = jnp.concatenate([low, block, high], axis=dim)
    return block


def from_behind(block, axis, distance):
    devices = range(lax.axis_size(axis))
    route = [(i - distance, i) for i in devices if i - distance in devices]
    return lax.ppermute(block, axis, route)


def unit_table(length):
    counter = jnp.arange(length, dtype=jnp.int32)
    phase_int = counter[:, None] * counter[None, :] % length
    angles = 2.0 * jnp.pi / length * phase_int.astype(jnp.float32)
    factor = length ** (-0.5)
    return (jnp.cos(angles) * factor, jnp.sin(angles) * factor)


def twiddle_table(row_len, col_len, period):
    phase_int = (
        jnp.arange(row_len, dtype=jnp.int32)[:, None]
        * jnp.arange(col_len, dtype=jnp.int32)[None, :]
        % period
    )
    angles = 2.0 * jnp.pi / period * phase_int.astype(jnp.float32)
    return (jnp.cos(angles), jnp.sin(angles))


def split_parts(packed):
    half_width = packed.shape[-1] // 2
    return (packed[..., :half_width], packed[..., half_width:])


def join_parts(real_part, imag_part):
    return jnp.concatenate([real_part, imag_part], axis=-1)


def complex_contract(packed, cos_table, sin_table, subscripts, conj_sign):
    cos_out = jnp.einsum(subscripts, packed, cos_table, precision=PRECISE)
    sin_out = jnp.einsum(subscripts, packed, sin_table, precision=PRECISE)
    cos_re, cos_im = split_parts(cos_out)
    sin_re, sin_im = split_parts(sin_out)
    return join_parts(cos_re - conj_sign * sin_im, cos_im + conj_sign * sin_re)


def rotate(packed, cos_table, sin_table, conj_sign):
    real_part, imag_part = split_parts(packed)
    return join_parts(
        real_part * cos_table - conj_sign * imag_part * sin_table,
        imag_part * cos_table + conj_sign * real_part * sin_table,
    )


def forward_x(volume):
    slices, row_count = (volume.shape[0], volume.shape[1])
    cos_a, sin_a = unit_table(XA)
    cos_b, sin_b = unit_table(XB)
    first_table = jnp.concatenate([cos_a, -sin_a], axis=1)
    grid_view = volume.reshape(slices, row_count, XA, XB)
    mixing = jnp.einsum("zyab,am->zybm", grid_view, first_table, precision=PRECISE)
    tw_cos, tw_sin = twiddle_table(XB, XA, NX)
    mixing = rotate(mixing, tw_cos, tw_sin, -1.0)
    return complex_contract(mixing, cos_b, sin_b, "zybm,bl->zlym", -1.0)


def inverse_x(packed):
    slices, row_count = (packed.shape[0], packed.shape[2])
    cos_a, sin_a = unit_table(XA)
    cos_b, sin_b = unit_table(XB)
    mixing = complex_contract(packed, cos_b, sin_b, "zlym,lb->zybm", 1.0)
    tw_cos, tw_sin = twiddle_table(XB, XA, NX)
    mixing = rotate(mixing, tw_cos, tw_sin, 1.0)
    last_table = jnp.concatenate([cos_a, -sin_a], axis=0)
    grid_view = jnp.einsum("zybm,ma->zyab", mixing, last_table, precision=PRECISE)
    return grid_view.reshape(slices, row_count, NX)


def forward_y(packed):
    slices, blocks, width = (packed.shape[0], packed.shape[1], packed.shape[3])
    cos_a, sin_a = unit_table(YA)
    cos_b, sin_b = unit_table(YB)
    grid_view = packed.reshape(slices, blocks, YA, YB, width)
    mixing = complex_contract(grid_view, cos_a, sin_a, "zjcdm,ck->zjkdm", -1.0)
    tw_cos, tw_sin = twiddle_table(YA, YB, NY)
    mixing = rotate(mixing, tw_cos[:, :, None], tw_sin[:, :, None], -1.0)
    result = complex_contract(mixing, cos_b, sin_b, "zjkdm,dl->zjlkm", -1.0)
    return result.reshape(slices, blocks, NY, width)


def inverse_y(packed):
    slices, blocks, width = (packed.shape[0], packed.shape[1], packed.shape[3])
    cos_a, sin_a = unit_table(YA)
    cos_b, sin_b = unit_table(YB)
    grid_view = packed.reshape(slices, blocks, YB, YA, width)
    mixing = complex_contract(grid_view, cos_b, sin_b, "zjlkm,ld->zjkdm", 1.0)
    tw_cos, tw_sin = twiddle_table(YA, YB, NY)
    mixing = rotate(mixing, tw_cos[:, :, None], tw_sin[:, :, None], 1.0)
    result = complex_contract(mixing, cos_a, sin_a, "zjkdm,kc->zjcdm", 1.0)
    return result.reshape(slices, blocks, NY, width)


def tilt_coefficients(band_offset, interp_weight, first_block, blocks):
    offsets = lax.dynamic_slice_in_dim(band_offset.reshape(XB, XA), first_block, blocks, 0)
    weights = lax.dynamic_slice_in_dim(interp_weight.reshape(2, XB, XA), first_block, blocks, 1)
    lower_tap = (jnp.concatenate([offsets, offsets], axis=1) < 0)[:, None, :]
    first_weight = jnp.concatenate([weights[0], weights[0]], axis=1)[:, None, :]
    second_weight = jnp.concatenate([weights[1], weights[1]], axis=1)[:, None, :]
    return (lower_tap, first_weight, second_weight)


def tilt(field_in, coefficients, adjoint):
    lower_tap, first_weight, second_weight = coefficients
    padded = with_halo(field_in, (("gz", 0),), 1)
    below_rim = padded[:-2]
    middle = padded[1:-1]
    above_rim = padded[2:]
    if adjoint:
        return jnp.where(
            lower_tap,
            first_weight * above_rim + second_weight * middle,
            first_weight * middle + second_weight * below_rim,
        )
    return jnp.where(
        lower_tap,
        first_weight * below_rim + second_weight * middle,
        first_weight * middle + second_weight * above_rim,
    )


def to_pencil(slab_part):
    return lax.all_to_all(slab_part, "gy", split_axis=1, concat_axis=2, tiled=True)


def to_slab(pencil_part):
    return lax.all_to_all(pencil_part, "gy", split_axis=2, concat_axis=1, tiled=True)


def back_project(packed, pencil_coef):
    return inverse_x(to_slab(inverse_y(tilt(packed, pencil_coef, True))))


def edge_masks(slices, row_count):
    z_global = lax.axis_index("gz") * slices + jnp.arange(slices, dtype=jnp.int32)
    y_global = lax.axis_index("gy") * row_count + jnp.arange(row_count, dtype=jnp.int32)
    keep_z = (z_global < slices * lax.axis_size("gz") - 1).astype(jnp.float32)[:, None, None]
    keep_y = (y_global < row_count * lax.axis_size("gy") - 1).astype(jnp.float32)[None, :, None]
    return (keep_z, keep_y)


def forward_diff(field_in, keep_z, keep_y):
    slices, row_count = (field_in.shape[0], field_in.shape[1])
    next_z = from_behind(field_in, "gz", -1)
    next_y = from_behind(field_in[:, :1], "gy", -1)
    along_z = (jnp.concatenate([field_in[1:], next_z], axis=0) - field_in) * keep_z
    along_y = (jnp.concatenate([field_in[:, 1:], next_y], axis=1) - field_in) * keep_y
    zero_col = jnp.zeros((slices, row_count, 1), jnp.float32)
    along_x = jnp.concatenate([field_in[:, :, 1:] - field_in[:, :, :-1], zero_col], axis=2)
    return jnp.stack([along_z, along_y, along_x])


def transpose_diff(components, keep_z, keep_y):
    slices, row_count = (components.shape[1], components.shape[2])
    zero_col = jnp.zeros((slices, row_count, 1), jnp.float32)
    comp_z = components[0] * keep_z
    comp_y = components[1] * keep_y
    comp_x = jnp.concatenate([components[2][:, :, :-1], zero_col], axis=2)
    prev_z = from_behind(comp_z, "gz", 1)
    prev_y = from_behind(comp_y[:, -1:], "gy", 1)
    result = jnp.concatenate([prev_z, comp_z[:-1]], axis=0) - comp_z
    result = result + jnp.concatenate([prev_y, comp_y[:, :-1]], axis=1) - comp_y
    result = result + jnp.concatenate([zero_col, comp_x[:, :, :-1]], axis=2) - comp_x
    return result


def shards(data, band_offset, interp_weight):
    slices = data.shape[0]
    blocks = data.shape[1]
    width = data.shape[3]
    row_count = NY // lax.axis_size("gy")
    slab_coef = tilt_coefficients(band_offset, interp_weight, 0, XB)
    pencil_coef = tilt_coefficients(
        band_offset, interp_weight, lax.axis_index("gy") * blocks, blocks
    )
    keep_z, keep_y = edge_masks(slices, row_count)
    measured = data.astype(jnp.float32)
    volume = jnp.zeros((slices, row_count, NX), jnp.float32)
    grad_volume = jnp.zeros((3, slices, row_count, NX), jnp.float32)
    split_var = grad_volume
    dual_var = grad_volume
    data_back = back_project(measured, pencil_coef)
    normal_part = jnp.zeros_like(volume)
    tilted = jnp.zeros((slices, XB, row_count, width), jnp.float32)
    for iteration in range(ITERS):
        data_grad = normal_part - data_back
        if iteration > 0:
            tv_gap = grad_volume - split_var + dual_var / PENALTY
            descent = data_grad + PENALTY * transpose_diff(tv_gap, keep_z, keep_y)
        else:
            descent = data_grad
        slope_field = forward_diff(descent, keep_z, keep_y)
        projected = tilt(forward_x(descent), slab_coef, False)
        line_totals = lax.psum(
            (
                jnp.sum(descent * descent),
                jnp.sum(projected * projected),
                jnp.sum(slope_field * slope_field),
            ),
            ("gz", "gy"),
        )
        step_length = line_totals[0] / (line_totals[1] + PENALTY * line_totals[2])
        volume = volume - step_length * descent
        grad_volume = grad_volume - step_length * slope_field
        tilted = tilted - step_length * projected
        if iteration + 1 < ITERS:
            normal_part = normal_part - step_length * inverse_x(tilt(projected, slab_coef, True))
        if iteration + 1 < ITERS:
            shifted = grad_volume + dual_var / PENALTY
            split_var = shifted - jnp.clip(shifted, -TV_WEIGHT / PENALTY, TV_WEIGHT / PENALTY)
            dual_var = PENALTY * (grad_volume - split_var)
    residual = forward_y(to_pencil(tilted)) - measured
    return (volume, residual)


def solution(mesh):
    in_specs = (P("gz", "gy", None, None), P(), P())
    out_specs = (P("gz", "gy", None), P("gz", "gy", None, None))
    return jax.shard_map(shards, mesh=mesh, in_specs=in_specs, out_specs=out_specs, check_vma=False)
```

profile of v0, /device:TPU:14, one launch (start us, length us, event | category | flops | bytes accessed | tf_op | source)
XLA Modules:
  0.0 636.3 jit_solution(3766947406622630724)
XLA Ops:
  6.0 7.0 %collective-permute-start.1 = (f32[1,4,2048,128]{3,2,1,0:T(8,128)}, f32[1,4,2048,128]{3,2,1,0:T(8,128)}, u32[]{:S(2)}, u32[]{:S(2)}) collective-permute-start(f32[1,4,2048,128]{3,2,1,0:T(8,128)} %convert_element_type.136), channel_id=1, source_target_pairs={{0,16},{1,17},{2,18},{3,19},{4,20},{5,21},{6,22},{7,23},{8,24},{9,... | collective-permute-start | bytes 12582920 | tf_op jit(solution)/shard_map/ppermute | solution.py:25
  22.7 6.3 fusion.30
  29.0 6.5 %fusion.33 = f32[1,4,32,64,128]{4,3,2,1,0:T(8,128)S(1)} fusion(f32[4,64,32,128]{3,2,1,0:T(8,128)S(1)} %bitcast.225), kind=kOutput, calls=%fused_computation.83 | convolution fusion | flops 805367808 | bytes 8388608 | tf_op jit(solution)/shard_map/zjlkm,ld->zjkdm/dot_general | solution.py:68
  39.8 6.2 fusion.36
  46.0 7.1 %fusion.39 = f32[1,4,32,64,128]{4,2,3,1,0:T(8,128)} fusion(f32[4,32,64,128]{3,2,1,0:T(8,128)S(1)} %maximum_bitcast_fusion), kind=kOutput, calls=%fused_computation.85 | convolution fusion | flops 402668544 | bytes 8388608 | tf_op jit(solution)/shard_map/zjkdm,kc->zjcdm/dot_general | solution.py:68
  53.1 9.0 %slice_subtract_fusion.2 = (f32[1,4,32,64,64]{4,2,3,1,0:T(8,128)}, f32[1,4,32,64,64]{4,2,3,1,0:T(8,128)}) fusion(f32[1,4,32,64,128]{4,2,3,1,0:T(8,128)} %fusion.39, f32[1,4,32,64,128]{4,2,3,1,0:T(8,128)S(1)} %fusion.36), kind=kLoop, calls=%fused_computation.27 | loop fusion | flops 1048576 | bytes 12582912 | tf_op jit(solution)/shard_map/sub | solution.py:71
  62.1 4.6 pad_maximum_fusion.1
  69.2 10.0 %copy.84 = f32[1,4,2048,128]{3,1,0,2:T(4,128)} copy(f32[1,4,2048,128]{3,2,1,0:T(8,128)S(1)} %bitcast.233) | data formatting | bytes 8388608 | tf_op jit(solution)/shard_map/reshape | solution.py:127
  79.1 7.7 %all-to-all-start = ((f32[1,4,2048,128]{3,1,0,2:T(4,128)}), f32[1,4,2048,128]{3,1,0,2:T(4,128)}, u32[]{:S(2)}, u32[]{:S(2)}) async-start(f32[1,4,2048,128]{3,1,0,2:T(4,128)} %copy.84), calls=%async_computation | async-start | bytes 8388608 | tf_op jit(solution)/shard_map/all_to_all | solution.py:163
  87.7 94.7 %all-to-all-done = f32[1,4,2048,128]{3,1,0,2:T(4,128)} async-done(((f32[1,4,2048,128]{3,1,0,2:T(4,128)}), f32[1,4,2048,128]{3,1,0,2:T(4,128)}, u32[]{:S(2)}, u32[]{:S(2)}) %all-to-all-start) | async-done | bytes 4194336 | tf_op jit(solution)/shard_map/all_to_all | solution.py:163
  200.6 7.2 %multiply_reduce_fusion.4 = (f32[]{:T(128)}, f32[64,128,64]{1,0,2:T(8,128)S(1)}) fusion(f32[128,64,128]{2,1,0:T(8,128)S(1)} %maximum_bitcast_fusion.1, f32[64,64]{0,1:T(8,128)S(1)} %get-tuple-element.59, f32[64,64]{0,1:T(8,128)S(1)} %get-tuple-element.58), kind=kOutput, calls=%fused_computation.124 | convolution fusion | flops 806887424 | bytes 6324228 | tf_op jit(solution)/shard_map/zybm,ma->zyab/dot_general | solution.py:102
  215.5 6.7 %convolution_bitcast_fusion.7 = f32[1,128,64,128]{3,2,1,0:T(8,128)S(1)} fusion(f32[128,64,64]{1,2,0:T(8,128)} %copy.117, f32[64,64]{0,1:T(8,128)S(1)} %get-tuple-element.59, f32[64,64]{0,1:T(8,128)S(1)} %get-tuple-element.58), kind=kOutput, calls=%fused_computation.95 | convolution fusion | flops 805314560 | bytes 6324224 | tf_op jit(solution)/shard_map/zyab,am->zybm/dot_general | solution.py:88
  224.0 4.8 convolution_bitcast_fusion.6
  228.8 4.8 convolution_bitcast_fusion.5
  253.6 7.6 %multiply_reduce_fusion.2 = (f32[]{:T(128)}, f32[1,64,128,128]{3,1,2,0:T(8,128)}) fusion(f32[1,64,128,128]{3,1,2,0:T(8,128)} %collective-permute-done.3, f32[64,128]{1,0:T(8,128)S(1)} %get-tuple-element.61, f32[1,64,128,128]{3,1,2,0:T(8,128)} %collective-permute-done.2, f32[64,128]{1,0:T(8,128)S(1)} %get-tuple-element.60, ...), kind=kLoop, calls=%fused_computation.61 | loop fusion | flops 10485759 | bytes 16850948 | tf_op jit(solution)/shard_map/reduce_sum | solution.py:233
  262.5 9.9 %collective-permute-start.7 = (f32[1,64,128,128]{3,1,2,0:T(8,128)}, f32[1,64,128,128]{3,1,2,0:T(8,128)}, u32[]{:S(2)}, u32[]{:S(2)}) collective-permute-start(f32[1,64,128,128]{3,1,2,0:T(8,128)} %get-tuple-element.21), channel_id=1, source_target_pairs={{0,16},{1,17},{2,18},{3,19},{4,20},{5,21},{6,22},{7,23},{8,24},{9,... | collective-permute-start | bytes 12582920 | tf_op jit(solution)/shard_map/ppermute | solution.py:25
  285.4 40.2 %all-reduce.4 = (f32[]{:T(128)}, f32[]{:T(128)}, f32[]{:T(128)}) all-reduce(f32[]{:T(128)} %get-tuple-element.52, f32[]{:T(128)} %get-tuple-element.20, f32[]{:T(128)} %multiply_reduce_fusion), channel_id=1, replica_groups=mesh['gz'=2,'gy'=16] {'gz','gy'}, use_global_device_ids=true, to_apply=%region_1.2 | all-reduce | flops 3 | bytes 24 | tf_op jit(solution)/shard_map/psum | solution.py:230
  348.8 6.2 add_select_fusion.1
  368.3 6.6 %subtract_bitcast_fusion = f32[1,128,64,64]{1,2,3,0:T(8,128)S(1)} fusion(f32[64,128,64]{1,0,2:T(8,128)S(1)} %copy-done.16, f32[128,64,128]{2,1,0:T(8,128)S(1)} %maximum_bitcast_fusion.3, f32[]{:T(128)S(6)} %div.7, f32[64,64]{0,1:T(8,128)S(1)} %get-tuple-element.59, f32[64,64]{0,1:T(8,128)S(1)} %get-tuple-element.58), kind=kOutput, calls=%fused_computation.117 | convolution fusion | flops 806887424 | bytes 8421380 | tf_op jit(solution)/shard_map/zybm,ma->zyab/dot_general | solution.py:102
  377.6 4.9 multiply_reduce_fusion.3
  382.5 4.6 copy.120
  387.0 6.9 %convolution_bitcast_fusion.4 = f32[1,128,64,128]{3,2,1,0:T(8,128)S(1)} fusion(f32[128,64,64]{1,2,0:T(8,128)} %copy.120, f32[64,64]{0,1:T(8,128)S(1)} %get-tuple-element.59, f32[64,64]{0,1:T(8,128)S(1)} %get-tuple-element.58), kind=kOutput, calls=%fused_computation.92 | convolution fusion | flops 805314560 | bytes 6324224 | tf_op jit(solution)/shard_map/zyab,am->zybm/dot_general | solution.py:88
  395.7 4.8 convolution_bitcast_fusion.3
  400.5 4.8 convolution_bitcast_fusion.2
  434.5 6.4 %multiply_reduce_fusion.1 = (f32[]{:T(128)}, f32[1,64,128,128]{3,1,2,0:T(8,128)}) fusion(f32[1,64,128,128]{3,1,2,0:T(8,128)} %collective-permute-done.11, f32[64,128]{1,0:T(8,128)S(1)} %get-tuple-element.61, f32[1,64,128,128]{3,1,2,0:T(8,128)} %collective-permute-done.10, f32[64,128]{1,0:T(8,128)S(1)} %get-tuple-element.60, ...), kind=kLoop, calls=%fused_computation.54 | loop fusion | flops 10485759 | bytes 16850948 | tf_op jit(solution)/shard_map/reduce_sum | solution.py:233
  440.9 44.4 %all-reduce.3 = (f32[]{:T(128)}, f32[]{:T(128)}, f32[]{:T(128)}) all-reduce(f32[]{:T(128)} %get-tuple-element.18, f32[]{:T(128)} %get-tuple-element.16, f32[]{:T(128)} %fusion.1), channel_id=1, replica_groups=mesh['gz'=2,'gy'=16] {'gz','gy'}, use_global_device_ids=true, to_apply=%region_7.8 | all-reduce | flops 3 | bytes 24 | tf_op jit(solution)/shard_map/psum | solution.py:230
  496.1 6.1 all-to-all-start.1
  508.6 86.2 %all-to-all-done.1 = f32[1,64,128,128]{3,2,0,1:T(8,128)} async-done(((f32[1,64,128,128]{3,2,0,1:T(8,128)}), f32[1,64,128,128]{3,2,0,1:T(8,128)}, u32[]{:S(2)}, u32[]{:S(2)}) %all-to-all-start.1) | async-done | bytes 4194336 | tf_op jit(solution)/shard_map/all_to_all | solution.py:159
  597.3 5.9 fusion.18
  603.2 6.3 fusion.20
  617.7 4.8 convolution_bitcast_fusion.1
  622.5 4.8 convolution_bitcast_fusion
  (165 shorter events, 186.8 us)
Async XLA Ops:
  0.6 17.5 %copy-start.9 = (bf16[1,4,2048,128]{3,2,1,0:T(8,128)(2,1)S(1)}, bf16[1,4,2048,128]{3,2,1,0:T(8,128)(2,1)}, u32[]{:S(2)}) copy-start(bf16[1,4,2048,128]{3,2,1,0:T(8,128)(2,1)} %param.3) | copy-start | bytes 6291460
  0.6 12.3 %copy-start.25 = (f32[2,4096]{1,0:T(2,128)S(1)}, f32[2,4096]{1,0:T(2,128)}, u32[]{:S(2)}) copy-start(f32[2,4096]{1,0:T(2,128)} %param.5) | copy-start | bytes 98308
  0.7 12.4 %copy-start.26 = (s32[4096]{0:T(1024)S(1)}, s32[4096]{0:T(1024)}, u32[]{:S(2)}) copy-start(s32[4096]{0:T(1024)} %param.4) | copy-start | bytes 49156
  4.7 9.4 %collective-permute-start = (f32[1,4,2048,128]{3,2,1,0:T(8,128)}, f32[1,4,2048,128]{3,2,1,0:T(8,128)}, u32[]{:S(2)}, u32[]{:S(2)}) collective-permute-start(f32[1,4,2048,128]{3,2,1,0:T(8,128)} %convert_element_type.136), channel_id=1, source_target_pairs={{16,0},{17,1},{18,2},{19,3},{20,4},{21,5},{22,6},{23,7},{24,8},{25... | collective-permute-start | bytes 12582920 | tf_op jit(solution)/shard_map/ppermute | solution.py:28
  6.0 12.2 %collective-permute-start.1 = (f32[1,4,2048,128]{3,2,1,0:T(8,128)}, f32[1,4,2048,128]{3,2,1,0:T(8,128)}, u32[]{:S(2)}, u32[]{:S(2)}) collective-permute-start(f32[1,4,2048,128]{3,2,1,0:T(8,128)} %convert_element_type.136), channel_id=1, source_target_pairs={{0,16},{1,17},{2,18},{3,19},{4,20},{5,21},{6,22},{7,23},{8,24},{9,... | collective-permute-start | bytes 12582920 | tf_op jit(solution)/shard_map/ppermute | solution.py:25
  13.4 22.0 %copy-start.23 = (f32[32,64]{1,0:T(8,128)}, f32[32,64]{1,0:T(8,128)S(1)}, u32[]{:S(2)}) copy-start(f32[32,64]{1,0:T(8,128)S(1)} %get-tuple-element.57) | copy-start | bytes 24580
  79.1 103.3 %all-to-all-start = ((f32[1,4,2048,128]{3,1,0,2:T(4,128)}), f32[1,4,2048,128]{3,1,0,2:T(4,128)}, u32[]{:S(2)}, u32[]{:S(2)}) async-start(f32[1,4,2048,128]{3,1,0,2:T(4,128)} %copy.84), calls=%async_computation | async-start | bytes 8388608 | tf_op jit(solution)/shard_map/all_to_all | solution.py:163
  236.4 4.5 copy-start.4
  240.9 12.2 %collective-permute-start.2 = (f32[1,64,128,128]{3,1,2,0:T(8,128)}, f32[1,64,128,128]{3,1,2,0:T(8,128)}, u32[]{:S(2)}, u32[]{:S(2)}) collective-permute-start(f32[1,64,128,128]{3,1,2,0:T(8,128)} %pad_maximum_fusion.2), channel_id=1, source_target_pairs={{0,16},{1,17},{2,18},{3,19},{4,20},{5,21},{6,22},{7,23},{8,24},{9,... | collective-permute-start | bytes 12582920 | tf_op jit(solution)/shard_map/ppermute | solution.py:25
  244.2 9.4 %collective-permute-start.3 = (f32[1,64,128,128]{3,1,2,0:T(8,128)}, f32[1,64,128,128]{3,1,2,0:T(8,128)}, u32[]{:S(2)}, u32[]{:S(2)}) collective-permute-start(f32[1,64,128,128]{3,1,2,0:T(8,128)} %pad_maximum_fusion.2), channel_id=1, source_target_pairs={{16,0},{17,1},{18,2},{19,3},{20,4},{21,5},{22,6},{23,7},{24,8},{25... | collective-permute-start | bytes 12582920 | tf_op jit(solution)/shard_map/ppermute | solution.py:28
  248.7 29.1 %copy-start = (f32[1,128,64,64]{1,3,2,0:T(8,128)}, f32[1,128,64,64]{1,3,2,0:T(8,128)S(1)}, u32[]{:S(2)}) copy-start(f32[1,128,64,64]{1,3,2,0:T(8,128)S(1)} %copy.93) | copy-start | bytes 6291460
  248.7 29.1 %collective-permute-start.4 = (f32[1,128,4096]{1,2,0:T(8,128)S(1)}, f32[1,128,4096]{1,2,0:T(8,128)}, u32[]{:S(2)}, u32[]{:S(2)}) collective-permute-start(f32[1,128,4096]{1,2,0:T(8,128)S(1)} %bitcast.218), channel_id=1, source_target_pairs={{16,0},{17,1},{18,2},{19,3},{20,4},{21,5},{22,6},{23,7},{24,8},{25... | collective-permute-start | bytes 6291464 | tf_op jit(solution)/shard_map/ppermute | solution.py:36
  250.6 25.2 %collective-permute-start.5 = (f32[1,1,4096]{2,1,0:T(1,128)S(1)}, f32[1,1,4096]{2,1,0:T(1,128)S(1)}, u32[]{:S(2)}, u32[]{:S(2)}) collective-permute-start(f32[1,1,4096]{2,1,0:T(1,128)S(1)} %copy.94), channel_id=1, source_target_pairs={{1,0},{2,1},{3,2},{4,3},{5,4},{6,5},{7,6},{8,7},{9,8},{10,9},{11,1... | collective-permute-start | bytes 49160 | tf_op jit(solution)/shard_map/ppermute | solution.py:36
  261.2 87.5 %collective-permute-start.6 = (f32[1,64,128,128]{3,1,2,0:T(8,128)}, f32[1,64,128,128]{3,1,2,0:T(8,128)}, u32[]{:S(2)}, u32[]{:S(2)}) collective-permute-start(f32[1,64,128,128]{3,1,2,0:T(8,128)} %get-tuple-element.21), channel_id=1, source_target_pairs={{16,0},{17,1},{18,2},{19,3},{20,4},{21,5},{22,6},{23,7},{24,8},{25... | collective-permute-start | bytes 12582920 | tf_op jit(solution)/shard_map/ppermute | solution.py:28
  262.5 86.2 %collective-permute-start.7 = (f32[1,64,128,128]{3,1,2,0:T(8,128)}, f32[1,64,128,128]{3,1,2,0:T(8,128)}, u32[]{:S(2)}, u32[]{:S(2)}) collective-permute-start(f32[1,64,128,128]{3,1,2,0:T(8,128)} %get-tuple-element.21), channel_id=1, source_target_pairs={{0,16},{1,17},{2,18},{3,19},{4,20},{5,21},{6,22},{7,23},{8,24},{9,... | collective-permute-start | bytes 12582920 | tf_op jit(solution)/shard_map/ppermute | solution.py:25
  277.8 5.4 copy-start.13
  281.9 45.6 %copy-start.14 = (f32[1,1,128,4096]{2,3,1,0:T(8,128)S(1)}, f32[1,1,128,4096]{2,3,1,0:T(8,128)}, u32[]{:S(2)}) copy-start(f32[1,1,128,4096]{2,3,1,0:T(8,128)} %pad_bitcast_fusion.1) | copy-start | bytes 6291460
  333.1 12.0 %copy-start.17 = (f32[1,128,4096]{1,2,0:T(8,128)}, f32[1,128,4096]{1,2,0:T(8,128)S(1)}, u32[]{:S(2)}) copy-start(f32[1,128,4096]{1,2,0:T(8,128)S(1)} %fusion.48) | copy-start | bytes 6291460
  337.4 9.4 %collective-permute-start.9 = (f32[1,1,4096]{2,1,0:T(1,128)S(1)}, f32[1,1,4096]{2,1,0:T(1,128)S(1)}, u32[]{:S(2)}, u32[]{:S(2)}) collective-permute-start(f32[1,1,4096]{2,1,0:T(1,128)S(1)} %copy.98), channel_id=1, source_target_pairs={{0,1},{1,2},{2,3},{3,4},{4,5},{5,6},{6,7},{7,8},{8,9},{9,10},{10,1... | collective-permute-start | bytes 49160 | tf_op jit(solution)/shard_map/ppermute | solution.py:36
  345.2 31.0 %collective-permute-start.8 = (f32[1,128,4096]{1,2,0:T(8,128)}, f32[1,128,4096]{1,2,0:T(8,128)S(1)}, u32[]{:S(2)}, u32[]{:S(2)}) collective-permute-start(f32[1,128,4096]{1,2,0:T(8,128)} %get-tuple-element.38), channel_id=1, source_target_pairs={{0,16},{1,17},{2,18},{3,19},{4,20},{5,21},{6,22},{7,23},{8,24},{9,... | collective-permute-start | bytes 6291464 | tf_op jit(solution)/shard_map/ppermute | solution.py:36
  366.7 10.8 %slice-start = ((s8[6291456]{0:T(1024)(128)(4,1)}), s8[2097152]{0:T(1024)(128)(4,1)S(1)}, s32[]{:S(2)}) async-start(s8[6291456]{0:T(1024)(128)(4,1)} %bitcast.222), calls=%async_computation.2 | async-start | bytes 4194304
  368.3 9.2 %slice-start.1 = ((s8[6291456]{0:T(1024)(128)(4,1)}), s8[4194304]{0:T(1024)(128)(4,1)S(1)}, s32[]{:S(2)}) async-start(s8[6291456]{0:T(1024)(128)(4,1)} %bitcast.222), calls=%async_computation.3 | async-start | bytes 8388608
  368.3 9.2 %copy-start.21 = (f32[1,128,4096]{1,2,0:T(8,128)S(1)}, f32[1,128,4096]{1,2,0:T(8,128)}, u32[]{:S(2)}) copy-start(f32[1,128,4096]{1,2,0:T(8,128)} %get-tuple-element.39) | copy-start | bytes 6291460
  407.8 3.7 copy-start.5
  407.9 4.5 copy-start.7
  412.4 21.9 %collective-permute-start.10 = (f32[1,64,128,128]{3,1,2,0:T(8,128)}, f32[1,64,128,128]{3,1,2,0:T(8,128)}, u32[]{:S(2)}, u32[]{:S(2)}) collective-permute-start(f32[1,64,128,128]{3,1,2,0:T(8,128)} %pad_maximum_fusion.3), channel_id=1, source_target_pairs={{0,16},{1,17},{2,18},{3,19},{4,20},{5,21},{6,22},{7,23},{8,24},{9,... | collective-permute-start | bytes 12582920 | tf_op jit(solution)/shard_map/ppermute | solution.py:25
  415.7 18.6 %collective-permute-start.11 = (f32[1,64,128,128]{3,1,2,0:T(8,128)}, f32[1,64,128,128]{3,1,2,0:T(8,128)}, u32[]{:S(2)}, u32[]{:S(2)}) collective-permute-start(f32[1,64,128,128]{3,1,2,0:T(8,128)} %pad_maximum_fusion.3), channel_id=1, source_target_pairs={{16,0},{17,1},{18,2},{19,3},{20,4},{21,5},{22,6},{23,7},{24,8},{25... | collective-permute-start | bytes 12582920 | tf_op jit(solution)/shard_map/ppermute | solution.py:28
  417.0 11.3 %collective-permute-start.12 = (f32[1,128,4096]{1,2,0:T(8,128)S(1)}, f32[1,128,4096]{1,2,0:T(8,128)}, u32[]{:S(2)}, u32[]{:S(2)}) collective-permute-start(f32[1,128,4096]{1,2,0:T(8,128)S(1)} %get-tuple-element.19), channel_id=1, source_target_pairs={{16,0},{17,1},{18,2},{19,3},{20,4},{21,5},{22,6},{23,7},{24,8},{25... | collective-permute-start | bytes 6291464 | tf_op jit(solution)/shard_map/ppermute | solution.py:36
  418.9 7.4 %collective-permute-start.13 = (f32[1,1,4096]{2,1,0:T(1,128)S(1)}, f32[1,1,4096]{2,1,0:T(1,128)S(1)}, u32[]{:S(2)}, u32[]{:S(2)}) collective-permute-start(f32[1,1,4096]{2,1,0:T(1,128)S(1)} %copy.103), channel_id=1, source_target_pairs={{1,0},{2,1},{3,2},{4,3},{5,4},{6,5},{7,6},{8,7},{9,8},{10,9},{11,1... | collective-permute-start | bytes 49160 | tf_op jit(solution)/shard_map/ppermute | solution.py:36
  428.3 3.6 copy-start.19
  428.3 5.9 copy-start.8
  496.1 98.7 %all-to-all-start.1 = ((f32[1,64,128,128]{3,2,0,1:T(8,128)}), f32[1,64,128,128]{3,2,0,1:T(8,128)}, u32[]{:S(2)}, u32[]{:S(2)}) async-start(f32[1,64,128,128]{3,2,0,1:T(8,128)} %copy.105), calls=%async_computation.1 | async-start | bytes 8388608 | tf_op jit(solution)/shard_map/all_to_all | solution.py:159
  (14 other events, 33.7 us)
where the time goes:
time: 646 us; the launch traced here: 636 us
  waiting for transfers between devices  187 us (29%)
  other arithmetic  117 us (18%)
  matrix products  111 us (17%)
  blocking collectives  84.6 us (13%)
  local copies, waits for them, and re-layouts  75.7 us (12%)
  starting transfers between devices  54.7 us (8%)
    all_to_all x1, waiting for transfers between devices, to_slab(): lax.all_to_all(pencil_part, 'gy', split_axis=2, concat_axis=1, tiled=True)  94.7 us
    all_to_all x1, waiting for transfers between devices, to_pencil(): lax.all_to_all(slab_part, 'gy', split_axis=1, concat_axis=2, tiled=True)  86.2 us
    psum x2, blocking collectives, shards(): lax.psum((jnp.sum(descent * descent), jnp.sum(projected * projected), jnp...  84.6 us
    dot_general x8, matrix products, complex_contract(): sin_out = jnp.einsum(subscripts, packed, sin_table, precision=PRECISE)  42.3 us
    dot_general x8, matrix products, complex_contract(): cos_out = jnp.einsum(subscripts, packed, cos_table, precision=PRECISE)  41.6 us
    ppermute x4, starting transfers between devices, with_halo(): lax.ppermute(lax.slice_in_dim(block, block.shape[dim] - width, None, axis...  23.5 us
    sub x4, other arithmetic, complex_contract(): return join_parts(cos_re - conj_sign * sin_im, cos_im + conj_sign * sin_re)  16.8 us
    sub x6, other arithmetic, rotate(): real_part * cos_table - conj_sign * imag_part * sin_table  16.6 us
  transfers between devices with their start and end apart: 16, of which 6 were waited for; matrix products, arithmetic and copies ran while one was open for 13% of the time, Pallas kernels for 0%

commit v1 on v0

--- a/solution.py
+++ b/solution.py
@@ -1,7 +1,697 @@
+import functools
+
 import jax
 import jax.numpy as jnp
+import numpy as np
 from jax import lax
+from jax.experimental import pallas as pl
+from jax.experimental.pallas import tpu as pltpu
 from jax.sharding import PartitionSpec as P
+
+PENALTY = 0.5
+TV_WEIGHT = 0.25
+CLIP = TV_WEIGHT / PENALTY
+HALF = 64
+YR = 8
+LANES = 128
+F32 = jnp.float32
+BF16 = jnp.bfloat16
+VMEM_LIMIT = 48 * 1024 * 1024
+
+
+def dft_parts(length, scale):
+    index = np.arange(length)
+    angles = 2.0 * np.pi / length * (index[:, None] * index[None, :] % length)
+    return np.cos(angles) * scale, np.sin(angles) * scale
+
+
+def two_parts(table):
+    table = jnp.asarray(table.astype(np.float32))
+    high = table.astype(BF16)
+    low = (table - high.astype(F32)).astype(BF16)
+    return high, low
+
+
+def host_parts(table):
+    table = table.astype(np.float32)
+    high = table.astype(BF16)
+    low = (table - high.astype(np.float32)).astype(BF16)
+    return high, low
+
+
+def y_matrix(ny, forward, sign):
+    n = ny // YR
+    cos, sin = dft_parts(n, sign * ny**-0.5)
+    if forward:
+        table = np.block([[cos, sin], [-sin, cos]])
+    else:
+        table = np.block([[cos, -sin], [sin, cos]])
+    return jnp.asarray(np.concatenate(host_parts(table), axis=0))
+
+
+def y_twiddle(ny):
+    n = ny // YR
+    angles = 2.0 * np.pi / ny * (np.arange(YR)[:, None] * np.arange(n)[None, :])
+    table = np.stack([np.cos(angles), np.sin(angles)]).astype(np.float32)
+    return jnp.asarray(np.ascontiguousarray(np.broadcast_to(table[..., None], (2, YR, n, LANES))))
+
+
+def x_inverse_matrix(nx, ka):
+    cos, sin = dft_parts(ka, nx**-0.5)
+    return jnp.asarray(np.concatenate(host_parts(np.concatenate([cos, -sin], axis=0)), axis=1))
+
+
+def x_forward_matrix(nx, ka):
+    cos, sin = dft_parts(ka, nx**-0.5)
+    return jnp.asarray(np.concatenate(host_parts(np.concatenate([cos, -sin], axis=1)), axis=1))
+
+
+def x_twiddle(nx, ka):
+    kb = nx // ka
+    angles = 2.0 * np.pi / nx * (np.arange(kb)[:, None] * np.arange(ka)[None, :])
+    table = np.stack([np.cos(angles), np.sin(angles)]).astype(np.float32)
+    return jnp.asarray(np.ascontiguousarray(np.broadcast_to(table[:, :, None], (2, kb, 8, ka))))
+
+
+def short_fft(planes, sign):
+    n = len(planes)
+    if n == 1:
+        return planes
+    even = short_fft(planes[0::2], sign)
+    odd = short_fft(planes[1::2], sign)
+    half = n // 2
+    out = [None] * n
+    for k in range(half):
+        er, ei = even[k]
+        tr, ti = odd[k]
+        if 4 * k == n:
+            if sign > 0:
+                out[k] = (er - ti, ei + tr)
+                out[k + half] = (er + ti, ei - tr)
+            else:
+                out[k] = (er + ti, ei - tr)
+                out[k + half] = (er - ti, ei + tr)
+            continue
+        if k > 0:
+            c = float(np.cos(2.0 * np.pi * k / n))
+            s = float(sign * np.sin(2.0 * np.pi * k / n))
+            if 8 * k == n:
+                tr, ti = (tr - ti, ti + tr) if sign > 0 else (tr + ti, ti - tr)
+                tr, ti = tr * c, ti * c
+            elif 8 * k == 3 * n:
+                m = float(np.sin(2.0 * np.pi * k / n))
+                tr, ti = (-(tr + ti), tr - ti) if sign > 0 else (ti - tr, -(tr + ti))
+                tr, ti = tr * m, ti * m
+            else:
+                tr, ti = tr * c - ti * s, ti * c + tr * s
+        out[k] = (er + tr, ei + ti)
+        out[k + half] = (er - tr, ei - ti)
+    return out
+
+
+def split2(x):
+    high = x.astype(BF16)
+    return high, (x - high.astype(F32)).astype(BF16)
+
+
+def dot(a, b):
+    return jnp.dot(a, b, preferred_element_type=F32)
+
+
+def fold(x):
+    rows, lanes = x.shape
+    x = jnp.sum(x.reshape(rows // 8, 8, lanes), axis=0)
+    total = x[:, :LANES]
+    for i in range(1, lanes // LANES):
+        total = total + x[:, i * LANES : (i + 1) * LANES]
+    return total
+
+
+def full_sum(x):
+    return jnp.sum(jnp.sum(x, axis=0, keepdims=True), axis=1, keepdims=True)
+
+
+def step_of(sums_ref):
+    total = jnp.sum(sums_ref[...], axis=0)
+    parts = jnp.sum(total, axis=1, keepdims=True)
+    return parts[0:1] / (parts[1:2] + PENALTY * parts[2:3])
+
+
+def put_sums(out_ref, values):
+    rows = [jnp.sum(v, axis=0, keepdims=True) for v in values]
+    index = lax.broadcasted_iota(jnp.int32, (8, LANES), 0)
+    block = jnp.zeros((8, LANES), F32)
+    for i, row in enumerate(rows):
+        block = jnp.where(index == i, jnp.broadcast_to(row, (8, LANES)), block)
+    for i in range(out_ref.shape[0]):
+        out_ref[i] = block
+
+
+def mix_adjoint(coef, planes):
+    own, below, above = coef
+    out = []
+    for z in range(len(planes)):
+        value = own * planes[z]
+        if z + 1 < len(planes):
+            value = value + below * planes[z + 1]
+        if z > 0:
+            value = value + above * planes[z - 1]
+        out.append(value)
+    return out
+
+
+def mix(coef, planes):
+    own, below, above = coef
+    out = []
+    for z in range(len(planes)):
+        value = own * planes[z]
+        if z > 0:
+            value = value + below * planes[z - 1]
+        if z + 1 < len(planes):
+            value = value + above * planes[z + 1]
+        out.append(value)
+    return out
+
+
+def y_inverse_kernel(rows, gz, data_ref, table_ref, tw_ref, out_ref, re_s, im_s, mix_s):
+    ny = data_ref.shape[1]
+    n = ny // YR
+    gy = out_ref.shape[0] // gz
+    lane = lax.broadcasted_iota(jnp.int32, (n, LANES), 1)
+
+    def unpack(i, carry):
+        part = pl.ds(pl.multiple_of(i * n, n), n)
+        first = data_ref[0, part, :].astype(F32)
+        second = data_ref[1, part, :].astype(F32)
+        re_s[part, :] = jnp.where(lane < HALF, first, pltpu.roll(second, HALF, 1))
+        im_s[part, :] = jnp.where(lane < HALF, pltpu.roll(first, HALF, 1), second)
+        return carry
+
+    lax.fori_loop(0, YR, unpack, 0)
+
+    table = table_ref[...]
+    for k in range(0, YR, 2):
+        pieces = [
+            jnp.concatenate([s[pl.ds(k + d, n, stride=YR), :] for d in range(2)], axis=1)
+            for s in (re_s, im_s)
+        ]
+        both = dot(table, jnp.concatenate(pieces, axis=0).astype(BF16))
+        both = both[: 2 * n] + both[2 * n :]
+        for d in range(2):
+            mix_s[k + d] = both[:, d * LANES : (d + 1) * LANES]
+
+    def combine(i, carry):
+        start = pl.multiple_of(i * 8, 8)
+        part = pl.ds(start, 8)
+        planes = []
+        for k in range(YR):
+            re = mix_s[k, part, :]
+            im = mix_s[k, pl.ds(pl.multiple_of(n + i * 8, 8), 8), :]
+            if k > 0:
+                c = tw_ref[0, k, part, :]
+                s = tw_ref[1, k, part, :]
+                re, im = re * c - im * s, im * c + re * s
+            planes.append((re, im))
+        for k, (re, im) in enumerate(short_fft(planes, 1)):
+            y = k * n + start
+            flat = y // rows
+            to = (flat % gz) * gy + flat // gz
+            at = pl.ds(pl.multiple_of(y % rows, 8), 8)
+            out_ref[to, 0, at, :] = re
+            out_ref[to, 1, at, :] = im
+        return carry
+
+    lax.fori_loop(0, n // 8, combine, 0, unroll=2)
+
+
+def y_inverse(data, rows, gz, gy):
+    blocks, ny, width = data.shape
+    n = ny // YR
+    return pl.pallas_call(
+        functools.partial(y_inverse_kernel, rows, gz),
+        grid=(blocks // 2,),
+        in_specs=[
+            pl.BlockSpec((2, ny, width), lambda c: (c, 0, 0)),
+            pl.BlockSpec((4 * n, 2 * n), lambda c: (0, 0)),
+            pl.BlockSpec((2, YR, n, LANES), lambda c: (0, 0, 0, 0)),
+        ],
+        out_specs=pl.BlockSpec((gz * gy, 2, rows, LANES), lambda c: (0, 0, 0, c)),
+        out_shape=jax.ShapeDtypeStruct((gz * gy, 2, rows, blocks * HALF), F32),
+        scratch_shapes=[
+            pltpu.VMEM((ny, LANES), F32),
+            pltpu.VMEM((ny, LANES), F32),
+            pltpu.VMEM((YR, 2 * n, LANES), F32),
+        ],
+        compiler_params=pltpu.CompilerParams(vmem_limit_bytes=VMEM_LIMIT),
+        name="y_inverse",
+    )(data, y_matrix(ny, False, -1.0), y_twiddle(ny))
+
+
+def y_forward_kernel(gz, spec_ref, data_ref, table_ref, tw_ref, out_ref, re_s, im_s, mix_s):
+    ny = data_ref.shape[1]
+    n = ny // YR
+    peers, _, rows, _ = spec_ref.shape
+    gy = peers // gz
+
+    def unpack(i, carry):
+        part = pl.ds(pl.multiple_of(i * rows, rows), rows)
+        source = (i % gz) * gy + i // gz
+        re_s[part, :] = spec_ref[source, 0]
+        im_s[part, :] = spec_ref[source, 1]
+        return carry
+
+    lax.fori_loop(0, peers, unpack, 0)
+
+    table = table_ref[...]
+    for k in range(0, YR, 2):
+        pieces = [
+            jnp.concatenate([s[pl.ds(k + d, n, stride=YR), :] for d in range(2)], axis=1)
+            for s in (re_s, im_s)
+        ]
+        high, low = split2(jnp.concatenate(pieces, axis=0))
+        both = dot(table, high)
+        both = both[: 2 * n] + both[2 * n :] + dot(table[: 2 * n], low)
+        for d in range(2):
+            mix_s[k + d] = both[:, d * LANES : (d + 1) * LANES]
+
+    lane = lax.broadcasted_iota(jnp.int32, (16, LANES), 1)
+
+    def combine(i, carry):
+        start = pl.multiple_of(i * 16, 16)
+        part = pl.ds(start, 16)
+        planes = []
+        for k in range(YR):
+            re = mix_s[k, part, :]
+            im = mix_s[k, pl.ds(pl.multiple_of(n + i * 16, 16), 16), :]
+            if k > 0:
+                c = tw_ref[0, k, part, :]
+                s = tw_ref[1, k, part, :]
+                re, im = re * c + im * s, im * c - re * s
+            planes.append((re, im))
+        for k, (re, im) in enumerate(short_fft(planes, -1)):
+            at = pl.ds(pl.multiple_of(k * n + start, 16), 16)
+            first = jnp.where(lane < HALF, re, pltpu.roll(im, HALF, 1))
+            second = jnp.where(lane < HALF, pltpu.roll(re, HALF, 1), im)
+            out_ref[0, at, :] = first - data_ref[0, at, :].astype(F32)
+            out_ref[1, at, :] = second - data_ref[1, at, :].astype(F32)
+        return carry
+
+    lax.fori_loop(0, n // 16, combine, 0)
+
+
+def y_forward(spec, data, gz):
+    blocks, ny, width = data.shape
+    peers, _, rows, _ = spec.shape
+    n = ny // YR
+    return pl.pallas_call(
+        functools.partial(y_forward_kernel, gz),
+        grid=(blocks // 2,),
+        in_specs=[
+            pl.BlockSpec((peers, 2, rows, LANES), lambda c: (0, 0, 0, c)),
+            pl.BlockSpec((2, ny, width), lambda c: (c, 0, 0)),
+            pl.BlockSpec((4 * n, 2 * n), lambda c: (0, 0)),
+            pl.BlockSpec((2, YR, n, LANES), lambda c: (0, 0, 0, 0)),
+        ],
+        out_specs=pl.BlockSpec((2, ny, width), lambda c: (c, 0, 0)),
+        out_shape=jax.ShapeDtypeStruct((blocks, ny, width), F32),
+        scratch_shapes=[
+            pltpu.VMEM((ny, LANES), F32),
+            pltpu.VMEM((ny, LANES), F32),
+            pltpu.VMEM((YR, 2 * n, LANES), F32),
+        ],
+        compiler_params=pltpu.CompilerParams(vmem_limit_bytes=VMEM_LIMIT),
+        name="y_forward",
+    )(spec, data, y_matrix(ny, True, 1.0), y_twiddle(ny))
+
+
+def plane_chunk(planes, rows):
+    chunk = max(1, 512 // rows)
+    while planes % chunk:
+        chunk -= 1
+    return chunk
+
+
+def x_inverse_kernel(zs, spec_ref, coef_ref, tw_ref, table_ref, out_ref, head_ref, tail_ref, re_s, im_s):
+    planes, _, rows, ka = spec_ref.shape
+    kb = planes // zs
+
+    def columns(i, carry):
+        part = pl.ds(pl.multiple_of(i * 8, 8), 8)
+        for start in range(0, ka, LANES):
+            lanes = slice(start, start + LANES)
+            mixed = [[None] * kb for _ in range(zs)]
+            for k in range(kb):
+                coef = [coef_ref[j, k, :, lanes] for j in range(3)]
+                re = mix_adjoint(coef, [spec_ref[z * kb + k, 0, part, lanes] for z in range(zs)])
+                im = mix_adjoint(coef, [spec_ref[z * kb + k, 1, part, lanes] for z in range(zs)])
+                for z in range(zs):
+                    mixed[z][k] = (re[z], im[z])
+            for z in range(zs):
+                for b, (re, im) in enumerate(short_fft(mixed[z], 1)):
+                    if b > 0:
+                        c = tw_ref[0, b, :, lanes]
+                        s = tw_ref[1, b, :, lanes]
+                        re, im = re * c - im * s, im * c + re * s
+                    re_s[z * kb + b, part, lanes] = re
+                    im_s[z * kb + b, part, lanes] = im
+        return carry
+
+    lax.fori_loop(0, rows // 8, columns, 0)
+
+    chunk = plane_chunk(planes, rows)
+
+    def multiply(i, carry):
+        part = pl.ds(i * chunk, chunk)
+        both = jnp.concatenate(
+            [re_s[part].reshape(chunk * rows, ka), im_s[part].reshape(chunk * rows, ka)], axis=1
+        )
+        high, low = split2(both)
+        value = dot(high, table_ref[...])
+        value = value[:, :ka] + value[:, ka:] + dot(low, table_ref[:, :ka])
+        out_ref[part] = value.reshape(chunk, rows, ka)
+        return carry
+
+    lax.fori_loop(0, planes // chunk, multiply, 0)
+
+    for p in range(planes):
+        for r in range(head_ref.shape[0]):
+            head_ref[r, p : p + 1, :] = out_ref[p, r : r + 1, :]
+        tail_ref[p : p + 1, :] = out_ref[p, rows - 1 : rows, :]
+
+
+def x_inverse(spec, coef, zs, nx):
+    planes, _, rows, ka = spec.shape
+    vmem = pl.BlockSpec(memory_space=pltpu.VMEM)
+    return pl.pallas_call(
+        functools.partial(x_inverse_kernel, zs),
+        in_specs=[vmem] * 4,
+        out_specs=[vmem] * 3,
+        out_shape=[
+            jax.ShapeDtypeStruct((planes, rows, ka), F32),
+            jax.ShapeDtypeStruct((2, planes, ka), F32),
+            jax.ShapeDtypeStruct((planes, ka), F32),
+        ],
+        scratch_shapes=[pltpu.VMEM((planes, rows, ka), F32)] * 2,
+        compiler_params=pltpu.CompilerParams(vmem_limit_bytes=VMEM_LIMIT),
+        name="x_inverse",
+    )(spec, coef, x_twiddle(nx, ka), x_inverse_matrix(nx, ka))
+
+
+def forward_into(zs, field_ref, coef_ref, tw_ref, table_ref, spec_ref, re_s, im_s):
+    planes, rows, ka = field_ref.shape
+    kb = planes // zs
+    chunk = plane_chunk(planes, rows)
+
+    def multiply(i, carry):
+        part = pl.ds(i * chunk, chunk)
+        high, low = split2(field_ref[part].reshape(chunk * rows, ka))
+        value = dot(high, table_ref[...])
+        value = value[:, : 2 * ka] + value[:, 2 * ka :] + dot(low, table_ref[:, : 2 * ka])
+        re_s[part] = value[:, :ka].reshape(chunk, rows, ka)
+        im_s[part] = value[:, ka:].reshape(chunk, rows, ka)
+        return carry
+
+    lax.fori_loop(0, planes // chunk, multiply, 0)
+
+    def columns(i, total):
+        part = pl.ds(pl.multiple_of(i * 8, 8), 8)
+        for start in range(0, ka, LANES):
+            lanes = slice(start, start + LANES)
+            spectra = []
+            for z in range(zs):
+                turned = []
+                for b in range(kb):
+                    re = re_s[z * kb + b, part, lanes]
+                    im = im_s[z * kb + b, part, lanes]
+                    if b > 0:
+                        c = tw_ref[0, b, :, lanes]
+                        s = tw_ref[1, b, :, lanes]
+                        re, im = re * c + im * s, im * c - re * s
+                    turned.append((re, im))
+                spectra.append(short_fft(turned, -1))
+            for k in range(kb):
+                coef = [coef_ref[j, k, :, lanes] for j in range(3)]
+                for p in range(2):
+                    for z, value in enumerate(mix(coef, [spectra[z][k][p] for z in range(zs)])):
+                        spec_ref[z * kb + k, p, part, lanes] = value
+                        total = total + value * value
+        return total
+
+    return lax.fori_loop(0, rows // 8, columns, jnp.zeros((8, LANES), F32))
+
+
+def next_plane(field_ref, p, kb):
+    rows, ka = field_ref.shape[1:]
+    if (p + 1) % kb:
+        return field_ref[p + 1]
+    lane = lax.broadcasted_iota(jnp.int32, (rows, ka), 1)
+    return jnp.where(lane == ka - 1, field_ref[p], pltpu.roll(field_ref[p + 1 - kb], ka - 1, 1))
+
+
+def prev_plane(field_ref, p, kb):
+    rows, ka = field_ref.shape[1:]
+    if p % kb:
+        return field_ref[p - 1]
+    lane = lax.broadcasted_iota(jnp.int32, (rows, ka), 1)
+    return jnp.where(lane == 0, field_ref[p], pltpu.roll(field_ref[p + kb - 1], 1, 1))
+
+
+def first_kernel(zs, field_ref, coef_ref, tw_ref, table_ref, spec_ref, sums_ref, re_s, im_s):
+    planes, rows, ka = field_ref.shape
+    kb = planes // zs
+    projected = forward_into(zs, field_ref, coef_ref, tw_ref, table_ref, spec_ref, re_s, im_s)
+    row = lax.broadcasted_iota(jnp.int32, (rows, ka), 0)
+    square = jnp.zeros((8, LANES), F32)
+    slope = jnp.zeros((8, LANES), F32)
+    for p in range(planes):
+        here = field_ref[p]
+        square = square + fold(here * here)
+        along_x = next_plane(field_ref, p, kb) - here
+        along_y = jnp.where(row == rows - 1, 0.0, pltpu.roll(here, rows - 1, 0) - here)
+        terms = along_x * along_x + along_y * along_y
+        if p + kb < planes:
+            along_z = field_ref[p + kb] - here
+            terms = terms + along_z * along_z
+        slope = slope + fold(terms)
+    sums_ref[0] = square
+    sums_ref[1] = projected
+    sums_ref[2] = slope
+
+
+def first_projection(field, coef, zs, nx):
+    planes, rows, ka = field.shape
+    vmem = pl.BlockSpec(memory_space=pltpu.VMEM)
+    return pl.pallas_call(
+        functools.partial(first_kernel, zs),
+        in_specs=[vmem] * 4,
+        out_specs=[vmem] * 2,
+        out_shape=[
+            jax.ShapeDtypeStruct((planes, 2, rows, ka), F32),
+            jax.ShapeDtypeStruct((3, 8, LANES), F32),
+        ],
+        scratch_shapes=[pltpu.VMEM((planes, rows, ka), F32)] * 2,
+        compiler_params=pltpu.CompilerParams(vmem_limit_bytes=VMEM_LIMIT),
+        name="first_projection",
+    )(field, coef, x_twiddle(nx, ka), x_forward_matrix(nx, ka))
+
+
+def border_kernel(edge_ref, sums_ref, tail_ref, next_ref, out_ref):
+    step = (next_ref[0] - tail_ref[...]) * jnp.where(edge_ref[1] > 0, 0.0, 1.0)
+    put_sums(out_ref, [sums_ref[0], sums_ref[1], sums_ref[2] + fold(step * step)])
+
+
+def border_sums(edge, sums, tail, next_head, devices):
+    vmem = pl.BlockSpec(memory_space=pltpu.VMEM)
+    return pl.pallas_call(
+        border_kernel,
+        in_specs=[pl.BlockSpec(memory_space=pltpu.SMEM)] + [vmem] * 3,
+        out_specs=vmem,
+        out_shape=jax.ShapeDtypeStruct((devices, 8, LANES), F32),
+        name="border_sums",
+    )(edge, sums, tail, next_head)
+
+
+def second_kernel(
+    zs, edge_ref, sums_ref, d0_ref, nd0_ref, tail_ref, prev_ref, next_ref, nnext_ref,
+    coef_ref, tw_ref, table_ref, d1_ref, spec_ref, eta_ref, out_ref, re_s, im_s, row_s,
+):
+    planes, rows, ka = d0_ref.shape
+    kb = planes // zs
+    eta_here = step_of(sums_ref)
+    eta_ref[...] = jnp.broadcast_to(eta_here, (8, LANES))
+    eta = jnp.max(eta_here)
+    first = edge_ref[0] > 0
+    last = edge_ref[1] > 0
+
+    def shrink(difference):
+        return jnp.clip(-eta * difference, -CLIP, CLIP)
+
+    lane2 = lax.broadcasted_iota(jnp.int32, (kb, ka), 1)
+    row2 = lax.broadcasted_iota(jnp.int32, (kb, ka), 0)
+    for z in range(zs):
+        part = slice(z * kb, (z + 1) * kb)
+        here = next_ref[0, part, :]
+        value = here - eta * nnext_ref[0, part, :]
+        up = pltpu.roll(here, kb - 1, 0)
+        up = jnp.where(
+            row2 == kb - 1, jnp.where(lane2 == ka - 1, here, pltpu.roll(up, ka - 1, 1)), up
+        )
+        down = pltpu.roll(here, 1, 0)
+        down = jnp.where(row2 == 0, jnp.where(lane2 == 0, here, pltpu.roll(down, 1, 1)), down)
+        value = value + shrink(here - down) - shrink(up - here)
+        value = value + shrink(here - tail_ref[part, :]) - shrink(next_ref[1, part, :] - here)
+        if z > 0:
+            value = value + shrink(here - next_ref[0, (z - 1) * kb : z * kb, :])
+        if z + 1 < zs:
+            value = value - shrink(next_ref[0, (z + 1) * kb : (z + 2) * kb, :] - here)
+        row_s[part, :] = value
+
+    row = lax.broadcasted_iota(jnp.int32, (rows, ka), 0)
+    square = jnp.zeros((8, LANES), F32)
+    for p in range(planes):
+        here = d0_ref[p]
+        value = here - eta * nd0_ref[p]
+        value = value + shrink(here - prev_plane(d0_ref, p, kb))
+        value = value - shrink(next_plane(d0_ref, p, kb) - here)
+        below = jnp.where(last, here[rows - 1 :, :], next_ref[0, p : p + 1, :])
+        above = jnp.where(first, here[:1, :], prev_ref[p : p + 1, :])
+        upper = shrink(jnp.where(row == rows - 1, below, pltpu.roll(here, rows - 1, 0)) - here)
+        lower = jnp.where(row == 0, shrink(here[:1, :] - above), pltpu.roll(upper, 1, 0))
+        value = value + lower - upper
+        if p >= kb:
+            value = value + shrink(here - d0_ref[p - kb])
+        if p + kb < planes:
+            value = value - shrink(d0_ref[p + kb] - here)
+        d1_ref[p] = value
+        square = square + fold(value * value)
+
+    slope = jnp.zeros((8, LANES), F32)
+    for p in range(planes):
+        here = d1_ref[p]
+        along_x = next_plane(d1_ref, p, kb) - here
+        below = jnp.where(last, here[rows - 1 :, :], row_s[p : p + 1, :])
+        along_y = jnp.where(row == rows - 1, below, pltpu.roll(here, rows - 1, 0)) - here
+        terms = along_x * along_x + along_y * along_y
+        if p + kb < planes:
+            along_z = d1_ref[p + kb] - here
+            terms = terms + along_z * along_z
+        slope = slope + fold(terms)
+
+    projected = forward_into(zs, d1_ref, coef_ref, tw_ref, table_ref, spec_ref, re_s, im_s)
+    put_sums(out_ref, [square, projected, slope])
+
+
+def second_descent(edge, sums, d0, nd0, tail, prev_tail, next_head, next_nhead, coef, zs, nx):
+    planes, rows, ka = d0.shape
+    devices = sums.shape[0]
+    vmem = pl.BlockSpec(memory_space=pltpu.VMEM)
+    return pl.pallas_call(
+        functools.partial(second_kernel, zs),
+        in_specs=[pl.BlockSpec(memory_space=pltpu.SMEM)] + [vmem] * 10,
+        out_specs=[vmem] * 4,
+        out_shape=[
+            jax.ShapeDtypeStruct((planes, rows, ka), F32),
+            jax.ShapeDtypeStruct((planes, 2, rows, ka), F32),
+            jax.ShapeDtypeStruct((8, LANES), F32),
+            jax.ShapeDtypeStruct((devices, 8, LANES), F32),
+        ],
+        scratch_shapes=[
+            pltpu.VMEM((planes, rows, ka), F32),
+            pltpu.VMEM((planes, rows, ka), F32),
+            pltpu.VMEM((planes, ka), F32),
+        ],
+        compiler_params=pltpu.CompilerParams(vmem_limit_bytes=VMEM_LIMIT),
+        name="second_descent",
+    )(
+        edge, sums, d0, nd0, tail, prev_tail, next_head, next_nhead, coef,
+        x_twiddle(nx, ka), x_forward_matrix(nx, ka),
+    )
+
+
+def combine_kernel(sums_ref, eta_ref, first_ref, second_ref, out_ref, steps_ref):
+    eta0 = jnp.max(eta_ref[...])
+    eta1 = jnp.max(step_of(sums_ref))
+    out_ref[...] = -(eta0 * first_ref[...] + eta1 * second_ref[...])
+    steps_ref[0] = eta_ref[...]
+    steps_ref[1] = jnp.full((8, LANES), eta1, F32)
+
+
+def combine_spectra(sums, eta, first, second):
+    planes, parts, rows, ka = first.shape
+    devices = sums.shape[0]
+    count = 4 if planes % 4 == 0 else 1
+    block = pl.BlockSpec((count, parts, rows, ka), lambda i: (i, 0, 0, 0))
+    return pl.pallas_call(
+        combine_kernel,
+        grid=(planes // count,),
+        in_specs=[
+            pl.BlockSpec((devices, 8, LANES), lambda i: (0, 0, 0)),
+            pl.BlockSpec((8, LANES), lambda i: (0, 0)),
+            block,
+            block,
+        ],
+        out_specs=[block, pl.BlockSpec((2, 8, LANES), lambda i: (0, 0, 0))],
+        out_shape=[
+            jax.ShapeDtypeStruct(first.shape, F32),
+            jax.ShapeDtypeStruct((2, 8, LANES), F32),
+        ],
+        name="combine_spectra",
+    )(sums, eta, first, second)
+
+
+def everywhere(sums):
+    return lax.all_to_all(sums, ("gz", "gy"), 0, 0, tiled=True)
+
+
+def shards(data, band_offset, interp_weight):
+    gz = lax.axis_size("gz")
+    gy = lax.axis_size("gy")
+    devices = gz * gy
+    data = data[0]
+    blocks, ny, width = data.shape
+    rows = ny // devices
+    ka = blocks * HALF
+    nx = ka * gy
+
+    flat = lax.axis_index("gy") * gz + lax.axis_index("gz")
+    edge = jnp.stack([(flat == 0).astype(jnp.int32), (flat == devices - 1).astype(jnp.int32)])
+    order = [(i % gz) * gy + i // gz for i in range(devices)]
+    up = [(order[i + 1], order[i]) for i in range(devices - 1)]
+    down = [(order[i], order[i + 1]) for i in range(devices - 1)]
+
+    lower = band_offset < 0
+    weight = interp_weight
+    coef = jnp.stack(
+        [
+            jnp.where(lower, weight[1], weight[0]),
+            jnp.where(lower, weight[0], 0.0),
+            jnp.where(lower, 0.0, weight[1]),
+        ]
+    ).reshape(3, gy, 1, ka)
+    coef = jnp.broadcast_to(coef, (3, gy, 8, ka))
+
+    spec = y_inverse(data, rows, gz, gy)
+    spec = lax.all_to_all(spec, ("gz", "gy"), 0, 0, tiled=True)
+    d0, head, tail = x_inverse(spec, coef, gz, nx)
+    next_head = lax.ppermute(head, ("gz", "gy"), up)
+    prev_tail = lax.ppermute(tail, ("gz", "gy"), down)
+    spec0, sums = first_projection(d0, coef, gz, nx)
+    sums = everywhere(border_sums(edge, sums, tail, next_head, devices))
+    nd0, nhead, _ = x_inverse(spec0, coef, gz, nx)
+    next_nhead = lax.ppermute(nhead, ("gz", "gy"), up)
+    d1, spec1, eta, sums = second_descent(
+        edge, sums, d0, nd0, tail, prev_tail, next_head, next_nhead, coef, gz, nx
+    )
+    sums = everywhere(sums)
+    spec, steps = combine_spectra(sums, eta, spec0, spec1)
+    spec = lax.all_to_all(spec, ("gz", "gy"), 0, 0, tiled=True)
+    residual = y_forward(spec, data, gz)
+
+    volume = -(steps[0, 0, 0] * d0 + steps[1, 0, 0] * d1)
+    volume = volume.reshape(gz, gy, rows, ka).transpose(0, 2, 3, 1).reshape(gz, rows, nx)
+    volume = lax.all_to_all(volume, "gz", 0, 1, tiled=True)
+    return (volume, residual[None])
+
 
 NX = 4096
 NY = 2048
@@ -10,10 +700,6 @@
 ITERS = 2
 XA = 64
 YA = 32
-
-
-PENALTY = 0.5
-TV_WEIGHT = 0.25
 PRECISE = lax.Precision.HIGHEST
 
 
@@ -200,7 +886,7 @@
     return result
 
 
-def shards(data, band_offset, interp_weight):
+def plain_shards(data, band_offset, interp_weight):
     slices = data.shape[0]
     blocks = data.shape[1]
     width = data.shape[3]
@@ -249,7 +935,20 @@
     return (volume, residual)
 
 
+def tiles_fit(mesh, ny, blocks):
+    rows = ny // (mesh.shape["gz"] * mesh.shape["gy"])
+    return rows % 16 == 0 and blocks // mesh.shape["gy"] % 2 == 0
+
+
 def solution(mesh):
     in_specs = (P("gz", "gy", None, None), P(), P())
     out_specs = (P("gz", "gy", None), P("gz", "gy", None, None))
-    return jax.shard_map(shards, mesh=mesh, in_specs=in_specs, out_specs=out_specs, check_vma=False)
+
+    def run(data, band_offset, interp_weight):
+        body = shards if tiles_fit(mesh, data.shape[2], data.shape[1]) else plain_shards
+        call = jax.shard_map(
+            body, mesh=mesh, in_specs=in_specs, out_specs=out_specs, check_vma=False
+        )
+        return call(data, band_offset, interp_weight)
+
+    return run

time: 646 us -> 334 us (0.52)
  the two profiles are of different devices: /device:TPU:14 before, /device:TPU:0 now
where the time goes in v1:
time: 334 us; the launch traced here: 333 us
  waiting for transfers between devices  193 us (58%)
  Pallas kernels  66.1 us (20%)
  blocking collectives  24 us (7%)
  local copies, waits for them, and re-layouts  23.7 us (7%)
  starting transfers between devices  20.3 us (6%)
  other arithmetic  5.14 us (2%)
    all_to_all x2, waiting for transfers between devices, shards(): spec = lax.all_to_all(spec, ('gz', 'gy'), 0, 0, tiled=True)  192 us
    all_to_all x1, blocking collectives, everywhere(): return lax.all_to_all(sums, ('gz', 'gy'), 0, 0, tiled=True)  17.7 us
    unnamed x49, local copies, waits for them, and re-layouts  14.7 us
    pallas_call x2, Pallas kernels, x_inverse(): pl.pallas_call(functools.partial(x_inverse_kernel, zs), in_specs=[vmem] *...  14.2 us
    pallas_call x1, Pallas kernels, y_inverse(): pl.pallas_call(functools.partial(y_inverse_kernel, rows, gz), grid=(block...  11.8 us
    pallas_call x1, Pallas kernels, y_forward(): pl.pallas_call(functools.partial(y_forward_kernel, gz), grid=(blocks // 2...  11.7 us
    pallas_call x1, Pallas kernels, second_descent(): pl.pallas_call(functools.partial(second_kernel, zs), in_specs=[pl.BlockSp...  11.5 us
    all_to_all x2, starting transfers between devices, shards(): spec = lax.all_to_all(spec, ('gz', 'gy'), 0, 0, tiled=True)  11.3 us
  transfers between devices with their start and end apart: 6, of which 3 were waited for; matrix products, arithmetic and copies ran while one was open for 0% of the time, Pallas kernels for 4%

profile of v1, /device:TPU:0, one launch (start us, length us, event | category | flops | bytes accessed | tf_op | source)
XLA Modules:
  0.0 333.2 jit_solution(323001817382935932)
XLA Ops:
  0.6 1.6 copy-done
  2.2 1.6 copy-done.2
  3.8 1.2 copy-done.10
  5.0 11.8 %y_inverse.1 = f32[32,2,64,256]{3,2,1,0:T(8,128)} custom-call(bf16[4,2048,128]{2,1,0:T(8,128)(2,1)S(1)} %bitcast.15, bf16[1024,512]{1,0:T(8,128)(2,1)S(1)} %copy-done.10, f32[2,8,256,128]{3,2,1,0:T(8,128)S(1)} %copy-done.2), custom_call_target="tpu_custom_call" | custom-call | tf_op jit(solution)/shard_map/y_inverse/pallas_call | solution.py:230
  16.9 7.4 %all-to-all-start = ((f32[32,2,64,256]{3,2,1,0:T(8,128)}), f32[32,2,64,256]{3,2,1,0:T(8,128)}, u32[]{:S(2)}, u32[]{:S(2)}) async-start(f32[32,2,64,256]{3,2,1,0:T(8,128)} %y_inverse.1), calls=%async_computation | async-start | bytes 8388608 | tf_op jit(solution)/shard_map/all_to_all | solution.py:674
  24.4 96.1 %all-to-all-done.spec_ref = f32[32,2,64,256]{3,2,1,0:T(8,128)} async-done(((f32[32,2,64,256]{3,2,1,0:T(8,128)}), f32[32,2,64,256]{3,2,1,0:T(8,128)}, u32[]{:S(2)}, u32[]{:S(2)}) %all-to-all-start) | async-done | bytes 4194336 | tf_op jit(solution)/shard_map/all_to_all | solution.py:674
  120.6 1.0 copy-done.8
  121.6 6.8 %x_inverse.2 = (f32[32,64,256]{2,1,0:T(8,128)S(1)}, f32[2,32,256]{2,1,0:T(8,128)S(1)}, f32[32,256]{1,0:T(8,128)S(1)}) custom-call(f32[32,2,64,256]{3,2,1,0:T(8,128)} %all-to-all-done.spec_ref, f32[3,16,8,256]{3,2,1,0:T(8,128)S(1)} %broadcast_in_dim.18.coef_ref, f32[2,16,8,256]{3,2,1,0:T(8,128)S(1)} %copy-done.4, bf16[512,512]{1,0:T(8,128)(2,1)S(1)} %copy-done.8), custom_call_target="tpu_custom_call" | custom-call | tf_op jit(solution)/shard_map/x_inverse/pallas_call | solution.py:385
  128.4 1.3 collective-permute-start
  130.4 6.9 %first_projection.1 = (f32[32,2,64,256]{3,2,1,0:T(8,128)}, f32[3,8,128]{2,1,0:T(8,128)S(1)}) custom-call(f32[32,64,256]{2,1,0:T(8,128)S(1)} %get-tuple-element.15.field_ref.d0_ref, f32[3,16,8,256]{3,2,1,0:T(8,128)S(1)} %broadcast_in_dim.18.coef_ref, f32[2,16,8,256]{3,2,1,0:T(8,128)S(1)} %copy-done.4, bf16[256,1024]{1,0:T(8,128)(2,1)S(1)} %copy-done.6), custom_call_target="tpu_custom_call" | custom-call | tf_op jit(solution)/shard_map/first_projection/pallas_call | solution.py:484
  138.5 1.6 border_sums.1
  140.1 3.4 %all-to-all-start.1 = ((f32[32,8,128]{2,1,0:T(8,128)}), f32[32,8,128]{2,1,0:T(8,128)S(1)}, u32[]{:S(2)}, u32[]{:S(2)}) async-start(f32[32,8,128]{2,1,0:T(8,128)} %border_sums.1), calls=%async_computation.1 | async-start | bytes 262144 | tf_op jit(solution)/shard_map/all_to_all | solution.py:643
  143.5 1.0 copy-done.9
  144.5 7.4 %x_inverse.3 = (f32[32,64,256]{2,1,0:T(8,128)S(1)}, f32[2,32,256]{2,1,0:T(8,128)S(1)}, f32[32,256]{1,0:T(8,128)}) custom-call(f32[32,2,64,256]{3,2,1,0:T(8,128)} %get-tuple-element.19.spec_ref.first_ref, f32[3,16,8,256]{3,2,1,0:T(8,128)S(1)} %broadcast_in_dim.18.coef_ref, f32[2,16,8,256]{3,2,1,0:T(8,128)S(1)} %copy-done.4, bf16[512,512]{1,0:T(8,128)(2,1)S(1)} %copy-done.9), custom_call_target="tpu_custom_call" | custom-call | tf_op jit(solution)/shard_map/x_inverse/pallas_call | solution.py:385
  151.9 1.3 copy-done.5
  153.2 1.3 collective-permute-start.2
  154.5 3.0 collective-permute-start.1
  157.6 0.8 collective-permute-done.1.prev_ref
  159.9 11.5 %second_descent.1 = (f32[32,64,256]{2,1,0:T(8,128)S(1)}, f32[32,2,64,256]{3,2,1,0:T(8,128)}, f32[8,128]{1,0:T(8,128)S(1)}, f32[32,8,128]{2,1,0:T(8,128)S(1)}) custom-call(s32[2]{0:T(128)S(1)} %copy-done.20, f32[32,8,128]{2,1,0:T(8,128)S(1)} %all-to-all-done.1.sums_ref, f32[32,64,256]{2,1,0:T(8,128)S(1)} %get-tuple-element.15.field_ref.d0_ref, ...), custom_call_target="tpu_custom_call" | custom-call | tf_op jit(solution)/shard_map/second_descent/pallas_call | solution.py:588
  171.3 1.3 copy-done.7
  172.7 17.7 %all_to_all.32.sums_ref = f32[32,8,128]{2,1,0:T(8,128)} all-to-all(f32[32,8,128]{2,1,0:T(8,128)S(1)} %get-tuple-element.22), channel_id=1, replica_groups=mesh['gz'=2,'gy'=16] {'gz','gy'}, dimensions={0} | all-to-all | bytes 262144 | tf_op jit(solution)/shard_map/all_to_all | solution.py:643
  190.3 8.4 %combine_spectra.1 = (f32[32,2,64,256]{3,2,1,0:T(8,128)}, f32[2,8,128]{2,1,0:T(8,128)}) custom-call(f32[32,8,128]{2,1,0:T(8,128)} %all_to_all.32.sums_ref, f32[8,128]{1,0:T(8,128)} %copy-done.19, f32[32,2,64,256]{3,2,1,0:T(8,128)} %get-tuple-element.19.spec_ref.first_ref, f32[32,2,64,256]{3,2,1,0:T(8,128)} %get-tuple-element.24.second_ref), custom_call_target="tpu_custom_call" | custom-call | tf_op jit(solution)/shard_map/combine_spectra/pallas_call | solution.py:624
  198.7 1.2 fusion.2
  199.9 4.5 %add_negate_fusion = f32[32,64,256]{2,1,0:T(8,128)} fusion(f32[32,64,256]{2,1,0:T(8,128)} %copy-done.7, f32[32,64,256]{2,1,0:T(8,128)S(1)} %get-tuple-element.15.field_ref.d0_ref, f32[]{:T(128)} %bitcast.7, f32[]{:T(128)} %bitcast.6), kind=kLoop, calls=%fused_computation | loop fusion | flops 2097152 | bytes 6291464 | tf_op jit(solution)/shard_map/neg | solution.py:690
  204.4 4.9 %copy.20 = f32[2,16,64,256]{2,1,3,0:T(8,128)} copy(f32[2,16,64,256]{3,2,1,0:T(8,128)} %bitcast.18) | data formatting | bytes 4194304 | tf_op jit(solution)/shard_map/reshape | solution.py:691
  209.3 2.8 copy.21
  212.1 6.3 %all_to_all.33 = f32[2,64,4096]{2,1,0:T(8,128)} all-to-all(f32[2,64,4096]{2,1,0:T(8,128)S(1)} %copy.21), channel_id=1, replica_groups=mesh['gz'=2,'gy'=16] {'gz'}, dimensions={0} | all-to-all | bytes 4194304 | tf_op jit(solution)/shard_map/all_to_all | solution.py:692
  218.4 3.9 %all-to-all-start.4 = ((f32[32,2,64,256]{3,2,1,0:T(8,128)}), f32[32,2,64,256]{3,2,1,0:T(8,128)}, u32[]{:S(2)}, u32[]{:S(2)}) async-start(f32[32,2,64,256]{3,2,1,0:T(8,128)} %get-tuple-element.27), calls=%async_computation.4 | async-start | bytes 8388608 | tf_op jit(solution)/shard_map/all_to_all | solution.py:687
  222.3 96.2 %all-to-all-done.4.spec_ref = f32[32,2,64,256]{3,2,1,0:T(8,128)} async-done(((f32[32,2,64,256]{3,2,1,0:T(8,128)}), f32[32,2,64,256]{3,2,1,0:T(8,128)}, u32[]{:S(2)}, u32[]{:S(2)}) %all-to-all-start.4) | async-done | bytes 4194336 | tf_op jit(solution)/shard_map/all_to_all | solution.py:687
  318.5 1.6 copy-done.3
  320.1 11.7 %y_forward.1 = f32[4,2048,128]{2,1,0:T(8,128)} custom-call(f32[32,2,64,256]{3,2,1,0:T(8,128)} %all-to-all-done.4.spec_ref, bf16[4,2048,128]{2,1,0:T(8,128)(2,1)S(1)} %bitcast.16, bf16[1024,512]{1,0:T(8,128)(2,1)S(1)} %copy-done.11, f32[2,8,256,128]{3,2,1,0:T(8,128)S(1)} %copy-done.3), custom_call_target="tpu_custom_call" | custom-call | tf_op jit(solution)/shard_map/y_forward/pallas_call | solution.py:306
  331.8 1.3 copy.23
  (52 shorter events, 3.5 us)
Async XLA Ops:
  0.6 1.6 copy-start
  2.2 1.6 copy-start.2
  3.8 1.2 copy-start.10
  16.9 7.5 %copy-start.22 = (f32[2,4096]{1,0:T(2,128)S(1)}, f32[2,4096]{1,0:T(2,128)}, u32[]{:S(2)}) copy-start(f32[2,4096]{1,0:T(2,128)} %param.17) | copy-start | bytes 98308
  16.9 7.5 %copy-start.23 = (s32[4096]{0:T(1024)S(1)}, s32[4096]{0:T(1024)}, u32[]{:S(2)}) copy-start(s32[4096]{0:T(1024)} %param.16) | copy-start | bytes 49156
  16.9 103.7 %copy-start.4 = (f32[2,16,8,256]{3,2,1,0:T(8,128)S(1)}, f32[2,16,8,256]{3,2,1,0:T(8,128)}, u32[]{:S(2)}) copy-start(f32[2,16,8,256]{3,2,1,0:T(8,128)} %constant.32.clone.tw_ref) | copy-start | bytes 786436
  16.9 103.7 %all-to-all-start = ((f32[32,2,64,256]{3,2,1,0:T(8,128)}), f32[32,2,64,256]{3,2,1,0:T(8,128)}, u32[]{:S(2)}, u32[]{:S(2)}) async-start(f32[32,2,64,256]{3,2,1,0:T(8,128)} %y_inverse.1), calls=%async_computation | async-start | bytes 8388608 | tf_op jit(solution)/shard_map/all_to_all | solution.py:674
  120.6 1.0 copy-start.8
  121.6 8.8 %copy-start.6 = (bf16[256,1024]{1,0:T(8,128)(2,1)S(1)}, bf16[256,1024]{1,0:T(8,128)(2,1)}, u32[]{:S(2)}) copy-start(bf16[256,1024]{1,0:T(8,128)(2,1)} %constant.34.clone.table_ref) | copy-start | bytes 1572868
  128.4 9.5 %copy-start.14 = (f32[32,256]{1,0:T(8,128)}, f32[32,256]{1,0:T(8,128)S(1)}, u32[]{:S(2)}) copy-start(f32[32,256]{1,0:T(8,128)S(1)} %get-tuple-element.17.tail_ref) | copy-start | bytes 98308
  128.4 9.5 %collective-permute-start = (f32[2,32,256]{2,1,0:T(8,128)S(1)}, f32[2,32,256]{2,1,0:T(8,128)S(1)}, u32[]{:S(2)}, u32[]{:S(2)}) collective-permute-start(f32[2,32,256]{2,1,0:T(8,128)S(1)} %get-tuple-element.18), channel_id=1, source_target_pairs={{16,0},{1,16},{17,1},{2,17},{18,2},{3,18},{19,3},{4,19},{20,4},{5,... | collective-permute-start | bytes 196616 | tf_op jit(solution)/shard_map/ppermute | solution.py:676
  137.3 0.6 copy-start.18
  137.9 0.6 copy-start.12
  140.1 19.0 %all-to-all-start.1 = ((f32[32,8,128]{2,1,0:T(8,128)}), f32[32,8,128]{2,1,0:T(8,128)S(1)}, u32[]{:S(2)}, u32[]{:S(2)}) async-start(f32[32,8,128]{2,1,0:T(8,128)} %border_sums.1), calls=%async_computation.1 | async-start | bytes 262144 | tf_op jit(solution)/shard_map/all_to_all | solution.py:643
  143.5 1.0 copy-start.9
  144.5 10.0 %copy-start.15 = (f32[32,256]{1,0:T(8,128)S(1)}, f32[32,256]{1,0:T(8,128)}, u32[]{:S(2)}) copy-start(f32[32,256]{1,0:T(8,128)} %copy-done.14) | copy-start | bytes 98308
  144.5 14.5 %copy-start.13 = (f32[2,32,256]{2,1,0:T(8,128)S(1)}, f32[2,32,256]{2,1,0:T(8,128)}, u32[]{:S(2)}) copy-start(f32[2,32,256]{2,1,0:T(8,128)} %copy-done.12) | copy-start | bytes 196612
  144.5 14.5 %copy-start.20 = (s32[2]{0:T(128)S(1)}, s32[2]{0:T(128)}, u32[]{:S(2)}) copy-start(s32[2]{0:T(128)} %add_convert_fusion.edge_ref) | copy-start | bytes 28
  151.9 1.3 copy-start.5
  153.2 5.2 %collective-permute-start.2 = (f32[2,32,256]{2,1,0:T(8,128)S(1)}, f32[2,32,256]{2,1,0:T(8,128)S(1)}, u32[]{:S(2)}, u32[]{:S(2)}) collective-permute-start(f32[2,32,256]{2,1,0:T(8,128)S(1)} %get-tuple-element.21), channel_id=1, source_target_pairs={{16,0},{1,16},{17,1},{2,17},{18,2},{3,18},{19,3},{4,19},{20,4},{5,... | collective-permute-start | bytes 196616 | tf_op jit(solution)/shard_map/ppermute | solution.py:681
  154.5 3.9 %collective-permute-start.1 = (f32[32,256]{1,0:T(8,128)S(1)}, f32[32,256]{1,0:T(8,128)S(1)}, u32[]{:S(2)}, u32[]{:S(2)}) collective-permute-start(f32[32,256]{1,0:T(8,128)S(1)} %copy-done.15), channel_id=1, source_target_pairs={{0,16},{16,1},{1,17},{17,2},{2,18},{18,3},{3,19},{19,4},{4,20},{20... | collective-permute-start | bytes 98312 | tf_op jit(solution)/shard_map/ppermute | solution.py:677
  158.4 0.6 copy-start.16
  159.0 0.8 copy-start.17
  171.3 1.3 copy-start.7
  172.7 17.7 %copy-start.19 = (f32[8,128]{1,0:T(8,128)}, f32[8,128]{1,0:T(8,128)S(1)}, u32[]{:S(2)}) copy-start(f32[8,128]{1,0:T(8,128)S(1)} %get-tuple-element.23.eta_ref) | copy-start | bytes 12292
  218.4 100.1 %copy-start.1 = (bf16[1,4,2048,128]{3,2,1,0:T(8,128)(2,1)S(1)}, bf16[1,4,2048,128]{3,2,1,0:T(8,128)(2,1)}, u32[]{:S(2)}) copy-start(bf16[1,4,2048,128]{3,2,1,0:T(8,128)(2,1)} %param.15) | copy-start | bytes 6291460
  218.4 100.1 %copy-start.11 = (bf16[1024,512]{1,0:T(8,128)(2,1)S(1)}, bf16[1024,512]{1,0:T(8,128)(2,1)}, u32[]{:S(2)}) copy-start(bf16[1024,512]{1,0:T(8,128)(2,1)} %constant.35.clone.table_ref) | copy-start | bytes 3145732
  218.4 100.1 %all-to-all-start.4 = ((f32[32,2,64,256]{3,2,1,0:T(8,128)}), f32[32,2,64,256]{3,2,1,0:T(8,128)}, u32[]{:S(2)}, u32[]{:S(2)}) async-start(f32[32,2,64,256]{3,2,1,0:T(8,128)} %get-tuple-element.27), calls=%async_computation.4 | async-start | bytes 8388608 | tf_op jit(solution)/shard_map/all_to_all | solution.py:687
  318.5 1.6 copy-start.3
  320.1 11.7 %copy-start.21 = (f32[2,64,4096]{2,1,0:T(8,128)S(1)}, f32[2,64,4096]{2,1,0:T(8,128)}, u32[]{:S(2)}) copy-start(f32[2,64,4096]{2,1,0:T(8,128)} %all_to_all.33) | copy-start | bytes 6291460

commit v2 on v1

--- a/solution.py
+++ b/solution.py
@@ -58,7 +58,7 @@
 
 def x_inverse_matrix(nx, ka):
     cos, sin = dft_parts(ka, nx**-0.5)
-    return jnp.asarray(np.concatenate(host_parts(np.concatenate([cos, -sin], axis=0)), axis=1))
+    return np.concatenate(host_parts(np.concatenate([cos, -sin], axis=0)), axis=1)
 
 
 def x_forward_matrix(nx, ka):
@@ -173,10 +173,11 @@
     return out
 
 
-def y_inverse_kernel(rows, gz, data_ref, table_ref, tw_ref, out_ref, re_s, im_s, mix_s):
+def y_inverse_kernel(gz, edge_ref, data_ref, table_ref, tw_ref, *refs):
+    out_refs, (re_s, im_s, mix_s) = refs[:gz], refs[gz:]
     ny = data_ref.shape[1]
     n = ny // YR
-    gy = out_ref.shape[0] // gz
+    rows = out_refs[0].shape[2]
     lane = lax.broadcasted_iota(jnp.int32, (n, LANES), 1)
 
     def unpack(i, carry):
@@ -200,67 +201,78 @@
         for d in range(2):
             mix_s[k + d] = both[:, d * LANES : (d + 1) * LANES]
 
-    def combine(i, carry):
-        start = pl.multiple_of(i * 8, 8)
-        part = pl.ds(start, 8)
-        planes = []
-        for k in range(YR):
-            re = mix_s[k, part, :]
-            im = mix_s[k, pl.ds(pl.multiple_of(n + i * 8, 8), 8), :]
-            if k > 0:
-                c = tw_ref[0, k, part, :]
-                s = tw_ref[1, k, part, :]
-                re, im = re * c - im * s, im * c + re * s
-            planes.append((re, im))
-        for k, (re, im) in enumerate(short_fft(planes, 1)):
-            y = k * n + start
-            flat = y // rows
-            to = (flat % gz) * gy + flat // gz
-            at = pl.ds(pl.multiple_of(y % rows, 8), 8)
-            out_ref[to, 0, at, :] = re
-            out_ref[to, 1, at, :] = im
-        return carry
-
-    lax.fori_loop(0, n // 8, combine, 0, unroll=2)
-
-
-def y_inverse(data, rows, gz, gy):
-    blocks, ny, width = data.shape
+    steps = rows // 8
+    for r in range(gz):
+        core = lax.rem(edge_ref[2] + r, gz)
+
+        def combine(i, carry):
+            y2 = ((i // steps) * gz + core) * rows + lax.rem(i, steps) * 8
+            part = pl.ds(pl.multiple_of(y2, 8), 8)
+            planes = []
+            for k in range(YR):
+                re = mix_s[k, part, :]
+                im = mix_s[k, pl.ds(pl.multiple_of(n + y2, 8), 8), :]
+                if k > 0:
+                    c = tw_ref[0, k, part, :]
+                    s = tw_ref[1, k, part, :]
+                    re, im = re * c - im * s, im * c + re * s
+                planes.append((re, im))
+            at = pl.ds(pl.multiple_of(lax.rem(i, steps) * 8, 8), 8)
+            for k, (re, im) in enumerate(short_fft(planes, 1)):
+                to = k * (n // (gz * rows)) + i // steps
+                out_refs[r][to, 0, at, :] = re
+                out_refs[r][to, 1, at, :] = im
+            return carry
+
+        lax.fori_loop(0, n // gz // 8, combine, 0, unroll=2)
+
+
+def y_inverse(edge, data, c, rows, gz, gy):
+    _, ny, width = data.shape
     n = ny // YR
+    piece = (gy, 2, rows, LANES)
     return pl.pallas_call(
-        functools.partial(y_inverse_kernel, rows, gz),
-        grid=(blocks // 2,),
+        functools.partial(y_inverse_kernel, gz),
+        grid=(1,),
         in_specs=[
-            pl.BlockSpec((2, ny, width), lambda c: (c, 0, 0)),
-            pl.BlockSpec((4 * n, 2 * n), lambda c: (0, 0)),
-            pl.BlockSpec((2, YR, n, LANES), lambda c: (0, 0, 0, 0)),
+            pl.BlockSpec(memory_space=pltpu.SMEM),
+            pl.BlockSpec((2, ny, width), lambda i: (c, 0, 0)),
+            pl.BlockSpec((4 * n, 2 * n), lambda i: (0, 0)),
+            pl.BlockSpec((2, YR, n, LANES), lambda i: (0, 0, 0, 0)),
         ],
-        out_specs=pl.BlockSpec((gz * gy, 2, rows, LANES), lambda c: (0, 0, 0, c)),
-        out_shape=jax.ShapeDtypeStruct((gz * gy, 2, rows, blocks * HALF), F32),
+        out_specs=[pl.BlockSpec(piece, lambda i: (0, 0, 0, 0))] * gz,
+        out_shape=[jax.ShapeDtypeStruct(piece, F32)] * gz,
         scratch_shapes=[
             pltpu.VMEM((ny, LANES), F32),
             pltpu.VMEM((ny, LANES), F32),
             pltpu.VMEM((YR, 2 * n, LANES), F32),
         ],
         compiler_params=pltpu.CompilerParams(vmem_limit_bytes=VMEM_LIMIT),
+        cost_estimate=pl.CostEstimate(
+            flops=16 * n * n * YR * LANES, bytes_accessed=8 * ny * LANES, transcendentals=0
+        ),
         name="y_inverse",
-    )(data, y_matrix(ny, False, -1.0), y_twiddle(ny))
-
-
-def y_forward_kernel(gz, spec_ref, data_ref, table_ref, tw_ref, out_ref, re_s, im_s, mix_s):
+    )(edge, data, y_matrix(ny, False, -1.0), y_twiddle(ny))
+
+
+def y_forward_kernel(gz, edge_ref, *refs):
+    spec_refs, refs = refs[:gz], refs[gz:]
+    data_ref, table_ref, tw_ref = refs[:3]
+    out_ref, re_s, im_s, mix_s = refs[-4:]
     ny = data_ref.shape[1]
     n = ny // YR
-    peers, _, rows, _ = spec_ref.shape
-    gy = peers // gz
-
-    def unpack(i, carry):
-        part = pl.ds(pl.multiple_of(i * rows, rows), rows)
-        source = (i % gz) * gy + i // gz
-        re_s[part, :] = spec_ref[source, 0]
-        im_s[part, :] = spec_ref[source, 1]
-        return carry
-
-    lax.fori_loop(0, peers, unpack, 0)
+    gy, _, rows, _ = spec_refs[0].shape
+
+    for r in range(gz):
+        core = lax.rem(edge_ref[2] + gz - r, gz)
+
+        def unpack(i, carry):
+            part = pl.ds(pl.multiple_of((i * gz + core) * rows, rows), rows)
+            re_s[part, :] = spec_refs[r][i, 0]
+            im_s[part, :] = spec_refs[r][i, 1]
+            return carry
+
+        lax.fori_loop(0, gy, unpack, 0)
 
     table = table_ref[...]
     for k in range(0, YR, 2):
@@ -299,29 +311,37 @@
     lax.fori_loop(0, n // 16, combine, 0)
 
 
-def y_forward(spec, data, gz):
+def y_forward(edge, spec, data, c, so_far):
+    gz = len(spec)
     blocks, ny, width = data.shape
-    peers, _, rows, _ = spec.shape
     n = ny // YR
+    piece = spec[0].shape
+    before = [] if so_far is None else [so_far]
     return pl.pallas_call(
         functools.partial(y_forward_kernel, gz),
-        grid=(blocks // 2,),
-        in_specs=[
-            pl.BlockSpec((peers, 2, rows, LANES), lambda c: (0, 0, 0, c)),
-            pl.BlockSpec((2, ny, width), lambda c: (c, 0, 0)),
-            pl.BlockSpec((4 * n, 2 * n), lambda c: (0, 0)),
-            pl.BlockSpec((2, YR, n, LANES), lambda c: (0, 0, 0, 0)),
-        ],
-        out_specs=pl.BlockSpec((2, ny, width), lambda c: (c, 0, 0)),
+        grid=(1,),
+        in_specs=[pl.BlockSpec(memory_space=pltpu.SMEM)]
+        + [pl.BlockSpec(piece, lambda i: (0, 0, 0, 0))] * gz
+        + [
+            pl.BlockSpec((2, ny, width), lambda i: (c, 0, 0)),
+            pl.BlockSpec((4 * n, 2 * n), lambda i: (0, 0)),
+            pl.BlockSpec((2, YR, n, LANES), lambda i: (0, 0, 0, 0)),
+        ]
+        + [pl.BlockSpec(memory_space=pl.ANY)] * len(before),
+        out_specs=pl.BlockSpec((2, ny, width), lambda i: (c, 0, 0)),
         out_shape=jax.ShapeDtypeStruct((blocks, ny, width), F32),
         scratch_shapes=[
             pltpu.VMEM((ny, LANES), F32),
             pltpu.VMEM((ny, LANES), F32),
             pltpu.VMEM((YR, 2 * n, LANES), F32),
         ],
+        input_output_aliases={gz + 4: 0} if before else {},
         compiler_params=pltpu.CompilerParams(vmem_limit_bytes=VMEM_LIMIT),
+        cost_estimate=pl.CostEstimate(
+            flops=24 * n * n * YR * LANES, bytes_accessed=16 * ny * LANES, transcendentals=0
+        ),
         name="y_forward",
-    )(spec, data, y_matrix(ny, True, 1.0), y_twiddle(ny))
+    )(edge, *spec, data, y_matrix(ny, True, 1.0), y_twiddle(ny), *before)
 
 
 def plane_chunk(planes, rows):
@@ -331,113 +351,155 @@
     return chunk
 
 
-def x_inverse_kernel(zs, spec_ref, coef_ref, tw_ref, table_ref, out_ref, head_ref, tail_ref, re_s, im_s):
-    planes, _, rows, ka = spec_ref.shape
-    kb = planes // zs
-
-    def columns(i, carry):
-        part = pl.ds(pl.multiple_of(i * 8, 8), 8)
-        for start in range(0, ka, LANES):
-            lanes = slice(start, start + LANES)
-            mixed = [[None] * kb for _ in range(zs)]
-            for k in range(kb):
-                coef = [coef_ref[j, k, :, lanes] for j in range(3)]
-                re = mix_adjoint(coef, [spec_ref[z * kb + k, 0, part, lanes] for z in range(zs)])
-                im = mix_adjoint(coef, [spec_ref[z * kb + k, 1, part, lanes] for z in range(zs)])
-                for z in range(zs):
-                    mixed[z][k] = (re[z], im[z])
-            for z in range(zs):
-                for b, (re, im) in enumerate(short_fft(mixed[z], 1)):
-                    if b > 0:
-                        c = tw_ref[0, b, :, lanes]
-                        s = tw_ref[1, b, :, lanes]
-                        re, im = re * c - im * s, im * c + re * s
-                    re_s[z * kb + b, part, lanes] = re
-                    im_s[z * kb + b, part, lanes] = im
-        return carry
-
-    lax.fori_loop(0, rows // 8, columns, 0)
-
-    chunk = plane_chunk(planes, rows)
+def for_core(edge_ref, gz, body):
+    for core in range(gz):
+        pl.when(edge_ref[2] == core)(functools.partial(body, core))
+
+
+def x_inverse_kernel(gz, chunks, way, partial, borders, edge_ref, *refs):
+    count = len(chunks) * gz
+    spec_refs, refs = refs[:count], refs[count:]
+    coef_ref, tw_ref, table_ref = refs[:3]
+    refs = refs[3:]
+    if partial:
+        so_far_ref, refs = refs[0], refs[1:]
+    out_ref, refs = refs[0], refs[1:]
+    if borders:
+        head_ref, tail_ref = refs[:2]
+    re_s, im_s = refs[-2:]
+    kb, _, rows, width = spec_refs[0].shape
+    planes, _, ka = out_ref.shape
+
+    def transform(core):
+        def columns(i, carry):
+            part = pl.ds(pl.multiple_of(i * 8, 8), 8)
+            for at, chunk in enumerate(chunks):
+                lanes = slice(chunk * width, (chunk + 1) * width)
+                to = slice(at * width, (at + 1) * width)
+                slices = [spec_refs[at * gz + (way * (z - core)) % gz] for z in range(gz)]
+                mixed = [[None] * kb for _ in range(gz)]
+                for k in range(kb):
+                    coef = [coef_ref[j, k, :, lanes] for j in range(3)]
+                    re = mix_adjoint(coef, [s[k, 0, part, :] for s in slices])
+                    im = mix_adjoint(coef, [s[k, 1, part, :] for s in slices])
+                    for z in range(gz):
+                        mixed[z][k] = (re[z], im[z])
+                for z in range(gz):
+                    for b, (re, im) in enumerate(short_fft(mixed[z], 1)):
+                        if b > 0:
+                            c = tw_ref[0, b, :, lanes]
+                            s = tw_ref[1, b, :, lanes]
+                            re, im = re * c - im * s, im * c + re * s
+                        re_s[z * kb + b, part, to] = re
+                        im_s[z * kb + b, part, to] = im
+            return carry
+
+        lax.fori_loop(0, rows // 8, columns, 0)
+
+    for_core(edge_ref, gz, transform)
+
+    step = plane_chunk(planes, rows)
+    depth = len(chunks) * width
 
     def multiply(i, carry):
-        part = pl.ds(i * chunk, chunk)
+        part = pl.ds(i * step, step)
         both = jnp.concatenate(
-            [re_s[part].reshape(chunk * rows, ka), im_s[part].reshape(chunk * rows, ka)], axis=1
+            [re_s[part].reshape(step * rows, depth), im_s[part].reshape(step * rows, depth)], axis=1
         )
         high, low = split2(both)
         value = dot(high, table_ref[...])
         value = value[:, :ka] + value[:, ka:] + dot(low, table_ref[:, :ka])
-        out_ref[part] = value.reshape(chunk, rows, ka)
+        value = value.reshape(step, rows, ka)
+        out_ref[part] = value + so_far_ref[part] if partial else value
         return carry
 
-    lax.fori_loop(0, planes // chunk, multiply, 0)
-
-    for p in range(planes):
-        for r in range(head_ref.shape[0]):
-            head_ref[r, p : p + 1, :] = out_ref[p, r : r + 1, :]
-        tail_ref[p : p + 1, :] = out_ref[p, rows - 1 : rows, :]
-
-
-def x_inverse(spec, coef, zs, nx):
-    planes, _, rows, ka = spec.shape
+    lax.fori_loop(0, planes // step, multiply, 0)
+
+    if borders:
+        for p in range(planes):
+            for r in range(head_ref.shape[0]):
+                head_ref[r, p : p + 1, :] = out_ref[p, r : r + 1, :]
+            tail_ref[p : p + 1, :] = out_ref[p, rows - 1 : rows, :]
+
+
+def x_inverse(edge, spec, chunks, way, coef, nx, so_far=None, borders=True):
+    gz = len(spec[0])
+    kb, _, rows, width = spec[0][0].shape
+    planes, ka = gz * kb, coef.shape[-1]
+    depth = len(chunks) * width
+    table = x_inverse_matrix(nx, ka)
+    if depth < ka:
+        keep = [slice(c * width, (c + 1) * width) for c in chunks]
+        table = np.concatenate([table[s] for s in keep] + [table[ka:][s] for s in keep], axis=0)
     vmem = pl.BlockSpec(memory_space=pltpu.VMEM)
+    arrays = [piece for pieces in spec for piece in pieces]
+    before = [] if so_far is None else [so_far]
+    out_shape = [jax.ShapeDtypeStruct((planes, rows, ka), F32)]
+    if borders:
+        out_shape.append(jax.ShapeDtypeStruct((2, planes, ka), F32))
+        out_shape.append(jax.ShapeDtypeStruct((planes, ka), F32))
     return pl.pallas_call(
-        functools.partial(x_inverse_kernel, zs),
-        in_specs=[vmem] * 4,
-        out_specs=[vmem] * 3,
-        out_shape=[
-            jax.ShapeDtypeStruct((planes, rows, ka), F32),
-            jax.ShapeDtypeStruct((2, planes, ka), F32),
-            jax.ShapeDtypeStruct((planes, ka), F32),
-        ],
-        scratch_shapes=[pltpu.VMEM((planes, rows, ka), F32)] * 2,
+        functools.partial(x_inverse_kernel, gz, chunks, way, bool(before), borders),
+        in_specs=[pl.BlockSpec(memory_space=pltpu.SMEM)]
+        + [vmem] * (len(arrays) + 3 + len(before)),
+        out_specs=[vmem] * len(out_shape),
+        out_shape=out_shape,
+        scratch_shapes=[pltpu.VMEM((planes, rows, depth), F32)] * 2,
         compiler_params=pltpu.CompilerParams(vmem_limit_bytes=VMEM_LIMIT),
+        cost_estimate=pl.CostEstimate(
+            flops=12 * planes * rows * depth * ka,
+            bytes_accessed=4 * planes * rows * (2 * depth + ka),
+            transcendentals=0,
+        ),
         name="x_inverse",
-    )(spec, coef, x_twiddle(nx, ka), x_inverse_matrix(nx, ka))
-
-
-def forward_into(zs, field_ref, coef_ref, tw_ref, table_ref, spec_ref, re_s, im_s):
+    )(edge, *arrays, coef, x_twiddle(nx, ka), jnp.asarray(table), *before)
+
+
+def forward_into(gz, edge_ref, field_ref, coef_ref, tw_ref, table_ref, spec_refs, sum_s, re_s, im_s):
     planes, rows, ka = field_ref.shape
-    kb = planes // zs
-    chunk = plane_chunk(planes, rows)
+    kb = planes // gz
+    width = spec_refs[0].shape[3]
+    step = plane_chunk(planes, rows)
 
     def multiply(i, carry):
-        part = pl.ds(i * chunk, chunk)
-        high, low = split2(field_ref[part].reshape(chunk * rows, ka))
+        part = pl.ds(i * step, step)
+        high, low = split2(field_ref[part].reshape(step * rows, ka))
         value = dot(high, table_ref[...])
         value = value[:, : 2 * ka] + value[:, 2 * ka :] + dot(low, table_ref[:, : 2 * ka])
-        re_s[part] = value[:, :ka].reshape(chunk, rows, ka)
-        im_s[part] = value[:, ka:].reshape(chunk, rows, ka)
+        re_s[part] = value[:, :ka].reshape(step, rows, ka)
+        im_s[part] = value[:, ka:].reshape(step, rows, ka)
         return carry
 
-    lax.fori_loop(0, planes // chunk, multiply, 0)
-
-    def columns(i, total):
-        part = pl.ds(pl.multiple_of(i * 8, 8), 8)
-        for start in range(0, ka, LANES):
-            lanes = slice(start, start + LANES)
-            spectra = []
-            for z in range(zs):
-                turned = []
-                for b in range(kb):
-                    re = re_s[z * kb + b, part, lanes]
-                    im = im_s[z * kb + b, part, lanes]
-                    if b > 0:
-                        c = tw_ref[0, b, :, lanes]
-                        s = tw_ref[1, b, :, lanes]
-                        re, im = re * c + im * s, im * c - re * s
-                    turned.append((re, im))
-                spectra.append(short_fft(turned, -1))
-            for k in range(kb):
-                coef = [coef_ref[j, k, :, lanes] for j in range(3)]
-                for p in range(2):
-                    for z, value in enumerate(mix(coef, [spectra[z][k][p] for z in range(zs)])):
-                        spec_ref[z * kb + k, p, part, lanes] = value
-                        total = total + value * value
-        return total
-
-    return lax.fori_loop(0, rows // 8, columns, jnp.zeros((8, LANES), F32))
+    lax.fori_loop(0, planes // step, multiply, 0)
+
+    def transform(core):
+        def columns(i, total):
+            part = pl.ds(pl.multiple_of(i * 8, 8), 8)
+            for chunk in range(ka // width):
+                lanes = slice(chunk * width, (chunk + 1) * width)
+                spectra = []
+                for z in range(gz):
+                    turned = []
+                    for b in range(kb):
+                        re = re_s[z * kb + b, part, lanes]
+                        im = im_s[z * kb + b, part, lanes]
+                        if b > 0:
+                            c = tw_ref[0, b, :, lanes]
+                            s = tw_ref[1, b, :, lanes]
+                            re, im = re * c + im * s, im * c - re * s
+                        turned.append((re, im))
+                    spectra.append(short_fft(turned, -1))
+                for k in range(kb):
+                    coef = [coef_ref[j, k, :, lanes] for j in range(3)]
+                    for p in range(2):
+                        for z, value in enumerate(mix(coef, [spectra[z][k][p] for z in range(gz)])):
+                            spec_refs[chunk * gz + (z - core) % gz][k, p, part, :] = value
+                            total = total + value * value
+            return total
+
+        sum_s[...] = lax.fori_loop(0, rows // 8, columns, jnp.zeros((8, LANES), F32))
+
+    for_core(edge_ref, gz, transform)
 
 
 def next_plane(field_ref, p, kb):
@@ -456,10 +518,21 @@
     return jnp.where(lane == 0, field_ref[p], pltpu.roll(field_ref[p + kb - 1], 1, 1))
 
 
-def first_kernel(zs, field_ref, coef_ref, tw_ref, table_ref, spec_ref, sums_ref, re_s, im_s):
+def spec_shapes(gz, field):
+    planes, rows, ka = field.shape
+    piece = jax.ShapeDtypeStruct((planes // gz, 2, rows, LANES), F32)
+    return [piece] * (gz * (ka // LANES))
+
+
+def by_chunk(gz, pieces):
+    return [list(pieces[at : at + gz]) for at in range(0, len(pieces), gz)]
+
+
+def first_kernel(gz, edge_ref, field_ref, coef_ref, tw_ref, table_ref, sums_ref, *refs):
+    spec_refs, (sum_s, re_s, im_s) = refs[:-3], refs[-3:]
     planes, rows, ka = field_ref.shape
-    kb = planes // zs
-    projected = forward_into(zs, field_ref, coef_ref, tw_ref, table_ref, spec_ref, re_s, im_s)
+    kb = planes // gz
+    forward_into(gz, edge_ref, field_ref, coef_ref, tw_ref, table_ref, spec_refs, sum_s, re_s, im_s)
     row = lax.broadcasted_iota(jnp.int32, (rows, ka), 0)
     square = jnp.zeros((8, LANES), F32)
     slope = jnp.zeros((8, LANES), F32)
@@ -474,25 +547,27 @@
             terms = terms + along_z * along_z
         slope = slope + fold(terms)
     sums_ref[0] = square
-    sums_ref[1] = projected
+    sums_ref[1] = sum_s[...]
     sums_ref[2] = slope
 
 
-def first_projection(field, coef, zs, nx):
+def first_projection(edge, field, coef, gz, nx):
     planes, rows, ka = field.shape
     vmem = pl.BlockSpec(memory_space=pltpu.VMEM)
-    return pl.pallas_call(
-        functools.partial(first_kernel, zs),
-        in_specs=[vmem] * 4,
-        out_specs=[vmem] * 2,
-        out_shape=[
-            jax.ShapeDtypeStruct((planes, 2, rows, ka), F32),
-            jax.ShapeDtypeStruct((3, 8, LANES), F32),
-        ],
-        scratch_shapes=[pltpu.VMEM((planes, rows, ka), F32)] * 2,
+    pieces = spec_shapes(gz, field)
+    sums, *spec = pl.pallas_call(
+        functools.partial(first_kernel, gz),
+        in_specs=[pl.BlockSpec(memory_space=pltpu.SMEM)] + [vmem] * 4,
+        out_specs=[vmem] * (1 + len(pieces)),
+        out_shape=[jax.ShapeDtypeStruct((3, 8, LANES), F32)] + pieces,
+        scratch_shapes=[pltpu.VMEM((8, LANES), F32)] + [pltpu.VMEM((planes, rows, ka), F32)] * 2,
         compiler_params=pltpu.CompilerParams(vmem_limit_bytes=VMEM_LIMIT),
+        cost_estimate=pl.CostEstimate(
+            flops=12 * planes * rows * ka * ka, bytes_accessed=12 * planes * rows * ka, transcendentals=0
+        ),
         name="first_projection",
-    )(field, coef, x_twiddle(nx, ka), x_forward_matrix(nx, ka))
+    )(edge, field, coef, x_twiddle(nx, ka), x_forward_matrix(nx, ka))
+    return by_chunk(gz, spec), sums
 
 
 def border_kernel(edge_ref, sums_ref, tail_ref, next_ref, out_ref):
@@ -512,11 +587,12 @@
 
 
 def second_kernel(
-    zs, edge_ref, sums_ref, d0_ref, nd0_ref, tail_ref, prev_ref, next_ref, nnext_ref,
-    coef_ref, tw_ref, table_ref, d1_ref, spec_ref, eta_ref, out_ref, re_s, im_s, row_s,
+    gz, edge_ref, sums_ref, d0_ref, nd0_ref, tail_ref, prev_ref, next_ref, nnext_ref,
+    coef_ref, tw_ref, table_ref, d1_ref, eta_ref, out_ref, *refs,
 ):
+    spec_refs, (sum_s, re_s, im_s, row_s) = refs[:-4], refs[-4:]
     planes, rows, ka = d0_ref.shape
-    kb = planes // zs
+    kb = planes // gz
     eta_here = step_of(sums_ref)
     eta_ref[...] = jnp.broadcast_to(eta_here, (8, LANES))
     eta = jnp.max(eta_here)
@@ -528,7 +604,7 @@
 
     lane2 = lax.broadcasted_iota(jnp.int32, (kb, ka), 1)
     row2 = lax.broadcasted_iota(jnp.int32, (kb, ka), 0)
-    for z in range(zs):
+    for z in range(gz):
         part = slice(z * kb, (z + 1) * kb)
         here = next_ref[0, part, :]
         value = here - eta * nnext_ref[0, part, :]
@@ -542,7 +618,7 @@
         value = value + shrink(here - tail_ref[part, :]) - shrink(next_ref[1, part, :] - here)
         if z > 0:
             value = value + shrink(here - next_ref[0, (z - 1) * kb : z * kb, :])
-        if z + 1 < zs:
+        if z + 1 < gz:
             value = value - shrink(next_ref[0, (z + 1) * kb : (z + 2) * kb, :] - here)
         row_s[part, :] = value
 
@@ -577,70 +653,89 @@
             terms = terms + along_z * along_z
         slope = slope + fold(terms)
 
-    projected = forward_into(zs, d1_ref, coef_ref, tw_ref, table_ref, spec_ref, re_s, im_s)
-    put_sums(out_ref, [square, projected, slope])
-
-
-def second_descent(edge, sums, d0, nd0, tail, prev_tail, next_head, next_nhead, coef, zs, nx):
+    forward_into(gz, edge_ref, d1_ref, coef_ref, tw_ref, table_ref, spec_refs, sum_s, re_s, im_s)
+    put_sums(out_ref, [square, sum_s[...], slope])
+
+
+def second_descent(edge, sums, d0, nd0, tail, prev_tail, next_head, next_nhead, coef, gz, nx):
     planes, rows, ka = d0.shape
     devices = sums.shape[0]
     vmem = pl.BlockSpec(memory_space=pltpu.VMEM)
-    return pl.pallas_call(
-        functools.partial(second_kernel, zs),
+    pieces = spec_shapes(gz, d0)
+    d1, eta, out, *spec = pl.pallas_call(
+        functools.partial(second_kernel, gz),
         in_specs=[pl.BlockSpec(memory_space=pltpu.SMEM)] + [vmem] * 10,
-        out_specs=[vmem] * 4,
+        out_specs=[vmem] * (3 + len(pieces)),
         out_shape=[
             jax.ShapeDtypeStruct((planes, rows, ka), F32),
-            jax.ShapeDtypeStruct((planes, 2, rows, ka), F32),
             jax.ShapeDtypeStruct((8, LANES), F32),
             jax.ShapeDtypeStruct((devices, 8, LANES), F32),
-        ],
+        ]
+        + pieces,
         scratch_shapes=[
+            pltpu.VMEM((8, LANES), F32),
             pltpu.VMEM((planes, rows, ka), F32),
             pltpu.VMEM((planes, rows, ka), F32),
             pltpu.VMEM((planes, ka), F32),
         ],
         compiler_params=pltpu.CompilerParams(vmem_limit_bytes=VMEM_LIMIT),
+        cost_estimate=pl.CostEstimate(
+            flops=12 * planes * rows * ka * ka, bytes_accessed=20 * planes * rows * ka, transcendentals=0
+        ),
         name="second_descent",
     )(
         edge, sums, d0, nd0, tail, prev_tail, next_head, next_nhead, coef,
         x_twiddle(nx, ka), x_forward_matrix(nx, ka),
     )
-
-
-def combine_kernel(sums_ref, eta_ref, first_ref, second_ref, out_ref, steps_ref):
+    return d1, by_chunk(gz, spec), eta, out
+
+
+def combine_kernel(sums_ref, eta_ref, *refs):
+    count = (len(refs) - 1) // 3
+    first_refs, second_refs, out_refs = refs[:count], refs[count : 2 * count], refs[2 * count : -1]
     eta0 = jnp.max(eta_ref[...])
     eta1 = jnp.max(step_of(sums_ref))
-    out_ref[...] = -(eta0 * first_ref[...] + eta1 * second_ref[...])
-    steps_ref[0] = eta_ref[...]
-    steps_ref[1] = jnp.full((8, LANES), eta1, F32)
+    refs[-1][0] = eta_ref[...]
+    refs[-1][1] = jnp.full((8, LANES), eta1, F32)
+    for first, second, out in zip(first_refs, second_refs, out_refs):
+
+        def one(i, carry):
+            out[i] = -(eta0 * first[i] + eta1 * second[i])
+            return carry
+
+        lax.fori_loop(0, out.shape[0], one, 0)
 
 
 def combine_spectra(sums, eta, first, second):
-    planes, parts, rows, ka = first.shape
-    devices = sums.shape[0]
-    count = 4 if planes % 4 == 0 else 1
-    block = pl.BlockSpec((count, parts, rows, ka), lambda i: (i, 0, 0, 0))
-    return pl.pallas_call(
+    gz = len(first[0])
+    first = [piece for pieces in first for piece in pieces]
+    second = [piece for pieces in second for piece in pieces]
+    vmem = pl.BlockSpec(memory_space=pltpu.VMEM)
+    *spec, steps = pl.pallas_call(
         combine_kernel,
-        grid=(planes // count,),
-        in_specs=[
-            pl.BlockSpec((devices, 8, LANES), lambda i: (0, 0, 0)),
-            pl.BlockSpec((8, LANES), lambda i: (0, 0)),
-            block,
-            block,
-        ],
-        out_specs=[block, pl.BlockSpec((2, 8, LANES), lambda i: (0, 0, 0))],
-        out_shape=[
-            jax.ShapeDtypeStruct(first.shape, F32),
-            jax.ShapeDtypeStruct((2, 8, LANES), F32),
-        ],
+        in_specs=[vmem] * (2 + 2 * len(first)),
+        out_specs=[vmem] * (1 + len(first)),
+        out_shape=[jax.ShapeDtypeStruct(piece.shape, F32) for piece in first]
+        + [jax.ShapeDtypeStruct((2, 8, LANES), F32)],
+        compiler_params=pltpu.CompilerParams(vmem_limit_bytes=VMEM_LIMIT),
         name="combine_spectra",
-    )(sums, eta, first, second)
+    )(sums, eta, *first, *second)
+    return by_chunk(gz, spec), steps
 
 
 def everywhere(sums):
     return lax.all_to_all(sums, ("gz", "gy"), 0, 0, tiled=True)
+
+
+def to_core(piece, r):
+    gz = lax.axis_size("gz")
+    return lax.ppermute(piece, "gz", [(i, (i + r) % gz) for i in range(gz)]) if r else piece
+
+
+def transpose(pieces):
+    return [
+        lax.all_to_all(to_core(piece, r), "gy", 0, 0, tiled=True) for r, piece in enumerate(pieces)
+    ]
 
 
 def shards(data, band_offset, interp_weight):
@@ -652,9 +747,11 @@
     rows = ny // devices
     ka = blocks * HALF
     nx = ka * gy
-
-    flat = lax.axis_index("gy") * gz + lax.axis_index("gz")
-    edge = jnp.stack([(flat == 0).astype(jnp.int32), (flat == devices - 1).astype(jnp.int32)])
+    chunks = blocks // 2
+
+    core = lax.axis_index("gz")
+    flat = lax.axis_index("gy") * gz + core
+    edge = jnp.stack([flat == 0, flat == devices - 1, core]).astype(jnp.int32)
     order = [(i % gz) * gy + i // gz for i in range(devices)]
     up = [(order[i + 1], order[i]) for i in range(devices - 1)]
     down = [(order[i], order[i + 1]) for i in range(devices - 1)]
@@ -670,27 +767,38 @@
     ).reshape(3, gy, 1, ka)
     coef = jnp.broadcast_to(coef, (3, gy, 8, ka))
 
-    spec = y_inverse(data, rows, gz, gy)
-    spec = lax.all_to_all(spec, ("gz", "gy"), 0, 0, tiled=True)
-    d0, head, tail = x_inverse(spec, coef, gz, nx)
+    d0 = None
+    for c in range(chunks):
+        spec = transpose(y_inverse(edge, data, c, rows, gz, gy))
+        final = c + 1 == chunks
+        out = x_inverse(edge, [spec], [c], -1, coef, nx, d0, final)
+        d0 = out[0]
+    head, tail = out[1:]
     next_head = lax.ppermute(head, ("gz", "gy"), up)
     prev_tail = lax.ppermute(tail, ("gz", "gy"), down)
-    spec0, sums = first_projection(d0, coef, gz, nx)
+    spec0, sums = first_projection(edge, d0, coef, gz, nx)
     sums = everywhere(border_sums(edge, sums, tail, next_head, devices))
-    nd0, nhead, _ = x_inverse(spec0, coef, gz, nx)
+    nd0, nhead, _ = x_inverse(edge, spec0, list(range(chunks)), 1, coef, nx)
     next_nhead = lax.ppermute(nhead, ("gz", "gy"), up)
     d1, spec1, eta, sums = second_descent(
         edge, sums, d0, nd0, tail, prev_tail, next_head, next_nhead, coef, gz, nx
     )
     sums = everywhere(sums)
     spec, steps = combine_spectra(sums, eta, spec0, spec1)
-    spec = lax.all_to_all(spec, ("gz", "gy"), 0, 0, tiled=True)
-    residual = y_forward(spec, data, gz)
+    residual = None
+    for c in range(chunks):
+        residual = y_forward(edge, transpose(spec[c]), data, c, residual)
 
     volume = -(steps[0, 0, 0] * d0 + steps[1, 0, 0] * d1)
     volume = volume.reshape(gz, gy, rows, ka).transpose(0, 2, 3, 1).reshape(gz, rows, nx)
-    volume = lax.all_to_all(volume, "gz", 0, 1, tiled=True)
-    return (volume, residual[None])
+    parts = [
+        to_core(lax.dynamic_index_in_dim(volume, lax.rem(core + r, gz), 0, False), r)
+        for r in range(gz)
+    ]
+    volume = jnp.zeros((gz, rows, nx), F32)
+    for r, part in enumerate(parts):
+        volume = lax.dynamic_update_index_in_dim(volume, part, lax.rem(core + gz - r, gz), 0)
+    return (volume.reshape(1, gz * rows, nx), residual[None])
 
 
 NX = 4096
@@ -940,6 +1048,253 @@
     return rows % 16 == 0 and blocks // mesh.shape["gy"] % 2 == 0
 
 
+NX = 4096
+NY = 2048
+XB = 64
+YB = 64
+ITERS = 2
+XA = 64
+YA = 32
+PRECISE = lax.Precision.HIGHEST
+
+
+def with_halo(block, sides, width):
+    for axis, dim in sides:
+        count = lax.axis_size(axis)
+        forward = [(i, i + 1) for i in range(count - 1)]
+        backward = [(target, source) for source, target in forward]
+        low = lax.ppermute(
+            lax.slice_in_dim(block, block.shape[dim] - width, None, axis=dim), axis, forward
+        )
+        high = lax.ppermute(lax.slice_in_dim(block, 0, width, axis=dim), axis, backward)
+        block = jnp.concatenate([low, block, high], axis=dim)
+    return block
+
+
+def from_behind(block, axis, distance):
+    devices = range(lax.axis_size(axis))
+    route = [(i - distance, i) for i in devices if i - distance in devices]
+    return lax.ppermute(block, axis, route)
+
+
+def unit_table(length):
+    counter = jnp.arange(length, dtype=jnp.int32)
+    phase_int = counter[:, None] * counter[None, :] % length
+    angles = 2.0 * jnp.pi / length * phase_int.astype(jnp.float32)
+    factor = length ** (-0.5)
+    return (jnp.cos(angles) * factor, jnp.sin(angles) * factor)
+
+
+def twiddle_table(row_len, col_len, period):
+    phase_int = (
+        jnp.arange(row_len, dtype=jnp.int32)[:, None]
+        * jnp.arange(col_len, dtype=jnp.int32)[None, :]
+        % period
+    )
+    angles = 2.0 * jnp.pi / period * phase_int.astype(jnp.float32)
+    return (jnp.cos(angles), jnp.sin(angles))
+
+
+def split_parts(packed):
+    half_width = packed.shape[-1] // 2
+    return (packed[..., :half_width], packed[..., half_width:])
+
+
+def join_parts(real_part, imag_part):
+    return jnp.concatenate([real_part, imag_part], axis=-1)
+
+
+def complex_contract(packed, cos_table, sin_table, subscripts, conj_sign):
+    cos_out = jnp.einsum(subscripts, packed, cos_table, precision=PRECISE)
+    sin_out = jnp.einsum(subscripts, packed, sin_table, precision=PRECISE)
+    cos_re, cos_im = split_parts(cos_out)
+    sin_re, sin_im = split_parts(sin_out)
+    return join_parts(cos_re - conj_sign * sin_im, cos_im + conj_sign * sin_re)
+
+
+def rotate(packed, cos_table, sin_table, conj_sign):
+    real_part, imag_part = split_parts(packed)
+    return join_parts(
+        real_part * cos_table - conj_sign * imag_part * sin_table,
+        imag_part * cos_table + conj_sign * real_part * sin_table,
+    )
+
+
+def forward_x(volume):
+    slices, row_count = (volume.shape[0], volume.shape[1])
+    cos_a, sin_a = unit_table(XA)
+    cos_b, sin_b = unit_table(XB)
+    first_table = jnp.concatenate([cos_a, -sin_a], axis=1)
+    grid_view = volume.reshape(slices, row_count, XA, XB)
+    mixing = jnp.einsum("zyab,am->zybm", grid_view, first_table, precision=PRECISE)
+    tw_cos, tw_sin = twiddle_table(XB, XA, NX)
+    mixing = rotate(mixing, tw_cos, tw_sin, -1.0)
+    return complex_contract(mixing, cos_b, sin_b, "zybm,bl->zlym", -1.0)
+
+
+def inverse_x(packed):
+    slices, row_count = (packed.shape[0], packed.shape[2])
+    cos_a, sin_a = unit_table(XA)
+    cos_b, sin_b = unit_table(XB)
+    mixing = complex_contract(packed, cos_b, sin_b, "zlym,lb->zybm", 1.0)
+    tw_cos, tw_sin = twiddle_table(XB, XA, NX)
+    mixing = rotate(mixing, tw_cos, tw_sin, 1.0)
+    last_table = jnp.concatenate([cos_a, -sin_a], axis=0)
+    grid_view = jnp.einsum("zybm,ma->zyab", mixing, last_table, precision=PRECISE)
+    return grid_view.reshape(slices, row_count, NX)
+
+
+def forward_y(packed):
+    slices, blocks, width = (packed.shape[0], packed.shape[1], packed.shape[3])
+    cos_a, sin_a = unit_table(YA)
+    cos_b, sin_b = unit_table(YB)
+    grid_view = packed.reshape(slices, blocks, YA, YB, width)
+    mixing = complex_contract(grid_view, cos_a, sin_a, "zjcdm,ck->zjkdm", -1.0)
+    tw_cos, tw_sin = twiddle_table(YA, YB, NY)
+    mixing = rotate(mixing, tw_cos[:, :, None], tw_sin[:, :, None], -1.0)
+    result = complex_contract(mixing, cos_b, sin_b, "zjkdm,dl->zjlkm", -1.0)
+    return result.reshape(slices, blocks, NY, width)
+
+
+def inverse_y(packed):
+    slices, blocks, width = (packed.shape[0], packed.shape[1], packed.shape[3])
+    cos_a, sin_a = unit_table(YA)
+    cos_b, sin_b = unit_table(YB)
+    grid_view = packed.reshape(slices, blocks, YB, YA, width)
+    mixing = complex_contract(grid_view, cos_b, sin_b, "zjlkm,ld->zjkdm", 1.0)
+    tw_cos, tw_sin = twiddle_table(YA, YB, NY)
+    mixing = rotate(mixing, tw_cos[:, :, None], tw_sin[:, :, None], 1.0)
+    result = complex_contract(mixing, cos_a, sin_a, "zjkdm,kc->zjcdm", 1.0)
+    return result.reshape(slices, blocks, NY, width)
+
+
+def tilt_coefficients(band_offset, interp_weight, first_block, blocks):
+    offsets = lax.dynamic_slice_in_dim(band_offset.reshape(XB, XA), first_block, blocks, 0)
+    weights = lax.dynamic_slice_in_dim(interp_weight.reshape(2, XB, XA), first_block, blocks, 1)
+    lower_tap = (jnp.concatenate([offsets, offsets], axis=1) < 0)[:, None, :]
+    first_weight = jnp.concatenate([weights[0], weights[0]], axis=1)[:, None, :]
+    second_weight = jnp.concatenate([weights[1], weights[1]], axis=1)[:, None, :]
+    return (lower_tap, first_weight, second_weight)
+
+
+def tilt(field_in, coefficients, adjoint):
+    lower_tap, first_weight, second_weight = coefficients
+    padded = with_halo(field_in, (("gz", 0),), 1)
+    below_rim = padded[:-2]
+    middle = padded[1:-1]
+    above_rim = padded[2:]
+    if adjoint:
+        return jnp.where(
+            lower_tap,
+            first_weight * above_rim + second_weight * middle,
+            first_weight * middle + second_weight * below_rim,
+        )
+    return jnp.where(
+        lower_tap,
+        first_weight * below_rim + second_weight * middle,
+        first_weight * middle + second_weight * above_rim,
+    )
+
+
+def to_pencil(slab_part):
+    return lax.all_to_all(slab_part, "gy", split_axis=1, concat_axis=2, tiled=True)
+
+
+def to_slab(pencil_part):
+    return lax.all_to_all(pencil_part, "gy", split_axis=2, concat_axis=1, tiled=True)
+
+
+def back_project(packed, pencil_coef):
+    return inverse_x(to_slab(inverse_y(tilt(packed, pencil_coef, True))))
+
+
+def edge_masks(slices, row_count):
+    z_global = lax.axis_index("gz") * slices + jnp.arange(slices, dtype=jnp.int32)
+    y_global = lax.axis_index("gy") * row_count + jnp.arange(row_count, dtype=jnp.int32)
+    keep_z = (z_global < slices * lax.axis_size("gz") - 1).astype(jnp.float32)[:, None, None]
+    keep_y = (y_global < row_count * lax.axis_size("gy") - 1).astype(jnp.float32)[None, :, None]
+    return (keep_z, keep_y)
+
+
+def forward_diff(field_in, keep_z, keep_y):
+    slices, row_count = (field_in.shape[0], field_in.shape[1])
+    next_z = from_behind(field_in, "gz", -1)
+    next_y = from_behind(field_in[:, :1], "gy", -1)
+    along_z = (jnp.concatenate([field_in[1:], next_z], axis=0) - field_in) * keep_z
+    along_y = (jnp.concatenate([field_in[:, 1:], next_y], axis=1) - field_in) * keep_y
+    zero_col = jnp.zeros((slices, row_count, 1), jnp.float32)
+    along_x = jnp.concatenate([field_in[:, :, 1:] - field_in[:, :, :-1], zero_col], axis=2)
+    return jnp.stack([along_z, along_y, along_x])
+
+
+def transpose_diff(components, keep_z, keep_y):
+    slices, row_count = (components.shape[1], components.shape[2])
+    zero_col = jnp.zeros((slices, row_count, 1), jnp.float32)
+    comp_z = components[0] * keep_z
+    comp_y = components[1] * keep_y
+    comp_x = jnp.concatenate([components[2][:, :, :-1], zero_col], axis=2)
+    prev_z = from_behind(comp_z, "gz", 1)
+    prev_y = from_behind(comp_y[:, -1:], "gy", 1)
+    result = jnp.concatenate([prev_z, comp_z[:-1]], axis=0) - comp_z
+    result = result + jnp.concatenate([prev_y, comp_y[:, :-1]], axis=1) - comp_y
+    result = result + jnp.concatenate([zero_col, comp_x[:, :, :-1]], axis=2) - comp_x
+    return result
+
+
+def plain_shards(data, band_offset, interp_weight):
+    slices = data.shape[0]
+    blocks = data.shape[1]
+    width = data.shape[3]
+    row_count = NY // lax.axis_size("gy")
+    slab_coef = tilt_coefficients(band_offset, interp_weight, 0, XB)
+    pencil_coef = tilt_coefficients(
+        band_offset, interp_weight, lax.axis_index("gy") * blocks, blocks
+    )
+    keep_z, keep_y = edge_masks(slices, row_count)
+    measured = data.astype(jnp.float32)
+    volume = jnp.zeros((slices, row_count, NX), jnp.float32)
+    grad_volume = jnp.zeros((3, slices, row_count, NX), jnp.float32)
+    split_var = grad_volume
+    dual_var = grad_volume
+    data_back = back_project(measured, pencil_coef)
+    normal_part = jnp.zeros_like(volume)
+    tilted = jnp.zeros((slices, XB, row_count, width), jnp.float32)
+    for iteration in range(ITERS):
+        data_grad = normal_part - data_back
+        if iteration > 0:
+            tv_gap = grad_volume - split_var + dual_var / PENALTY
+            descent = data_grad + PENALTY * transpose_diff(tv_gap, keep_z, keep_y)
+        else:
+            descent = data_grad
+        slope_field = forward_diff(descent, keep_z, keep_y)
+        projected = tilt(forward_x(descent), slab_coef, False)
+        line_totals = lax.psum(
+            (
+                jnp.sum(descent * descent),
+                jnp.sum(projected * projected),
+                jnp.sum(slope_field * slope_field),
+            ),
+            ("gz", "gy"),
+        )
+        step_length = line_totals[0] / (line_totals[1] + PENALTY * line_totals[2])
+        volume = volume - step_length * descent
+        grad_volume = grad_volume - step_length * slope_field
+        tilted = tilted - step_length * projected
+        if iteration + 1 < ITERS:
+            normal_part = normal_part - step_length * inverse_x(tilt(projected, slab_coef, True))
+        if iteration + 1 < ITERS:
+            shifted = grad_volume + dual_var / PENALTY
+            split_var = shifted - jnp.clip(shifted, -TV_WEIGHT / PENALTY, TV_WEIGHT / PENALTY)
+            dual_var = PENALTY * (grad_volume - split_var)
+    residual = forward_y(to_pencil(tilted)) - measured
+    return (volume, residual)
+
+
+def tiles_fit(mesh, ny, blocks):
+    rows = ny // (mesh.shape["gz"] * mesh.shape["gy"])
+    return rows % 16 == 0 and mesh.shape["gy"] % YR == 0 and blocks // mesh.shape["gy"] % 2 == 0
+
+
 def solution(mesh):
     in_specs = (P("gz", "gy", None, None), P(), P())
     out_specs = (P("gz", "gy", None), P("gz", "gy", None, None))

time: 334 us -> 345 us (1.033)
  waiting for transfers between devices: 193 us -> 114 us
  starting transfers between devices: 20.3 us -> 55 us
  local copies, waits for them, and re-layouts: 23.7 us -> 57.1 us
  blocking collectives: 24 us -> 47.5 us
    all_to_all x2 -> x7, waiting for transfers between devices: 192 us -> 104 us  [transpose(): lax.all_to_all(to_core(piece, r), 'gy', 0, 0, tiled=True)]
    all_to_all x2 -> x7, starting transfers between devices: 11.3 us -> 42.2 us  [transpose(): lax.all_to_all(to_core(piece, r), 'gy', 0, 0, tiled=True)]
    all_to_all x1, blocking collectives: 6.3 us -> 30 us  [transpose(): lax.all_to_all(to_core(piece, r), 'gy', 0, 0, tiled=True)]
    unnamed x49 -> x102, local copies, waits for them, and re-layouts: 14.7 us -> 36 us
    dynamic_slice x0 -> x3, local copies, waits for them, and re-layouts: none -> 10.8 us  [shards(): lax.dynamic_index_in_dim(volume, lax.rem(core + r, gz), 0, False)]
    ppermute x0 -> x5, waiting for transfers between devices: none -> 8.97 us  [to_core(): lax.ppermute(piece, 'gz', [(i, (i + r) % gz) for i in range(gz)])]
    pallas_call x7 -> x10, Pallas kernels: 64.5 us -> 61.4 us  [the longest x3 15.1 us: x_inverse(): pl.pallas_call(functools.partial(x_inverse_kernel, gz, chunks, way, bool(...]
    reshape x2 -> x1, local copies, waits for them, and re-layouts: 7.68 us -> 4.85 us  [shards(): volume.reshape(gz, gy, rows, ka).transpose(0, 2, 3, 1).reshape(gz, rows, nx)]
  transfers between devices with their start and end apart: 6 -> 16, of which waited for: 3 -> 11; matrix products, arithmetic and copies ran while one was open for 0% -> 8% of each run, Pallas kernels for 4% -> 9%
where the time goes in v2:
time: 345 us; the launch traced here: 343 us
  waiting for transfers between devices  114 us (33%)
  Pallas kernels  63 us (18%)
  local copies, waits for them, and re-layouts  57.1 us (17%)
  starting transfers between devices  55 us (16%)
  blocking collectives  47.5 us (14%)
  other arithmetic  5.43 us (2%)
    all_to_all x7, waiting for transfers between devices, transpose(): lax.all_to_all(to_core(piece, r), 'gy', 0, 0, tiled=True)  104 us
    all_to_all x7, starting transfers between devices, transpose(): lax.all_to_all(to_core(piece, r), 'gy', 0, 0, tiled=True)  42.2 us
    unnamed x102, local copies, waits for them, and re-layouts  36 us
    all_to_all x1, blocking collectives, transpose(): lax.all_to_all(to_core(piece, r), 'gy', 0, 0, tiled=True)  30 us
    all_to_all x1, blocking collectives, everywhere(): return lax.all_to_all(sums, ('gz', 'gy'), 0, 0, tiled=True)  17.5 us
    pallas_call x3, Pallas kernels, x_inverse(): pl.pallas_call(functools.partial(x_inverse_kernel, gz, chunks, way, bool(...  15.1 us
    pallas_call x2, Pallas kernels, y_forward(): pl.pallas_call(functools.partial(y_forward_kernel, gz), grid=(1,), in_spe...  14.8 us
    pallas_call x1, Pallas kernels, second_descent(): pl.pallas_call(functools.partial(second_kernel, gz), in_specs=[pl.BlockSp...  11.2 us
  transfers between devices with their start and end apart: 16, of which 11 were waited for; matrix products, arithmetic and copies ran while one was open for 8% of the time, Pallas kernels for 9%

profile of v2, /device:TPU:0, one launch (start us, length us, event | category | flops | bytes accessed | tf_op | source)
XLA Modules:
  0.0 343.3 jit_solution(7192531678445860000)
XLA Ops:
  3.5 4.5 %y_inverse.3 = (f32[16,2,64,128]{3,2,1,0:T(8,128)S(1)}, f32[16,2,64,128]{3,2,1,0:T(8,128)S(1)}) custom-call(s32[3]{0:T(128)S(1)} %pad_add_fusion.edge_ref, bf16[4,2048,128]{2,1,0:T(8,128)(2,1)S(1)} %bitcast.19, bf16[1024,512]{1,0:T(8,128)(2,1)S(1)} %copy-done.7, f32[2,8,256,128]{3,2,1,0:T(8,128)} %constant.60.clone.tw_ref.refs_4_), custom_call_target="tpu_custom_call" | custom-call | flops 1073741824 | bytes 2097152 | tf_op jit(solution)/shard_map/y_inverse/pallas_call | solution.py:234
  10.0 8.4 %all-to-all-start.2 = ((f32[16,2,64,128]{3,2,1,0:T(8,128)}), f32[16,2,64,128]{3,2,1,0:T(8,128)S(1)}, u32[]{:S(2)}, u32[]{:S(2)}) async-start(f32[16,2,64,128]{3,2,1,0:T(8,128)} %copy-done.12), calls=%async_computation.2 | async-start | bytes 2097152 | tf_op jit(solution)/shard_map/all_to_all | solution.py:737
  19.7 4.5 %y_inverse.2 = (f32[16,2,64,128]{3,2,1,0:T(8,128)S(1)}, f32[16,2,64,128]{3,2,1,0:T(8,128)S(1)}) custom-call(s32[3]{0:T(128)S(1)} %pad_add_fusion.edge_ref, bf16[4,2048,128]{2,1,0:T(8,128)(2,1)S(1)} %bitcast.20, bf16[1024,512]{1,0:T(8,128)(2,1)S(1)} %copy-done.8, f32[2,8,256,128]{3,2,1,0:T(8,128)} %constant.60.clone.tw_ref.refs_4_), custom_call_target="tpu_custom_call" | custom-call | flops 1073741824 | bytes 2097152 | tf_op jit(solution)/shard_map/y_inverse/pallas_call | solution.py:234
  26.2 16.7 %all-to-all-done.2.refs_0_ = f32[16,2,64,128]{3,2,1,0:T(8,128)S(1)} async-done(((f32[16,2,64,128]{3,2,1,0:T(8,128)}), f32[16,2,64,128]{3,2,1,0:T(8,128)S(1)}, u32[]{:S(2)}, u32[]{:S(2)}) %all-to-all-start.2) | async-done | bytes 1048608 | tf_op jit(solution)/shard_map/all_to_all | solution.py:737
  42.9 5.9 %all-to-all-start = ((f32[16,2,64,128]{3,2,1,0:T(8,128)}), f32[16,2,64,128]{3,2,1,0:T(8,128)}, u32[]{:S(2)}, u32[]{:S(2)}) async-start(f32[16,2,64,128]{3,2,1,0:T(8,128)} %copy-done.11), calls=%async_computation | async-start | bytes 2097152 | tf_op jit(solution)/shard_map/all_to_all | solution.py:737
  51.9 19.9 %all-to-all-done.refs_0_ = f32[16,2,64,128]{3,2,1,0:T(8,128)} async-done(((f32[16,2,64,128]{3,2,1,0:T(8,128)}), f32[16,2,64,128]{3,2,1,0:T(8,128)}, u32[]{:S(2)}, u32[]{:S(2)}) %all-to-all-start) | async-done | bytes 1048608 | tf_op jit(solution)/shard_map/all_to_all | solution.py:737
  71.8 6.1 %all-to-all-start.3 = ((f32[16,2,64,128]{3,2,1,0:T(8,128)}), f32[16,2,64,128]{3,2,1,0:T(8,128)}, u32[]{:S(2)}, u32[]{:S(2)}) async-start(f32[16,2,64,128]{3,2,1,0:T(8,128)} %collective-permute-done.1), calls=%async_computation.3 | async-start | bytes 2097152 | tf_op jit(solution)/shard_map/all_to_all | solution.py:737
  80.9 19.8 %all-to-all-done.3.refs_1_ = f32[16,2,64,128]{3,2,1,0:T(8,128)} async-done(((f32[16,2,64,128]{3,2,1,0:T(8,128)}), f32[16,2,64,128]{3,2,1,0:T(8,128)}, u32[]{:S(2)}, u32[]{:S(2)}) %all-to-all-start.3) | async-done | bytes 1048608 | tf_op jit(solution)/shard_map/all_to_all | solution.py:737
  100.8 6.1 %all-to-all-start.1 = ((f32[16,2,64,128]{3,2,1,0:T(8,128)}), f32[16,2,64,128]{3,2,1,0:T(8,128)}, u32[]{:S(2)}, u32[]{:S(2)}) async-start(f32[16,2,64,128]{3,2,1,0:T(8,128)} %collective-permute-done), calls=%async_computation.1 | async-start | bytes 2097152 | tf_op jit(solution)/shard_map/all_to_all | solution.py:737
  108.9 3.8 %x_inverse.3.refs_5_ = f32[32,64,256]{2,1,0:T(8,128)S(1)} custom-call(s32[3]{0:T(128)S(1)} %pad_add_fusion.edge_ref, f32[16,2,64,128]{3,2,1,0:T(8,128)S(1)} %all-to-all-done.2.refs_0_, f32[16,2,64,128]{3,2,1,0:T(8,128)} %all-to-all-done.3.refs_1_, f32[3,16,8,256]{3,2,1,0:T(8,128)S(1)} %broadcast_in_dim.27.refs_2_.coef_ref.refs_4_, ...), custom_call_target="tpu_custom_call" | custom-call | flops 805306368 | bytes 4194304 | tf_op jit(solution)/shard_map/x_inverse/pallas_call | solution.py:441
  114.0 15.7 %all-to-all-done.1.refs_1_ = f32[16,2,64,128]{3,2,1,0:T(8,128)} async-done(((f32[16,2,64,128]{3,2,1,0:T(8,128)}), f32[16,2,64,128]{3,2,1,0:T(8,128)}, u32[]{:S(2)}, u32[]{:S(2)}) %all-to-all-start.1) | async-done | bytes 1048608 | tf_op jit(solution)/shard_map/all_to_all | solution.py:737
  131.7 4.9 %x_inverse.4 = (f32[32,64,256]{2,1,0:T(8,128)S(1)}, f32[2,32,256]{2,1,0:T(8,128)S(1)}, f32[32,256]{1,0:T(8,128)S(1)}) custom-call(s32[3]{0:T(128)S(1)} %pad_add_fusion.edge_ref, f32[16,2,64,128]{3,2,1,0:T(8,128)} %all-to-all-done.refs_0_, f32[16,2,64,128]{3,2,1,0:T(8,128)} %all-to-all-done.1.refs_1_, ...), custom_call_target="tpu_custom_call" | custom-call | flops 805306368 | bytes 4194304 | tf_op jit(solution)/shard_map/x_inverse/pallas_call | solution.py:441
  139.2 7.1 %first_projection.1 = (f32[3,8,128]{2,1,0:T(8,128)S(1)}, f32[16,2,64,128]{3,2,1,0:T(8,128)S(1)}, f32[16,2,64,128]{3,2,1,0:T(8,128)S(1)}, f32[16,2,64,128]{3,2,1,0:T(8,128)S(1)}, f32[16,2,64,128]{3,2,1,0:T(8,128)S(1)}) custom-call(s32[3]{0:T(128)S(1)} %pad_add_fusion.edge_ref, f32[32,64,256]{2,1,0:T(8,128)} %copy-done.9, ...), custom_call_target="tpu_custom_call" | custom-call | flops 1610612736 | bytes 6291456 | tf_op jit(solution)/shard_map/first_projection/pallas_call | solution.py:558
  151.5 6.4 %all-to-all-start.4 = ((f32[32,8,128]{2,1,0:T(8,128)}), f32[32,8,128]{2,1,0:T(8,128)}, u32[]{:S(2)}, u32[]{:S(2)}) async-start(f32[32,8,128]{2,1,0:T(8,128)} %border_sums.1), calls=%async_computation.4 | async-start | bytes 262144 | tf_op jit(solution)/shard_map/all_to_all | solution.py:727
  164.2 6.3 %x_inverse.5 = (f32[32,64,256]{2,1,0:T(8,128)}, f32[2,32,256]{2,1,0:T(8,128)S(1)}, f32[32,256]{1,0:T(8,128)}) custom-call(s32[3]{0:T(128)S(1)} %copy-done.31, f32[16,2,64,128]{3,2,1,0:T(8,128)S(1)} %get-tuple-element.36.refs_0_, f32[16,2,64,128]{3,2,1,0:T(8,128)S(1)} %copy-done.14, f32[16,2,64,128]{3,2,1,0:T(8,128)S(1)} %copy-done.16, ...), custom_call_target="tpu_custom_call" | custom-call | flops 1610612736 | bytes 6291456 | tf_op jit(solution)/shard_map/x_inverse/pallas_call | solution.py:441
  181.3 11.2 %second_descent.1 = (f32[32,64,256]{2,1,0:T(8,128)}, f32[8,128]{1,0:T(8,128)S(1)}, f32[32,8,128]{2,1,0:T(8,128)S(1)}, f32[16,2,64,128]{3,2,1,0:T(8,128)S(1)}, f3...) custom-call(s32[3]{0:T(128)S(1)} %copy-done.32, ...), custom_call_target="tpu_custom_call" | custom-call | flops 1610612736 | bytes 10485760 | tf_op jit(solution)/shard_map/second_descent/pallas_call | solution.py:665
  196.6 17.5 %all_to_all.50.sums_ref = f32[32,8,128]{2,1,0:T(8,128)S(1)} all-to-all(f32[32,8,128]{2,1,0:T(8,128)S(1)} %get-tuple-element.42), channel_id=1, replica_groups=mesh['gz'=2,'gy'=16] {'gz','gy'}, dimensions={0} | all-to-all | bytes 262144 | tf_op jit(solution)/shard_map/all_to_all | solution.py:727
  214.1 4.1 %combine_spectra.1 = (f32[16,2,64,128]{3,2,1,0:T(8,128)S(1)}, f32[16,2,64,128]{3,2,1,0:T(8,128)S(1)}, f32[16,2,64,128]{3,2,1,0:T(8,128)S(1)}, f32[16,2,64,128]{3,2,1,0:T(8,128)S(1)}, f32[2,8,128]{2,1,0:T(8,128)S(1)}) custom-call(f32[32,8,128]{2,1,0:T(8,128)S(1)} %all_to_all.50.sums_ref, f32[8,128]{1,0:T(8,128)S(1)} %get-tuple-element.43.eta_ref, ...), custom_call_target="tpu_custom_call" | custom-call | tf_op jit(solution)/shard_map/combine_spectra/pallas_call | solution.py:714
  219.2 30.0 %all_to_all.51.refs_0_ = f32[16,2,64,128]{3,2,1,0:T(8,128)} all-to-all(f32[16,2,64,128]{3,2,1,0:T(8,128)S(1)} %get-tuple-element.52), channel_id=1, replica_groups=mesh['gz'=2,'gy'=16] {'gy'}, dimensions={0} | all-to-all | bytes 2097152 | tf_op jit(solution)/shard_map/all_to_all | solution.py:737
  249.2 3.9 %all-to-all-start.6 = ((f32[16,2,64,128]{3,2,1,0:T(8,128)}), f32[16,2,64,128]{3,2,1,0:T(8,128)S(1)}, u32[]{:S(2)}, u32[]{:S(2)}) async-start(f32[16,2,64,128]{3,2,1,0:T(8,128)} %copy-done.10), calls=%async_computation.6 | async-start | bytes 2097152 | tf_op jit(solution)/shard_map/all_to_all | solution.py:737
  256.2 20.6 %all-to-all-done.6.refs_0_ = f32[16,2,64,128]{3,2,1,0:T(8,128)S(1)} async-done(((f32[16,2,64,128]{3,2,1,0:T(8,128)}), f32[16,2,64,128]{3,2,1,0:T(8,128)S(1)}, u32[]{:S(2)}, u32[]{:S(2)}) %all-to-all-start.6) | async-done | bytes 1048608 | tf_op jit(solution)/shard_map/all_to_all | solution.py:737
  276.8 5.9 %all-to-all-start.9 = ((f32[16,2,64,128]{3,2,1,0:T(8,128)}), f32[16,2,64,128]{3,2,1,0:T(8,128)}, u32[]{:S(2)}, u32[]{:S(2)}) async-start(f32[16,2,64,128]{3,2,1,0:T(8,128)} %collective-permute-done.7), calls=%async_computation.9 | async-start | bytes 2097152 | tf_op jit(solution)/shard_map/all_to_all | solution.py:737
  283.3 5.3 %add_negate_fusion = f32[32,64,256]{2,1,0:T(8,128)} fusion(f32[32,64,256]{2,1,0:T(8,128)} %get-tuple-element.49, f32[32,64,256]{2,1,0:T(8,128)} %copy-done.9, f32[]{:T(128)} %bitcast.8, f32[]{:T(128)} %bitcast.7), kind=kLoop, calls=%fused_computation | loop fusion | flops 2097152 | bytes 6291464 | tf_op jit(solution)/shard_map/neg | solution.py:792
  288.6 4.9 %copy.28 = f32[2,16,64,256]{2,1,3,0:T(8,128)} copy(f32[2,16,64,256]{3,2,1,0:T(8,128)} %bitcast.25) | data formatting | bytes 4194304 | tf_op jit(solution)/shard_map/reshape | solution.py:793
  293.5 4.5 %constant_dynamic-slice_fusion = (f32[1,64,4096]{1,2,0:T(8,128)}, f32[1,64,4096]{1,2,0:T(8,128)}) fusion(f32[2,64,4096]{1,2,0:T(8,128)} %bitcast.24, s32[]{:T(128)S(6)} %select_n.29, s32[]{:T(128)S(6)} %select_n.27), kind=kLoop, calls=%fused_computation.6 | loop fusion | bytes 4194312 | tf_op jit(solution)/shard_map/jit(dynamic_index_in_dim)/dynamic_slice | solution.py:795
  297.9 3.2 copy.30
  301.6 4.1 %all-to-all-done.9.refs_1_ = f32[16,2,64,128]{3,2,1,0:T(8,128)} async-done(((f32[16,2,64,128]{3,2,1,0:T(8,128)}), f32[16,2,64,128]{3,2,1,0:T(8,128)}, u32[]{:S(2)}, u32[]{:S(2)}) %all-to-all-start.9) | async-done | bytes 1048608 | tf_op jit(solution)/shard_map/all_to_all | solution.py:737
  305.7 6.0 %all-to-all-start.7 = ((f32[16,2,64,128]{3,2,1,0:T(8,128)}), f32[16,2,64,128]{3,2,1,0:T(8,128)}, u32[]{:S(2)}, u32[]{:S(2)}) async-start(f32[16,2,64,128]{3,2,1,0:T(8,128)} %collective-permute-done.6), calls=%async_computation.7 | async-start | bytes 2097152 | tf_op jit(solution)/shard_map/all_to_all | solution.py:737
  311.7 3.1 copy.29
  319.8 7.4 %y_forward.2.refs_5_ = f32[4,2048,128]{2,1,0:T(8,128)} custom-call(s32[3]{0:T(128)S(1)} %copy-done.32, f32[16,2,64,128]{3,2,1,0:T(8,128)S(1)} %copy-done.6, f32[16,2,64,128]{3,2,1,0:T(8,128)} %all-to-all-done.9.refs_1_, bf16[4,2048,128]{2,1,0:T(8,128)(2,1)S(1)} %bitcast.21, bf16[1024,512]{1,0:T(8,128)(2,1)S(1)} %copy-done.3, ...), custom_call_target="tpu_custom_call" | custom-call | flops 1610612736 | bytes 4194304 | tf_op jit(solution)/shard_map/y_forward/pallas_call | solution.py:320
  327.2 7.4 %all-to-all-done.7.refs_1_ = f32[16,2,64,128]{3,2,1,0:T(8,128)} async-done(((f32[16,2,64,128]{3,2,1,0:T(8,128)}), f32[16,2,64,128]{3,2,1,0:T(8,128)}, u32[]{:S(2)}, u32[]{:S(2)}) %all-to-all-start.7) | async-done | bytes 1048608 | tf_op jit(solution)/shard_map/all_to_all | solution.py:737
  335.8 7.4 %y_forward.3 = f32[4,2048,128]{2,1,0:T(8,128)} custom-call(s32[3]{0:T(128)S(1)} %copy-done.32, f32[16,2,64,128]{3,2,1,0:T(8,128)S(1)} %copy-done.5, f32[16,2,64,128]{3,2,1,0:T(8,128)} %all-to-all-done.7.refs_1_, bf16[4,2048,128]{2,1,0:T(8,128)(2,1)S(1)} %bitcast.22, bf16[1024,512]{1,0:T(8,128)(2,1)S(1)} %copy-done.3, ...), custom_call_target="tpu_custom_call", output_to_operand_aliasing={{}: (6, {})} | custom-call | flops 1610612736 | bytes 4194304 | tf_op jit(solution)/shard_map/y_forward/pallas_call | solution.py:320
  (133 shorter events, 59.4 us)
Async XLA Ops:
  0.7 138.5 %copy-start.30 = (s32[3]{0:T(128)}, s32[3]{0:T(128)S(1)}, u32[]{:S(2)}) copy-start(s32[3]{0:T(128)S(1)} %pad_add_fusion.edge_ref) | copy-start | bytes 40
  0.7 1.6 copy-start
  10.0 8.5 %copy-start.1 = (bf16[1,4,2048,128]{3,2,1,0:T(8,128)(2,1)S(1)}, bf16[1,4,2048,128]{3,2,1,0:T(8,128)(2,1)}, u32[]{:S(2)}) copy-start(bf16[1,4,2048,128]{3,2,1,0:T(8,128)(2,1)} %param.21) | copy-start | bytes 6291460
  10.0 32.9 %all-to-all-start.2 = ((f32[16,2,64,128]{3,2,1,0:T(8,128)}), f32[16,2,64,128]{3,2,1,0:T(8,128)S(1)}, u32[]{:S(2)}, u32[]{:S(2)}) async-start(f32[16,2,64,128]{3,2,1,0:T(8,128)} %copy-done.12), calls=%async_computation.2 | async-start | bytes 2097152 | tf_op jit(solution)/shard_map/all_to_all | solution.py:737
  42.9 28.9 %all-to-all-start = ((f32[16,2,64,128]{3,2,1,0:T(8,128)}), f32[16,2,64,128]{3,2,1,0:T(8,128)}, u32[]{:S(2)}, u32[]{:S(2)}) async-start(f32[16,2,64,128]{3,2,1,0:T(8,128)} %copy-done.11), calls=%async_computation | async-start | bytes 2097152 | tf_op jit(solution)/shard_map/all_to_all | solution.py:737
  48.8 58.0 %copy-start.49 = (f32[2,4096]{1,0:T(2,128)S(1)}, f32[2,4096]{1,0:T(2,128)}, u32[]{:S(2)}) copy-start(f32[2,4096]{1,0:T(2,128)} %param.23) | copy-start | bytes 98308
  48.8 58.1 %copy-start.50 = (s32[4096]{0:T(1024)S(1)}, s32[4096]{0:T(1024)}, u32[]{:S(2)}) copy-start(s32[4096]{0:T(1024)} %param.22) | copy-start | bytes 49156
  48.8 3.1 collective-permute-start.1
  71.8 28.9 %all-to-all-start.3 = ((f32[16,2,64,128]{3,2,1,0:T(8,128)}), f32[16,2,64,128]{3,2,1,0:T(8,128)}, u32[]{:S(2)}, u32[]{:S(2)}) async-start(f32[16,2,64,128]{3,2,1,0:T(8,128)} %collective-permute-done.1), calls=%async_computation.3 | async-start | bytes 2097152 | tf_op jit(solution)/shard_map/all_to_all | solution.py:737
  77.9 3.1 collective-permute-start
  100.8 29.0 %all-to-all-start.1 = ((f32[16,2,64,128]{3,2,1,0:T(8,128)}), f32[16,2,64,128]{3,2,1,0:T(8,128)}, u32[]{:S(2)}, u32[]{:S(2)}) async-start(f32[16,2,64,128]{3,2,1,0:T(8,128)} %collective-permute-done), calls=%async_computation.1 | async-start | bytes 2097152 | tf_op jit(solution)/shard_map/all_to_all | solution.py:737
  131.7 7.5 %copy-start.25 = (f32[2,16,8,256]{3,2,1,0:T(8,128)S(1)}, f32[2,16,8,256]{3,2,1,0:T(8,128)}, u32[]{:S(2)}) copy-start(f32[2,16,8,256]{3,2,1,0:T(8,128)} %constant.61.clone.refs_3_.tw_ref.refs_5_) | copy-start | bytes 786436
  131.7 7.6 %copy-start.45 = (bf16[256,1024]{1,0:T(8,128)(2,1)S(1)}, bf16[256,1024]{1,0:T(8,128)(2,1)}, u32[]{:S(2)}) copy-start(bf16[256,1024]{1,0:T(8,128)(2,1)} %constant.64.clone.table_ref) | copy-start | bytes 1572868
  137.9 8.5 %copy-start.33 = (f32[32,256]{1,0:T(8,128)}, f32[32,256]{1,0:T(8,128)S(1)}, u32[]{:S(2)}) copy-start(f32[32,256]{1,0:T(8,128)S(1)} %get-tuple-element.34.tail_ref) | copy-start | bytes 98308
  137.9 12.0 %collective-permute-start.2 = (f32[2,32,256]{2,1,0:T(8,128)S(1)}, f32[2,32,256]{2,1,0:T(8,128)}, u32[]{:S(2)}, u32[]{:S(2)}) collective-permute-start(f32[2,32,256]{2,1,0:T(8,128)S(1)} %get-tuple-element.35), channel_id=1, source_target_pairs={{16,0},{1,16},{17,1},{2,17},{18,2},{3,18},{19,3},{4,19},{20,4},{5,... | collective-permute-start | bytes 196616 | tf_op jit(solution)/shard_map/ppermute | solution.py:777
  151.5 25.4 %all-to-all-start.4 = ((f32[32,8,128]{2,1,0:T(8,128)}), f32[32,8,128]{2,1,0:T(8,128)}, u32[]{:S(2)}, u32[]{:S(2)}) async-start(f32[32,8,128]{2,1,0:T(8,128)} %border_sums.1), calls=%async_computation.4 | async-start | bytes 262144 | tf_op jit(solution)/shard_map/all_to_all | solution.py:727
  164.2 7.6 %copy-start.34 = (f32[32,256]{1,0:T(8,128)S(1)}, f32[32,256]{1,0:T(8,128)}, u32[]{:S(2)}) copy-start(f32[32,256]{1,0:T(8,128)} %copy-done.33) | copy-start | bytes 98308
  164.2 12.8 %copy-start.32 = (s32[3]{0:T(128)S(1)}, s32[3]{0:T(128)}, u32[]{:S(2)}) copy-start(s32[3]{0:T(128)} %copy-done.30) | copy-start | bytes 40
  170.5 5.8 %collective-permute-start.4 = (f32[2,32,256]{2,1,0:T(8,128)S(1)}, f32[2,32,256]{2,1,0:T(8,128)S(1)}, u32[]{:S(2)}, u32[]{:S(2)}) collective-permute-start(f32[2,32,256]{2,1,0:T(8,128)S(1)} %get-tuple-element.41), channel_id=1, source_target_pairs={{16,0},{1,16},{17,1},{2,17},{18,2},{3,18},{19,3},{4,19},{20,4},{5,... | collective-permute-start | bytes 196616 | tf_op jit(solution)/shard_map/ppermute | solution.py:782
  171.8 3.9 %collective-permute-start.3 = (f32[32,256]{1,0:T(8,128)S(1)}, f32[32,256]{1,0:T(8,128)S(1)}, u32[]{:S(2)}, u32[]{:S(2)}) collective-permute-start(f32[32,256]{1,0:T(8,128)S(1)} %copy-done.34), channel_id=1, source_target_pairs={{0,16},{16,1},{1,17},{17,2},{2,18},{18,3},{3,19},{19,4},{4,20},{20... | collective-permute-start | bytes 98312 | tf_op jit(solution)/shard_map/ppermute | solution.py:778
  219.2 30.0 %copy-start.10 = (f32[16,2,64,128]{3,2,1,0:T(8,128)}, f32[16,2,64,128]{3,2,1,0:T(8,128)S(1)}, u32[]{:S(2)}) copy-start(f32[16,2,64,128]{3,2,1,0:T(8,128)S(1)} %get-tuple-element.50) | copy-start | bytes 3145732
  219.2 30.0 %copy-start.37 = (f32[16,2,64,128]{3,2,1,0:T(8,128)}, f32[16,2,64,128]{3,2,1,0:T(8,128)S(1)}, u32[]{:S(2)}) copy-start(f32[16,2,64,128]{3,2,1,0:T(8,128)S(1)} %get-tuple-element.51) | copy-start | bytes 3145732
  249.2 27.6 %all-to-all-start.6 = ((f32[16,2,64,128]{3,2,1,0:T(8,128)}), f32[16,2,64,128]{3,2,1,0:T(8,128)S(1)}, u32[]{:S(2)}, u32[]{:S(2)}) async-start(f32[16,2,64,128]{3,2,1,0:T(8,128)} %copy-done.10), calls=%async_computation.6 | async-start | bytes 2097152 | tf_op jit(solution)/shard_map/all_to_all | solution.py:737
  253.1 3.1 collective-permute-start.7
  276.8 11.8 %copy-start.4 = (f32[16,2,64,128]{3,2,1,0:T(8,128)}, f32[16,2,64,128]{3,2,1,0:T(8,128)S(1)}, u32[]{:S(2)}) copy-start(f32[16,2,64,128]{3,2,1,0:T(8,128)S(1)} %all-to-all-done.6.refs_0_) | copy-start | bytes 3145732
  276.8 28.9 %all-to-all-start.9 = ((f32[16,2,64,128]{3,2,1,0:T(8,128)}), f32[16,2,64,128]{3,2,1,0:T(8,128)}, u32[]{:S(2)}, u32[]{:S(2)}) async-start(f32[16,2,64,128]{3,2,1,0:T(8,128)} %collective-permute-done.7), calls=%async_computation.9 | async-start | bytes 2097152 | tf_op jit(solution)/shard_map/all_to_all | solution.py:737
  282.7 18.9 %collective-permute-start.6 = (f32[16,2,64,128]{3,2,1,0:T(8,128)}, f32[16,2,64,128]{3,2,1,0:T(8,128)}, u32[]{:S(2)}, u32[]{:S(2)}) collective-permute-start(f32[16,2,64,128]{3,2,1,0:T(8,128)} %copy-done.37), channel_id=1, source_target_pairs={{0,16},{16,0},{1,17},{17,1},{2,18},{18,2},{3,19},{19,3},{4,20},{20... | collective-permute-start | bytes 3145736 | tf_op jit(solution)/shard_map/ppermute | solution.py:732
  301.1 16.4 %collective-permute-start.5 = (f32[64,4096]{1,0:T(8,128)}, f32[64,4096]{1,0:T(8,128)}, u32[]{:S(2)}, u32[]{:S(2)}) collective-permute-start(f32[64,4096]{1,0:T(8,128)} %bitcast.13), channel_id=1, source_target_pairs={{0,16},{16,0},{1,17},{17,1},{2,18},{18,2},{3,19},{19,3},{4,20},{20... | collective-permute-start | bytes 3145736 | tf_op jit(solution)/shard_map/ppermute | solution.py:732
  305.7 28.9 %all-to-all-start.7 = ((f32[16,2,64,128]{3,2,1,0:T(8,128)}), f32[16,2,64,128]{3,2,1,0:T(8,128)}, u32[]{:S(2)}, u32[]{:S(2)}) async-start(f32[16,2,64,128]{3,2,1,0:T(8,128)} %collective-permute-done.6), calls=%async_computation.7 | async-start | bytes 2097152 | tf_op jit(solution)/shard_map/all_to_all | solution.py:737
  314.9 1.5 copy-start.48
  316.4 3.3 copy-start.3
  316.4 3.3 copy-start.6
  (35 other events, 34.5 us)

commit v3 on v1

--- a/solution.py
+++ b/solution.py
@@ -14,9 +14,10 @@
 HALF = 64
 YR = 8
 LANES = 128
+EARLY = []
 F32 = jnp.float32
 BF16 = jnp.bfloat16
-VMEM_LIMIT = 48 * 1024 * 1024
+VMEM_LIMIT = 16 * 1024 * 1024
 
 
 def dft_parts(length, scale):
@@ -51,14 +52,14 @@
 
 def y_twiddle(ny):
     n = ny // YR
-    angles = 2.0 * np.pi / ny * (np.arange(YR)[:, None] * np.arange(n)[None, :])
+    angles = 2.0 * np.pi / ny * (np.array([1, 2, 4])[:, None] * np.arange(n)[None, :])
     table = np.stack([np.cos(angles), np.sin(angles)]).astype(np.float32)
-    return jnp.asarray(np.ascontiguousarray(np.broadcast_to(table[..., None], (2, YR, n, LANES))))
+    return jnp.asarray(np.ascontiguousarray(np.broadcast_to(table[..., None], (2, 3, n, LANES))))
 
 
 def x_inverse_matrix(nx, ka):
     cos, sin = dft_parts(ka, nx**-0.5)
-    return jnp.asarray(np.concatenate(host_parts(np.concatenate([cos, -sin], axis=0)), axis=1))
+    return np.concatenate(host_parts(np.concatenate([cos, -sin], axis=0)), axis=1)
 
 
 def x_forward_matrix(nx, ka):
@@ -173,94 +174,145 @@
     return out
 
 
-def y_inverse_kernel(rows, gz, data_ref, table_ref, tw_ref, out_ref, re_s, im_s, mix_s):
-    ny = data_ref.shape[1]
+def steps_of(gz, gy):
+    return [(r, s) for s in reversed(range(gy)) for r in range(gz)]
+
+
+def send(piece, step):
+    r, s = step
+    if r == 0 and s == 0:
+        return piece
+    gz, gy = lax.axis_size("gz"), lax.axis_size("gy")
+    route = [
+        (g * gy + c, (g + r) % gz * gy + (c ^ s)) for g in range(gz) for c in range(gy)
+    ]
+    return lax.ppermute(piece, ("gz", "gy"), route)
+
+
+def towards(edge_ref, gz, step):
+    r, s = step
+    return lax.rem(edge_ref[2] + r, gz), edge_ref[3] ^ s
+
+
+def source(edge_ref, gz, step):
+    r, s = step
+    return lax.rem(edge_ref[2] + gz - r, gz), edge_ref[3] ^ s
+
+
+def y_turns(tw_ref, part):
+    one, two, four = [(tw_ref[0, i, part, :], tw_ref[1, i, part, :]) for i in range(3)]
+
+    def both(a, b):
+        return a[0] * b[0] - a[1] * b[1], a[1] * b[0] + a[0] * b[1]
+
+    three = both(one, two)
+    return [one, two, three, four, both(one, four), both(two, four), both(three, four)]
+
+
+def y_inverse_kernel(gz, steps, edge_ref, data_ref, table_ref, tw_ref, *refs):
+    out_refs, (re_s, im_s, mix_s, part_s) = refs[: len(steps)], refs[len(steps) :]
+    blocks, ny, _ = data_ref.shape
     n = ny // YR
-    gy = out_ref.shape[0] // gz
+    gy, _, rows, _ = part_s.shape
     lane = lax.broadcasted_iota(jnp.int32, (n, LANES), 1)
-
-    def unpack(i, carry):
-        part = pl.ds(pl.multiple_of(i * n, n), n)
-        first = data_ref[0, part, :].astype(F32)
-        second = data_ref[1, part, :].astype(F32)
-        re_s[part, :] = jnp.where(lane < HALF, first, pltpu.roll(second, HALF, 1))
-        im_s[part, :] = jnp.where(lane < HALF, pltpu.roll(first, HALF, 1), second)
-        return carry
-
-    lax.fori_loop(0, YR, unpack, 0)
-
     table = table_ref[...]
-    for k in range(0, YR, 2):
-        pieces = [
-            jnp.concatenate([s[pl.ds(k + d, n, stride=YR), :] for d in range(2)], axis=1)
-            for s in (re_s, im_s)
-        ]
-        both = dot(table, jnp.concatenate(pieces, axis=0).astype(BF16))
-        both = both[: 2 * n] + both[2 * n :]
-        for d in range(2):
-            mix_s[k + d] = both[:, d * LANES : (d + 1) * LANES]
-
-    def combine(i, carry):
-        start = pl.multiple_of(i * 8, 8)
-        part = pl.ds(start, 8)
-        planes = []
-        for k in range(YR):
-            re = mix_s[k, part, :]
-            im = mix_s[k, pl.ds(pl.multiple_of(n + i * 8, 8), 8), :]
-            if k > 0:
-                c = tw_ref[0, k, part, :]
-                s = tw_ref[1, k, part, :]
-                re, im = re * c - im * s, im * c + re * s
-            planes.append((re, im))
-        for k, (re, im) in enumerate(short_fft(planes, 1)):
-            y = k * n + start
-            flat = y // rows
-            to = (flat % gz) * gy + flat // gz
-            at = pl.ds(pl.multiple_of(y % rows, 8), 8)
-            out_ref[to, 0, at, :] = re
-            out_ref[to, 1, at, :] = im
-        return carry
-
-    lax.fori_loop(0, n // 8, combine, 0, unroll=2)
-
-
-def y_inverse(data, rows, gz, gy):
+
+    for chunk in range(blocks // 2):
+        lanes = slice(chunk * LANES, (chunk + 1) * LANES)
+
+        def unpack(i, carry):
+            part = pl.ds(pl.multiple_of(i * n, n), n)
+            first = data_ref[2 * chunk, part, :].astype(F32)
+            second = data_ref[2 * chunk + 1, part, :].astype(F32)
+            re_s[part, :] = jnp.where(lane < HALF, first, pltpu.roll(second, HALF, 1))
+            im_s[part, :] = jnp.where(lane < HALF, pltpu.roll(first, HALF, 1), second)
+            return carry
+
+        lax.fori_loop(0, YR, unpack, 0)
+
+        for k in range(0, YR, 2):
+            pieces = [
+                jnp.concatenate([s[pl.ds(k + d, n, stride=YR), :] for d in range(2)], axis=1)
+                for s in (re_s, im_s)
+            ]
+            both = dot(table, jnp.concatenate(pieces, axis=0).astype(BF16))
+            both = both[: 2 * n] + both[2 * n :]
+            for d in range(2):
+                mix_s[k + d] = both[:, d * LANES : (d + 1) * LANES]
+
+        tiles = rows // 8
+        for r in range(gz):
+            core = lax.rem(edge_ref[2] + r, gz)
+
+            def combine(i, carry):
+                y2 = ((i // tiles) * gz + core) * rows + lax.rem(i, tiles) * 8
+                part = pl.ds(pl.multiple_of(y2, 8), 8)
+                turns = [None] + y_turns(tw_ref, part)
+                planes = []
+                for k in range(YR):
+                    re = mix_s[k, part, :]
+                    im = mix_s[k, pl.ds(pl.multiple_of(n + y2, 8), 8), :]
+                    if k > 0:
+                        c, s = turns[k]
+                        re, im = re * c - im * s, im * c + re * s
+                    planes.append((re, im))
+                at = pl.ds(pl.multiple_of(lax.rem(i, tiles) * 8, 8), 8)
+                for k, (re, im) in enumerate(short_fft(planes, 1)):
+                    to = (k * (n // (gz * rows)) + i // tiles) ^ edge_ref[3]
+                    part_s[to, 0, at, :] = re
+                    part_s[to, 1, at, :] = im
+                return carry
+
+            lax.fori_loop(0, n // gz // 8, combine, 0, unroll=2)
+            for step, out_ref in zip(steps, out_refs):
+                if step[0] == r:
+                    out_ref[:, :, lanes] = part_s[step[1]]
+
+
+def y_inverse(edge, data, steps, rows, gz, gy):
     blocks, ny, width = data.shape
     n = ny // YR
+    vmem = pl.BlockSpec(memory_space=pltpu.VMEM)
+    piece = jax.ShapeDtypeStruct((2, rows, blocks * HALF), F32)
     return pl.pallas_call(
-        functools.partial(y_inverse_kernel, rows, gz),
-        grid=(blocks // 2,),
-        in_specs=[
-            pl.BlockSpec((2, ny, width), lambda c: (c, 0, 0)),
-            pl.BlockSpec((4 * n, 2 * n), lambda c: (0, 0)),
-            pl.BlockSpec((2, YR, n, LANES), lambda c: (0, 0, 0, 0)),
-        ],
-        out_specs=pl.BlockSpec((gz * gy, 2, rows, LANES), lambda c: (0, 0, 0, c)),
-        out_shape=jax.ShapeDtypeStruct((gz * gy, 2, rows, blocks * HALF), F32),
+        functools.partial(y_inverse_kernel, gz, steps),
+        in_specs=[pl.BlockSpec(memory_space=pltpu.SMEM)] + [vmem] * 3,
+        out_specs=[vmem] * len(steps),
+        out_shape=[piece] * len(steps),
         scratch_shapes=[
             pltpu.VMEM((ny, LANES), F32),
             pltpu.VMEM((ny, LANES), F32),
             pltpu.VMEM((YR, 2 * n, LANES), F32),
+            pltpu.VMEM((gy, 2, rows, LANES), F32),
         ],
         compiler_params=pltpu.CompilerParams(vmem_limit_bytes=VMEM_LIMIT),
         name="y_inverse",
-    )(data, y_matrix(ny, False, -1.0), y_twiddle(ny))
-
-
-def y_forward_kernel(gz, spec_ref, data_ref, table_ref, tw_ref, out_ref, re_s, im_s, mix_s):
+    )(edge, data, y_matrix(ny, False, -1.0), y_twiddle(ny))
+
+
+def y_forward_kernel(gz, early, steps, edge_ref, eta_ref, *refs):
+    count = len(early)
+    first_refs, second_refs = refs[:count], refs[count : 2 * count]
+    spec_refs, refs = refs[2 * count : 2 * count + len(steps)], refs[2 * count + len(steps) :]
+    data_ref, table_ref, tw_ref, out_ref, re_s, im_s, mix_s = refs
     ny = data_ref.shape[1]
     n = ny // YR
-    peers, _, rows, _ = spec_ref.shape
-    gy = peers // gz
-
-    def unpack(i, carry):
-        part = pl.ds(pl.multiple_of(i * rows, rows), rows)
-        source = (i % gz) * gy + i // gz
-        re_s[part, :] = spec_ref[source, 0]
-        im_s[part, :] = spec_ref[source, 1]
-        return carry
-
-    lax.fori_loop(0, peers, unpack, 0)
+    rows = spec_refs[0].shape[1]
+    chunk = pl.program_id(0)
+    lanes = pl.ds(pl.multiple_of(chunk * LANES, LANES), LANES)
+    eta0 = jnp.max(eta_ref[0])
+    eta1 = jnp.max(eta_ref[1])
+
+    def place(step):
+        core, chip = source(edge_ref, gz, step)
+        return pl.ds(pl.multiple_of((chip * gz + core) * rows, rows), rows)
+
+    for step, first_ref, second_ref in zip(early, first_refs, second_refs):
+        for p, s in enumerate((re_s, im_s)):
+            s[place(step), :] = -(eta0 * first_ref[p, :, lanes] + eta1 * second_ref[p, :, lanes])
+    for step, spec_ref in zip(steps, spec_refs):
+        for p, s in enumerate((re_s, im_s)):
+            s[place(step), :] = spec_ref[p, :, lanes]
 
     table = table_ref[...]
     for k in range(0, YR, 2):
@@ -279,40 +331,36 @@
     def combine(i, carry):
         start = pl.multiple_of(i * 16, 16)
         part = pl.ds(start, 16)
+        turns = [None] + y_turns(tw_ref, part)
         planes = []
         for k in range(YR):
             re = mix_s[k, part, :]
             im = mix_s[k, pl.ds(pl.multiple_of(n + i * 16, 16), 16), :]
             if k > 0:
-                c = tw_ref[0, k, part, :]
-                s = tw_ref[1, k, part, :]
+                c, s = turns[k]
                 re, im = re * c + im * s, im * c - re * s
             planes.append((re, im))
         for k, (re, im) in enumerate(short_fft(planes, -1)):
             at = pl.ds(pl.multiple_of(k * n + start, 16), 16)
             first = jnp.where(lane < HALF, re, pltpu.roll(im, HALF, 1))
             second = jnp.where(lane < HALF, pltpu.roll(re, HALF, 1), im)
-            out_ref[0, at, :] = first - data_ref[0, at, :].astype(F32)
-            out_ref[1, at, :] = second - data_ref[1, at, :].astype(F32)
+            out_ref[0, at, :] = first - data_ref[2 * chunk, at, :].astype(F32)
+            out_ref[1, at, :] = second - data_ref[2 * chunk + 1, at, :].astype(F32)
         return carry
 
     lax.fori_loop(0, n // 16, combine, 0)
 
 
-def y_forward(spec, data, gz):
+def y_forward(edge, etas, early, first, second, steps, spec, data, gz):
     blocks, ny, width = data.shape
-    peers, _, rows, _ = spec.shape
     n = ny // YR
+    vmem = pl.BlockSpec(memory_space=pltpu.VMEM)
+    arrays = [etas, *first, *second, *spec, data, y_matrix(ny, True, 1.0), y_twiddle(ny)]
     return pl.pallas_call(
-        functools.partial(y_forward_kernel, gz),
+        functools.partial(y_forward_kernel, gz, early, steps),
         grid=(blocks // 2,),
-        in_specs=[
-            pl.BlockSpec((peers, 2, rows, LANES), lambda c: (0, 0, 0, c)),
-            pl.BlockSpec((2, ny, width), lambda c: (c, 0, 0)),
-            pl.BlockSpec((4 * n, 2 * n), lambda c: (0, 0)),
-            pl.BlockSpec((2, YR, n, LANES), lambda c: (0, 0, 0, 0)),
-        ],
-        out_specs=pl.BlockSpec((2, ny, width), lambda c: (c, 0, 0)),
+        in_specs=[pl.BlockSpec(memory_space=pltpu.SMEM)] + [vmem] * len(arrays),
+        out_specs=pl.BlockSpec((2, ny, width), lambda i: (i, 0, 0)),
         out_shape=jax.ShapeDtypeStruct((blocks, ny, width), F32),
         scratch_shapes=[
             pltpu.VMEM((ny, LANES), F32),
@@ -321,7 +369,7 @@
         ],
         compiler_params=pltpu.CompilerParams(vmem_limit_bytes=VMEM_LIMIT),
         name="y_forward",
-    )(spec, data, y_matrix(ny, True, 1.0), y_twiddle(ny))
+    )(edge, *arrays)
 
 
 def plane_chunk(planes, rows):
@@ -331,22 +379,32 @@
     return chunk
 
 
-def x_inverse_kernel(zs, spec_ref, coef_ref, tw_ref, table_ref, out_ref, head_ref, tail_ref, re_s, im_s):
-    planes, _, rows, ka = spec_ref.shape
-    kb = planes // zs
+def x_inverse_kernel(gz, steps, edge_ref, *refs):
+    count = max(1, len(steps))
+    spec_refs, refs = refs[:count], refs[count:]
+    coef_ref, tw_ref, table_ref, out_ref, head_ref, tail_ref, re_s, im_s = refs[:8]
+    planes, rows, ka = out_ref.shape
+    kb = planes // gz
+
+    spec_ref = spec_refs[0]
+    if steps:
+        spec_ref = refs[8]
+        for step, piece_ref in zip(steps, spec_refs):
+            core, chip = source(edge_ref, gz, step)
+            spec_ref[core * kb + chip] = piece_ref[...]
 
     def columns(i, carry):
         part = pl.ds(pl.multiple_of(i * 8, 8), 8)
         for start in range(0, ka, LANES):
             lanes = slice(start, start + LANES)
-            mixed = [[None] * kb for _ in range(zs)]
+            mixed = [[None] * kb for _ in range(gz)]
             for k in range(kb):
                 coef = [coef_ref[j, k, :, lanes] for j in range(3)]
-                re = mix_adjoint(coef, [spec_ref[z * kb + k, 0, part, lanes] for z in range(zs)])
-                im = mix_adjoint(coef, [spec_ref[z * kb + k, 1, part, lanes] for z in range(zs)])
-                for z in range(zs):
+                re = mix_adjoint(coef, [spec_ref[z * kb + k, 0, part, lanes] for z in range(gz)])
+                im = mix_adjoint(coef, [spec_ref[z * kb + k, 1, part, lanes] for z in range(gz)])
+                for z in range(gz):
                     mixed[z][k] = (re[z], im[z])
-            for z in range(zs):
+            for z in range(gz):
                 for b, (re, im) in enumerate(short_fft(mixed[z], 1)):
                     if b > 0:
                         c = tw_ref[0, b, :, lanes]
@@ -358,20 +416,20 @@
 
     lax.fori_loop(0, rows // 8, columns, 0)
 
-    chunk = plane_chunk(planes, rows)
+    step = plane_chunk(planes, rows)
 
     def multiply(i, carry):
-        part = pl.ds(i * chunk, chunk)
+        part = pl.ds(i * step, step)
         both = jnp.concatenate(
-            [re_s[part].reshape(chunk * rows, ka), im_s[part].reshape(chunk * rows, ka)], axis=1
+            [re_s[part].reshape(step * rows, ka), im_s[part].reshape(step * rows, ka)], axis=1
         )
         high, low = split2(both)
         value = dot(high, table_ref[...])
         value = value[:, :ka] + value[:, ka:] + dot(low, table_ref[:, :ka])
-        out_ref[part] = value.reshape(chunk, rows, ka)
+        out_ref[part] = value.reshape(step, rows, ka)
         return carry
 
-    lax.fori_loop(0, planes // chunk, multiply, 0)
+    lax.fori_loop(0, planes // step, multiply, 0)
 
     for p in range(planes):
         for r in range(head_ref.shape[0]):
@@ -379,46 +437,50 @@
         tail_ref[p : p + 1, :] = out_ref[p, rows - 1 : rows, :]
 
 
-def x_inverse(spec, coef, zs, nx):
-    planes, _, rows, ka = spec.shape
+def x_inverse(edge, spec, steps, coef, gz, nx):
+    kb, ka = coef.shape[1], coef.shape[-1]
+    planes, rows = gz * kb, spec[0].shape[-2]
     vmem = pl.BlockSpec(memory_space=pltpu.VMEM)
+    scratch = [pltpu.VMEM((planes, rows, ka), F32)] * 2
+    if steps:
+        scratch = scratch + [pltpu.VMEM((planes, 2, rows, ka), F32)]
     return pl.pallas_call(
-        functools.partial(x_inverse_kernel, zs),
-        in_specs=[vmem] * 4,
+        functools.partial(x_inverse_kernel, gz, steps),
+        in_specs=[pl.BlockSpec(memory_space=pltpu.SMEM)] + [vmem] * (len(spec) + 3),
         out_specs=[vmem] * 3,
         out_shape=[
             jax.ShapeDtypeStruct((planes, rows, ka), F32),
             jax.ShapeDtypeStruct((2, planes, ka), F32),
             jax.ShapeDtypeStruct((planes, ka), F32),
         ],
-        scratch_shapes=[pltpu.VMEM((planes, rows, ka), F32)] * 2,
+        scratch_shapes=scratch,
         compiler_params=pltpu.CompilerParams(vmem_limit_bytes=VMEM_LIMIT),
         name="x_inverse",
-    )(spec, coef, x_twiddle(nx, ka), x_inverse_matrix(nx, ka))
-
-
-def forward_into(zs, field_ref, coef_ref, tw_ref, table_ref, spec_ref, re_s, im_s):
+    )(edge, *spec, coef, x_twiddle(nx, ka), jnp.asarray(x_inverse_matrix(nx, ka)))
+
+
+def forward_into(gz, field_ref, coef_ref, tw_ref, table_ref, spec_ref, re_s, im_s):
     planes, rows, ka = field_ref.shape
-    kb = planes // zs
-    chunk = plane_chunk(planes, rows)
+    kb = planes // gz
+    step = plane_chunk(planes, rows)
 
     def multiply(i, carry):
-        part = pl.ds(i * chunk, chunk)
-        high, low = split2(field_ref[part].reshape(chunk * rows, ka))
+        part = pl.ds(i * step, step)
+        high, low = split2(field_ref[part].reshape(step * rows, ka))
         value = dot(high, table_ref[...])
         value = value[:, : 2 * ka] + value[:, 2 * ka :] + dot(low, table_ref[:, : 2 * ka])
-        re_s[part] = value[:, :ka].reshape(chunk, rows, ka)
-        im_s[part] = value[:, ka:].reshape(chunk, rows, ka)
+        re_s[part] = value[:, :ka].reshape(step, rows, ka)
+        im_s[part] = value[:, ka:].reshape(step, rows, ka)
         return carry
 
-    lax.fori_loop(0, planes // chunk, multiply, 0)
+    lax.fori_loop(0, planes // step, multiply, 0)
 
     def columns(i, total):
         part = pl.ds(pl.multiple_of(i * 8, 8), 8)
         for start in range(0, ka, LANES):
             lanes = slice(start, start + LANES)
             spectra = []
-            for z in range(zs):
+            for z in range(gz):
                 turned = []
                 for b in range(kb):
                     re = re_s[z * kb + b, part, lanes]
@@ -432,12 +494,19 @@
             for k in range(kb):
                 coef = [coef_ref[j, k, :, lanes] for j in range(3)]
                 for p in range(2):
-                    for z, value in enumerate(mix(coef, [spectra[z][k][p] for z in range(zs)])):
+                    for z, value in enumerate(mix(coef, [spectra[z][k][p] for z in range(gz)])):
                         spec_ref[z * kb + k, p, part, lanes] = value
                         total = total + value * value
         return total
 
     return lax.fori_loop(0, rows // 8, columns, jnp.zeros((8, LANES), F32))
+
+
+def cut(gz, steps, edge_ref, spec_ref, piece_refs):
+    kb = spec_ref.shape[0] // gz
+    for step, piece_ref in zip(steps, piece_refs):
+        core, chip = towards(edge_ref, gz, step)
+        piece_ref[...] = spec_ref[core * kb + chip]
 
 
 def next_plane(field_ref, p, kb):
@@ -456,10 +525,14 @@
     return jnp.where(lane == 0, field_ref[p], pltpu.roll(field_ref[p + kb - 1], 1, 1))
 
 
-def first_kernel(zs, field_ref, coef_ref, tw_ref, table_ref, spec_ref, sums_ref, re_s, im_s):
+def first_kernel(
+    gz, early, edge_ref, field_ref, coef_ref, tw_ref, table_ref, sums_ref, spec_ref, *refs
+):
+    piece_refs, (re_s, im_s) = refs[:-2], refs[-2:]
     planes, rows, ka = field_ref.shape
-    kb = planes // zs
-    projected = forward_into(zs, field_ref, coef_ref, tw_ref, table_ref, spec_ref, re_s, im_s)
+    kb = planes // gz
+    projected = forward_into(gz, field_ref, coef_ref, tw_ref, table_ref, spec_ref, re_s, im_s)
+    cut(gz, early, edge_ref, spec_ref, piece_refs)
     row = lax.broadcasted_iota(jnp.int32, (rows, ka), 0)
     square = jnp.zeros((8, LANES), F32)
     slope = jnp.zeros((8, LANES), F32)
@@ -478,21 +551,23 @@
     sums_ref[2] = slope
 
 
-def first_projection(field, coef, zs, nx):
+def first_projection(edge, field, early, coef, gz, nx):
     planes, rows, ka = field.shape
     vmem = pl.BlockSpec(memory_space=pltpu.VMEM)
-    return pl.pallas_call(
-        functools.partial(first_kernel, zs),
-        in_specs=[vmem] * 4,
-        out_specs=[vmem] * 2,
+    sums, spec, *pieces = pl.pallas_call(
+        functools.partial(first_kernel, gz, early),
+        in_specs=[pl.BlockSpec(memory_space=pltpu.SMEM)] + [vmem] * 4,
+        out_specs=[vmem] * (2 + len(early)),
         out_shape=[
+            jax.ShapeDtypeStruct((3, 8, LANES), F32),
             jax.ShapeDtypeStruct((planes, 2, rows, ka), F32),
-            jax.ShapeDtypeStruct((3, 8, LANES), F32),
-        ],
+        ]
+        + [jax.ShapeDtypeStruct((2, rows, ka), F32)] * len(early),
         scratch_shapes=[pltpu.VMEM((planes, rows, ka), F32)] * 2,
         compiler_params=pltpu.CompilerParams(vmem_limit_bytes=VMEM_LIMIT),
         name="first_projection",
-    )(field, coef, x_twiddle(nx, ka), x_forward_matrix(nx, ka))
+    )(edge, field, coef, x_twiddle(nx, ka), x_forward_matrix(nx, ka))
+    return spec, pieces, sums
 
 
 def border_kernel(edge_ref, sums_ref, tail_ref, next_ref, out_ref):
@@ -512,11 +587,12 @@
 
 
 def second_kernel(
-    zs, edge_ref, sums_ref, d0_ref, nd0_ref, tail_ref, prev_ref, next_ref, nnext_ref,
-    coef_ref, tw_ref, table_ref, d1_ref, spec_ref, eta_ref, out_ref, re_s, im_s, row_s,
+    gz, early, edge_ref, sums_ref, d0_ref, nd0_ref, tail_ref, prev_ref, next_ref, nnext_ref,
+    coef_ref, tw_ref, table_ref, d1_ref, eta_ref, out_ref, spec_ref, *refs,
 ):
+    piece_refs, (re_s, im_s, row_s) = refs[:-3], refs[-3:]
     planes, rows, ka = d0_ref.shape
-    kb = planes // zs
+    kb = planes // gz
     eta_here = step_of(sums_ref)
     eta_ref[...] = jnp.broadcast_to(eta_here, (8, LANES))
     eta = jnp.max(eta_here)
@@ -528,7 +604,7 @@
 
     lane2 = lax.broadcasted_iota(jnp.int32, (kb, ka), 1)
     row2 = lax.broadcasted_iota(jnp.int32, (kb, ka), 0)
-    for z in range(zs):
+    for z in range(gz):
         part = slice(z * kb, (z + 1) * kb)
         here = next_ref[0, part, :]
         value = here - eta * nnext_ref[0, part, :]
@@ -542,7 +618,7 @@
         value = value + shrink(here - tail_ref[part, :]) - shrink(next_ref[1, part, :] - here)
         if z > 0:
             value = value + shrink(here - next_ref[0, (z - 1) * kb : z * kb, :])
-        if z + 1 < zs:
+        if z + 1 < gz:
             value = value - shrink(next_ref[0, (z + 1) * kb : (z + 2) * kb, :] - here)
         row_s[part, :] = value
 
@@ -577,24 +653,26 @@
             terms = terms + along_z * along_z
         slope = slope + fold(terms)
 
-    projected = forward_into(zs, d1_ref, coef_ref, tw_ref, table_ref, spec_ref, re_s, im_s)
+    projected = forward_into(gz, d1_ref, coef_ref, tw_ref, table_ref, spec_ref, re_s, im_s)
+    cut(gz, early, edge_ref, spec_ref, piece_refs)
     put_sums(out_ref, [square, projected, slope])
 
 
-def second_descent(edge, sums, d0, nd0, tail, prev_tail, next_head, next_nhead, coef, zs, nx):
+def second_descent(edge, sums, d0, nd0, tail, prev_tail, next_head, next_nhead, early, coef, gz, nx):
     planes, rows, ka = d0.shape
     devices = sums.shape[0]
     vmem = pl.BlockSpec(memory_space=pltpu.VMEM)
-    return pl.pallas_call(
-        functools.partial(second_kernel, zs),
+    d1, eta, out, spec, *pieces = pl.pallas_call(
+        functools.partial(second_kernel, gz, early),
         in_specs=[pl.BlockSpec(memory_space=pltpu.SMEM)] + [vmem] * 10,
-        out_specs=[vmem] * 4,
+        out_specs=[vmem] * (4 + len(early)),
         out_shape=[
             jax.ShapeDtypeStruct((planes, rows, ka), F32),
-            jax.ShapeDtypeStruct((planes, 2, rows, ka), F32),
             jax.ShapeDtypeStruct((8, LANES), F32),
             jax.ShapeDtypeStruct((devices, 8, LANES), F32),
-        ],
+            jax.ShapeDtypeStruct((planes, 2, rows, ka), F32),
+        ]
+        + [jax.ShapeDtypeStruct((2, rows, ka), F32)] * len(early),
         scratch_shapes=[
             pltpu.VMEM((planes, rows, ka), F32),
             pltpu.VMEM((planes, rows, ka), F32),
@@ -606,37 +684,33 @@
         edge, sums, d0, nd0, tail, prev_tail, next_head, next_nhead, coef,
         x_twiddle(nx, ka), x_forward_matrix(nx, ka),
     )
-
-
-def combine_kernel(sums_ref, eta_ref, first_ref, second_ref, out_ref, steps_ref):
+    return d1, spec, pieces, eta, out
+
+
+def combine_kernel(gz, steps, edge_ref, sums_ref, eta_ref, first_ref, second_ref, steps_ref, *piece_refs):
+    kb = first_ref.shape[0] // gz
     eta0 = jnp.max(eta_ref[...])
     eta1 = jnp.max(step_of(sums_ref))
-    out_ref[...] = -(eta0 * first_ref[...] + eta1 * second_ref[...])
     steps_ref[0] = eta_ref[...]
     steps_ref[1] = jnp.full((8, LANES), eta1, F32)
-
-
-def combine_spectra(sums, eta, first, second):
-    planes, parts, rows, ka = first.shape
-    devices = sums.shape[0]
-    count = 4 if planes % 4 == 0 else 1
-    block = pl.BlockSpec((count, parts, rows, ka), lambda i: (i, 0, 0, 0))
-    return pl.pallas_call(
-        combine_kernel,
-        grid=(planes // count,),
-        in_specs=[
-            pl.BlockSpec((devices, 8, LANES), lambda i: (0, 0, 0)),
-            pl.BlockSpec((8, LANES), lambda i: (0, 0)),
-            block,
-            block,
-        ],
-        out_specs=[block, pl.BlockSpec((2, 8, LANES), lambda i: (0, 0, 0))],
-        out_shape=[
-            jax.ShapeDtypeStruct(first.shape, F32),
-            jax.ShapeDtypeStruct((2, 8, LANES), F32),
-        ],
+    for step, piece_ref in zip(steps, piece_refs):
+        core, chip = towards(edge_ref, gz, step)
+        at = core * kb + chip
+        piece_ref[...] = -(eta0 * first_ref[at] + eta1 * second_ref[at])
+
+
+def combine_spectra(edge, sums, eta, first, second, steps, gz):
+    vmem = pl.BlockSpec(memory_space=pltpu.VMEM)
+    etas, *pieces = pl.pallas_call(
+        functools.partial(combine_kernel, gz, steps),
+        in_specs=[pl.BlockSpec(memory_space=pltpu.SMEM)] + [vmem] * 4,
+        out_specs=[vmem] * (1 + len(steps)),
+        out_shape=[jax.ShapeDtypeStruct((2, 8, LANES), F32)]
+        + [jax.ShapeDtypeStruct(first.shape[1:], F32)] * len(steps),
+        compiler_params=pltpu.CompilerParams(vmem_limit_bytes=VMEM_LIMIT),
         name="combine_spectra",
-    )(sums, eta, first, second)
+    )(edge, sums, eta, first, second)
+    return pieces, etas
 
 
 def everywhere(sums):
@@ -653,8 +727,12 @@
     ka = blocks * HALF
     nx = ka * gy
 
-    flat = lax.axis_index("gy") * gz + lax.axis_index("gz")
-    edge = jnp.stack([(flat == 0).astype(jnp.int32), (flat == devices - 1).astype(jnp.int32)])
+    core = lax.axis_index("gz")
+    flat = lax.axis_index("gy") * gz + core
+    edge = jnp.stack([flat == 0, flat == devices - 1, core, lax.axis_index("gy")]).astype(jnp.int32)
+    steps = steps_of(gz, gy)
+    early = [step for step in steps if step in EARLY]
+    late = [step for step in steps if step not in EARLY]
     order = [(i % gz) * gy + i // gz for i in range(devices)]
     up = [(order[i + 1], order[i]) for i in range(devices - 1)]
     down = [(order[i], order[i + 1]) for i in range(devices - 1)]
@@ -670,27 +748,35 @@
     ).reshape(3, gy, 1, ka)
     coef = jnp.broadcast_to(coef, (3, gy, 8, ka))
 
-    spec = y_inverse(data, rows, gz, gy)
-    spec = lax.all_to_all(spec, ("gz", "gy"), 0, 0, tiled=True)
-    d0, head, tail = x_inverse(spec, coef, gz, nx)
+    pieces = y_inverse(edge, data, steps, rows, gz, gy)
+    pieces = [send(piece, step) for piece, step in zip(pieces, steps)]
+    d0, head, tail = x_inverse(edge, pieces, steps, coef, gz, nx)
     next_head = lax.ppermute(head, ("gz", "gy"), up)
     prev_tail = lax.ppermute(tail, ("gz", "gy"), down)
-    spec0, sums = first_projection(d0, coef, gz, nx)
+    spec0, first, sums = first_projection(edge, d0, early, coef, gz, nx)
     sums = everywhere(border_sums(edge, sums, tail, next_head, devices))
-    nd0, nhead, _ = x_inverse(spec0, coef, gz, nx)
+    first = [send(piece, step) for piece, step in zip(first, early)]
+    nd0, nhead, _ = x_inverse(edge, [spec0], [], coef, gz, nx)
     next_nhead = lax.ppermute(nhead, ("gz", "gy"), up)
-    d1, spec1, eta, sums = second_descent(
-        edge, sums, d0, nd0, tail, prev_tail, next_head, next_nhead, coef, gz, nx
+    d1, spec1, second, eta, sums = second_descent(
+        edge, sums, d0, nd0, tail, prev_tail, next_head, next_nhead, early, coef, gz, nx
     )
+    second = [send(piece, step) for piece, step in zip(second, early)]
     sums = everywhere(sums)
-    spec, steps = combine_spectra(sums, eta, spec0, spec1)
-    spec = lax.all_to_all(spec, ("gz", "gy"), 0, 0, tiled=True)
-    residual = y_forward(spec, data, gz)
-
-    volume = -(steps[0, 0, 0] * d0 + steps[1, 0, 0] * d1)
+    pieces, etas = combine_spectra(edge, sums, eta, spec0, spec1, late, gz)
+    pieces = [send(piece, step) for piece, step in zip(pieces, late)]
+    residual = y_forward(edge, etas, early, first, second, late, pieces, data, gz)
+
+    volume = -(etas[0, 0, 0] * d0 + etas[1, 0, 0] * d1)
     volume = volume.reshape(gz, gy, rows, ka).transpose(0, 2, 3, 1).reshape(gz, rows, nx)
-    volume = lax.all_to_all(volume, "gz", 0, 1, tiled=True)
-    return (volume, residual[None])
+    parts = [
+        send(lax.dynamic_index_in_dim(volume, lax.rem(core + r, gz), 0, False), (r, 0))
+        for r in range(gz)
+    ]
+    volume = jnp.zeros((gz, rows, nx), F32)
+    for r, part in enumerate(parts):
+        volume = lax.dynamic_update_index_in_dim(volume, part, lax.rem(core + gz - r, gz), 0)
+    return (volume.reshape(1, gz * rows, nx), residual[None])
 
 
 NX = 4096
@@ -937,7 +1023,7 @@
 
 def tiles_fit(mesh, ny, blocks):
     rows = ny // (mesh.shape["gz"] * mesh.shape["gy"])
-    return rows % 16 == 0 and blocks // mesh.shape["gy"] % 2 == 0
+    return rows % 16 == 0 and mesh.shape["gy"] % YR == 0 and blocks // mesh.shape["gy"] % 2 == 0
 
 
 def solution(mesh):

time: 334 us -> 392 us (1.17)
  starting transfers between devices: 20.3 us -> 122 us
  waiting for transfers between devices: 193 us -> 102 us
  local copies, waits for them, and re-layouts: 23.7 us -> 97.2 us
  Pallas kernels: 66.1 us -> 46.4 us
  blocking collectives: 24 us -> 17.6 us
    all_to_all x2 -> x0, waiting for transfers between devices: 192 us -> none  [shards(): spec = lax.all_to_all(spec, ('gz', 'gy'), 0, 0, tiled=True)]
    ppermute x0 -> x63, starting transfers between devices: none -> 111 us  [send(): return lax.ppermute(piece, ('gz', 'gy'), route)]
    ppermute x0 -> x63, waiting for transfers between devices: none -> 101 us  [send(): return lax.ppermute(piece, ('gz', 'gy'), route)]
    unnamed x49 -> x244, local copies, waits for them, and re-layouts: 14.7 us -> 77.9 us
    pallas_call x7, Pallas kernels: 64.5 us -> 44.9 us  [the longest x2 11.3 us: x_inverse(): pl.pallas_call(functools.partial(x_inverse_kernel, gz, steps), in_specs=[...]
    all_to_all x2 -> x0, starting transfers between devices: 11.3 us -> none  [shards(): spec = lax.all_to_all(spec, ('gz', 'gy'), 0, 0, tiled=True)]
    dynamic_slice x0 -> x3, local copies, waits for them, and re-layouts: none -> 10.9 us  [shards(): lax.dynamic_index_in_dim(volume, lax.rem(core + r, gz), 0, False)]
    all_to_all x1 -> x0, blocking collectives: 6.3 us -> none  [shards(): volume = lax.all_to_all(volume, 'gz', 0, 1, tiled=True)]
  transfers between devices with their start and end apart: 6 -> 67, of which waited for: 3 -> 35; matrix products, arithmetic and copies ran while one was open for 0% -> 6% of each run, Pallas kernels for 4% -> 6%
where the time goes in v3:
time: 392 us; the launch traced here: 390 us
  starting transfers between devices  122 us (31%)
  waiting for transfers between devices  102 us (26%)
  local copies, waits for them, and re-layouts  97.2 us (25%)
  Pallas kernels  46.4 us (12%)
  blocking collectives  17.6 us (4%)
  other arithmetic  4.48 us (1%)
    ppermute x63, starting transfers between devices, send(): return lax.ppermute(piece, ('gz', 'gy'), route)  111 us
    ppermute x63, waiting for transfers between devices, send(): return lax.ppermute(piece, ('gz', 'gy'), route)  101 us
    unnamed x244, local copies, waits for them, and re-layouts  77.9 us
    all_to_all x1, blocking collectives, everywhere(): return lax.all_to_all(sums, ('gz', 'gy'), 0, 0, tiled=True)  17.6 us
    pallas_call x2, Pallas kernels, x_inverse(): pl.pallas_call(functools.partial(x_inverse_kernel, gz, steps), in_specs=[...  11.3 us
    dynamic_slice x3, local copies, waits for them, and re-layouts, shards(): lax.dynamic_index_in_dim(volume, lax.rem(core + r, gz), 0, False)  10.9 us
    pallas_call x1, Pallas kernels, y_forward(): pl.pallas_call(functools.partial(y_forward_kernel, gz, early, steps), gri...  10.5 us
    pallas_call x1, Pallas kernels, second_descent(): pl.pallas_call(functools.partial(second_kernel, gz, early), in_specs=[pl....  8.12 us
  transfers between devices with their start and end apart: 67, of which 35 were waited for; matrix products, arithmetic and copies ran while one was open for 6% of the time, Pallas kernels for 6%

profile of v3, /device:TPU:0, one launch (start us, length us, event | category | flops | bytes accessed | tf_op | source)
XLA Modules:
  0.0 390.3 jit_solution(8025873230210781930)
XLA Ops:
  4.7 6.8 %y_inverse.1 = (f32[2,64,256]{2,1,0:T(8,128)S(1)}, f32[2,64,256]{2,1,0:T(8,128)S(1)}, f32[2,64,256]{2,1,0:T(8,128)S(1)}, f32[2,64,256]{2,1,0:T(8,128)S(1)}, f32[...) custom-call(s32[4]{0:T(128)S(1)} %pad_add_fusion.edge_ref, ...), custom_call_target="tpu_custom_call" | custom-call | tf_op jit(solution)/shard_map/y_inverse/pallas_call | solution.py:277
  11.5 7.0 %collective-permute-start = (f32[2,64,256]{2,1,0:T(8,128)S(1)}, f32[2,64,256]{2,1,0:T(8,128)S(1)}, u32[]{:S(2)}, u32[]{:S(2)}) collective-permute-start(f32[2,64,256]{2,1,0:T(8,128)S(1)} %get-tuple-element.78), channel_id=1, source_target_pairs={{0,15},{1,14},{2,13},{3,12},{4,11},{5,10},{6,9},{7,8},{8,7},{9,6},... | collective-permute-start | bytes 393224 | tf_op jit(solution)/shard_map/ppermute | solution.py:189
  28.0 12.2 %collective-permute-start.14 = (f32[2,64,256]{2,1,0:T(8,128)S(1)}, f32[2,64,256]{2,1,0:T(8,128)S(1)}, u32[]{:S(2)}, u32[]{:S(2)}) collective-permute-start(f32[2,64,256]{2,1,0:T(8,128)S(1)} %get-tuple-element.92), channel_id=1, source_target_pairs={{0,8},{1,9},{2,10},{3,11},{4,12},{5,13},{6,14},{7,15},{8,0},{9,1},... | collective-permute-start | bytes 393224 | tf_op jit(solution)/shard_map/ppermute | solution.py:189
  42.3 7.4 %collective-permute-done.11.refs_11_ = f32[2,64,256]{2,1,0:T(8,128)S(1)} collective-permute-done((f32[2,64,256]{2,1,0:T(8,128)S(1)}, f32[2,64,256]{2,1,0:T(8,128)S(1)}, u32[]{:S(2)}, u32[]{:S(2)}) %collective-permute-start.11) | collective-permute-done | bytes 131104 | tf_op jit(solution)/shard_map/ppermute | solution.py:189
  51.0 4.8 %collective-permute-done.12.refs_12_ = f32[2,64,256]{2,1,0:T(8,128)S(1)} collective-permute-done((f32[2,64,256]{2,1,0:T(8,128)S(1)}, f32[2,64,256]{2,1,0:T(8,128)S(1)}, u32[]{:S(2)}, u32[]{:S(2)}) %collective-permute-start.12) | collective-permute-done | bytes 131104 | tf_op jit(solution)/shard_map/ppermute | solution.py:189
  66.9 3.3 collective-permute-done.17.refs_17_
  74.7 3.3 collective-permute-done.19.refs_19_
  109.5 11.8 %collective-permute-start.9 = (f32[2,64,256]{2,1,0:T(8,128)S(1)}, f32[2,64,256]{2,1,0:T(8,128)S(1)}, u32[]{:S(2)}, u32[]{:S(2)}) collective-permute-start(f32[2,64,256]{2,1,0:T(8,128)S(1)} %get-tuple-element.87), channel_id=1, source_target_pairs={{0,27},{1,26},{2,25},{3,24},{4,31},{5,30},{6,29},{7,28},{8,19},{9,... | collective-permute-start | bytes 393224 | tf_op jit(solution)/shard_map/ppermute | solution.py:189
  123.3 10.6 %collective-permute-done.8.refs_8_ = f32[2,64,256]{2,1,0:T(8,128)S(1)} collective-permute-done((f32[2,64,256]{2,1,0:T(8,128)S(1)}, f32[2,64,256]{2,1,0:T(8,128)S(1)}, u32[]{:S(2)}, u32[]{:S(2)}) %collective-permute-start.8) | collective-permute-done | bytes 131104 | tf_op jit(solution)/shard_map/ppermute | solution.py:189
  165.1 5.6 %x_inverse.2 = (f32[32,64,256]{2,1,0:T(8,128)S(1)}, f32[2,32,256]{2,1,0:T(8,128)S(1)}, f32[32,256]{1,0:T(8,128)S(1)}) custom-call(s32[4]{0:T(128)S(1)} %pad_add_fusion.edge_ref, f32[2,64,256]{2,1,0:T(8,128)S(1)} %collective-permute-done.refs_0_, f32[2,64,256]{2,1,0:T(8,128)S(1)} %copy-done.21, f32[2,64,256]{2,1,0:T(8,128)S(1)} %copy-done.43, ...), custom_call_target="tpu_custom_call" | custom-call | tf_op jit(solution)/shard_map/x_inverse/pallas_call | solution.py:447
  172.0 6.1 %first_projection.1 = (f32[3,8,128]{2,1,0:T(8,128)S(1)}, f32[32,2,64,256]{3,2,1,0:T(8,128)S(1)}) custom-call(s32[4]{0:T(128)S(1)} %pad_add_fusion.edge_ref, f32[32,64,256]{2,1,0:T(8,128)S(1)} %get-tuple-element.110.field_ref.d0_ref, f32[3,16,8,256]{3,2,1,0:T(8,128)S(1)} %broadcast_in_dim.27.refs_32_.coef_ref.refs_1_, f32[2,16,8,256]{3,2,1,0:T(8,128)S(1)} %copy-done.5, ...), custom_call_target="tpu_custom_call" | custom-call | tf_op jit(solution)/shard_map/first_projection/pallas_call | solution.py:557
  182.9 4.6 %all-to-all-start = ((f32[32,8,128]{2,1,0:T(8,128)}), f32[32,8,128]{2,1,0:T(8,128)S(1)}, u32[]{:S(2)}, u32[]{:S(2)}) async-start(f32[32,8,128]{2,1,0:T(8,128)} %border_sums.1), calls=%async_computation | async-start | bytes 262144 | tf_op jit(solution)/shard_map/all_to_all | solution.py:717
  191.4 5.7 %x_inverse.3 = (f32[32,64,256]{2,1,0:T(8,128)S(1)}, f32[2,32,256]{2,1,0:T(8,128)S(1)}, f32[32,256]{1,0:T(8,128)}) custom-call(s32[4]{0:T(128)S(1)} %copy-done.83, f32[32,2,64,256]{3,2,1,0:T(8,128)S(1)} %copy-done.1, f32[3,16,8,256]{3,2,1,0:T(8,128)S(1)} %broadcast_in_dim.27.refs_32_.coef_ref.refs_1_, f32[2,16,8,256]{3,2,1,0:T(8,128)S(1)} %copy-done.5, ...), custom_call_target="tpu_custom_call" | custom-call | tf_op jit(solution)/shard_map/x_inverse/pallas_call | solution.py:447
  199.7 3.2 collective-permute-start.32
  206.7 8.1 %second_descent.1 = (f32[32,64,256]{2,1,0:T(8,128)S(1)}, f32[8,128]{1,0:T(8,128)S(1)}, f32[32,8,128]{2,1,0:T(8,128)S(1)}, f32[32,2,64,256]{3,2,1,0:T(8,128)S(1)}) custom-call(s32[4]{0:T(128)S(1)} %copy-done.84, f32[32,8,128]{2,1,0:T(8,128)S(1)} %all-to-all-done.sums_ref, f32[32,64,256]{2,1,0:T(8,128)S(1)} %get-tuple-element.110.field_ref.d0_ref, ...), custom_call_target="tpu_custom_call" | custom-call | tf_op jit(solution)/shard_map/second_descent/pallas_call | solution.py:665
  216.1 17.6 %all_to_all.10.sums_ref = f32[32,8,128]{2,1,0:T(8,128)S(1)} all-to-all(f32[32,8,128]{2,1,0:T(8,128)S(1)} %get-tuple-element.117), channel_id=1, replica_groups=mesh['gz'=2,'gy'=16] {'gz','gy'}, dimensions={0} | all-to-all | bytes 262144 | tf_op jit(solution)/shard_map/all_to_all | solution.py:717
  251.4 3.1 collective-permute-start.36
  256.1 3.3 collective-permute-start.38
  263.9 4.4 %add_negate_fusion = f32[32,64,256]{2,1,0:T(8,128)} fusion(f32[32,64,256]{2,1,0:T(8,128)} %copy-done.10, f32[32,64,256]{2,1,0:T(8,128)S(1)} %get-tuple-element.110.field_ref.d0_ref, f32[]{:T(128)} %bitcast.9, f32[]{:T(128)} %bitcast.8), kind=kLoop, calls=%fused_computation | loop fusion | flops 2097152 | bytes 6291464 | tf_op jit(solution)/shard_map/neg | solution.py:770
  268.3 4.9 %copy.21 = f32[2,16,64,256]{2,1,3,0:T(8,128)} copy(f32[2,16,64,256]{3,2,1,0:T(8,128)} %bitcast.23) | data formatting | bytes 4194304 | tf_op jit(solution)/shard_map/reshape | solution.py:771
  277.2 12.1 %collective-permute-start.43 = (f32[2,64,256]{2,1,0:T(8,128)S(1)}, f32[2,64,256]{2,1,0:T(8,128)S(1)}, u32[]{:S(2)}, u32[]{:S(2)}) collective-permute-start(f32[2,64,256]{2,1,0:T(8,128)S(1)} %copy-done.111), channel_id=1, source_target_pairs={{0,11},{1,10},{2,9},{3,8},{4,15},{5,14},{6,13},{7,12},{8,3},{9,2},... | collective-permute-start | bytes 393224 | tf_op jit(solution)/shard_map/ppermute | solution.py:189
  290.6 8.6 %collective-permute-start.45 = (f32[2,64,256]{2,1,0:T(8,128)S(1)}, f32[2,64,256]{2,1,0:T(8,128)S(1)}, u32[]{:S(2)}, u32[]{:S(2)}) collective-permute-start(f32[2,64,256]{2,1,0:T(8,128)S(1)} %copy-done.107), channel_id=1, source_target_pairs={{0,10},{1,11},{2,8},{3,9},{4,14},{5,15},{6,12},{7,13},{8,2},{9,3},... | collective-permute-start | bytes 393224 | tf_op jit(solution)/shard_map/ppermute | solution.py:189
  299.2 4.5 %constant_dynamic-slice_fusion = (f32[1,64,4096]{1,2,0:T(8,128)}, f32[1,64,4096]{1,2,0:T(8,128)}) fusion(f32[2,64,4096]{1,2,0:T(8,128)} %bitcast.22, s32[]{:T(128)S(6)} %select_n.29, s32[]{:T(128)S(6)} %select_n.27), kind=kLoop, calls=%fused_computation.6 | loop fusion | bytes 4194312 | tf_op jit(solution)/shard_map/jit(dynamic_index_in_dim)/dynamic_slice | solution.py:773
  303.7 3.3 copy.23
  308.3 3.8 collective-permute-done.43.refs_8_
  312.6 11.4 %collective-permute-done.45.refs_10_ = f32[2,64,256]{2,1,0:T(8,128)S(1)} collective-permute-done((f32[2,64,256]{2,1,0:T(8,128)S(1)}, f32[2,64,256]{2,1,0:T(8,128)S(1)}, u32[]{:S(2)}, u32[]{:S(2)}) %collective-permute-start.45) | collective-permute-done | bytes 131104 | tf_op jit(solution)/shard_map/ppermute | solution.py:189
  324.0 7.3 %collective-permute-done.46.refs_11_ = f32[2,64,256]{2,1,0:T(8,128)S(1)} collective-permute-done((f32[2,64,256]{2,1,0:T(8,128)S(1)}, f32[2,64,256]{2,1,0:T(8,128)S(1)}, u32[]{:S(2)}, u32[]{:S(2)}) %collective-permute-start.46) | collective-permute-done | bytes 131104 | tf_op jit(solution)/shard_map/ppermute | solution.py:189
  331.3 4.8 %collective-permute-done.47.refs_12_ = f32[2,64,256]{2,1,0:T(8,128)S(1)} collective-permute-done((f32[2,64,256]{2,1,0:T(8,128)S(1)}, f32[2,64,256]{2,1,0:T(8,128)S(1)}, u32[]{:S(2)}, u32[]{:S(2)}) %collective-permute-start.47) | collective-permute-done | bytes 131104 | tf_op jit(solution)/shard_map/ppermute | solution.py:189
  337.7 3.9 %collective-permute-done.49.refs_14_ = f32[2,64,256]{2,1,0:T(8,128)S(1)} collective-permute-done((f32[2,64,256]{2,1,0:T(8,128)S(1)}, f32[2,64,256]{2,1,0:T(8,128)S(1)}, u32[]{:S(2)}, u32[]{:S(2)}) %collective-permute-start.49) | collective-permute-done | bytes 131104 | tf_op jit(solution)/shard_map/ppermute | solution.py:189
  342.7 4.6 %collective-permute-done.51.refs_16_ = f32[2,64,256]{2,1,0:T(8,128)S(1)} collective-permute-done((f32[2,64,256]{2,1,0:T(8,128)S(1)}, f32[2,64,256]{2,1,0:T(8,128)S(1)}, u32[]{:S(2)}, u32[]{:S(2)}) %collective-permute-start.51) | collective-permute-done | bytes 131104 | tf_op jit(solution)/shard_map/ppermute | solution.py:189
  364.8 3.1 copy.22
  377.1 10.5 %y_forward.1 = f32[4,2048,128]{2,1,0:T(8,128)} custom-call(s32[4]{0:T(128)S(1)} %copy-done.84, f32[2,8,128]{2,1,0:T(8,128)S(1)} %get-tuple-element.120.eta_ref, f32[2,64,256]{2,1,0:T(8,128)S(1)} %collective-permute-done.35.refs_0_, f32[2,64,256]{2,1,0:T(8,128)S(1)} %collective-permute-done.36.refs_1_, f32[2,64,256]{2,1,0:T(8,128)S(1)} %collective-permute-done.37.refs_2_, ...), custom_call_target="tpu_custom_call" | custom-call | tf_op jit(solution)/shard_map/y_forward/pallas_call | solution.py:359
  (373 shorter events, 177.5 us)
Async XLA Ops:
  18.5 23.1 %collective-permute-start.10 = (f32[2,64,256]{2,1,0:T(8,128)S(1)}, f32[2,64,256]{2,1,0:T(8,128)S(1)}, u32[]{:S(2)}, u32[]{:S(2)}) collective-permute-start(f32[2,64,256]{2,1,0:T(8,128)S(1)} %get-tuple-element.88), channel_id=1, source_target_pairs={{0,10},{1,11},{2,8},{3,9},{4,14},{5,15},{6,12},{7,13},{8,2},{9,3},... | collective-permute-start | bytes 393224 | tf_op jit(solution)/shard_map/ppermute | solution.py:189
  19.6 30.1 %collective-permute-start.11 = (f32[2,64,256]{2,1,0:T(8,128)S(1)}, f32[2,64,256]{2,1,0:T(8,128)S(1)}, u32[]{:S(2)}, u32[]{:S(2)}) collective-permute-start(f32[2,64,256]{2,1,0:T(8,128)S(1)} %get-tuple-element.89), channel_id=1, source_target_pairs={{0,26},{1,27},{2,24},{3,25},{4,30},{5,31},{6,28},{7,29},{8,18},{9,... | collective-permute-start | bytes 393224 | tf_op jit(solution)/shard_map/ppermute | solution.py:189
  21.9 34.0 %collective-permute-start.12 = (f32[2,64,256]{2,1,0:T(8,128)S(1)}, f32[2,64,256]{2,1,0:T(8,128)S(1)}, u32[]{:S(2)}, u32[]{:S(2)}) collective-permute-start(f32[2,64,256]{2,1,0:T(8,128)S(1)} %get-tuple-element.90), channel_id=1, source_target_pairs={{0,9},{1,8},{2,11},{3,10},{4,13},{5,12},{6,15},{7,14},{8,1},{9,0},... | collective-permute-start | bytes 393224 | tf_op jit(solution)/shard_map/ppermute | solution.py:189
  23.6 33.2 %collective-permute-start.13 = (f32[2,64,256]{2,1,0:T(8,128)S(1)}, f32[2,64,256]{2,1,0:T(8,128)S(1)}, u32[]{:S(2)}, u32[]{:S(2)}) collective-permute-start(f32[2,64,256]{2,1,0:T(8,128)S(1)} %get-tuple-element.91), channel_id=1, source_target_pairs={{0,25},{1,24},{2,27},{3,26},{4,29},{5,28},{6,31},{7,30},{8,17},{9,... | collective-permute-start | bytes 393224 | tf_op jit(solution)/shard_map/ppermute | solution.py:189
  28.0 33.5 %collective-permute-start.14 = (f32[2,64,256]{2,1,0:T(8,128)S(1)}, f32[2,64,256]{2,1,0:T(8,128)S(1)}, u32[]{:S(2)}, u32[]{:S(2)}) collective-permute-start(f32[2,64,256]{2,1,0:T(8,128)S(1)} %get-tuple-element.92), channel_id=1, source_target_pairs={{0,8},{1,9},{2,10},{3,11},{4,12},{5,13},{6,14},{7,15},{8,0},{9,1},... | collective-permute-start | bytes 393224 | tf_op jit(solution)/shard_map/ppermute | solution.py:189
  41.7 20.8 %collective-permute-start.15 = (f32[2,64,256]{2,1,0:T(8,128)S(1)}, f32[2,64,256]{2,1,0:T(8,128)S(1)}, u32[]{:S(2)}, u32[]{:S(2)}) collective-permute-start(f32[2,64,256]{2,1,0:T(8,128)S(1)} %get-tuple-element.93), channel_id=1, source_target_pairs={{0,24},{1,25},{2,26},{3,27},{4,28},{5,29},{6,30},{7,31},{8,16},{9,... | collective-permute-start | bytes 393224 | tf_op jit(solution)/shard_map/ppermute | solution.py:189
  49.7 15.9 %collective-permute-start.16 = (f32[2,64,256]{2,1,0:T(8,128)S(1)}, f32[2,64,256]{2,1,0:T(8,128)S(1)}, u32[]{:S(2)}, u32[]{:S(2)}) collective-permute-start(f32[2,64,256]{2,1,0:T(8,128)S(1)} %get-tuple-element.94), channel_id=1, source_target_pairs={{0,7},{1,6},{2,5},{3,4},{4,3},{5,2},{6,1},{7,0},{8,15},{9,14},{10,... | collective-permute-start | bytes 393224 | tf_op jit(solution)/shard_map/ppermute | solution.py:189
  57.5 15.9 %collective-permute-start.18 = (f32[2,64,256]{2,1,0:T(8,128)S(1)}, f32[2,64,256]{2,1,0:T(8,128)S(1)}, u32[]{:S(2)}, u32[]{:S(2)}) collective-permute-start(f32[2,64,256]{2,1,0:T(8,128)S(1)} %get-tuple-element.96), channel_id=1, source_target_pairs={{0,6},{1,7},{2,4},{3,5},{4,2},{5,3},{6,0},{7,1},{8,14},{9,15},{10,... | collective-permute-start | bytes 393224 | tf_op jit(solution)/shard_map/ppermute | solution.py:189
  62.2 15.8 %collective-permute-start.19 = (f32[2,64,256]{2,1,0:T(8,128)S(1)}, f32[2,64,256]{2,1,0:T(8,128)S(1)}, u32[]{:S(2)}, u32[]{:S(2)}) collective-permute-start(f32[2,64,256]{2,1,0:T(8,128)S(1)} %get-tuple-element.97), channel_id=1, source_target_pairs={{0,22},{1,23},{2,20},{3,21},{4,18},{5,19},{6,16},{7,17},{8,30},{9,... | collective-permute-start | bytes 393224 | tf_op jit(solution)/shard_map/ppermute | solution.py:189
  63.1 15.5 %collective-permute-start.2 = (f32[2,64,256]{2,1,0:T(8,128)S(1)}, f32[2,64,256]{2,1,0:T(8,128)S(1)}, u32[]{:S(2)}, u32[]{:S(2)}) collective-permute-start(f32[2,64,256]{2,1,0:T(8,128)S(1)} %get-tuple-element.80), channel_id=1, source_target_pairs={{0,14},{1,15},{2,12},{3,13},{4,10},{5,11},{6,8},{7,9},{8,6},{9,7},... | collective-permute-start | bytes 393224 | tf_op jit(solution)/shard_map/ppermute | solution.py:189
  66.3 14.8 %collective-permute-start.20 = (f32[2,64,256]{2,1,0:T(8,128)S(1)}, f32[2,64,256]{2,1,0:T(8,128)S(1)}, u32[]{:S(2)}, u32[]{:S(2)}) collective-permute-start(f32[2,64,256]{2,1,0:T(8,128)S(1)} %get-tuple-element.98), channel_id=1, source_target_pairs={{0,5},{1,4},{2,7},{3,6},{4,1},{5,0},{6,3},{7,2},{8,13},{9,12},{10,... | collective-permute-start | bytes 393224 | tf_op jit(solution)/shard_map/ppermute | solution.py:189
  98.8 22.5 %collective-permute-start.5 = (f32[2,64,256]{2,1,0:T(8,128)S(1)}, f32[2,64,256]{2,1,0:T(8,128)S(1)}, u32[]{:S(2)}, u32[]{:S(2)}) collective-permute-start(f32[2,64,256]{2,1,0:T(8,128)S(1)} %get-tuple-element.83), channel_id=1, source_target_pairs={{0,29},{1,28},{2,31},{3,30},{4,25},{5,24},{6,27},{7,26},{8,21},{9,... | collective-permute-start | bytes 393224 | tf_op jit(solution)/shard_map/ppermute | solution.py:189
  101.9 20.0 %collective-permute-start.6 = (f32[2,64,256]{2,1,0:T(8,128)S(1)}, f32[2,64,256]{2,1,0:T(8,128)S(1)}, u32[]{:S(2)}, u32[]{:S(2)}) collective-permute-start(f32[2,64,256]{2,1,0:T(8,128)S(1)} %get-tuple-element.84), channel_id=1, source_target_pairs={{0,12},{1,13},{2,14},{3,15},{4,8},{5,9},{6,10},{7,11},{8,4},{9,5},... | collective-permute-start | bytes 393224 | tf_op jit(solution)/shard_map/ppermute | solution.py:189
  104.3 18.4 %collective-permute-start.7 = (f32[2,64,256]{2,1,0:T(8,128)S(1)}, f32[2,64,256]{2,1,0:T(8,128)S(1)}, u32[]{:S(2)}, u32[]{:S(2)}) collective-permute-start(f32[2,64,256]{2,1,0:T(8,128)S(1)} %get-tuple-element.85), channel_id=1, source_target_pairs={{0,28},{1,29},{2,30},{3,31},{4,24},{5,25},{6,26},{7,27},{8,20},{9,... | collective-permute-start | bytes 393224 | tf_op jit(solution)/shard_map/ppermute | solution.py:189
  106.7 27.1 %collective-permute-start.8 = (f32[2,64,256]{2,1,0:T(8,128)S(1)}, f32[2,64,256]{2,1,0:T(8,128)S(1)}, u32[]{:S(2)}, u32[]{:S(2)}) collective-permute-start(f32[2,64,256]{2,1,0:T(8,128)S(1)} %get-tuple-element.86), channel_id=1, source_target_pairs={{0,11},{1,10},{2,9},{3,8},{4,15},{5,14},{6,13},{7,12},{8,3},{9,2},... | collective-permute-start | bytes 393224 | tf_op jit(solution)/shard_map/ppermute | solution.py:189
  109.5 26.7 %collective-permute-start.9 = (f32[2,64,256]{2,1,0:T(8,128)S(1)}, f32[2,64,256]{2,1,0:T(8,128)S(1)}, u32[]{:S(2)}, u32[]{:S(2)}) collective-permute-start(f32[2,64,256]{2,1,0:T(8,128)S(1)} %get-tuple-element.87), channel_id=1, source_target_pairs={{0,27},{1,26},{2,25},{3,24},{4,31},{5,30},{6,29},{7,28},{8,19},{9,... | collective-permute-start | bytes 393224 | tf_op jit(solution)/shard_map/ppermute | solution.py:189
  182.9 21.4 %all-to-all-start = ((f32[32,8,128]{2,1,0:T(8,128)}), f32[32,8,128]{2,1,0:T(8,128)S(1)}, u32[]{:S(2)}, u32[]{:S(2)}) async-start(f32[32,8,128]{2,1,0:T(8,128)} %border_sums.1), calls=%async_computation | async-start | bytes 262144 | tf_op jit(solution)/shard_map/all_to_all | solution.py:717
  251.4 21.7 %collective-permute-start.36 = (f32[2,64,256]{2,1,0:T(8,128)}, f32[2,64,256]{2,1,0:T(8,128)S(1)}, u32[]{:S(2)}, u32[]{:S(2)}) collective-permute-start(f32[2,64,256]{2,1,0:T(8,128)} %copy-done.118), channel_id=1, source_target_pairs={{0,31},{1,30},{2,29},{3,28},{4,27},{5,26},{6,25},{7,24},{8,23},{9,... | collective-permute-start | bytes 393224 | tf_op jit(solution)/shard_map/ppermute | solution.py:189
  254.5 20.6 %collective-permute-start.37 = (f32[2,64,256]{2,1,0:T(8,128)}, f32[2,64,256]{2,1,0:T(8,128)S(1)}, u32[]{:S(2)}, u32[]{:S(2)}) collective-permute-start(f32[2,64,256]{2,1,0:T(8,128)} %copy-done.117), channel_id=1, source_target_pairs={{0,14},{1,15},{2,12},{3,13},{4,10},{5,11},{6,8},{7,9},{8,6},{9,7},... | collective-permute-start | bytes 393224 | tf_op jit(solution)/shard_map/ppermute | solution.py:189
  256.1 21.1 %collective-permute-start.38 = (f32[2,64,256]{2,1,0:T(8,128)}, f32[2,64,256]{2,1,0:T(8,128)S(1)}, u32[]{:S(2)}, u32[]{:S(2)}) collective-permute-start(f32[2,64,256]{2,1,0:T(8,128)} %copy-done.116), channel_id=1, source_target_pairs={{0,30},{1,31},{2,28},{3,29},{4,26},{5,27},{6,24},{7,25},{8,22},{9,... | collective-permute-start | bytes 393224 | tf_op jit(solution)/shard_map/ppermute | solution.py:189
  259.4 29.9 %collective-permute-start.39 = (f32[2,64,256]{2,1,0:T(8,128)}, f32[2,64,256]{2,1,0:T(8,128)S(1)}, u32[]{:S(2)}, u32[]{:S(2)}) collective-permute-start(f32[2,64,256]{2,1,0:T(8,128)} %copy-done.115), channel_id=1, source_target_pairs={{0,13},{1,12},{2,15},{3,14},{4,9},{5,8},{6,11},{7,10},{8,5},{9,4},... | collective-permute-start | bytes 393224 | tf_op jit(solution)/shard_map/ppermute | solution.py:189
  261.3 29.3 %collective-permute-start.40 = (f32[2,64,256]{2,1,0:T(8,128)}, f32[2,64,256]{2,1,0:T(8,128)S(1)}, u32[]{:S(2)}, u32[]{:S(2)}) collective-permute-start(f32[2,64,256]{2,1,0:T(8,128)} %copy-done.114), channel_id=1, source_target_pairs={{0,29},{1,28},{2,31},{3,30},{4,25},{5,24},{6,27},{7,26},{8,21},{9,... | collective-permute-start | bytes 393224 | tf_op jit(solution)/shard_map/ppermute | solution.py:189
  273.2 33.8 %collective-permute-start.41 = (f32[2,64,256]{2,1,0:T(8,128)}, f32[2,64,256]{2,1,0:T(8,128)S(1)}, u32[]{:S(2)}, u32[]{:S(2)}) collective-permute-start(f32[2,64,256]{2,1,0:T(8,128)} %get-tuple-element.128), channel_id=1, source_target_pairs={{0,12},{1,13},{2,14},{3,15},{4,8},{5,9},{6,10},{7,11},{8,4},{9,5},... | collective-permute-start | bytes 393224 | tf_op jit(solution)/shard_map/ppermute | solution.py:189
  275.1 32.7 %collective-permute-start.42 = (f32[2,64,256]{2,1,0:T(8,128)S(1)}, f32[2,64,256]{2,1,0:T(8,128)S(1)}, u32[]{:S(2)}, u32[]{:S(2)}) collective-permute-start(f32[2,64,256]{2,1,0:T(8,128)S(1)} %copy-done.113), channel_id=1, source_target_pairs={{0,28},{1,29},{2,30},{3,31},{4,24},{5,25},{6,26},{7,27},{8,20},{9,... | collective-permute-start | bytes 393224 | tf_op jit(solution)/shard_map/ppermute | solution.py:189
  277.2 34.9 %collective-permute-start.43 = (f32[2,64,256]{2,1,0:T(8,128)S(1)}, f32[2,64,256]{2,1,0:T(8,128)S(1)}, u32[]{:S(2)}, u32[]{:S(2)}) collective-permute-start(f32[2,64,256]{2,1,0:T(8,128)S(1)} %copy-done.111), channel_id=1, source_target_pairs={{0,11},{1,10},{2,9},{3,8},{4,15},{5,14},{6,13},{7,12},{8,3},{9,2},... | collective-permute-start | bytes 393224 | tf_op jit(solution)/shard_map/ppermute | solution.py:189
  289.3 23.0 %collective-permute-start.44 = (f32[2,64,256]{2,1,0:T(8,128)S(1)}, f32[2,64,256]{2,1,0:T(8,128)S(1)}, u32[]{:S(2)}, u32[]{:S(2)}) collective-permute-start(f32[2,64,256]{2,1,0:T(8,128)S(1)} %copy-done.109), channel_id=1, source_target_pairs={{0,27},{1,26},{2,25},{3,24},{4,31},{5,30},{6,29},{7,28},{8,19},{9,... | collective-permute-start | bytes 393224 | tf_op jit(solution)/shard_map/ppermute | solution.py:189
  290.6 33.5 %collective-permute-start.45 = (f32[2,64,256]{2,1,0:T(8,128)S(1)}, f32[2,64,256]{2,1,0:T(8,128)S(1)}, u32[]{:S(2)}, u32[]{:S(2)}) collective-permute-start(f32[2,64,256]{2,1,0:T(8,128)S(1)} %copy-done.107), channel_id=1, source_target_pairs={{0,10},{1,11},{2,8},{3,9},{4,14},{5,15},{6,12},{7,13},{8,2},{9,3},... | collective-permute-start | bytes 393224 | tf_op jit(solution)/shard_map/ppermute | solution.py:189
  307.0 80.7 %collective-permute-start.34 = (f32[64,4096]{1,0:T(8,128)}, f32[64,4096]{1,0:T(8,128)}, u32[]{:S(2)}, u32[]{:S(2)}) collective-permute-start(f32[64,4096]{1,0:T(8,128)} %bitcast.26), channel_id=1, source_target_pairs={{0,16},{1,17},{2,18},{3,19},{4,20},{5,21},{6,22},{7,23},{8,24},{9,... | collective-permute-start | bytes 3145736 | tf_op jit(solution)/shard_map/ppermute | solution.py:189
  307.8 23.5 %collective-permute-start.46 = (f32[2,64,256]{2,1,0:T(8,128)S(1)}, f32[2,64,256]{2,1,0:T(8,128)S(1)}, u32[]{:S(2)}, u32[]{:S(2)}) collective-permute-start(f32[2,64,256]{2,1,0:T(8,128)S(1)} %copy-done.105), channel_id=1, source_target_pairs={{0,26},{1,27},{2,24},{3,25},{4,30},{5,31},{6,28},{7,29},{8,18},{9,... | collective-permute-start | bytes 393224 | tf_op jit(solution)/shard_map/ppermute | solution.py:189
  312.1 24.0 %collective-permute-start.47 = (f32[2,64,256]{2,1,0:T(8,128)S(1)}, f32[2,64,256]{2,1,0:T(8,128)S(1)}, u32[]{:S(2)}, u32[]{:S(2)}) collective-permute-start(f32[2,64,256]{2,1,0:T(8,128)S(1)} %copy-done.103), channel_id=1, source_target_pairs={{0,9},{1,8},{2,11},{3,10},{4,13},{5,12},{6,15},{7,14},{8,1},{9,0},... | collective-permute-start | bytes 393224 | tf_op jit(solution)/shard_map/ppermute | solution.py:189
  312.3 25.3 %collective-permute-start.48 = (f32[2,64,256]{2,1,0:T(8,128)S(1)}, f32[2,64,256]{2,1,0:T(8,128)S(1)}, u32[]{:S(2)}, u32[]{:S(2)}) collective-permute-start(f32[2,64,256]{2,1,0:T(8,128)S(1)} %copy-done.101), channel_id=1, source_target_pairs={{0,25},{1,24},{2,27},{3,26},{4,29},{5,28},{6,31},{7,30},{8,17},{9,... | collective-permute-start | bytes 393224 | tf_op jit(solution)/shard_map/ppermute | solution.py:189
  324.0 17.6 %collective-permute-start.49 = (f32[2,64,256]{2,1,0:T(8,128)S(1)}, f32[2,64,256]{2,1,0:T(8,128)S(1)}, u32[]{:S(2)}, u32[]{:S(2)}) collective-permute-start(f32[2,64,256]{2,1,0:T(8,128)S(1)} %copy-done.99), channel_id=1, source_target_pairs={{0,8},{1,9},{2,10},{3,11},{4,12},{5,13},{6,14},{7,15},{8,0},{9,1},... | collective-permute-start | bytes 393224 | tf_op jit(solution)/shard_map/ppermute | solution.py:189
  (157 other events, 1495.1 us)

commit v4 on v3

--- a/solution.py
+++ b/solution.py
@@ -14,10 +14,11 @@
 HALF = 64
 YR = 8
 LANES = 128
-EARLY = []
 F32 = jnp.float32
 BF16 = jnp.bfloat16
-VMEM_LIMIT = 16 * 1024 * 1024
+MIB = 1024 * 1024
+Y_GRANT = 16 * MIB
+X_GRANT = 16 * MIB
 
 
 def dft_parts(length, scale):
@@ -132,8 +133,8 @@
     return jnp.sum(jnp.sum(x, axis=0, keepdims=True), axis=1, keepdims=True)
 
 
-def step_of(sums_ref):
-    total = jnp.sum(sums_ref[...], axis=0)
+def step_of(sums_refs):
+    total = sum(jnp.sum(sums_ref[...], axis=0) for sums_ref in sums_refs)
     parts = jnp.sum(total, axis=1, keepdims=True)
     return parts[0:1] / (parts[1:2] + PENALTY * parts[2:3])
 
@@ -174,29 +175,8 @@
     return out
 
 
-def steps_of(gz, gy):
-    return [(r, s) for s in reversed(range(gy)) for r in range(gz)]
-
-
-def send(piece, step):
-    r, s = step
-    if r == 0 and s == 0:
-        return piece
-    gz, gy = lax.axis_size("gz"), lax.axis_size("gy")
-    route = [
-        (g * gy + c, (g + r) % gz * gy + (c ^ s)) for g in range(gz) for c in range(gy)
-    ]
-    return lax.ppermute(piece, ("gz", "gy"), route)
-
-
-def towards(edge_ref, gz, step):
-    r, s = step
-    return lax.rem(edge_ref[2] + r, gz), edge_ref[3] ^ s
-
-
-def source(edge_ref, gz, step):
-    r, s = step
-    return lax.rem(edge_ref[2] + gz - r, gz), edge_ref[3] ^ s
+def core_on(edge_ref, gz, r):
+    return lax.rem(edge_ref[2] + gz + r, gz)
 
 
 def y_turns(tw_ref, part):
@@ -209,11 +189,11 @@
     return [one, two, three, four, both(one, four), both(two, four), both(three, four)]
 
 
-def y_inverse_kernel(gz, steps, edge_ref, data_ref, table_ref, tw_ref, *refs):
-    out_refs, (re_s, im_s, mix_s, part_s) = refs[: len(steps)], refs[len(steps) :]
+def y_inverse_kernel(gz, edge_ref, data_ref, table_ref, tw_ref, *refs):
+    out_refs, (re_s, im_s, mix_s) = refs[:gz], refs[gz:]
     blocks, ny, _ = data_ref.shape
     n = ny // YR
-    gy, _, rows, _ = part_s.shape
+    rows = out_refs[0].shape[2]
     lane = lax.broadcasted_iota(jnp.int32, (n, LANES), 1)
     table = table_ref[...]
 
@@ -242,7 +222,7 @@
 
         tiles = rows // 8
         for r in range(gz):
-            core = lax.rem(edge_ref[2] + r, gz)
+            core = core_on(edge_ref, gz, r)
 
             def combine(i, carry):
                 y2 = ((i // tiles) * gz + core) * rows + lax.rem(i, tiles) * 8
@@ -258,61 +238,73 @@
                     planes.append((re, im))
                 at = pl.ds(pl.multiple_of(lax.rem(i, tiles) * 8, 8), 8)
                 for k, (re, im) in enumerate(short_fft(planes, 1)):
-                    to = (k * (n // (gz * rows)) + i // tiles) ^ edge_ref[3]
-                    part_s[to, 0, at, :] = re
-                    part_s[to, 1, at, :] = im
+                    to = k * (n // (gz * rows)) + i // tiles
+                    out_refs[r][to, 0, at, lanes] = re
+                    out_refs[r][to, 1, at, lanes] = im
                 return carry
 
             lax.fori_loop(0, n // gz // 8, combine, 0, unroll=2)
-            for step, out_ref in zip(steps, out_refs):
-                if step[0] == r:
-                    out_ref[:, :, lanes] = part_s[step[1]]
-
-
-def y_inverse(edge, data, steps, rows, gz, gy):
+
+
+def y_inverse(edge, data, rows, gz, gy):
     blocks, ny, width = data.shape
     n = ny // YR
     vmem = pl.BlockSpec(memory_space=pltpu.VMEM)
-    piece = jax.ShapeDtypeStruct((2, rows, blocks * HALF), F32)
     return pl.pallas_call(
-        functools.partial(y_inverse_kernel, gz, steps),
+        functools.partial(y_inverse_kernel, gz),
         in_specs=[pl.BlockSpec(memory_space=pltpu.SMEM)] + [vmem] * 3,
-        out_specs=[vmem] * len(steps),
-        out_shape=[piece] * len(steps),
+        out_specs=[vmem] * gz,
+        out_shape=[jax.ShapeDtypeStruct((gy, 2, rows, blocks * HALF), F32)] * gz,
         scratch_shapes=[
             pltpu.VMEM((ny, LANES), F32),
             pltpu.VMEM((ny, LANES), F32),
             pltpu.VMEM((YR, 2 * n, LANES), F32),
-            pltpu.VMEM((gy, 2, rows, LANES), F32),
         ],
-        compiler_params=pltpu.CompilerParams(vmem_limit_bytes=VMEM_LIMIT),
+        compiler_params=pltpu.CompilerParams(vmem_limit_bytes=Y_GRANT),
         name="y_inverse",
     )(edge, data, y_matrix(ny, False, -1.0), y_twiddle(ny))
 
 
-def y_forward_kernel(gz, early, steps, edge_ref, eta_ref, *refs):
-    count = len(early)
-    first_refs, second_refs = refs[:count], refs[count : 2 * count]
-    spec_refs, refs = refs[2 * count : 2 * count + len(steps)], refs[2 * count + len(steps) :]
-    data_ref, table_ref, tw_ref, out_ref, re_s, im_s, mix_s = refs
+def merge_kernel(gz, edge_ref, *refs):
+    out_ref = refs[-1]
+    for r in range(gz):
+        core = core_on(edge_ref, gz, -r)
+
+        def one(i, carry):
+            out_ref[i, core] = refs[r][i]
+            return carry
+
+        lax.fori_loop(0, out_ref.shape[0], one, 0)
+
+
+def merge(edge, pieces):
+    gz = len(pieces)
+    vmem = pl.BlockSpec(memory_space=pltpu.VMEM)
+    gy, *rest = pieces[0].shape
+    return pl.pallas_call(
+        functools.partial(merge_kernel, gz),
+        in_specs=[pl.BlockSpec(memory_space=pltpu.SMEM)] + [vmem] * gz,
+        out_specs=vmem,
+        out_shape=jax.ShapeDtypeStruct((gy, gz, *rest), F32),
+        compiler_params=pltpu.CompilerParams(vmem_limit_bytes=2 * MIB),
+        name="merge",
+    )(edge, *pieces)
+
+
+def y_forward_kernel(spec_ref, data_ref, table_ref, tw_ref, out_ref, re_s, im_s, mix_s):
     ny = data_ref.shape[1]
     n = ny // YR
-    rows = spec_refs[0].shape[1]
+    gy, gz, _, rows, _ = spec_ref.shape
     chunk = pl.program_id(0)
-    lanes = pl.ds(pl.multiple_of(chunk * LANES, LANES), LANES)
-    eta0 = jnp.max(eta_ref[0])
-    eta1 = jnp.max(eta_ref[1])
-
-    def place(step):
-        core, chip = source(edge_ref, gz, step)
-        return pl.ds(pl.multiple_of((chip * gz + core) * rows, rows), rows)
-
-    for step, first_ref, second_ref in zip(early, first_refs, second_refs):
-        for p, s in enumerate((re_s, im_s)):
-            s[place(step), :] = -(eta0 * first_ref[p, :, lanes] + eta1 * second_ref[p, :, lanes])
-    for step, spec_ref in zip(steps, spec_refs):
-        for p, s in enumerate((re_s, im_s)):
-            s[place(step), :] = spec_ref[p, :, lanes]
+
+    def unpack(i, carry):
+        for core in range(gz):
+            part = pl.ds(pl.multiple_of((i * gz + core) * rows, rows), rows)
+            re_s[part, :] = spec_ref[i, core, 0]
+            im_s[part, :] = spec_ref[i, core, 1]
+        return carry
+
+    lax.fori_loop(0, gy, unpack, 0)
 
     table = table_ref[...]
     for k in range(0, YR, 2):
@@ -351,15 +343,15 @@
     lax.fori_loop(0, n // 16, combine, 0)
 
 
-def y_forward(edge, etas, early, first, second, steps, spec, data, gz):
+def y_forward(spec, data):
     blocks, ny, width = data.shape
+    gy, gz, _, rows, _ = spec.shape
     n = ny // YR
     vmem = pl.BlockSpec(memory_space=pltpu.VMEM)
-    arrays = [etas, *first, *second, *spec, data, y_matrix(ny, True, 1.0), y_twiddle(ny)]
     return pl.pallas_call(
-        functools.partial(y_forward_kernel, gz, early, steps),
+        y_forward_kernel,
         grid=(blocks // 2,),
-        in_specs=[pl.BlockSpec(memory_space=pltpu.SMEM)] + [vmem] * len(arrays),
+        in_specs=[pl.BlockSpec((gy, gz, 2, rows, LANES), lambda i: (0, 0, 0, 0, i))] + [vmem] * 3,
         out_specs=pl.BlockSpec((2, ny, width), lambda i: (i, 0, 0)),
         out_shape=jax.ShapeDtypeStruct((blocks, ny, width), F32),
         scratch_shapes=[
@@ -367,9 +359,9 @@
             pltpu.VMEM((ny, LANES), F32),
             pltpu.VMEM((YR, 2 * n, LANES), F32),
         ],
-        compiler_params=pltpu.CompilerParams(vmem_limit_bytes=VMEM_LIMIT),
+        compiler_params=pltpu.CompilerParams(vmem_limit_bytes=Y_GRANT + 8 * MIB),
         name="y_forward",
-    )(edge, *arrays)
+    )(spec, data, y_matrix(ny, True, 1.0), y_twiddle(ny))
 
 
 def plane_chunk(planes, rows):
@@ -379,19 +371,11 @@
     return chunk
 
 
-def x_inverse_kernel(gz, steps, edge_ref, *refs):
-    count = max(1, len(steps))
-    spec_refs, refs = refs[:count], refs[count:]
-    coef_ref, tw_ref, table_ref, out_ref, head_ref, tail_ref, re_s, im_s = refs[:8]
-    planes, rows, ka = out_ref.shape
-    kb = planes // gz
-
-    spec_ref = spec_refs[0]
-    if steps:
-        spec_ref = refs[8]
-        for step, piece_ref in zip(steps, spec_refs):
-            core, chip = source(edge_ref, gz, step)
-            spec_ref[core * kb + chip] = piece_ref[...]
+def x_inverse_kernel(
+    spec_ref, coef_ref, tw_ref, table_ref, out_ref, head_ref, tail_ref, re_s, im_s
+):
+    kb, gz, _, rows, ka = spec_ref.shape
+    planes = gz * kb
 
     def columns(i, carry):
         part = pl.ds(pl.multiple_of(i * 8, 8), 8)
@@ -400,8 +384,8 @@
             mixed = [[None] * kb for _ in range(gz)]
             for k in range(kb):
                 coef = [coef_ref[j, k, :, lanes] for j in range(3)]
-                re = mix_adjoint(coef, [spec_ref[z * kb + k, 0, part, lanes] for z in range(gz)])
-                im = mix_adjoint(coef, [spec_ref[z * kb + k, 1, part, lanes] for z in range(gz)])
+                re = mix_adjoint(coef, [spec_ref[k, z, 0, part, lanes] for z in range(gz)])
+                im = mix_adjoint(coef, [spec_ref[k, z, 1, part, lanes] for z in range(gz)])
                 for z in range(gz):
                     mixed[z][k] = (re[z], im[z])
             for z in range(gz):
@@ -437,26 +421,23 @@
         tail_ref[p : p + 1, :] = out_ref[p, rows - 1 : rows, :]
 
 
-def x_inverse(edge, spec, steps, coef, gz, nx):
-    kb, ka = coef.shape[1], coef.shape[-1]
-    planes, rows = gz * kb, spec[0].shape[-2]
+def x_inverse(spec, coef, nx):
+    kb, gz, _, rows, ka = spec.shape
+    planes = gz * kb
     vmem = pl.BlockSpec(memory_space=pltpu.VMEM)
-    scratch = [pltpu.VMEM((planes, rows, ka), F32)] * 2
-    if steps:
-        scratch = scratch + [pltpu.VMEM((planes, 2, rows, ka), F32)]
     return pl.pallas_call(
-        functools.partial(x_inverse_kernel, gz, steps),
-        in_specs=[pl.BlockSpec(memory_space=pltpu.SMEM)] + [vmem] * (len(spec) + 3),
+        x_inverse_kernel,
+        in_specs=[vmem] * 4,
         out_specs=[vmem] * 3,
         out_shape=[
             jax.ShapeDtypeStruct((planes, rows, ka), F32),
             jax.ShapeDtypeStruct((2, planes, ka), F32),
             jax.ShapeDtypeStruct((planes, ka), F32),
         ],
-        scratch_shapes=scratch,
-        compiler_params=pltpu.CompilerParams(vmem_limit_bytes=VMEM_LIMIT),
+        scratch_shapes=[pltpu.VMEM((planes, rows, ka), F32)] * 2,
+        compiler_params=pltpu.CompilerParams(vmem_limit_bytes=X_GRANT),
         name="x_inverse",
-    )(edge, *spec, coef, x_twiddle(nx, ka), jnp.asarray(x_inverse_matrix(nx, ka)))
+    )(spec, coef, x_twiddle(nx, ka), jnp.asarray(x_inverse_matrix(nx, ka)))
 
 
 def forward_into(gz, field_ref, coef_ref, tw_ref, table_ref, spec_ref, re_s, im_s):
@@ -495,18 +476,22 @@
                 coef = [coef_ref[j, k, :, lanes] for j in range(3)]
                 for p in range(2):
                     for z, value in enumerate(mix(coef, [spectra[z][k][p] for z in range(gz)])):
-                        spec_ref[z * kb + k, p, part, lanes] = value
+                        spec_ref[k, z, p, part, lanes] = value
                         total = total + value * value
         return total
 
     return lax.fori_loop(0, rows // 8, columns, jnp.zeros((8, LANES), F32))
 
 
-def cut(gz, steps, edge_ref, spec_ref, piece_refs):
-    kb = spec_ref.shape[0] // gz
-    for step, piece_ref in zip(steps, piece_refs):
-        core, chip = towards(edge_ref, gz, step)
-        piece_ref[...] = spec_ref[core * kb + chip]
+def cut(gz, edge_ref, spec_ref, piece_refs):
+    for r, piece_ref in enumerate(piece_refs):
+        core = core_on(edge_ref, gz, r + 1)
+
+        def one(i, carry):
+            piece_ref[i] = spec_ref[i, core]
+            return carry
+
+        lax.fori_loop(0, spec_ref.shape[0], one, 0)
 
 
 def next_plane(field_ref, p, kb):
@@ -526,13 +511,13 @@
 
 
 def first_kernel(
-    gz, early, edge_ref, field_ref, coef_ref, tw_ref, table_ref, sums_ref, spec_ref, *refs
+    gz, edge_ref, field_ref, coef_ref, tw_ref, table_ref, sums_ref, spec_ref, *refs
 ):
     piece_refs, (re_s, im_s) = refs[:-2], refs[-2:]
     planes, rows, ka = field_ref.shape
     kb = planes // gz
     projected = forward_into(gz, field_ref, coef_ref, tw_ref, table_ref, spec_ref, re_s, im_s)
-    cut(gz, early, edge_ref, spec_ref, piece_refs)
+    cut(gz, edge_ref, spec_ref, piece_refs)
     row = lax.broadcasted_iota(jnp.int32, (rows, ka), 0)
     square = jnp.zeros((8, LANES), F32)
     slope = jnp.zeros((8, LANES), F32)
@@ -551,20 +536,24 @@
     sums_ref[2] = slope
 
 
-def first_projection(edge, field, early, coef, gz, nx):
+def spec_shapes(gz, field):
+    planes, rows, ka = field.shape
+    kb = planes // gz
+    whole = jax.ShapeDtypeStruct((kb, gz, 2, rows, ka), F32)
+    return [whole] + [jax.ShapeDtypeStruct((kb, 2, rows, ka), F32)] * (gz - 1)
+
+
+def first_projection(edge, field, coef, gz, nx):
     planes, rows, ka = field.shape
     vmem = pl.BlockSpec(memory_space=pltpu.VMEM)
+    shapes = spec_shapes(gz, field)
     sums, spec, *pieces = pl.pallas_call(
-        functools.partial(first_kernel, gz, early),
+        functools.partial(first_kernel, gz),
         in_specs=[pl.BlockSpec(memory_space=pltpu.SMEM)] + [vmem] * 4,
-        out_specs=[vmem] * (2 + len(early)),
-        out_shape=[
-            jax.ShapeDtypeStruct((3, 8, LANES), F32),
-            jax.ShapeDtypeStruct((planes, 2, rows, ka), F32),
-        ]
-        + [jax.ShapeDtypeStruct((2, rows, ka), F32)] * len(early),
+        out_specs=[vmem] * (1 + len(shapes)),
+        out_shape=[jax.ShapeDtypeStruct((3, 8, LANES), F32)] + shapes,
         scratch_shapes=[pltpu.VMEM((planes, rows, ka), F32)] * 2,
-        compiler_params=pltpu.CompilerParams(vmem_limit_bytes=VMEM_LIMIT),
+        compiler_params=pltpu.CompilerParams(vmem_limit_bytes=X_GRANT),
         name="first_projection",
     )(edge, field, coef, x_twiddle(nx, ka), x_forward_matrix(nx, ka))
     return spec, pieces, sums
@@ -575,25 +564,27 @@
     put_sums(out_ref, [sums_ref[0], sums_ref[1], sums_ref[2] + fold(step * step)])
 
 
-def border_sums(edge, sums, tail, next_head, devices):
+def border_sums(edge, sums, tail, next_head, copies):
     vmem = pl.BlockSpec(memory_space=pltpu.VMEM)
     return pl.pallas_call(
         border_kernel,
         in_specs=[pl.BlockSpec(memory_space=pltpu.SMEM)] + [vmem] * 3,
         out_specs=vmem,
-        out_shape=jax.ShapeDtypeStruct((devices, 8, LANES), F32),
+        out_shape=jax.ShapeDtypeStruct((copies, 8, LANES), F32),
+        compiler_params=pltpu.CompilerParams(vmem_limit_bytes=2 * MIB),
         name="border_sums",
     )(edge, sums, tail, next_head)
 
 
 def second_kernel(
-    gz, early, edge_ref, sums_ref, d0_ref, nd0_ref, tail_ref, prev_ref, next_ref, nnext_ref,
-    coef_ref, tw_ref, table_ref, d1_ref, eta_ref, out_ref, spec_ref, *refs,
+    gz, edge_ref, d0_ref, nd0_ref, tail_ref, prev_ref, next_ref, nnext_ref,
+    coef_ref, tw_ref, table_ref, *refs,
 ):
+    sums_refs, (d1_ref, eta_ref, out_ref, spec_ref, *refs) = refs[:gz], refs[gz:]
     piece_refs, (re_s, im_s, row_s) = refs[:-3], refs[-3:]
     planes, rows, ka = d0_ref.shape
     kb = planes // gz
-    eta_here = step_of(sums_ref)
+    eta_here = step_of(sums_refs)
     eta_ref[...] = jnp.broadcast_to(eta_here, (8, LANES))
     eta = jnp.max(eta_here)
     first = edge_ref[0] > 0
@@ -654,67 +645,88 @@
         slope = slope + fold(terms)
 
     projected = forward_into(gz, d1_ref, coef_ref, tw_ref, table_ref, spec_ref, re_s, im_s)
-    cut(gz, early, edge_ref, spec_ref, piece_refs)
+    cut(gz, edge_ref, spec_ref, piece_refs)
     put_sums(out_ref, [square, projected, slope])
 
 
-def second_descent(edge, sums, d0, nd0, tail, prev_tail, next_head, next_nhead, early, coef, gz, nx):
+def second_descent(edge, sums, d0, nd0, tail, prev_tail, next_head, next_nhead, coef, gz, nx):
     planes, rows, ka = d0.shape
-    devices = sums.shape[0]
     vmem = pl.BlockSpec(memory_space=pltpu.VMEM)
+    shapes = spec_shapes(gz, d0)
     d1, eta, out, spec, *pieces = pl.pallas_call(
-        functools.partial(second_kernel, gz, early),
-        in_specs=[pl.BlockSpec(memory_space=pltpu.SMEM)] + [vmem] * 10,
-        out_specs=[vmem] * (4 + len(early)),
+        functools.partial(second_kernel, gz),
+        in_specs=[pl.BlockSpec(memory_space=pltpu.SMEM)] + [vmem] * (9 + gz),
+        out_specs=[vmem] * (3 + len(shapes)),
         out_shape=[
             jax.ShapeDtypeStruct((planes, rows, ka), F32),
             jax.ShapeDtypeStruct((8, LANES), F32),
-            jax.ShapeDtypeStruct((devices, 8, LANES), F32),
-            jax.ShapeDtypeStruct((planes, 2, rows, ka), F32),
+            jax.ShapeDtypeStruct(sums[0].shape, F32),
         ]
-        + [jax.ShapeDtypeStruct((2, rows, ka), F32)] * len(early),
+        + shapes,
         scratch_shapes=[
             pltpu.VMEM((planes, rows, ka), F32),
             pltpu.VMEM((planes, rows, ka), F32),
             pltpu.VMEM((planes, ka), F32),
         ],
-        compiler_params=pltpu.CompilerParams(vmem_limit_bytes=VMEM_LIMIT),
+        compiler_params=pltpu.CompilerParams(vmem_limit_bytes=X_GRANT),
         name="second_descent",
     )(
-        edge, sums, d0, nd0, tail, prev_tail, next_head, next_nhead, coef,
-        x_twiddle(nx, ka), x_forward_matrix(nx, ka),
+        edge, d0, nd0, tail, prev_tail, next_head, next_nhead, coef,
+        x_twiddle(nx, ka), x_forward_matrix(nx, ka), *sums,
     )
     return d1, spec, pieces, eta, out
 
 
-def combine_kernel(gz, steps, edge_ref, sums_ref, eta_ref, first_ref, second_ref, steps_ref, *piece_refs):
-    kb = first_ref.shape[0] // gz
+def combine_kernel(gz, edge_ref, eta_ref, *refs):
+    sums_refs, refs = refs[:gz], refs[gz:]
+    first_refs, second_refs, (out_ref, steps_ref) = refs[:gz], refs[gz : 2 * gz], refs[2 * gz :]
     eta0 = jnp.max(eta_ref[...])
-    eta1 = jnp.max(step_of(sums_ref))
+    eta1 = jnp.max(step_of(sums_refs))
     steps_ref[0] = eta_ref[...]
     steps_ref[1] = jnp.full((8, LANES), eta1, F32)
-    for step, piece_ref in zip(steps, piece_refs):
-        core, chip = towards(edge_ref, gz, step)
-        at = core * kb + chip
-        piece_ref[...] = -(eta0 * first_ref[at] + eta1 * second_ref[at])
-
-
-def combine_spectra(edge, sums, eta, first, second, steps, gz):
+    for r in range(gz):
+        core = core_on(edge_ref, gz, -r)
+
+        def one(i, carry):
+            at = i if r else (i, core)
+            out_ref[i, core] = -(eta0 * first_refs[r][at] + eta1 * second_refs[r][at])
+            return carry
+
+        lax.fori_loop(0, out_ref.shape[0], one, 0)
+
+
+def combine_spectra(edge, eta, sums, first, second):
+    gz = len(sums)
     vmem = pl.BlockSpec(memory_space=pltpu.VMEM)
-    etas, *pieces = pl.pallas_call(
-        functools.partial(combine_kernel, gz, steps),
-        in_specs=[pl.BlockSpec(memory_space=pltpu.SMEM)] + [vmem] * 4,
-        out_specs=[vmem] * (1 + len(steps)),
-        out_shape=[jax.ShapeDtypeStruct((2, 8, LANES), F32)]
-        + [jax.ShapeDtypeStruct(first.shape[1:], F32)] * len(steps),
-        compiler_params=pltpu.CompilerParams(vmem_limit_bytes=VMEM_LIMIT),
+    return pl.pallas_call(
+        functools.partial(combine_kernel, gz),
+        in_specs=[pl.BlockSpec(memory_space=pltpu.SMEM)] + [vmem] * (1 + 3 * gz),
+        out_specs=[vmem] * 2,
+        out_shape=[
+            jax.ShapeDtypeStruct(first[0].shape, F32),
+            jax.ShapeDtypeStruct((2, 8, LANES), F32),
+        ],
+        compiler_params=pltpu.CompilerParams(vmem_limit_bytes=2 * MIB),
         name="combine_spectra",
-    )(edge, sums, eta, first, second)
-    return pieces, etas
+    )(edge, eta, *sums, *first, *second)
+
+
+def to_core(piece, r):
+    gz = lax.axis_size("gz")
+    return lax.ppermute(piece, "gz", [(i, (i + r) % gz) for i in range(gz)]) if r else piece
+
+
+def from_cores(pieces):
+    return [to_core(piece, r + 1) for r, piece in enumerate(pieces)]
+
+
+def to_chips(parts):
+    return lax.all_to_all(parts, "gy", 0, 0, tiled=True)
 
 
 def everywhere(sums):
-    return lax.all_to_all(sums, ("gz", "gy"), 0, 0, tiled=True)
+    sums = to_chips(sums)
+    return [to_core(sums, r) for r in range(lax.axis_size("gz"))]
 
 
 def shards(data, band_offset, interp_weight):
@@ -729,10 +741,7 @@
 
     core = lax.axis_index("gz")
     flat = lax.axis_index("gy") * gz + core
-    edge = jnp.stack([flat == 0, flat == devices - 1, core, lax.axis_index("gy")]).astype(jnp.int32)
-    steps = steps_of(gz, gy)
-    early = [step for step in steps if step in EARLY]
-    late = [step for step in steps if step not in EARLY]
+    edge = jnp.stack([flat == 0, flat == devices - 1, core]).astype(jnp.int32)
     order = [(i % gz) * gy + i // gz for i in range(devices)]
     up = [(order[i + 1], order[i]) for i in range(devices - 1)]
     down = [(order[i], order[i + 1]) for i in range(devices - 1)]
@@ -748,29 +757,28 @@
     ).reshape(3, gy, 1, ka)
     coef = jnp.broadcast_to(coef, (3, gy, 8, ka))
 
-    pieces = y_inverse(edge, data, steps, rows, gz, gy)
-    pieces = [send(piece, step) for piece, step in zip(pieces, steps)]
-    d0, head, tail = x_inverse(edge, pieces, steps, coef, gz, nx)
+    own, *others = y_inverse(edge, data, rows, gz, gy)
+    spec = to_chips(merge(edge, [own] + from_cores(others)))
+    d0, head, tail = x_inverse(spec, coef, nx)
     next_head = lax.ppermute(head, ("gz", "gy"), up)
     prev_tail = lax.ppermute(tail, ("gz", "gy"), down)
-    spec0, first, sums = first_projection(edge, d0, early, coef, gz, nx)
-    sums = everywhere(border_sums(edge, sums, tail, next_head, devices))
-    first = [send(piece, step) for piece, step in zip(first, early)]
-    nd0, nhead, _ = x_inverse(edge, [spec0], [], coef, gz, nx)
+    spec0, others0, sums = first_projection(edge, d0, coef, gz, nx)
+    sums = everywhere(border_sums(edge, sums, tail, next_head, gy))
+    others0 = from_cores(others0)
+    nd0, nhead, _ = x_inverse(spec0, coef, nx)
     next_nhead = lax.ppermute(nhead, ("gz", "gy"), up)
-    d1, spec1, second, eta, sums = second_descent(
-        edge, sums, d0, nd0, tail, prev_tail, next_head, next_nhead, early, coef, gz, nx
+    d1, spec1, others1, eta, sums = second_descent(
+        edge, sums, d0, nd0, tail, prev_tail, next_head, next_nhead, coef, gz, nx
     )
-    second = [send(piece, step) for piece, step in zip(second, early)]
     sums = everywhere(sums)
-    pieces, etas = combine_spectra(edge, sums, eta, spec0, spec1, late, gz)
-    pieces = [send(piece, step) for piece, step in zip(pieces, late)]
-    residual = y_forward(edge, etas, early, first, second, late, pieces, data, gz)
+    others1 = from_cores(others1)
+    spec, etas = combine_spectra(edge, eta, sums, [spec0] + others0, [spec1] + others1)
+    residual = y_forward(to_chips(spec), data)
 
     volume = -(etas[0, 0, 0] * d0 + etas[1, 0, 0] * d1)
     volume = volume.reshape(gz, gy, rows, ka).transpose(0, 2, 3, 1).reshape(gz, rows, nx)
     parts = [
-        send(lax.dynamic_index_in_dim(volume, lax.rem(core + r, gz), 0, False), (r, 0))
+        to_core(lax.dynamic_index_in_dim(volume, lax.rem(core + r, gz), 0, False), r)
         for r in range(gz)
     ]
     volume = jnp.zeros((gz, rows, nx), F32)

time: 392 us -> 309 us (0.79)
  the two profiles are of different devices: /device:TPU:0 before, /device:TPU:14 now
where the time goes in v4:
time: 309 us; the launch traced here: 308 us
  waiting for transfers between devices  174 us (56%)
  Pallas kernels  47.8 us (15%)
  local copies, waits for them, and re-layouts  38.8 us (13%)
  starting transfers between devices  29.7 us (10%)
  blocking collectives  12 us (4%)
  other arithmetic  4.59 us (1%)
    all_to_all x3, waiting for transfers between devices, to_chips(): return lax.all_to_all(parts, 'gy', 0, 0, tiled=True)  168 us
    all_to_all x3, starting transfers between devices, to_chips(): return lax.all_to_all(parts, 'gy', 0, 0, tiled=True)  20 us
    unnamed x44, local copies, waits for them, and re-layouts  19.8 us
    pallas_call x2, Pallas kernels, x_inverse(): pl.pallas_call(x_inverse_kernel, in_specs=[vmem] * 4, out_specs=[vmem] *...  12 us
    all_to_all x1, blocking collectives, to_chips(): return lax.all_to_all(parts, 'gy', 0, 0, tiled=True)  12 us
    pallas_call x1, Pallas kernels, y_forward(): pl.pallas_call(y_forward_kernel, grid=(blocks // 2,), in_specs=[pl.BlockS...  11.1 us
    dynamic_slice x3, local copies, waits for them, and re-layouts, shards(): lax.dynamic_index_in_dim(volume, lax.rem(core + r, gz), 0, False)  8.51 us
    pallas_call x1, Pallas kernels, second_descent(): pl.pallas_call(functools.partial(second_kernel, gz), in_specs=[pl.BlockSp...  8.35 us
  transfers between devices with their start and end apart: 12, of which 5 were waited for; matrix products, arithmetic and copies ran while one was open for 8% of the time, Pallas kernels for 6%

profile of v4, /device:TPU:14, one launch (start us, length us, event | category | flops | bytes accessed | tf_op | source)
XLA Modules:
  0.0 307.7 jit_solution(17287021849120483628)
XLA Ops:
  0.7 1.6 copy-done.4
  4.7 6.5 %y_inverse.1 = (f32[16,2,64,256]{3,2,1,0:T(8,128)S(1)}, f32[16,2,64,256]{3,2,1,0:T(8,128)S(1)}) custom-call(s32[3]{0:T(128)S(1)} %pad_add_fusion.edge_ref, bf16[4,2048,128]{2,1,0:T(8,128)(2,1)S(1)} %bitcast.19, bf16[1024,512]{1,0:T(8,128)(2,1)S(1)} %copy-done.17, f32[2,3,256,128]{3,2,1,0:T(8,128)S(1)} %copy-done.8), custom_call_target="tpu_custom_call" | custom-call | tf_op jit(solution)/shard_map/y_inverse/pallas_call | solution.py:253
  11.3 4.1 %collective-permute-done.refs_1_ = f32[16,2,64,256]{3,2,1,0:T(8,128)S(1)} collective-permute-done((f32[16,2,64,256]{3,2,1,0:T(8,128)S(1)}, f32[16,2,64,256]{3,2,1,0:T(8,128)S(1)}, u32[]{:S(2)}, u32[]{:S(2)}) %collective-permute-start) | collective-permute-done | bytes 2097184 | tf_op jit(solution)/shard_map/ppermute | solution.py:716
  16.4 2.0 copy-done.3
  18.4 7.3 %all-to-all-start = ((f32[16,2,2,64,256]{4,3,2,1,0:T(8,128)}), f32[16,2,2,64,256]{4,3,2,1,0:T(8,128)}, u32[]{:S(2)}, u32[]{:S(2)}) async-start(f32[16,2,2,64,256]{4,3,2,1,0:T(8,128)} %copy-done.3), calls=%async_computation | async-start | bytes 8388608 | tf_op jit(solution)/shard_map/all_to_all | solution.py:724
  25.8 95.4 %all-to-all-done.spec_ref = f32[16,2,2,64,256]{4,3,2,1,0:T(8,128)} async-done(((f32[16,2,2,64,256]{4,3,2,1,0:T(8,128)}), f32[16,2,2,64,256]{4,3,2,1,0:T(8,128)}, u32[]{:S(2)}, u32[]{:S(2)}) %all-to-all-start) | async-done | bytes 4194336 | tf_op jit(solution)/shard_map/all_to_all | solution.py:724
  122.2 6.8 %x_inverse.2 = (f32[32,64,256]{2,1,0:T(8,128)S(1)}, f32[2,32,256]{2,1,0:T(8,128)S(1)}, f32[32,256]{1,0:T(8,128)S(1)}) custom-call(f32[16,2,2,64,256]{4,3,2,1,0:T(8,128)} %all-to-all-done.spec_ref, f32[3,16,8,256]{3,2,1,0:T(8,128)S(1)} %broadcast_in_dim.27.coef_ref, f32[2,16,8,256]{3,2,1,0:T(8,128)S(1)} %copy-done.7, bf16[512,512]{1,0:T(8,128)(2,1)S(1)} %copy-done.14), custom_call_target="tpu_custom_call" | custom-call | tf_op jit(solution)/shard_map/x_inverse/pallas_call | solution.py:428
  129.0 1.9 collective-permute-start.2
  131.0 6.4 %first_projection.1 = (f32[3,8,128]{2,1,0:T(8,128)S(1)}, f32[16,2,2,64,256]{4,3,2,1,0:T(8,128)S(1)}, f32[16,2,64,256]{3,2,1,0:T(8,128)S(1)}) custom-call(s32[3]{0:T(128)S(1)} %pad_add_fusion.edge_ref, f32[32,64,256]{2,1,0:T(8,128)S(1)} %get-tuple-element.21.field_ref.d0_ref, f32[3,16,8,256]{3,2,1,0:T(8,128)S(1)} %broadcast_in_dim.27.coef_ref, ...), custom_call_target="tpu_custom_call" | custom-call | tf_op jit(solution)/shard_map/first_projection/pallas_call | solution.py:550
  137.4 2.0 copy-done
  139.4 1.3 copy-done.18
  141.9 5.3 %all-to-all-start.1 = ((f32[16,8,128]{2,1,0:T(8,128)}), f32[16,8,128]{2,1,0:T(8,128)S(1)}, u32[]{:S(2)}, u32[]{:S(2)}) async-start(f32[16,8,128]{2,1,0:T(8,128)} %border_sums.1), calls=%async_computation.1 | async-start | bytes 131072 | tf_op jit(solution)/shard_map/all_to_all | solution.py:724
  147.2 2.2 copy-done.1
  150.5 5.2 %x_inverse.3 = (f32[32,64,256]{2,1,0:T(8,128)S(1)}, f32[2,32,256]{2,1,0:T(8,128)}, f32[32,256]{1,0:T(8,128)}) custom-call(f32[16,2,2,64,256]{4,3,2,1,0:T(8,128)S(1)} %copy-done.1, f32[3,16,8,256]{3,2,1,0:T(8,128)S(1)} %broadcast_in_dim.27.coef_ref, f32[2,16,8,256]{3,2,1,0:T(8,128)S(1)} %copy-done.7, bf16[512,512]{1,0:T(8,128)(2,1)S(1)} %copy-done.15), custom_call_target="tpu_custom_call" | custom-call | tf_op jit(solution)/shard_map/x_inverse/pallas_call | solution.py:428
  157.0 1.9 collective-permute-start.3
  159.5 1.9 collective-permute-start.1
  161.4 2.8 collective-permute-start.6
  164.7 1.6 copy-done.11
  166.3 8.3 %second_descent.1 = (f32[32,64,256]{2,1,0:T(8,128)S(1)}, f32[8,128]{1,0:T(8,128)S(1)}, f32[16,8,128]{2,1,0:T(8,128)S(1)}, f32[16,2,2,64,256]{4,3,2,1,0:T(8,128)S(1)}, f32[16,2,64,256]{3,2,1,0:T(8,128)S(1)}) custom-call(s32[3]{0:T(128)S(1)} %pad_add_fusion.edge_ref, f32[32,64,256]{2,1,0:T(8,128)S(1)} %get-tuple-element.21.field_ref.d0_ref, ...), custom_call_target="tpu_custom_call" | custom-call | tf_op jit(solution)/shard_map/second_descent/pallas_call | solution.py:656
  175.2 12.0 %all_to_all.20.refs_0_ = f32[16,8,128]{2,1,0:T(8,128)S(1)} all-to-all(f32[16,8,128]{2,1,0:T(8,128)S(1)} %get-tuple-element.29), channel_id=1, replica_groups=mesh['gz'=2,'gy'=16] {'gy'}, dimensions={0} | all-to-all | bytes 131072 | tf_op jit(solution)/shard_map/all_to_all | solution.py:724
  188.5 1.4 combine_spectra.1
  189.9 2.0 copy-done.6
  191.9 7.4 %all-to-all-start.3 = ((f32[16,2,2,64,256]{4,3,2,1,0:T(8,128)}), f32[16,2,2,64,256]{4,3,2,1,0:T(8,128)}, u32[]{:S(2)}, u32[]{:S(2)}) async-start(f32[16,2,2,64,256]{4,3,2,1,0:T(8,128)} %copy-done.6), calls=%async_computation.3 | async-start | bytes 8388608 | tf_op jit(solution)/shard_map/all_to_all | solution.py:724
  199.8 4.5 %add_negate_fusion = f32[32,64,256]{2,1,0:T(8,128)} fusion(f32[32,64,256]{2,1,0:T(8,128)} %copy-done.12, f32[32,64,256]{2,1,0:T(8,128)S(1)} %get-tuple-element.21.field_ref.d0_ref, f32[]{:T(128)} %bitcast.8, f32[]{:T(128)} %bitcast.7), kind=kLoop, calls=%fused_computation | loop fusion | flops 2097152 | bytes 6291464 | tf_op jit(solution)/shard_map/neg | solution.py:778
  204.3 4.9 %copy.21 = f32[2,16,64,256]{2,1,3,0:T(8,128)} copy(f32[2,16,64,256]{3,2,1,0:T(8,128)} %bitcast.22) | data formatting | bytes 4194304 | tf_op jit(solution)/shard_map/reshape | solution.py:779
  209.2 3.8 %constant_dynamic-slice_fusion = (f32[1,64,4096]{1,2,0:T(8,128)}, f32[1,64,4096]{1,2,0:T(8,128)S(1)}) fusion(f32[2,64,4096]{1,2,0:T(8,128)} %bitcast.21, s32[]{:T(128)S(6)} %select_n.29, s32[]{:T(128)S(6)} %select_n.27), kind=kLoop, calls=%fused_computation.6 | loop fusion | bytes 4194312 | tf_op jit(solution)/shard_map/jit(dynamic_index_in_dim)/dynamic_slice | solution.py:781
  213.0 3.1 %copy.23 = f32[1,64,4096]{2,1,0:T(8,128)} copy(f32[1,64,4096]{1,2,0:T(8,128)} %get-tuple-element.38) | data formatting | bytes 2097152 | tf_op jit(solution)/shard_map/jit(dynamic_index_in_dim)/dynamic_slice | solution.py:781
  216.1 1.6 copy.22
  217.7 1.5 broadcast_in_dim.24
  220.3 2.5 bitcast_dynamic-update-slice_fusion
  222.7 72.6 %all-to-all-done.3.spec_ref = f32[16,2,2,64,256]{4,3,2,1,0:T(8,128)} async-done(((f32[16,2,2,64,256]{4,3,2,1,0:T(8,128)}), f32[16,2,2,64,256]{4,3,2,1,0:T(8,128)}, u32[]{:S(2)}, u32[]{:S(2)}) %all-to-all-start.3) | async-done | bytes 4194336 | tf_op jit(solution)/shard_map/all_to_all | solution.py:724
  296.6 11.1 %y_forward.1 = f32[4,2048,128]{2,1,0:T(8,128)} custom-call(f32[16,2,2,64,256]{4,3,2,1,0:T(8,128)} %all-to-all-done.3.spec_ref, bf16[4,2048,128]{2,1,0:T(8,128)(2,1)S(1)} %bitcast.20, bf16[1024,512]{1,0:T(8,128)(2,1)S(1)} %copy-done.16, f32[2,3,256,128]{3,2,1,0:T(8,128)S(1)} %copy-done.9), custom_call_target="tpu_custom_call" | custom-call | tf_op jit(solution)/shard_map/y_forward/pallas_call | solution.py:351
  (64 shorter events, 13.8 us)
Async XLA Ops:
  0.7 1.6 copy-start.4
  2.3 1.1 copy-start.8
  3.4 1.2 copy-start.17
  11.2 4.2 %collective-permute-start = (f32[16,2,64,256]{3,2,1,0:T(8,128)S(1)}, f32[16,2,64,256]{3,2,1,0:T(8,128)S(1)}, u32[]{:S(2)}, u32[]{:S(2)}) collective-permute-start(f32[16,2,64,256]{3,2,1,0:T(8,128)S(1)} %get-tuple-element.20), channel_id=1, source_target_pairs={{0,16},{16,0},{1,17},{17,1},{2,18},{18,2},{3,19},{19,3},{4,20},{20... | collective-permute-start | bytes 6291464 | tf_op jit(solution)/shard_map/ppermute | solution.py:716
  16.3 2.0 copy-start.3
  18.4 7.3 %copy-start.20 = (f32[2,4096]{1,0:T(2,128)S(1)}, f32[2,4096]{1,0:T(2,128)}, u32[]{:S(2)}) copy-start(f32[2,4096]{1,0:T(2,128)} %param.17) | copy-start | bytes 98308
  18.4 7.3 %copy-start.21 = (s32[4096]{0:T(1024)S(1)}, s32[4096]{0:T(1024)}, u32[]{:S(2)}) copy-start(s32[4096]{0:T(1024)} %param.16) | copy-start | bytes 49156
  18.4 102.8 %copy-start.7 = (f32[2,16,8,256]{3,2,1,0:T(8,128)S(1)}, f32[2,16,8,256]{3,2,1,0:T(8,128)}, u32[]{:S(2)}) copy-start(f32[2,16,8,256]{3,2,1,0:T(8,128)} %constant.57.clone.tw_ref) | copy-start | bytes 786436
  18.4 102.8 %all-to-all-start = ((f32[16,2,2,64,256]{4,3,2,1,0:T(8,128)}), f32[16,2,2,64,256]{4,3,2,1,0:T(8,128)}, u32[]{:S(2)}, u32[]{:S(2)}) async-start(f32[16,2,2,64,256]{4,3,2,1,0:T(8,128)} %copy-done.3), calls=%async_computation | async-start | bytes 8388608 | tf_op jit(solution)/shard_map/all_to_all | solution.py:724
  122.2 8.7 %copy-start.13 = (bf16[256,1024]{1,0:T(8,128)(2,1)S(1)}, bf16[256,1024]{1,0:T(8,128)(2,1)}, u32[]{:S(2)}) copy-start(bf16[256,1024]{1,0:T(8,128)(2,1)} %constant.59.clone.table_ref) | copy-start | bytes 1572868
  129.0 11.7 %collective-permute-start.2 = (f32[2,32,256]{2,1,0:T(8,128)S(1)}, f32[2,32,256]{2,1,0:T(8,128)S(1)}, u32[]{:S(2)}, u32[]{:S(2)}) collective-permute-start(f32[2,32,256]{2,1,0:T(8,128)S(1)} %get-tuple-element.25), channel_id=1, source_target_pairs={{16,0},{1,16},{17,1},{2,17},{18,2},{3,18},{19,3},{4,19},{20,4},{5,... | collective-permute-start | bytes 196616 | tf_op jit(solution)/shard_map/ppermute | solution.py:763
  137.3 2.0 copy-start
  139.4 1.3 copy-start.18
  141.9 17.0 %all-to-all-start.1 = ((f32[16,8,128]{2,1,0:T(8,128)}), f32[16,8,128]{2,1,0:T(8,128)S(1)}, u32[]{:S(2)}, u32[]{:S(2)}) async-start(f32[16,8,128]{2,1,0:T(8,128)} %border_sums.1), calls=%async_computation.1 | async-start | bytes 131072 | tf_op jit(solution)/shard_map/all_to_all | solution.py:724
  147.2 2.2 copy-start.1
  155.7 1.3 copy-start.10
  157.0 7.7 %collective-permute-start.3 = (f32[2,32,256]{2,1,0:T(8,128)}, f32[2,32,256]{2,1,0:T(8,128)S(1)}, u32[]{:S(2)}, u32[]{:S(2)}) collective-permute-start(f32[2,32,256]{2,1,0:T(8,128)} %get-tuple-element.26), channel_id=1, source_target_pairs={{16,0},{1,16},{17,1},{2,17},{18,2},{3,18},{19,3},{4,19},{20,4},{5,... | collective-permute-start | bytes 196616 | tf_op jit(solution)/shard_map/ppermute | solution.py:769
  158.9 5.8 %collective-permute-start.4 = (f32[16,8,128]{2,1,0:T(8,128)S(1)}, f32[16,8,128]{2,1,0:T(8,128)S(1)}, u32[]{:S(2)}, u32[]{:S(2)}) collective-permute-start(f32[16,8,128]{2,1,0:T(8,128)S(1)} %all-to-all-done.1.refs_0_), channel_id=1, source_target_pairs={{0,16},{16,0},{1,17},{17,1},{2,18},{18,2},{3,19},{19,3},{4,20},{20... | collective-permute-start | bytes 196616 | tf_op jit(solution)/shard_map/ppermute | solution.py:716
  159.5 5.2 %collective-permute-start.1 = (f32[32,256]{1,0:T(8,128)S(1)}, f32[32,256]{1,0:T(8,128)S(1)}, u32[]{:S(2)}, u32[]{:S(2)}) collective-permute-start(f32[32,256]{1,0:T(8,128)S(1)} %get-tuple-element.24.tail_ref), channel_id=1, source_target_pairs={{0,16},{16,1},{1,17},{17,2},{2,18},{18,3},{3,19},{19,4},{4,20},{20... | collective-permute-start | bytes 98312 | tf_op jit(solution)/shard_map/ppermute | solution.py:764
  161.4 27.0 %collective-permute-start.6 = (f32[16,2,64,256]{3,2,1,0:T(8,128)}, f32[16,2,64,256]{3,2,1,0:T(8,128)S(1)}, u32[]{:S(2)}, u32[]{:S(2)}) collective-permute-start(f32[16,2,64,256]{3,2,1,0:T(8,128)} %copy-done.18), channel_id=1, source_target_pairs={{0,16},{16,0},{1,17},{17,1},{2,18},{18,2},{3,19},{19,3},{4,20},{20... | collective-permute-start | bytes 6291464 | tf_op jit(solution)/shard_map/ppermute | solution.py:716
  164.7 1.6 copy-start.11
  166.3 22.1 %copy-start.2 = (f32[16,2,2,64,256]{4,3,2,1,0:T(8,128)S(1)}, f32[16,2,2,64,256]{4,3,2,1,0:T(8,128)}, u32[]{:S(2)}) copy-start(f32[16,2,2,64,256]{4,3,2,1,0:T(8,128)} %copy-done) | copy-start | bytes 12582916
  174.7 15.2 %copy-start.12 = (f32[32,64,256]{2,1,0:T(8,128)}, f32[32,64,256]{2,1,0:T(8,128)S(1)}, u32[]{:S(2)}) copy-start(f32[32,64,256]{2,1,0:T(8,128)S(1)} %get-tuple-element.34) | copy-start | bytes 6291460
  174.7 13.8 %collective-permute-start.7 = (f32[16,2,64,256]{3,2,1,0:T(8,128)S(1)}, f32[16,2,64,256]{3,2,1,0:T(8,128)S(1)}, u32[]{:S(2)}, u32[]{:S(2)}) collective-permute-start(f32[16,2,64,256]{3,2,1,0:T(8,128)S(1)} %get-tuple-element.32), channel_id=1, source_target_pairs={{0,16},{16,0},{1,17},{17,1},{2,18},{18,2},{3,19},{19,3},{4,20},{20... | collective-permute-start | bytes 6291464 | tf_op jit(solution)/shard_map/ppermute | solution.py:716
  187.2 1.3 collective-permute-start.5
  189.9 2.0 copy-start.6
  191.9 103.5 %all-to-all-start.3 = ((f32[16,2,2,64,256]{4,3,2,1,0:T(8,128)}), f32[16,2,2,64,256]{4,3,2,1,0:T(8,128)}, u32[]{:S(2)}, u32[]{:S(2)}) async-start(f32[16,2,2,64,256]{4,3,2,1,0:T(8,128)} %copy-done.6), calls=%async_computation.3 | async-start | bytes 8388608 | tf_op jit(solution)/shard_map/all_to_all | solution.py:724
  216.1 4.2 %collective-permute-start.8 = (f32[64,4096]{1,0:T(8,128)}, f32[64,4096]{1,0:T(8,128)}, u32[]{:S(2)}, u32[]{:S(2)}) collective-permute-start(f32[64,4096]{1,0:T(8,128)} %bitcast.13), channel_id=1, source_target_pairs={{0,16},{16,0},{1,17},{17,1},{2,18},{18,2},{3,19},{19,3},{4,20},{20... | collective-permute-start | bytes 3145736 | tf_op jit(solution)/shard_map/ppermute | solution.py:716
  217.7 1.5 copy-start.19
  219.2 76.1 %copy-start.5 = (bf16[1,4,2048,128]{3,2,1,0:T(8,128)(2,1)S(1)}, bf16[1,4,2048,128]{3,2,1,0:T(8,128)(2,1)}, u32[]{:S(2)}) copy-start(bf16[1,4,2048,128]{3,2,1,0:T(8,128)(2,1)} %param.15) | copy-start | bytes 6291460
  219.2 76.1 %copy-start.9 = (f32[2,3,256,128]{3,2,1,0:T(8,128)S(1)}, f32[2,3,256,128]{3,2,1,0:T(8,128)}, u32[]{:S(2)}) copy-start(f32[2,3,256,128]{3,2,1,0:T(8,128)} %constant.56.clone.tw_ref) | copy-start | bytes 2359300
  295.4 1.2 copy-start.16
  (2 other events, 2.1 us)

commit v5 on v4

--- a/solution.py
+++ b/solution.py
@@ -189,16 +189,30 @@
     return [one, two, three, four, both(one, four), both(two, four), both(three, four)]
 
 
-def y_inverse_kernel(gz, edge_ref, data_ref, table_ref, tw_ref, *refs):
-    out_refs, (re_s, im_s, mix_s) = refs[:gz], refs[gz:]
+def y_inverse_kernel(gz, edge_ref, data_hbm, table_hbm, tw_hbm, out_hbm, *refs):
+    other_refs, refs = refs[: gz - 1], refs[gz - 1 :]
+    data_ref, table_ref, tw_ref, own_s, re_s, im_s, mix_s, sems, out_sems = refs
     blocks, ny, _ = data_ref.shape
     n = ny // YR
-    rows = out_refs[0].shape[2]
+    rows = own_s.shape[2]
     lane = lax.broadcasted_iota(jnp.int32, (n, LANES), 1)
-    table = table_ref[...]
-
-    for chunk in range(blocks // 2):
+    pairs = blocks // 2
+
+    def fetch(chunk):
+        part = pl.ds(2 * chunk, 2)
+        return pltpu.make_async_copy(data_hbm.at[part], data_ref.at[part], sems.at[2 + chunk])
+
+    fetch_table = pltpu.make_async_copy(table_hbm, table_ref, sems.at[0])
+    fetch_tw = pltpu.make_async_copy(tw_hbm, tw_ref, sems.at[1])
+    fetch(0).start()
+    fetch_table.start()
+    fetch_tw.start()
+    for chunk in range(1, pairs):
+        fetch(chunk).start()
+
+    for chunk in range(pairs):
         lanes = slice(chunk * LANES, (chunk + 1) * LANES)
+        fetch(chunk).wait()
 
         def unpack(i, carry):
             part = pl.ds(pl.multiple_of(i * n, n), n)
@@ -209,13 +223,16 @@
             return carry
 
         lax.fori_loop(0, YR, unpack, 0)
+        if chunk == 0:
+            fetch_table.wait()
+            fetch_tw.wait()
 
         for k in range(0, YR, 2):
             pieces = [
                 jnp.concatenate([s[pl.ds(k + d, n, stride=YR), :] for d in range(2)], axis=1)
                 for s in (re_s, im_s)
             ]
-            both = dot(table, jnp.concatenate(pieces, axis=0).astype(BF16))
+            both = dot(table_ref[...], jnp.concatenate(pieces, axis=0).astype(BF16))
             both = both[: 2 * n] + both[2 * n :]
             for d in range(2):
                 mix_s[k + d] = both[:, d * LANES : (d + 1) * LANES]
@@ -223,6 +240,7 @@
         tiles = rows // 8
         for r in range(gz):
             core = core_on(edge_ref, gz, r)
+            target = other_refs[r - 1] if r else own_s
 
             def combine(i, carry):
                 y2 = ((i // tiles) * gz + core) * rows + lax.rem(i, tiles) * 8
@@ -239,56 +257,73 @@
                 at = pl.ds(pl.multiple_of(lax.rem(i, tiles) * 8, 8), 8)
                 for k, (re, im) in enumerate(short_fft(planes, 1)):
                     to = k * (n // (gz * rows)) + i // tiles
-                    out_refs[r][to, 0, at, lanes] = re
-                    out_refs[r][to, 1, at, lanes] = im
+                    target[to, 0, at, lanes] = re
+                    target[to, 1, at, lanes] = im
                 return carry
 
             lax.fori_loop(0, n // gz // 8, combine, 0, unroll=2)
+
+    give = pltpu.make_async_copy(own_s, out_hbm.at[:, edge_ref[2]], out_sems.at[0])
+    give.start()
+    give.wait()
 
 
 def y_inverse(edge, data, rows, gz, gy):
     blocks, ny, width = data.shape
     n = ny // YR
+    ka = blocks * HALF
     vmem = pl.BlockSpec(memory_space=pltpu.VMEM)
-    return pl.pallas_call(
+    hbm = pl.BlockSpec(memory_space=pltpu.HBM)
+    piece = jax.ShapeDtypeStruct((gy, 2, rows, ka), F32)
+    whole, *others = pl.pallas_call(
         functools.partial(y_inverse_kernel, gz),
-        in_specs=[pl.BlockSpec(memory_space=pltpu.SMEM)] + [vmem] * 3,
-        out_specs=[vmem] * gz,
-        out_shape=[jax.ShapeDtypeStruct((gy, 2, rows, blocks * HALF), F32)] * gz,
+        in_specs=[pl.BlockSpec(memory_space=pltpu.SMEM)] + [hbm] * 3,
+        out_specs=[hbm] + [vmem] * (gz - 1),
+        out_shape=[jax.ShapeDtypeStruct((gy, gz, 2, rows, ka), F32)] + [piece] * (gz - 1),
         scratch_shapes=[
+            pltpu.VMEM((blocks, ny, width), BF16),
+            pltpu.VMEM((4 * n, 2 * n), BF16),
+            pltpu.VMEM((2, 3, n, LANES), F32),
+            pltpu.VMEM((gy, 2, rows, ka), F32),
             pltpu.VMEM((ny, LANES), F32),
             pltpu.VMEM((ny, LANES), F32),
             pltpu.VMEM((YR, 2 * n, LANES), F32),
+            pltpu.SemaphoreType.DMA((2 + blocks // 2,)),
+            pltpu.SemaphoreType.DMA((1,)),
         ],
-        compiler_params=pltpu.CompilerParams(vmem_limit_bytes=Y_GRANT),
+        compiler_params=pltpu.CompilerParams(vmem_limit_bytes=Y_GRANT + 4 * MIB),
         name="y_inverse",
     )(edge, data, y_matrix(ny, False, -1.0), y_twiddle(ny))
+    return whole, others
 
 
 def merge_kernel(gz, edge_ref, *refs):
-    out_ref = refs[-1]
-    for r in range(gz):
-        core = core_on(edge_ref, gz, -r)
-
-        def one(i, carry):
-            out_ref[i, core] = refs[r][i]
-            return carry
-
-        lax.fori_loop(0, out_ref.shape[0], one, 0)
-
-
-def merge(edge, pieces):
-    gz = len(pieces)
-    vmem = pl.BlockSpec(memory_space=pltpu.VMEM)
-    gy, *rest = pieces[0].shape
+    pieces, (_, out_hbm, sems) = refs[: gz - 1], refs[gz - 1 :]
+    copies = [
+        pltpu.make_async_copy(piece, out_hbm.at[:, core_on(edge_ref, gz, -r - 1)], sems.at[r])
+        for r, piece in enumerate(pieces)
+    ]
+    for copy in copies:
+        copy.start()
+    for copy in copies:
+        copy.wait()
+
+
+def merge(edge, whole, pieces):
+    gz = whole.shape[1]
+    hbm = pl.BlockSpec(memory_space=pltpu.HBM)
     return pl.pallas_call(
         functools.partial(merge_kernel, gz),
-        in_specs=[pl.BlockSpec(memory_space=pltpu.SMEM)] + [vmem] * gz,
-        out_specs=vmem,
-        out_shape=jax.ShapeDtypeStruct((gy, gz, *rest), F32),
-        compiler_params=pltpu.CompilerParams(vmem_limit_bytes=2 * MIB),
+        in_specs=[pl.BlockSpec(memory_space=pltpu.SMEM)]
+        + [pl.BlockSpec(memory_space=pl.ANY)] * (gz - 1)
+        + [hbm],
+        out_specs=hbm,
+        out_shape=jax.ShapeDtypeStruct(whole.shape, F32),
+        scratch_shapes=[pltpu.SemaphoreType.DMA((gz - 1,))],
+        input_output_aliases={gz: 0},
+        compiler_params=pltpu.CompilerParams(vmem_limit_bytes=MIB),
         name="merge",
-    )(edge, *pieces)
+    )(edge, *pieces, whole)
 
 
 def y_forward_kernel(spec_ref, data_ref, table_ref, tw_ref, out_ref, re_s, im_s, mix_s):
@@ -371,127 +406,64 @@
     return chunk
 
 
-def x_inverse_kernel(
-    spec_ref, coef_ref, tw_ref, table_ref, out_ref, head_ref, tail_ref, re_s, im_s
-):
-    kb, gz, _, rows, ka = spec_ref.shape
-    planes = gz * kb
-
-    def columns(i, carry):
-        part = pl.ds(pl.multiple_of(i * 8, 8), 8)
-        for start in range(0, ka, LANES):
-            lanes = slice(start, start + LANES)
-            mixed = [[None] * kb for _ in range(gz)]
-            for k in range(kb):
-                coef = [coef_ref[j, k, :, lanes] for j in range(3)]
-                re = mix_adjoint(coef, [spec_ref[k, z, 0, part, lanes] for z in range(gz)])
-                im = mix_adjoint(coef, [spec_ref[k, z, 1, part, lanes] for z in range(gz)])
-                for z in range(gz):
-                    mixed[z][k] = (re[z], im[z])
-            for z in range(gz):
-                for b, (re, im) in enumerate(short_fft(mixed[z], 1)):
-                    if b > 0:
-                        c = tw_ref[0, b, :, lanes]
-                        s = tw_ref[1, b, :, lanes]
-                        re, im = re * c - im * s, im * c + re * s
-                    re_s[z * kb + b, part, lanes] = re
-                    im_s[z * kb + b, part, lanes] = im
-        return carry
-
-    lax.fori_loop(0, rows // 8, columns, 0)
-
-    step = plane_chunk(planes, rows)
-
-    def multiply(i, carry):
-        part = pl.ds(i * step, step)
-        both = jnp.concatenate(
-            [re_s[part].reshape(step * rows, ka), im_s[part].reshape(step * rows, ka)], axis=1
-        )
-        high, low = split2(both)
-        value = dot(high, table_ref[...])
-        value = value[:, :ka] + value[:, ka:] + dot(low, table_ref[:, :ka])
-        out_ref[part] = value.reshape(step, rows, ka)
-        return carry
-
-    lax.fori_loop(0, planes // step, multiply, 0)
-
-    for p in range(planes):
-        for r in range(head_ref.shape[0]):
-            head_ref[r, p : p + 1, :] = out_ref[p, r : r + 1, :]
-        tail_ref[p : p + 1, :] = out_ref[p, rows - 1 : rows, :]
-
-
-def x_inverse(spec, coef, nx):
-    kb, gz, _, rows, ka = spec.shape
-    planes = gz * kb
-    vmem = pl.BlockSpec(memory_space=pltpu.VMEM)
-    return pl.pallas_call(
-        x_inverse_kernel,
-        in_specs=[vmem] * 4,
-        out_specs=[vmem] * 3,
-        out_shape=[
-            jax.ShapeDtypeStruct((planes, rows, ka), F32),
-            jax.ShapeDtypeStruct((2, planes, ka), F32),
-            jax.ShapeDtypeStruct((planes, ka), F32),
-        ],
-        scratch_shapes=[pltpu.VMEM((planes, rows, ka), F32)] * 2,
-        compiler_params=pltpu.CompilerParams(vmem_limit_bytes=X_GRANT),
-        name="x_inverse",
-    )(spec, coef, x_twiddle(nx, ka), jnp.asarray(x_inverse_matrix(nx, ka)))
-
-
-def forward_into(gz, field_ref, coef_ref, tw_ref, table_ref, spec_ref, re_s, im_s):
-    planes, rows, ka = field_ref.shape
-    kb = planes // gz
-    step = plane_chunk(planes, rows)
-
-    def multiply(i, carry):
-        part = pl.ds(i * step, step)
-        high, low = split2(field_ref[part].reshape(step * rows, ka))
-        value = dot(high, table_ref[...])
-        value = value[:, : 2 * ka] + value[:, 2 * ka :] + dot(low, table_ref[:, : 2 * ka])
-        re_s[part] = value[:, :ka].reshape(step, rows, ka)
-        im_s[part] = value[:, ka:].reshape(step, rows, ka)
-        return carry
-
-    lax.fori_loop(0, planes // step, multiply, 0)
-
-    def columns(i, total):
-        part = pl.ds(pl.multiple_of(i * 8, 8), 8)
-        for start in range(0, ka, LANES):
-            lanes = slice(start, start + LANES)
-            spectra = []
-            for z in range(gz):
-                turned = []
-                for b in range(kb):
-                    re = re_s[z * kb + b, part, lanes]
-                    im = im_s[z * kb + b, part, lanes]
-                    if b > 0:
-                        c = tw_ref[0, b, :, lanes]
-                        s = tw_ref[1, b, :, lanes]
-                        re, im = re * c + im * s, im * c - re * s
-                    turned.append((re, im))
-                spectra.append(short_fft(turned, -1))
-            for k in range(kb):
-                coef = [coef_ref[j, k, :, lanes] for j in range(3)]
-                for p in range(2):
-                    for z, value in enumerate(mix(coef, [spectra[z][k][p] for z in range(gz)])):
-                        spec_ref[k, z, p, part, lanes] = value
-                        total = total + value * value
-        return total
-
-    return lax.fori_loop(0, rows // 8, columns, jnp.zeros((8, LANES), F32))
-
-
-def cut(gz, edge_ref, spec_ref, piece_refs):
-    for r, piece_ref in enumerate(piece_refs):
-        core = core_on(edge_ref, gz, r + 1)
-
-        def one(i, carry):
-            piece_ref[i] = spec_ref[i, core]
-            return carry
-
-        lax.fori_loop(0, spec_ref.shape[0], one, 0)
+def turn_rows(kb, planes_of, tw_ref, lanes, sign):
+    out = []
+    for b in range(kb):
+        re, im = planes_of(b)
+        if b > 0:
+            c = tw_ref[0, b, :, lanes]
+            s = tw_ref[1, b, :, lanes]
+            if sign > 0:
+                re, im = re * c - im * s, im * c + re * s
+            else:
+                re, im = re * c + im * s, im * c - re * s
+        out.append((re, im))
+    return out
+
+
+def inverse_columns(gz, kb, spectra, coef_ref, tw_ref, lanes, part, re_s, im_s):
+    mixed = [[None] * kb for _ in range(gz)]
+    for k in range(kb):
+        coef = [coef_ref[j, k, :, lanes] for j in range(3)]
+        re = mix_adjoint(coef, [spectra[z][k][0] for z in range(gz)])
+        im = mix_adjoint(coef, [spectra[z][k][1] for z in range(gz)])
+        for z in range(gz):
+            mixed[z][k] = (re[z], im[z])
+    for z in range(gz):
+        short = short_fft(mixed[z], 1)
+        for b, (re, im) in enumerate(turn_rows(kb, lambda b: short[b], tw_ref, lanes, 1)):
+            re_s[z * kb + b, part, lanes] = re
+            im_s[z * kb + b, part, lanes] = im
+
+
+def forward_columns(gz, kb, coef_ref, tw_ref, lanes, part, re_s, im_s):
+    spectra = []
+    for z in range(gz):
+        rows_of = lambda b: (re_s[z * kb + b, part, lanes], im_s[z * kb + b, part, lanes])
+        spectra.append(short_fft(turn_rows(kb, rows_of, tw_ref, lanes, -1), -1))
+    out = [[None] * kb for _ in range(gz)]
+    for k in range(kb):
+        coef = [coef_ref[j, k, :, lanes] for j in range(3)]
+        re = mix(coef, [spectra[z][k][0] for z in range(gz)])
+        im = mix(coef, [spectra[z][k][1] for z in range(gz)])
+        for z in range(gz):
+            out[z][k] = (re[z], im[z])
+    return out
+
+
+def inverse_product(re, im, table_ref):
+    ka = re.shape[1]
+    high, low = split2(jnp.concatenate([re, im], axis=1))
+    value = dot(high, table_ref[...])
+    return value[:, :ka] + value[:, ka:] + dot(low, table_ref[:, :ka])
+
+
+def forward_product(field, table_ref):
+    ka = field.shape[1]
+    high, low = split2(field)
+    value = dot(high, table_ref[...])
+    value = value[:, : 2 * ka] + value[:, 2 * ka :] + dot(low, table_ref[:, : 2 * ka])
+    return value[:, :ka], value[:, ka:]
 
 
 def next_plane(field_ref, p, kb):
@@ -536,27 +508,141 @@
     sums_ref[2] = slope
 
 
-def spec_shapes(gz, field):
-    planes, rows, ka = field.shape
-    kb = planes // gz
-    whole = jax.ShapeDtypeStruct((kb, gz, 2, rows, ka), F32)
-    return [whole] + [jax.ShapeDtypeStruct((kb, 2, rows, ka), F32)] * (gz - 1)
-
-
-def first_projection(edge, field, coef, gz, nx):
-    planes, rows, ka = field.shape
+def middle_kernel(
+    gz, edge_ref, spec_hbm, coef_ref, tw_ref, inverse_ref, forward_ref,
+    d0_ref, nd0_ref, head_ref, tail_ref, sums_ref, *refs,
+):
+    give_hbm, (spec_s, re_s, im_s, sems, out_sems) = refs[:gz], refs[gz:]
+    kb, _, _, rows, ka = spec_s.shape
+    planes = gz * kb
+    lane_parts = [slice(start, start + LANES) for start in range(0, ka, LANES)]
+    cuts = sems.shape[0]
+    cut = rows // cuts
+
+    def fetch(i):
+        part = pl.ds(i * cut, cut)
+        return pltpu.make_async_copy(
+            spec_hbm.at[:, :, :, part], spec_s.at[:, :, :, part], sems.at[i]
+        )
+
+    for i in range(cuts):
+        fetch(i).start()
+    for i in range(cuts):
+        fetch(i).wait()
+
+        def first_columns(j, carry):
+            part = pl.ds(pl.multiple_of(i * cut + j * 8, 8), 8)
+            for lanes in lane_parts:
+                spectra = [
+                    [(spec_s[k, z, 0, part, lanes], spec_s[k, z, 1, part, lanes]) for k in range(kb)]
+                    for z in range(gz)
+                ]
+                inverse_columns(gz, kb, spectra, coef_ref, tw_ref, lanes, part, re_s, im_s)
+            return carry
+
+        lax.fori_loop(0, cut // 8, first_columns, 0)
+
+    step = plane_chunk(planes, rows)
+    shape2, shape3 = (step * rows, ka), (step, rows, ka)
+
+    def there_and_back(i, carry):
+        part = pl.ds(i * step, step)
+        field = inverse_product(re_s[part].reshape(shape2), im_s[part].reshape(shape2), inverse_ref)
+        d0_ref[part] = field.reshape(shape3)
+        re, im = forward_product(field, forward_ref)
+        re_s[part] = re.reshape(shape3)
+        im_s[part] = im.reshape(shape3)
+        return carry
+
+    lax.fori_loop(0, planes // step, there_and_back, 0)
+
+    def second_columns(j, total):
+        part = pl.ds(pl.multiple_of(j * 8, 8), 8)
+        for lanes in lane_parts:
+            spectra = forward_columns(gz, kb, coef_ref, tw_ref, lanes, part, re_s, im_s)
+            for z in range(gz):
+                for k in range(kb):
+                    for p in range(2):
+                        value = spectra[z][k][p]
+                        spec_s[k, z, p, part, lanes] = value
+                        total = total + value * value
+            inverse_columns(gz, kb, spectra, coef_ref, tw_ref, lanes, part, re_s, im_s)
+        return total
+
+    projected = lax.fori_loop(0, rows // 8, second_columns, jnp.zeros((8, LANES), F32))
+    gives = [
+        pltpu.make_async_copy(spec_s.at[:, core_on(edge_ref, gz, r)], give_hbm[r], out_sems.at[r])
+        for r in range(gz)
+    ]
+    for give in gives:
+        give.start()
+
+    def back(i, carry):
+        part = pl.ds(i * step, step)
+        field = inverse_product(re_s[part].reshape(shape2), im_s[part].reshape(shape2), inverse_ref)
+        nd0_ref[part] = field.reshape(shape3)
+        return carry
+
+    lax.fori_loop(0, planes // step, back, 0)
+
+    for p in range(planes):
+        head_ref[0, p : p + 1, :] = d0_ref[p, :1, :]
+        head_ref[1, p : p + 1, :] = d0_ref[p, 1:2, :]
+        head_ref[2, p : p + 1, :] = nd0_ref[p, :1, :]
+        tail_ref[p : p + 1, :] = d0_ref[p, rows - 1 : rows, :]
+
+    row = lax.broadcasted_iota(jnp.int32, (rows, ka), 0)
+    square = jnp.zeros((8, LANES), F32)
+    slope = jnp.zeros((8, LANES), F32)
+    for p in range(planes):
+        here = d0_ref[p]
+        square = square + fold(here * here)
+        along_x = next_plane(d0_ref, p, kb) - here
+        along_y = jnp.where(row == rows - 1, 0.0, pltpu.roll(here, rows - 1, 0) - here)
+        terms = along_x * along_x + along_y * along_y
+        if p + kb < planes:
+            along_z = d0_ref[p + kb] - here
+            terms = terms + along_z * along_z
+        slope = slope + fold(terms)
+    sums_ref[0] = square
+    sums_ref[1] = projected
+    sums_ref[2] = slope
+    for give in gives:
+        give.wait()
+
+
+def middle(edge, spec, coef, nx):
+    kb, gz, _, rows, ka = spec.shape
+    planes = gz * kb
     vmem = pl.BlockSpec(memory_space=pltpu.VMEM)
-    shapes = spec_shapes(gz, field)
-    sums, spec, *pieces = pl.pallas_call(
-        functools.partial(first_kernel, gz),
-        in_specs=[pl.BlockSpec(memory_space=pltpu.SMEM)] + [vmem] * 4,
-        out_specs=[vmem] * (1 + len(shapes)),
-        out_shape=[jax.ShapeDtypeStruct((3, 8, LANES), F32)] + shapes,
-        scratch_shapes=[pltpu.VMEM((planes, rows, ka), F32)] * 2,
+    hbm = pl.BlockSpec(memory_space=pltpu.HBM)
+    field = jax.ShapeDtypeStruct((planes, rows, ka), F32)
+    d0, nd0, head, tail, sums, *pieces = pl.pallas_call(
+        functools.partial(middle_kernel, gz),
+        in_specs=[pl.BlockSpec(memory_space=pltpu.SMEM), hbm] + [vmem] * 4,
+        out_specs=[vmem] * 5 + [hbm] * gz,
+        out_shape=[
+            field,
+            field,
+            jax.ShapeDtypeStruct((3, planes, ka), F32),
+            jax.ShapeDtypeStruct((planes, ka), F32),
+            jax.ShapeDtypeStruct((3, 8, LANES), F32),
+        ]
+        + [jax.ShapeDtypeStruct((kb, 2, rows, ka), F32)] * gz,
+        scratch_shapes=[
+            pltpu.VMEM((kb, gz, 2, rows, ka), F32),
+            pltpu.VMEM((planes, rows, ka), F32),
+            pltpu.VMEM((planes, rows, ka), F32),
+            pltpu.SemaphoreType.DMA((2 if rows % 16 == 0 else 1,)),
+            pltpu.SemaphoreType.DMA((gz,)),
+        ],
         compiler_params=pltpu.CompilerParams(vmem_limit_bytes=X_GRANT),
-        name="first_projection",
-    )(edge, field, coef, x_twiddle(nx, ka), x_forward_matrix(nx, ka))
-    return spec, pieces, sums
+        name="middle",
+    )(
+        edge, spec, coef, x_twiddle(nx, ka), jnp.asarray(x_inverse_matrix(nx, ka)),
+        x_forward_matrix(nx, ka),
+    )
+    return d0, nd0, head, tail, sums, pieces
 
 
 def border_kernel(edge_ref, sums_ref, tail_ref, next_ref, out_ref):
@@ -577,11 +663,11 @@
 
 
 def second_kernel(
-    gz, edge_ref, d0_ref, nd0_ref, tail_ref, prev_ref, next_ref, nnext_ref,
+    gz, edge_ref, d0_ref, nd0_ref, tail_ref, prev_ref, next_ref,
     coef_ref, tw_ref, table_ref, *refs,
 ):
-    sums_refs, (d1_ref, eta_ref, out_ref, spec_ref, *refs) = refs[:gz], refs[gz:]
-    piece_refs, (re_s, im_s, row_s) = refs[:-3], refs[-3:]
+    sums_refs, (d1_ref, eta_ref, out_ref, *refs) = refs[:gz], refs[gz:]
+    piece_refs, (sum_s, re_s, im_s, row_s) = refs[:gz], refs[gz:]
     planes, rows, ka = d0_ref.shape
     kb = planes // gz
     eta_here = step_of(sums_refs)
@@ -598,7 +684,7 @@
     for z in range(gz):
         part = slice(z * kb, (z + 1) * kb)
         here = next_ref[0, part, :]
-        value = here - eta * nnext_ref[0, part, :]
+        value = here - eta * next_ref[2, part, :]
         up = pltpu.roll(here, kb - 1, 0)
         up = jnp.where(
             row2 == kb - 1, jnp.where(lane2 == ka - 1, here, pltpu.roll(up, ka - 1, 1)), up
@@ -644,26 +730,54 @@
             terms = terms + along_z * along_z
         slope = slope + fold(terms)
 
-    projected = forward_into(gz, d1_ref, coef_ref, tw_ref, table_ref, spec_ref, re_s, im_s)
-    cut(gz, edge_ref, spec_ref, piece_refs)
-    put_sums(out_ref, [square, projected, slope])
-
-
-def second_descent(edge, sums, d0, nd0, tail, prev_tail, next_head, next_nhead, coef, gz, nx):
+    step = plane_chunk(planes, rows)
+
+    def multiply(i, carry):
+        part = pl.ds(i * step, step)
+        re, im = forward_product(d1_ref[part].reshape(step * rows, ka), table_ref)
+        re_s[part] = re.reshape(step, rows, ka)
+        im_s[part] = im.reshape(step, rows, ka)
+        return carry
+
+    lax.fori_loop(0, planes // step, multiply, 0)
+
+    def transform(core):
+        def columns(j, total):
+            part = pl.ds(pl.multiple_of(j * 8, 8), 8)
+            for start in range(0, ka, LANES):
+                lanes = slice(start, start + LANES)
+                spectra = forward_columns(gz, kb, coef_ref, tw_ref, lanes, part, re_s, im_s)
+                for z in range(gz):
+                    for k in range(kb):
+                        for p in range(2):
+                            value = spectra[z][k][p]
+                            piece_refs[(z - core) % gz][k, p, part, lanes] = value
+                            total = total + value * value
+            return total
+
+        sum_s[...] = lax.fori_loop(0, rows // 8, columns, jnp.zeros((8, LANES), F32))
+
+    for core in range(gz):
+        pl.when(edge_ref[2] == core)(functools.partial(transform, core))
+    put_sums(out_ref, [square, sum_s[...], slope])
+
+
+def second_descent(edge, sums, d0, nd0, tail, prev_tail, next_head, coef, gz, nx):
     planes, rows, ka = d0.shape
     vmem = pl.BlockSpec(memory_space=pltpu.VMEM)
-    shapes = spec_shapes(gz, d0)
-    d1, eta, out, spec, *pieces = pl.pallas_call(
+    piece = jax.ShapeDtypeStruct((planes // gz, 2, rows, ka), F32)
+    d1, eta, out, *pieces = pl.pallas_call(
         functools.partial(second_kernel, gz),
-        in_specs=[pl.BlockSpec(memory_space=pltpu.SMEM)] + [vmem] * (9 + gz),
-        out_specs=[vmem] * (3 + len(shapes)),
+        in_specs=[pl.BlockSpec(memory_space=pltpu.SMEM)] + [vmem] * (8 + gz),
+        out_specs=[vmem] * (3 + gz),
         out_shape=[
             jax.ShapeDtypeStruct((planes, rows, ka), F32),
             jax.ShapeDtypeStruct((8, LANES), F32),
             jax.ShapeDtypeStruct(sums[0].shape, F32),
         ]
-        + shapes,
+        + [piece] * gz,
         scratch_shapes=[
+            pltpu.VMEM((8, LANES), F32),
             pltpu.VMEM((planes, rows, ka), F32),
             pltpu.VMEM((planes, rows, ka), F32),
             pltpu.VMEM((planes, ka), F32),
@@ -671,10 +785,10 @@
         compiler_params=pltpu.CompilerParams(vmem_limit_bytes=X_GRANT),
         name="second_descent",
     )(
-        edge, d0, nd0, tail, prev_tail, next_head, next_nhead, coef,
+        edge, d0, nd0, tail, prev_tail, next_head, coef,
         x_twiddle(nx, ka), x_forward_matrix(nx, ka), *sums,
     )
-    return d1, spec, pieces, eta, out
+    return d1, pieces, eta, out
 
 
 def combine_kernel(gz, edge_ref, eta_ref, *refs):
@@ -684,29 +798,32 @@
     eta1 = jnp.max(step_of(sums_refs))
     steps_ref[0] = eta_ref[...]
     steps_ref[1] = jnp.full((8, LANES), eta1, F32)
+    count = out_ref.shape[0]
+    start = pl.program_id(0) * count
     for r in range(gz):
         core = core_on(edge_ref, gz, -r)
-
-        def one(i, carry):
-            at = i if r else (i, core)
-            out_ref[i, core] = -(eta0 * first_refs[r][at] + eta1 * second_refs[r][at])
-            return carry
-
-        lax.fori_loop(0, out_ref.shape[0], one, 0)
+        for i in range(count):
+            out_ref[i, core] = -(eta0 * first_refs[r][start + i] + eta1 * second_refs[r][start + i])
 
 
 def combine_spectra(edge, eta, sums, first, second):
     gz = len(sums)
+    kb, *rest = first[0].shape
+    count = 4 if kb % 4 == 0 else 1
     vmem = pl.BlockSpec(memory_space=pltpu.VMEM)
     return pl.pallas_call(
         functools.partial(combine_kernel, gz),
+        grid=(kb // count,),
         in_specs=[pl.BlockSpec(memory_space=pltpu.SMEM)] + [vmem] * (1 + 3 * gz),
-        out_specs=[vmem] * 2,
+        out_specs=[
+            pl.BlockSpec((count, gz, *rest), lambda i: (i, 0, 0, 0, 0)),
+            pl.BlockSpec((2, 8, LANES), lambda i: (0, 0, 0)),
+        ],
         out_shape=[
-            jax.ShapeDtypeStruct(first[0].shape, F32),
+            jax.ShapeDtypeStruct((kb, gz, *rest), F32),
             jax.ShapeDtypeStruct((2, 8, LANES), F32),
         ],
-        compiler_params=pltpu.CompilerParams(vmem_limit_bytes=2 * MIB),
+        compiler_params=pltpu.CompilerParams(vmem_limit_bytes=6 * MIB),
         name="combine_spectra",
     )(edge, eta, *sums, *first, *second)
 
@@ -757,22 +874,19 @@
     ).reshape(3, gy, 1, ka)
     coef = jnp.broadcast_to(coef, (3, gy, 8, ka))
 
-    own, *others = y_inverse(edge, data, rows, gz, gy)
-    spec = to_chips(merge(edge, [own] + from_cores(others)))
-    d0, head, tail = x_inverse(spec, coef, nx)
+    whole, others = y_inverse(edge, data, rows, gz, gy)
+    spec = to_chips(merge(edge, whole, from_cores(others)))
+    d0, nd0, head, tail, sums, first = middle(edge, spec, coef, nx)
     next_head = lax.ppermute(head, ("gz", "gy"), up)
     prev_tail = lax.ppermute(tail, ("gz", "gy"), down)
-    spec0, others0, sums = first_projection(edge, d0, coef, gz, nx)
     sums = everywhere(border_sums(edge, sums, tail, next_head, gy))
-    others0 = from_cores(others0)
-    nd0, nhead, _ = x_inverse(spec0, coef, nx)
-    next_nhead = lax.ppermute(nhead, ("gz", "gy"), up)
-    d1, spec1, others1, eta, sums = second_descent(
-        edge, sums, d0, nd0, tail, prev_tail, next_head, next_nhead, coef, gz, nx
+    first = first[:1] + from_cores(first[1:])
+    d1, second, eta, sums = second_descent(
+        edge, sums, d0, nd0, tail, prev_tail, next_head, coef, gz, nx
     )
     sums = everywhere(sums)
-    others1 = from_cores(others1)
-    spec, etas = combine_spectra(edge, eta, sums, [spec0] + others0, [spec1] + others1)
+    second = second[:1] + from_cores(second[1:])
+    spec, etas = combine_spectra(edge, eta, sums, first, second)
     residual = y_forward(to_chips(spec), data)
 
     volume = -(etas[0, 0, 0] * d0 + etas[1, 0, 0] * d1)

time: 309 us -> 304 us (0.984)
  local copies, waits for them, and re-layouts: 38.8 us -> 28.3 us
  blocking collectives: 12 us -> 20.9 us
  starting transfers between devices: 29.7 us -> 22.7 us
    unnamed x44 -> x30, local copies, waits for them, and re-layouts: 19.8 us -> 9.23 us
    all_to_all x1 -> x2, blocking collectives: 12 us -> 20.9 us  [to_chips(): return lax.all_to_all(parts, 'gy', 0, 0, tiled=True)]
    all_to_all x3 -> x2, starting transfers between devices: 20 us -> 14.9 us  [to_chips(): return lax.all_to_all(parts, 'gy', 0, 0, tiled=True)]
    pallas_call x4 -> x2, Pallas kernels: 19.8 us -> 21.8 us  [the longest x1 19.9 us: middle(): pl.pallas_call(functools.partial(middle_kernel, gz), in_specs=[pl.BlockSp...]
    all_to_all x3 -> x2, waiting for transfers between devices: 168 us -> 168 us  [to_chips(): return lax.all_to_all(parts, 'gy', 0, 0, tiled=True)]
  transfers between devices with their start and end apart: 12 -> 10, of which waited for: 5 -> 6; matrix products, arithmetic and copies ran while one was open for 8% -> 8% of each run, Pallas kernels for 6% -> 3%
where the time goes in v5:
time: 304 us; the launch traced here: 303 us
  waiting for transfers between devices  176 us (58%)
  Pallas kernels  49.3 us (16%)
  local copies, waits for them, and re-layouts  28.3 us (9%)
  starting transfers between devices  22.7 us (7%)
  blocking collectives  20.9 us (7%)
  other arithmetic  4.65 us (2%)
    all_to_all x2, waiting for transfers between devices, to_chips(): return lax.all_to_all(parts, 'gy', 0, 0, tiled=True)  168 us
    all_to_all x2, blocking collectives, to_chips(): return lax.all_to_all(parts, 'gy', 0, 0, tiled=True)  20.9 us
    pallas_call x1, Pallas kernels, middle(): pl.pallas_call(functools.partial(middle_kernel, gz), in_specs=[pl.BlockSp...  19.9 us
    all_to_all x2, starting transfers between devices, to_chips(): return lax.all_to_all(parts, 'gy', 0, 0, tiled=True)  14.9 us
    pallas_call x1, Pallas kernels, y_forward(): pl.pallas_call(y_forward_kernel, grid=(blocks // 2,), in_specs=[pl.BlockS...  11.1 us
    unnamed x30, local copies, waits for them, and re-layouts  9.23 us
    dynamic_slice x3, local copies, waits for them, and re-layouts, shards(): lax.dynamic_index_in_dim(volume, lax.rem(core + r, gz), 0, False)  8.58 us
    pallas_call x1, Pallas kernels, second_descent(): pl.pallas_call(functools.partial(second_kernel, gz), in_specs=[pl.BlockSp...  8.24 us
  transfers between devices with their start and end apart: 10, of which 6 were waited for; matrix products, arithmetic and copies ran while one was open for 8% of the time, Pallas kernels for 3%

profile of v5, /device:TPU:14, one launch (start us, length us, event | category | flops | bytes accessed | tf_op | source)
XLA Modules:
  0.0 302.9 jit_solution(9087640690595447851)
XLA Ops:
  0.7 1.6 copy-done.1
  2.3 1.1 copy-done.4
  3.4 1.2 copy-done.10
  4.7 6.9 %y_inverse.1 = (f32[16,2,2,64,256]{4,3,2,1,0:T(8,128)S(1)}, f32[16,2,64,256]{3,2,1,0:T(8,128)S(1)}) custom-call(s32[3]{0:T(128)S(1)} %pad_add_fusion.edge_ref, bf16[4,2048,128]{2,1,0:T(8,128)(2,1)S(1)} %bitcast.19, bf16[1024,512]{1,0:T(8,128)(2,1)S(1)} %copy-done.10, f32[2,3,256,128]{3,2,1,0:T(8,128)S(1)} %copy-done.4), custom_call_target="tpu_custom_call" | custom-call | tf_op jit(solution)/shard_map/y_inverse/pallas_call | solution.py:278
  11.7 4.1 %collective-permute-done.refs_0_ = f32[16,2,64,256]{3,2,1,0:T(8,128)S(1)} collective-permute-done((f32[16,2,64,256]{3,2,1,0:T(8,128)S(1)}, f32[16,2,64,256]{3,2,1,0:T(8,128)S(1)}, u32[]{:S(2)}, u32[]{:S(2)}) %collective-permute-start) | collective-permute-done | bytes 2097184 | tf_op jit(solution)/shard_map/ppermute | solution.py:833
  16.5 2.0 copy-done
  18.6 7.3 %all-to-all-start = ((f32[16,2,2,64,256]{4,3,2,1,0:T(8,128)}), f32[16,2,2,64,256]{4,3,2,1,0:T(8,128)}, u32[]{:S(2)}, u32[]{:S(2)}) async-start(f32[16,2,2,64,256]{4,3,2,1,0:T(8,128)} %copy-done), calls=%async_computation | async-start | bytes 8388608 | tf_op jit(solution)/shard_map/all_to_all | solution.py:841
  26.0 95.4 %all-to-all-done.spec_hbm = f32[16,2,2,64,256]{4,3,2,1,0:T(8,128)} async-done(((f32[16,2,2,64,256]{4,3,2,1,0:T(8,128)}), f32[16,2,2,64,256]{4,3,2,1,0:T(8,128)}, u32[]{:S(2)}, u32[]{:S(2)}) %all-to-all-start) | async-done | bytes 4194336 | tf_op jit(solution)/shard_map/all_to_all | solution.py:841
  121.4 19.9 %middle.1 = (f32[32,64,256]{2,1,0:T(8,128)S(1)}, f32[32,64,256]{2,1,0:T(8,128)S(1)}, f32[3,32,256]{2,1,0:T(8,128)S(1)}, f32[32,256]{1,0:T(8,128)S(1)}, f32[3,8,1...) custom-call(s32[3]{0:T(128)S(1)} %pad_add_fusion.edge_ref, ...), custom_call_target="tpu_custom_call" | custom-call | tf_op jit(solution)/shard_map/middle/pallas_call | solution.py:620
  141.3 1.9 collective-permute-start.2
  143.2 2.2 collective-permute-done.2.next_ref
  146.0 9.7 %all_to_all.20.refs_0_ = f32[16,8,128]{2,1,0:T(8,128)S(1)} all-to-all(f32[16,8,128]{2,1,0:T(8,128)S(1)} %border_sums.1), channel_id=1, replica_groups=mesh['gz'=2,'gy'=16] {'gy'}, dimensions={0} | all-to-all | bytes 131072 | tf_op jit(solution)/shard_map/all_to_all | solution.py:841
  155.7 1.1 collective-permute-start.3
  156.8 1.9 collective-permute-start.1
  158.7 2.5 collective-permute-start.5
  162.0 8.2 %second_descent.1 = (f32[32,64,256]{2,1,0:T(8,128)S(1)}, f32[8,128]{1,0:T(8,128)S(1)}, f32[16,8,128]{2,1,0:T(8,128)S(1)}, f32[16,2,64,256]{3,2,1,0:T(8,128)S(1)}, f32[16,2,64,256]{3,2,1,0:T(8,128)S(1)}) custom-call(s32[3]{0:T(128)S(1)} %pad_add_fusion.edge_ref, f32[32,64,256]{2,1,0:T(8,128)S(1)} %get-tuple-element.20.d0_ref, ...), custom_call_target="tpu_custom_call" | custom-call | tf_op jit(solution)/shard_map/second_descent/pallas_call | solution.py:769
  170.5 11.3 %all_to_all.21.refs_0_ = f32[16,8,128]{2,1,0:T(8,128)S(1)} all-to-all(f32[16,8,128]{2,1,0:T(8,128)S(1)} %get-tuple-element.26), channel_id=1, replica_groups=mesh['gz'=2,'gy'=16] {'gy'}, dimensions={0} | all-to-all | bytes 131072 | tf_op jit(solution)/shard_map/all_to_all | solution.py:841
  181.8 1.3 collective-permute-done.4.refs_1_
  183.0 1.9 combine_spectra.1
  184.9 2.0 copy-done.3
  187.0 7.6 %all-to-all-start.3 = ((f32[16,2,2,64,256]{4,3,2,1,0:T(8,128)}), f32[16,2,2,64,256]{4,3,2,1,0:T(8,128)}, u32[]{:S(2)}, u32[]{:S(2)}) async-start(f32[16,2,2,64,256]{4,3,2,1,0:T(8,128)} %copy-done.3), calls=%async_computation.3 | async-start | bytes 8388608 | tf_op jit(solution)/shard_map/all_to_all | solution.py:841
  195.1 4.6 %add_negate_fusion = f32[32,64,256]{2,1,0:T(8,128)} fusion(f32[32,64,256]{2,1,0:T(8,128)} %copy-done.7, f32[32,64,256]{2,1,0:T(8,128)S(1)} %get-tuple-element.20.d0_ref, f32[]{:T(128)} %bitcast.8, f32[]{:T(128)} %bitcast.7), kind=kLoop, calls=%fused_computation | loop fusion | flops 2097152 | bytes 6291464 | tf_op jit(solution)/shard_map/neg | solution.py:892
  199.6 4.9 %copy.19 = f32[2,16,64,256]{2,1,3,0:T(8,128)} copy(f32[2,16,64,256]{3,2,1,0:T(8,128)} %bitcast.22) | data formatting | bytes 4194304 | tf_op jit(solution)/shard_map/reshape | solution.py:893
  204.5 3.8 %constant_dynamic-slice_fusion = (f32[1,64,4096]{1,2,0:T(8,128)}, f32[1,64,4096]{1,2,0:T(8,128)S(1)}) fusion(f32[2,64,4096]{1,2,0:T(8,128)} %bitcast.21, s32[]{:T(128)S(6)} %select_n.29, s32[]{:T(128)S(6)} %select_n.27), kind=kLoop, calls=%fused_computation.6 | loop fusion | bytes 4194312 | tf_op jit(solution)/shard_map/jit(dynamic_index_in_dim)/dynamic_slice | solution.py:895
  208.3 3.2 %copy.21 = f32[1,64,4096]{2,1,0:T(8,128)} copy(f32[1,64,4096]{1,2,0:T(8,128)} %get-tuple-element.36) | data formatting | bytes 2097152 | tf_op jit(solution)/shard_map/jit(dynamic_index_in_dim)/dynamic_slice | solution.py:895
  211.5 1.6 copy.20
  213.0 1.5 broadcast_in_dim.24
  214.6 1.0 constant_dynamic-update-slice_fusion
  215.6 2.5 bitcast_dynamic-update-slice_fusion
  218.1 72.5 %all-to-all-done.3.spec_ref = f32[16,2,2,64,256]{4,3,2,1,0:T(8,128)} async-done(((f32[16,2,2,64,256]{4,3,2,1,0:T(8,128)}), f32[16,2,2,64,256]{4,3,2,1,0:T(8,128)}, u32[]{:S(2)}, u32[]{:S(2)}) %all-to-all-start.3) | async-done | bytes 4194336 | tf_op jit(solution)/shard_map/all_to_all | solution.py:841
  290.6 1.2 copy-done.8
  291.8 11.1 %y_forward.1 = f32[4,2048,128]{2,1,0:T(8,128)} custom-call(f32[16,2,2,64,256]{4,3,2,1,0:T(8,128)} %all-to-all-done.3.spec_ref, bf16[4,2048,128]{2,1,0:T(8,128)(2,1)S(1)} %bitcast.20, bf16[1024,512]{1,0:T(8,128)(2,1)S(1)} %copy-done.8, f32[2,3,256,128]{3,2,1,0:T(8,128)S(1)} %copy-done.5), custom_call_target="tpu_custom_call" | custom-call | tf_op jit(solution)/shard_map/y_forward/pallas_call | solution.py:386
  (45 shorter events, 3.1 us)
Async XLA Ops:
  0.7 1.6 copy-start.1
  2.3 1.1 copy-start.4
  3.4 1.2 copy-start.10
  11.6 4.2 %collective-permute-start = (f32[16,2,64,256]{3,2,1,0:T(8,128)S(1)}, f32[16,2,64,256]{3,2,1,0:T(8,128)S(1)}, u32[]{:S(2)}, u32[]{:S(2)}) collective-permute-start(f32[16,2,64,256]{3,2,1,0:T(8,128)S(1)} %get-tuple-element.18), channel_id=1, source_target_pairs={{0,16},{16,0},{1,17},{17,1},{2,18},{18,2},{3,19},{19,3},{4,20},{20... | collective-permute-start | bytes 6291464 | tf_op jit(solution)/shard_map/ppermute | solution.py:833
  16.5 2.0 copy-start
  18.5 7.3 %copy-start.13 = (f32[2,4096]{1,0:T(2,128)S(1)}, f32[2,4096]{1,0:T(2,128)}, u32[]{:S(2)}) copy-start(f32[2,4096]{1,0:T(2,128)} %param.14) | copy-start | bytes 98308
  18.5 7.4 %copy-start.14 = (s32[4096]{0:T(1024)S(1)}, s32[4096]{0:T(1024)}, u32[]{:S(2)}) copy-start(s32[4096]{0:T(1024)} %param.13) | copy-start | bytes 49156
  18.5 102.9 %copy-start.6 = (bf16[256,1024]{1,0:T(8,128)(2,1)S(1)}, bf16[256,1024]{1,0:T(8,128)(2,1)}, u32[]{:S(2)}) copy-start(bf16[256,1024]{1,0:T(8,128)(2,1)} %constant.59.clone.forward_ref.table_ref) | copy-start | bytes 1572868
  18.5 102.9 %copy-start.9 = (f32[2,16,8,256]{3,2,1,0:T(8,128)S(1)}, f32[2,16,8,256]{3,2,1,0:T(8,128)}, u32[]{:S(2)}) copy-start(f32[2,16,8,256]{3,2,1,0:T(8,128)} %constant.57.clone.tw_ref) | copy-start | bytes 786436
  18.5 102.9 %copy-start.11 = (bf16[512,512]{1,0:T(8,128)(2,1)S(1)}, bf16[512,512]{1,0:T(8,128)(2,1)}, u32[]{:S(2)}) copy-start(bf16[512,512]{1,0:T(8,128)(2,1)} %constant.58.clone.inverse_ref) | copy-start | bytes 1572868
  18.6 102.8 %all-to-all-start = ((f32[16,2,2,64,256]{4,3,2,1,0:T(8,128)}), f32[16,2,2,64,256]{4,3,2,1,0:T(8,128)}, u32[]{:S(2)}, u32[]{:S(2)}) async-start(f32[16,2,2,64,256]{4,3,2,1,0:T(8,128)} %copy-done), calls=%async_computation | async-start | bytes 8388608 | tf_op jit(solution)/shard_map/all_to_all | solution.py:841
  141.3 4.1 %collective-permute-start.2 = (f32[3,32,256]{2,1,0:T(8,128)S(1)}, f32[3,32,256]{2,1,0:T(8,128)S(1)}, u32[]{:S(2)}, u32[]{:S(2)}) collective-permute-start(f32[3,32,256]{2,1,0:T(8,128)S(1)} %get-tuple-element.23), channel_id=1, source_target_pairs={{16,0},{1,16},{17,1},{2,17},{18,2},{3,18},{19,3},{4,19},{20,4},{5,... | collective-permute-start | bytes 294920 | tf_op jit(solution)/shard_map/ppermute | solution.py:880
  155.7 6.4 %collective-permute-start.3 = (f32[16,8,128]{2,1,0:T(8,128)S(1)}, f32[16,8,128]{2,1,0:T(8,128)S(1)}, u32[]{:S(2)}, u32[]{:S(2)}) collective-permute-start(f32[16,8,128]{2,1,0:T(8,128)S(1)} %all_to_all.20.refs_0_), channel_id=1, source_target_pairs={{0,16},{16,0},{1,17},{17,1},{2,18},{18,2},{3,19},{19,3},{4,20},{20... | collective-permute-start | bytes 196616 | tf_op jit(solution)/shard_map/ppermute | solution.py:833
  156.8 5.2 %collective-permute-start.1 = (f32[32,256]{1,0:T(8,128)S(1)}, f32[32,256]{1,0:T(8,128)S(1)}, u32[]{:S(2)}, u32[]{:S(2)}) collective-permute-start(f32[32,256]{1,0:T(8,128)S(1)} %get-tuple-element.22.tail_ref), channel_id=1, source_target_pairs={{0,16},{16,1},{1,17},{17,2},{2,18},{18,3},{3,19},{19,4},{4,20},{20... | collective-permute-start | bytes 98312 | tf_op jit(solution)/shard_map/ppermute | solution.py:881
  158.7 24.3 %collective-permute-start.5 = (f32[16,2,64,256]{3,2,1,0:T(8,128)S(1)}, f32[16,2,64,256]{3,2,1,0:T(8,128)S(1)}, u32[]{:S(2)}, u32[]{:S(2)}) collective-permute-start(f32[16,2,64,256]{3,2,1,0:T(8,128)S(1)} %get-tuple-element.28), channel_id=1, source_target_pairs={{0,16},{16,0},{1,17},{17,1},{2,18},{18,2},{3,19},{19,3},{4,20},{20... | collective-permute-start | bytes 6291464 | tf_op jit(solution)/shard_map/ppermute | solution.py:833
  170.3 14.7 %copy-start.7 = (f32[32,64,256]{2,1,0:T(8,128)}, f32[32,64,256]{2,1,0:T(8,128)S(1)}, u32[]{:S(2)}) copy-start(f32[32,64,256]{2,1,0:T(8,128)S(1)} %get-tuple-element.32) | copy-start | bytes 6291460
  170.3 12.8 %collective-permute-start.6 = (f32[16,2,64,256]{3,2,1,0:T(8,128)S(1)}, f32[16,2,64,256]{3,2,1,0:T(8,128)S(1)}, u32[]{:S(2)}, u32[]{:S(2)}) collective-permute-start(f32[16,2,64,256]{3,2,1,0:T(8,128)S(1)} %get-tuple-element.30), channel_id=1, source_target_pairs={{0,16},{16,0},{1,17},{17,1},{2,18},{18,2},{3,19},{19,3},{4,20},{20... | collective-permute-start | bytes 6291464 | tf_op jit(solution)/shard_map/ppermute | solution.py:833
  181.8 1.3 collective-permute-start.4
  184.9 2.0 copy-start.3
  187.0 103.6 %all-to-all-start.3 = ((f32[16,2,2,64,256]{4,3,2,1,0:T(8,128)}), f32[16,2,2,64,256]{4,3,2,1,0:T(8,128)}, u32[]{:S(2)}, u32[]{:S(2)}) async-start(f32[16,2,2,64,256]{4,3,2,1,0:T(8,128)} %copy-done.3), calls=%async_computation.3 | async-start | bytes 8388608 | tf_op jit(solution)/shard_map/all_to_all | solution.py:841
  211.5 4.2 %collective-permute-start.7 = (f32[64,4096]{1,0:T(8,128)}, f32[64,4096]{1,0:T(8,128)}, u32[]{:S(2)}, u32[]{:S(2)}) collective-permute-start(f32[64,4096]{1,0:T(8,128)} %bitcast.13), channel_id=1, source_target_pairs={{0,16},{16,0},{1,17},{17,1},{2,18},{18,2},{3,19},{19,3},{4,20},{20... | collective-permute-start | bytes 3145736 | tf_op jit(solution)/shard_map/ppermute | solution.py:833
  213.0 1.5 copy-start.12
  214.6 76.0 %copy-start.2 = (bf16[1,4,2048,128]{3,2,1,0:T(8,128)(2,1)S(1)}, bf16[1,4,2048,128]{3,2,1,0:T(8,128)(2,1)}, u32[]{:S(2)}) copy-start(bf16[1,4,2048,128]{3,2,1,0:T(8,128)(2,1)} %param.12) | copy-start | bytes 6291460
  214.6 76.0 %copy-start.5 = (f32[2,3,256,128]{3,2,1,0:T(8,128)S(1)}, f32[2,3,256,128]{3,2,1,0:T(8,128)}, u32[]{:S(2)}) copy-start(f32[2,3,256,128]{3,2,1,0:T(8,128)} %constant.56.clone.tw_hbm.tw_ref) | copy-start | bytes 2359300
  290.6 1.2 copy-start.8

commit v6 on v5

--- a/solution.py
+++ b/solution.py
@@ -17,8 +17,8 @@
 F32 = jnp.float32
 BF16 = jnp.bfloat16
 MIB = 1024 * 1024
-Y_GRANT = 16 * MIB
-X_GRANT = 16 * MIB
+Y_GRANT = 56 * MIB
+X_GRANT = 24 * MIB
 
 
 def dft_parts(length, scale):
@@ -53,9 +53,9 @@
 
 def y_twiddle(ny):
     n = ny // YR
-    angles = 2.0 * np.pi / ny * (np.array([1, 2, 4])[:, None] * np.arange(n)[None, :])
+    angles = 2.0 * np.pi / ny * (np.arange(1, YR)[:, None] * np.arange(n)[None, :])
     table = np.stack([np.cos(angles), np.sin(angles)]).astype(np.float32)
-    return jnp.asarray(np.ascontiguousarray(np.broadcast_to(table[..., None], (2, 3, n, LANES))))
+    return jnp.asarray(np.ascontiguousarray(np.broadcast_to(table[..., None], (2, YR - 1, n, LANES))))
 
 
 def x_inverse_matrix(nx, ka):
@@ -179,16 +179,6 @@
     return lax.rem(edge_ref[2] + gz + r, gz)
 
 
-def y_turns(tw_ref, part):
-    one, two, four = [(tw_ref[0, i, part, :], tw_ref[1, i, part, :]) for i in range(3)]
-
-    def both(a, b):
-        return a[0] * b[0] - a[1] * b[1], a[1] * b[0] + a[0] * b[1]
-
-    three = both(one, two)
-    return [one, two, three, four, both(one, four), both(two, four), both(three, four)]
-
-
 def y_inverse_kernel(gz, edge_ref, data_hbm, table_hbm, tw_hbm, out_hbm, *refs):
     other_refs, refs = refs[: gz - 1], refs[gz - 1 :]
     data_ref, table_ref, tw_ref, own_s, re_s, im_s, mix_s, sems, out_sems = refs
@@ -225,7 +215,6 @@
         lax.fori_loop(0, YR, unpack, 0)
         if chunk == 0:
             fetch_table.wait()
-            fetch_tw.wait()
 
         for k in range(0, YR, 2):
             pieces = [
@@ -237,6 +226,9 @@
             for d in range(2):
                 mix_s[k + d] = both[:, d * LANES : (d + 1) * LANES]
 
+        if chunk == 0:
+            fetch_tw.wait()
+
         tiles = rows // 8
         for r in range(gz):
             core = core_on(edge_ref, gz, r)
@@ -245,13 +237,13 @@
             def combine(i, carry):
                 y2 = ((i // tiles) * gz + core) * rows + lax.rem(i, tiles) * 8
                 part = pl.ds(pl.multiple_of(y2, 8), 8)
-                turns = [None] + y_turns(tw_ref, part)
                 planes = []
                 for k in range(YR):
                     re = mix_s[k, part, :]
                     im = mix_s[k, pl.ds(pl.multiple_of(n + y2, 8), 8), :]
                     if k > 0:
-                        c, s = turns[k]
+                        c = tw_ref[0, k - 1, part, :]
+                        s = tw_ref[1, k - 1, part, :]
                         re, im = re * c - im * s, im * c + re * s
                     planes.append((re, im))
                 at = pl.ds(pl.multiple_of(lax.rem(i, tiles) * 8, 8), 8)
@@ -283,7 +275,7 @@
         scratch_shapes=[
             pltpu.VMEM((blocks, ny, width), BF16),
             pltpu.VMEM((4 * n, 2 * n), BF16),
-            pltpu.VMEM((2, 3, n, LANES), F32),
+            pltpu.VMEM((2, YR - 1, n, LANES), F32),
             pltpu.VMEM((gy, 2, rows, ka), F32),
             pltpu.VMEM((ny, LANES), F32),
             pltpu.VMEM((ny, LANES), F32),
@@ -291,7 +283,7 @@
             pltpu.SemaphoreType.DMA((2 + blocks // 2,)),
             pltpu.SemaphoreType.DMA((1,)),
         ],
-        compiler_params=pltpu.CompilerParams(vmem_limit_bytes=Y_GRANT + 4 * MIB),
+        compiler_params=pltpu.CompilerParams(vmem_limit_bytes=Y_GRANT),
         name="y_inverse",
     )(edge, data, y_matrix(ny, False, -1.0), y_twiddle(ny))
     return whole, others
@@ -321,86 +313,132 @@
         out_shape=jax.ShapeDtypeStruct(whole.shape, F32),
         scratch_shapes=[pltpu.SemaphoreType.DMA((gz - 1,))],
         input_output_aliases={gz: 0},
-        compiler_params=pltpu.CompilerParams(vmem_limit_bytes=MIB),
+        compiler_params=pltpu.CompilerParams(vmem_limit_bytes=Y_GRANT),
         name="merge",
     )(edge, *pieces, whole)
 
 
-def y_forward_kernel(spec_ref, data_ref, table_ref, tw_ref, out_ref, re_s, im_s, mix_s):
-    ny = data_ref.shape[1]
+def y_forward_kernel(
+    spec_hbm, data_hbm, table_hbm, tw_hbm, out_hbm,
+    spec_ref, data_ref, table_ref, tw_ref, out_ref, re_s, im_s, mix_s, sems, spec_sems, out_sems,
+):
+    blocks, ny, _ = data_ref.shape
     n = ny // YR
     gy, gz, _, rows, _ = spec_ref.shape
-    chunk = pl.program_id(0)
-
-    def unpack(i, carry):
-        for core in range(gz):
-            part = pl.ds(pl.multiple_of((i * gz + core) * rows, rows), rows)
-            re_s[part, :] = spec_ref[i, core, 0]
-            im_s[part, :] = spec_ref[i, core, 1]
-        return carry
-
-    lax.fori_loop(0, gy, unpack, 0)
-
-    table = table_ref[...]
-    for k in range(0, YR, 2):
-        pieces = [
-            jnp.concatenate([s[pl.ds(k + d, n, stride=YR), :] for d in range(2)], axis=1)
-            for s in (re_s, im_s)
-        ]
-        high, low = split2(jnp.concatenate(pieces, axis=0))
-        both = dot(table, high)
-        both = both[: 2 * n] + both[2 * n :] + dot(table[: 2 * n], low)
-        for d in range(2):
-            mix_s[k + d] = both[:, d * LANES : (d + 1) * LANES]
+    pairs = blocks // 2
+    half = n // 2
+
+    def fetch(chunk):
+        lanes = pl.ds(chunk * LANES, LANES)
+        return pltpu.make_async_copy(
+            spec_hbm.at[:, :, :, :, lanes], spec_ref.at[:, :, :, :, lanes], spec_sems.at[chunk]
+        )
+
+    def give(chunk, part):
+        at = (pl.ds(2 * chunk, 2), slice(None), pl.ds(part * half, half))
+        return pltpu.make_async_copy(out_ref.at[at], out_hbm.at[at], out_sems.at[2 * chunk + part])
+
+    fetch_table = pltpu.make_async_copy(table_hbm, table_ref, sems.at[0])
+    fetch_tw = pltpu.make_async_copy(tw_hbm, tw_ref, sems.at[1])
+    fetch_data = pltpu.make_async_copy(data_hbm, data_ref, sems.at[2])
+    fetch(0).start()
+    fetch_table.start()
+    fetch_tw.start()
+    fetch_data.start()
+    for chunk in range(1, pairs):
+        fetch(chunk).start()
 
     lane = lax.broadcasted_iota(jnp.int32, (16, LANES), 1)
-
-    def combine(i, carry):
-        start = pl.multiple_of(i * 16, 16)
-        part = pl.ds(start, 16)
-        turns = [None] + y_turns(tw_ref, part)
-        planes = []
-        for k in range(YR):
-            re = mix_s[k, part, :]
-            im = mix_s[k, pl.ds(pl.multiple_of(n + i * 16, 16), 16), :]
-            if k > 0:
-                c, s = turns[k]
-                re, im = re * c + im * s, im * c - re * s
-            planes.append((re, im))
-        for k, (re, im) in enumerate(short_fft(planes, -1)):
-            at = pl.ds(pl.multiple_of(k * n + start, 16), 16)
-            first = jnp.where(lane < HALF, re, pltpu.roll(im, HALF, 1))
-            second = jnp.where(lane < HALF, pltpu.roll(re, HALF, 1), im)
-            out_ref[0, at, :] = first - data_ref[2 * chunk, at, :].astype(F32)
-            out_ref[1, at, :] = second - data_ref[2 * chunk + 1, at, :].astype(F32)
-        return carry
-
-    lax.fori_loop(0, n // 16, combine, 0)
+    for chunk in range(pairs):
+        lanes = slice(chunk * LANES, (chunk + 1) * LANES)
+        fetch(chunk).wait()
+
+        def unpack(i, carry):
+            for core in range(gz):
+                part = pl.ds(pl.multiple_of((i * gz + core) * rows, rows), rows)
+                re_s[part, :] = spec_ref[i, core, 0, :, lanes]
+                im_s[part, :] = spec_ref[i, core, 1, :, lanes]
+            return carry
+
+        lax.fori_loop(0, gy, unpack, 0)
+        if chunk == 0:
+            fetch_table.wait()
+
+        for k in range(0, YR, 2):
+            pieces = [
+                jnp.concatenate([s[pl.ds(k + d, n, stride=YR), :] for d in range(2)], axis=1)
+                for s in (re_s, im_s)
+            ]
+            high, low = split2(jnp.concatenate(pieces, axis=0))
+            both = dot(table_ref[...], high)
+            both = both[: 2 * n] + both[2 * n :] + dot(table_ref[: 2 * n], low)
+            for d in range(2):
+                mix_s[k + d] = both[:, d * LANES : (d + 1) * LANES]
+        if chunk == 0:
+            fetch_tw.wait()
+            fetch_data.wait()
+
+        def combine(i, carry):
+            start = pl.multiple_of(i * 16, 16)
+            part = pl.ds(start, 16)
+            planes = []
+            for k in range(YR):
+                re = mix_s[k, part, :]
+                im = mix_s[k, pl.ds(pl.multiple_of(n + i * 16, 16), 16), :]
+                if k > 0:
+                    c = tw_ref[0, k - 1, part, :]
+                    s = tw_ref[1, k - 1, part, :]
+                    re, im = re * c + im * s, im * c - re * s
+                planes.append((re, im))
+            for k, (re, im) in enumerate(short_fft(planes, -1)):
+                at = pl.ds(pl.multiple_of(k * n + start, 16), 16)
+                first = jnp.where(lane < HALF, re, pltpu.roll(im, HALF, 1))
+                second = jnp.where(lane < HALF, pltpu.roll(re, HALF, 1), im)
+                out_ref[2 * chunk, k, part, :] = first - data_ref[2 * chunk, at, :].astype(F32)
+                out_ref[2 * chunk + 1, k, part, :] = (
+                    second - data_ref[2 * chunk + 1, at, :].astype(F32)
+                )
+            return carry
+
+        for part in range(2):
+            lax.fori_loop(part * half // 16, (part + 1) * half // 16, combine, 0)
+            give(chunk, part).start()
+
+    for chunk in range(pairs):
+        for part in range(2):
+            give(chunk, part).wait()
 
 
 def y_forward(spec, data):
     blocks, ny, width = data.shape
-    gy, gz, _, rows, _ = spec.shape
     n = ny // YR
-    vmem = pl.BlockSpec(memory_space=pltpu.VMEM)
-    return pl.pallas_call(
+    hbm = pl.BlockSpec(memory_space=pltpu.HBM)
+    out = pl.pallas_call(
         y_forward_kernel,
-        grid=(blocks // 2,),
-        in_specs=[pl.BlockSpec((gy, gz, 2, rows, LANES), lambda i: (0, 0, 0, 0, i))] + [vmem] * 3,
-        out_specs=pl.BlockSpec((2, ny, width), lambda i: (i, 0, 0)),
-        out_shape=jax.ShapeDtypeStruct((blocks, ny, width), F32),
+        in_specs=[hbm] * 4,
+        out_specs=hbm,
+        out_shape=jax.ShapeDtypeStruct((blocks, YR, n, width), F32),
         scratch_shapes=[
+            pltpu.VMEM(spec.shape, F32),
+            pltpu.VMEM((blocks, ny, width), BF16),
+            pltpu.VMEM((4 * n, 2 * n), BF16),
+            pltpu.VMEM((2, YR - 1, n, LANES), F32),
+            pltpu.VMEM((blocks, YR, n, width), F32),
             pltpu.VMEM((ny, LANES), F32),
             pltpu.VMEM((ny, LANES), F32),
             pltpu.VMEM((YR, 2 * n, LANES), F32),
+            pltpu.SemaphoreType.DMA((3,)),
+            pltpu.SemaphoreType.DMA((blocks // 2,)),
+            pltpu.SemaphoreType.DMA((blocks,)),
         ],
-        compiler_params=pltpu.CompilerParams(vmem_limit_bytes=Y_GRANT + 8 * MIB),
+        compiler_params=pltpu.CompilerParams(vmem_limit_bytes=Y_GRANT),
         name="y_forward",
     )(spec, data, y_matrix(ny, True, 1.0), y_twiddle(ny))
+    return out.reshape(blocks, ny, width)
 
 
 def plane_chunk(planes, rows):
-    chunk = max(1, 512 // rows)
+    chunk = max(1, 1024 // rows)
     while planes % chunk:
         chunk -= 1
     return chunk
@@ -645,21 +683,22 @@
     return d0, nd0, head, tail, sums, pieces
 
 
-def border_kernel(edge_ref, sums_ref, tail_ref, next_ref, out_ref):
+def border_kernel(edge_ref, sums_ref, tail_ref, next_ref, prev_ref, out_ref):
+    del prev_ref
     step = (next_ref[0] - tail_ref[...]) * jnp.where(edge_ref[1] > 0, 0.0, 1.0)
     put_sums(out_ref, [sums_ref[0], sums_ref[1], sums_ref[2] + fold(step * step)])
 
 
-def border_sums(edge, sums, tail, next_head, copies):
+def border_sums(edge, sums, tail, next_head, prev_tail, copies):
     vmem = pl.BlockSpec(memory_space=pltpu.VMEM)
     return pl.pallas_call(
         border_kernel,
-        in_specs=[pl.BlockSpec(memory_space=pltpu.SMEM)] + [vmem] * 3,
+        in_specs=[pl.BlockSpec(memory_space=pltpu.SMEM)] + [vmem] * 4,
         out_specs=vmem,
         out_shape=jax.ShapeDtypeStruct((copies, 8, LANES), F32),
         compiler_params=pltpu.CompilerParams(vmem_limit_bytes=2 * MIB),
         name="border_sums",
-    )(edge, sums, tail, next_head)
+    )(edge, sums, tail, next_head, prev_tail)
 
 
 def second_kernel(
@@ -879,7 +918,7 @@
     d0, nd0, head, tail, sums, first = middle(edge, spec, coef, nx)
     next_head = lax.ppermute(head, ("gz", "gy"), up)
     prev_tail = lax.ppermute(tail, ("gz", "gy"), down)
-    sums = everywhere(border_sums(edge, sums, tail, next_head, gy))
+    sums = everywhere(border_sums(edge, sums, tail, next_head, prev_tail, gy))
     first = first[:1] + from_cores(first[1:])
     d1, second, eta, sums = second_descent(
         edge, sums, d0, nd0, tail, prev_tail, next_head, coef, gz, nx

time: 304 us -> 364 us (1.20)
  Pallas kernels: 49.3 us -> 116 us
  local copies, waits for them, and re-layouts: 28.3 us -> 17.9 us
  waiting for transfers between devices: 176 us -> 182 us
    pallas_call x1, Pallas kernels: 0.7 us -> 65.3 us  [merge(): pl.pallas_call(functools.partial(merge_kernel, gz), in_specs=[pl.BlockSpe...]
    unnamed x30 -> x20, local copies, waits for them, and re-layouts: 9.23 us -> 3.38 us
  transfers between devices with their start and end apart: 10 -> 10, of which waited for: 6 -> 7; matrix products, arithmetic and copies ran while one was open for 8% -> 5% of each run, Pallas kernels for 3% -> 2%
where the time goes in v6:
time: 364 us; the launch traced here: 363 us
  waiting for transfers between devices  182 us (50%)
  Pallas kernels  116 us (32%)
  blocking collectives  21.5 us (6%)
  starting transfers between devices  19.8 us (5%)
  local copies, waits for them, and re-layouts  17.9 us (5%)
  other arithmetic  5.07 us (1%)
    all_to_all x2, waiting for transfers between devices, to_chips(): return lax.all_to_all(parts, 'gy', 0, 0, tiled=True)  170 us
    pallas_call x1, Pallas kernels, merge(): pl.pallas_call(functools.partial(merge_kernel, gz), in_specs=[pl.BlockSpe...  65.3 us
    all_to_all x2, blocking collectives, to_chips(): return lax.all_to_all(parts, 'gy', 0, 0, tiled=True)  21.5 us
    pallas_call x1, Pallas kernels, middle(): pl.pallas_call(functools.partial(middle_kernel, gz), in_specs=[pl.BlockSp...  19 us
    all_to_all x2, starting transfers between devices, to_chips(): return lax.all_to_all(parts, 'gy', 0, 0, tiled=True)  14.7 us
    pallas_call x1, Pallas kernels, y_forward(): pl.pallas_call(y_forward_kernel, in_specs=[hbm] * 4, out_specs=hbm, out_s...  11.1 us
    pallas_call x1, Pallas kernels, y_inverse(): pl.pallas_call(functools.partial(y_inverse_kernel, gz), in_specs=[pl.Bloc...  10.4 us
    ppermute x6, waiting for transfers between devices, to_core(): lax.ppermute(piece, 'gz', [(i, (i + r) % gz) for i in range(gz)])  8.48 us
  transfers between devices with their start and end apart: 10, of which 7 were waited for; matrix products, arithmetic and copies ran while one was open for 5% of the time, Pallas kernels for 2%

profile of v6, /device:TPU:14, one launch (start us, length us, event | category | flops | bytes accessed | tf_op | source)
XLA Modules:
  0.0 363.2 jit_solution(2778005049268142508)
XLA Ops:
  0.6 0.6 pad_add_fusion.edge_ref
  1.2 10.4 %y_inverse.1 = (f32[16,2,2,64,256]{4,3,2,1,0:T(8,128)}, f32[16,2,64,256]{3,2,1,0:T(8,128)}) custom-call(s32[3]{0:T(128)} %pad_add_fusion.edge_ref, bf16[4,2048,128]{2,1,0:T(8,128)(2,1)} %bitcast.20, bf16[1024,512]{1,0:T(8,128)(2,1)} %constant.55.clone.table_hbm, f32[2,7,256,128]{3,2,1,0:T(8,128)} %constant.56.clone.tw_hbm), custom_call_target="tpu_custom_call" | custom-call | tf_op jit(solution)/shard_map/y_inverse/pallas_call | solution.py:270
  11.7 4.4 %collective-permute-done.refs_0_ = f32[16,2,64,256]{3,2,1,0:T(8,128)S(1)} collective-permute-done((f32[16,2,64,256]{3,2,1,0:T(8,128)}, f32[16,2,64,256]{3,2,1,0:T(8,128)S(1)}, u32[]{:S(2)}, u32[]{:S(2)}) %collective-permute-start) | collective-permute-done | bytes 2097184 | tf_op jit(solution)/shard_map/ppermute | solution.py:872
  16.1 1.3 copy-done.7
  17.4 65.3 %merge.1 = f32[16,2,2,64,256]{4,3,2,1,0:T(8,128)} custom-call(s32[3]{0:T(128)} %pad_add_fusion.edge_ref, f32[16,2,64,256]{3,2,1,0:T(8,128)} %copy-done.7, f32[16,2,2,64,256]{4,3,2,1,0:T(8,128)} %get-tuple-element.19.refs_1_), custom_call_target="tpu_custom_call", output_to_operand_aliasing={{}: (2, {})} | custom-call | tf_op jit(solution)/shard_map/merge/pallas_call | solution.py:307
  82.8 7.3 %all-to-all-start = ((f32[16,2,2,64,256]{4,3,2,1,0:T(8,128)}), f32[16,2,2,64,256]{4,3,2,1,0:T(8,128)}, u32[]{:S(2)}, u32[]{:S(2)}) async-start(f32[16,2,2,64,256]{4,3,2,1,0:T(8,128)} %merge.1), calls=%async_computation | async-start | bytes 8388608 | tf_op jit(solution)/shard_map/all_to_all | solution.py:880
  90.2 95.4 %all-to-all-done.spec_hbm = f32[16,2,2,64,256]{4,3,2,1,0:T(8,128)} async-done(((f32[16,2,2,64,256]{4,3,2,1,0:T(8,128)}), f32[16,2,2,64,256]{4,3,2,1,0:T(8,128)}, u32[]{:S(2)}, u32[]{:S(2)}) %all-to-all-start) | async-done | bytes 4194336 | tf_op jit(solution)/shard_map/all_to_all | solution.py:880
  185.7 19.0 %middle.1 = (f32[32,64,256]{2,1,0:T(8,128)S(1)}, f32[32,64,256]{2,1,0:T(8,128)S(1)}, f32[3,32,256]{2,1,0:T(8,128)S(1)}, f32[32,256]{1,0:T(8,128)S(1)}, f32[3,8,1...) custom-call(s32[3]{0:T(128)S(1)} %copy-done.5, ...), custom_call_target="tpu_custom_call" | custom-call | tf_op jit(solution)/shard_map/middle/pallas_call | solution.py:658
  204.6 1.9 collective-permute-start.2
  206.6 2.4 collective-permute-start.1
  209.0 2.8 collective-permute-done.1.prev_ref
  211.8 0.6 border_sums.1
  212.4 11.4 %all_to_all.20.refs_0_ = f32[16,8,128]{2,1,0:T(8,128)S(1)} all-to-all(f32[16,8,128]{2,1,0:T(8,128)S(1)} %border_sums.1), channel_id=1, replica_groups=mesh['gz'=2,'gy'=16] {'gy'}, dimensions={0} | all-to-all | bytes 131072 | tf_op jit(solution)/shard_map/all_to_all | solution.py:880
  223.8 0.5 collective-permute-start.5
  224.3 0.7 collective-permute-done.3.refs_1_
  225.1 7.9 %second_descent.1 = (f32[32,64,256]{2,1,0:T(8,128)S(1)}, f32[8,128]{1,0:T(8,128)S(1)}, f32[16,8,128]{2,1,0:T(8,128)S(1)}, f32[16,2,64,256]{3,2,1,0:T(8,128)S(1)}, f32[16,2,64,256]{3,2,1,0:T(8,128)S(1)}) custom-call(s32[3]{0:T(128)S(1)} %copy-done.5, f32[32,64,256]{2,1,0:T(8,128)S(1)} %get-tuple-element.20.d0_ref, ...), custom_call_target="tpu_custom_call" | custom-call | tf_op jit(solution)/shard_map/second_descent/pallas_call | solution.py:808
  233.0 0.2 collective-permute-start.6
  233.2 10.1 %all_to_all.21.refs_0_ = f32[16,8,128]{2,1,0:T(8,128)S(1)} all-to-all(f32[16,8,128]{2,1,0:T(8,128)S(1)} %get-tuple-element.26), channel_id=1, replica_groups=mesh['gz'=2,'gy'=16] {'gy'}, dimensions={0} | all-to-all | bytes 131072 | tf_op jit(solution)/shard_map/all_to_all | solution.py:880
  243.3 1.3 collective-permute-done.4.refs_1_
  244.6 1.9 combine_spectra.1
  246.5 2.0 copy-done
  248.5 7.4 %all-to-all-start.3 = ((f32[16,2,2,64,256]{4,3,2,1,0:T(8,128)}), f32[16,2,2,64,256]{4,3,2,1,0:T(8,128)}, u32[]{:S(2)}, u32[]{:S(2)}) async-start(f32[16,2,2,64,256]{4,3,2,1,0:T(8,128)} %copy-done), calls=%async_computation.3 | async-start | bytes 8388608 | tf_op jit(solution)/shard_map/all_to_all | solution.py:880
  255.9 0.5 fusion.2
  256.4 4.5 %add_negate_fusion = f32[32,64,256]{2,1,0:T(8,128)} fusion(f32[32,64,256]{2,1,0:T(8,128)} %copy-done.2, f32[32,64,256]{2,1,0:T(8,128)S(1)} %get-tuple-element.20.d0_ref, f32[]{:T(128)} %bitcast.8, f32[]{:T(128)} %bitcast.7), kind=kLoop, calls=%fused_computation | loop fusion | flops 2097152 | bytes 6291464 | tf_op jit(solution)/shard_map/neg | solution.py:931
  260.9 4.9 %copy.19 = f32[2,16,64,256]{2,1,3,0:T(8,128)} copy(f32[2,16,64,256]{3,2,1,0:T(8,128)} %bitcast.22) | data formatting | bytes 4194304 | tf_op jit(solution)/shard_map/reshape | solution.py:932
  265.7 3.8 %constant_dynamic-slice_fusion = (f32[1,64,4096]{1,2,0:T(8,128)}, f32[1,64,4096]{1,2,0:T(8,128)S(1)}) fusion(f32[2,64,4096]{1,2,0:T(8,128)} %bitcast.19, s32[]{:T(128)S(6)} %select_n.29, s32[]{:T(128)S(6)} %select_n.27), kind=kLoop, calls=%fused_computation.6 | loop fusion | bytes 4194312 | tf_op jit(solution)/shard_map/jit(dynamic_index_in_dim)/dynamic_slice | solution.py:934
  269.5 3.1 copy.21
  272.7 0.6 copy.20
  273.6 2.1 collective-permute-done.7
  275.7 1.3 bitcast_dynamic-update-slice_fusion
  277.0 74.9 %all-to-all-done.3.spec_hbm = f32[16,2,2,64,256]{4,3,2,1,0:T(8,128)} async-done(((f32[16,2,2,64,256]{4,3,2,1,0:T(8,128)}), f32[16,2,2,64,256]{4,3,2,1,0:T(8,128)}, u32[]{:S(2)}, u32[]{:S(2)}) %all-to-all-start.3) | async-done | bytes 4194336 | tf_op jit(solution)/shard_map/all_to_all | solution.py:880
  351.9 11.1 %y_forward.1 = f32[4,8,256,128]{3,2,1,0:T(8,128)} custom-call(f32[16,2,2,64,256]{4,3,2,1,0:T(8,128)} %all-to-all-done.3.spec_hbm, bf16[4,2048,128]{2,1,0:T(8,128)(2,1)} %bitcast.21, bf16[1024,512]{1,0:T(8,128)(2,1)} %constant.60.clone.table_hbm, f32[2,7,256,128]{3,2,1,0:T(8,128)} %constant.56.clone.tw_hbm), custom_call_target="tpu_custom_call" | custom-call | tf_op jit(solution)/shard_map/y_forward/pallas_call | solution.py:416
  (35 shorter events, 0.5 us)
Async XLA Ops:
  11.7 4.4 %collective-permute-start = (f32[16,2,64,256]{3,2,1,0:T(8,128)}, f32[16,2,64,256]{3,2,1,0:T(8,128)S(1)}, u32[]{:S(2)}, u32[]{:S(2)}) collective-permute-start(f32[16,2,64,256]{3,2,1,0:T(8,128)} %get-tuple-element.18), channel_id=1, source_target_pairs={{0,16},{16,0},{1,17},{17,1},{2,18},{18,2},{3,19},{19,3},{4,20},{20... | collective-permute-start | bytes 6291464 | tf_op jit(solution)/shard_map/ppermute | solution.py:872
  16.1 1.3 copy-start.7
  82.7 7.4 %copy-start.8 = (f32[2,4096]{1,0:T(2,128)S(1)}, f32[2,4096]{1,0:T(2,128)}, u32[]{:S(2)}) copy-start(f32[2,4096]{1,0:T(2,128)} %param.14) | copy-start | bytes 98308
  82.7 7.4 %copy-start.9 = (s32[4096]{0:T(1024)S(1)}, s32[4096]{0:T(1024)}, u32[]{:S(2)}) copy-start(s32[4096]{0:T(1024)} %param.13) | copy-start | bytes 49156
  82.8 102.9 %copy-start.1 = (bf16[256,1024]{1,0:T(8,128)(2,1)S(1)}, bf16[256,1024]{1,0:T(8,128)(2,1)}, u32[]{:S(2)}) copy-start(bf16[256,1024]{1,0:T(8,128)(2,1)} %constant.59.clone.forward_ref.table_ref) | copy-start | bytes 1572868
  82.8 102.9 %copy-start.3 = (f32[2,16,8,256]{3,2,1,0:T(8,128)S(1)}, f32[2,16,8,256]{3,2,1,0:T(8,128)}, u32[]{:S(2)}) copy-start(f32[2,16,8,256]{3,2,1,0:T(8,128)} %constant.57.clone.tw_ref) | copy-start | bytes 786436
  82.8 102.9 %copy-start.4 = (bf16[512,512]{1,0:T(8,128)(2,1)S(1)}, bf16[512,512]{1,0:T(8,128)(2,1)}, u32[]{:S(2)}) copy-start(bf16[512,512]{1,0:T(8,128)(2,1)} %constant.58.clone.inverse_ref) | copy-start | bytes 1572868
  82.8 102.9 %copy-start.5 = (s32[3]{0:T(128)S(1)}, s32[3]{0:T(128)}, u32[]{:S(2)}) copy-start(s32[3]{0:T(128)} %pad_add_fusion.edge_ref) | copy-start | bytes 40
  82.8 102.8 %all-to-all-start = ((f32[16,2,2,64,256]{4,3,2,1,0:T(8,128)}), f32[16,2,2,64,256]{4,3,2,1,0:T(8,128)}, u32[]{:S(2)}, u32[]{:S(2)}) async-start(f32[16,2,2,64,256]{4,3,2,1,0:T(8,128)} %merge.1), calls=%async_computation | async-start | bytes 8388608 | tf_op jit(solution)/shard_map/all_to_all | solution.py:880
  204.6 7.2 %collective-permute-start.2 = (f32[3,32,256]{2,1,0:T(8,128)S(1)}, f32[3,32,256]{2,1,0:T(8,128)S(1)}, u32[]{:S(2)}, u32[]{:S(2)}) collective-permute-start(f32[3,32,256]{2,1,0:T(8,128)S(1)} %get-tuple-element.23), channel_id=1, source_target_pairs={{16,0},{1,16},{17,1},{2,17},{18,2},{3,18},{19,3},{4,19},{20,4},{5,... | collective-permute-start | bytes 294920 | tf_op jit(solution)/shard_map/ppermute | solution.py:919
  206.6 5.2 %collective-permute-start.1 = (f32[32,256]{1,0:T(8,128)S(1)}, f32[32,256]{1,0:T(8,128)S(1)}, u32[]{:S(2)}, u32[]{:S(2)}) collective-permute-start(f32[32,256]{1,0:T(8,128)S(1)} %get-tuple-element.22.tail_ref), channel_id=1, source_target_pairs={{0,16},{16,1},{1,17},{17,2},{2,18},{18,3},{3,19},{19,4},{4,20},{20... | collective-permute-start | bytes 98312 | tf_op jit(solution)/shard_map/ppermute | solution.py:920
  223.8 1.3 collective-permute-start.3
  223.8 20.7 %collective-permute-start.5 = (f32[16,2,64,256]{3,2,1,0:T(8,128)S(1)}, f32[16,2,64,256]{3,2,1,0:T(8,128)S(1)}, u32[]{:S(2)}, u32[]{:S(2)}) collective-permute-start(f32[16,2,64,256]{3,2,1,0:T(8,128)S(1)} %get-tuple-element.28), channel_id=1, source_target_pairs={{0,16},{16,0},{1,17},{17,1},{2,18},{18,2},{3,19},{19,3},{4,20},{20... | collective-permute-start | bytes 6291464 | tf_op jit(solution)/shard_map/ppermute | solution.py:872
  233.0 13.5 %copy-start.2 = (f32[32,64,256]{2,1,0:T(8,128)}, f32[32,64,256]{2,1,0:T(8,128)S(1)}, u32[]{:S(2)}) copy-start(f32[32,64,256]{2,1,0:T(8,128)S(1)} %get-tuple-element.32) | copy-start | bytes 6291460
  233.0 11.6 %collective-permute-start.6 = (f32[16,2,64,256]{3,2,1,0:T(8,128)S(1)}, f32[16,2,64,256]{3,2,1,0:T(8,128)S(1)}, u32[]{:S(2)}, u32[]{:S(2)}) collective-permute-start(f32[16,2,64,256]{3,2,1,0:T(8,128)S(1)} %get-tuple-element.30), channel_id=1, source_target_pairs={{0,16},{16,0},{1,17},{17,1},{2,18},{18,2},{3,19},{19,3},{4,20},{20... | collective-permute-start | bytes 6291464 | tf_op jit(solution)/shard_map/ppermute | solution.py:872
  243.3 1.3 collective-permute-start.4
  246.4 2.0 copy-start
  248.5 103.5 %all-to-all-start.3 = ((f32[16,2,2,64,256]{4,3,2,1,0:T(8,128)}), f32[16,2,2,64,256]{4,3,2,1,0:T(8,128)}, u32[]{:S(2)}, u32[]{:S(2)}) async-start(f32[16,2,2,64,256]{4,3,2,1,0:T(8,128)} %copy-done), calls=%async_computation.3 | async-start | bytes 8388608 | tf_op jit(solution)/shard_map/all_to_all | solution.py:880
  272.7 3.0 collective-permute-start.7
  277.0 86.1 %copy-start.6 = (f32[2,64,4096]{2,1,0:T(8,128)}, f32[2,64,4096]{2,1,0:T(8,128)S(1)}, u32[]{:S(2)}) copy-start(f32[2,64,4096]{2,1,0:T(8,128)S(1)} %bitcast_dynamic-update-slice_fusion) | copy-start | bytes 6291460

commit v7 on v6

--- a/solution.py
+++ b/solution.py
@@ -18,7 +18,7 @@
 BF16 = jnp.bfloat16
 MIB = 1024 * 1024
 Y_GRANT = 56 * MIB
-X_GRANT = 24 * MIB
+X_GRANT = 20 * MIB
 
 
 def dft_parts(length, scale):
@@ -175,22 +175,23 @@
     return out
 
 
-def core_on(edge_ref, gz, r):
-    return lax.rem(edge_ref[2] + gz + r, gz)
-
-
-def y_inverse_kernel(gz, edge_ref, data_hbm, table_hbm, tw_hbm, out_hbm, *refs):
-    other_refs, refs = refs[: gz - 1], refs[gz - 1 :]
-    data_ref, table_ref, tw_ref, own_s, re_s, im_s, mix_s, sems, out_sems = refs
+def y_inverse_kernel(
+    data_hbm, table_hbm, tw_hbm, out_hbm,
+    data_ref, table_ref, tw_ref, out_ref, re_s, im_s, mix_s, sems, out_sems,
+):
     blocks, ny, _ = data_ref.shape
     n = ny // YR
-    rows = own_s.shape[2]
+    gz, _, _, rows, _ = out_ref.shape
     lane = lax.broadcasted_iota(jnp.int32, (n, LANES), 1)
     pairs = blocks // 2
 
     def fetch(chunk):
         part = pl.ds(2 * chunk, 2)
         return pltpu.make_async_copy(data_hbm.at[part], data_ref.at[part], sems.at[2 + chunk])
+
+    def give(chunk, core):
+        at = (core, slice(None), slice(None), slice(None), pl.ds(chunk * LANES, LANES))
+        return pltpu.make_async_copy(out_ref.at[at], out_hbm.at[at], out_sems.at[chunk * gz + core])
 
     fetch_table = pltpu.make_async_copy(table_hbm, table_ref, sems.at[0])
     fetch_tw = pltpu.make_async_copy(tw_hbm, tw_ref, sems.at[1])
@@ -230,9 +231,7 @@
             fetch_tw.wait()
 
         tiles = rows // 8
-        for r in range(gz):
-            core = core_on(edge_ref, gz, r)
-            target = other_refs[r - 1] if r else own_s
+        for core in range(gz):
 
             def combine(i, carry):
                 y2 = ((i // tiles) * gz + core) * rows + lax.rem(i, tiles) * 8
@@ -249,73 +248,42 @@
                 at = pl.ds(pl.multiple_of(lax.rem(i, tiles) * 8, 8), 8)
                 for k, (re, im) in enumerate(short_fft(planes, 1)):
                     to = k * (n // (gz * rows)) + i // tiles
-                    target[to, 0, at, lanes] = re
-                    target[to, 1, at, lanes] = im
+                    out_ref[core, to, 0, at, lanes] = re
+                    out_ref[core, to, 1, at, lanes] = im
                 return carry
 
             lax.fori_loop(0, n // gz // 8, combine, 0, unroll=2)
-
-    give = pltpu.make_async_copy(own_s, out_hbm.at[:, edge_ref[2]], out_sems.at[0])
-    give.start()
-    give.wait()
-
-
-def y_inverse(edge, data, rows, gz, gy):
+            give(chunk, core).start()
+
+    for chunk in range(pairs):
+        for core in range(gz):
+            give(chunk, core).wait()
+
+
+def y_inverse(data, rows, gz, gy):
     blocks, ny, width = data.shape
     n = ny // YR
     ka = blocks * HALF
-    vmem = pl.BlockSpec(memory_space=pltpu.VMEM)
     hbm = pl.BlockSpec(memory_space=pltpu.HBM)
-    piece = jax.ShapeDtypeStruct((gy, 2, rows, ka), F32)
-    whole, *others = pl.pallas_call(
-        functools.partial(y_inverse_kernel, gz),
-        in_specs=[pl.BlockSpec(memory_space=pltpu.SMEM)] + [hbm] * 3,
-        out_specs=[hbm] + [vmem] * (gz - 1),
-        out_shape=[jax.ShapeDtypeStruct((gy, gz, 2, rows, ka), F32)] + [piece] * (gz - 1),
+    return pl.pallas_call(
+        y_inverse_kernel,
+        in_specs=[hbm] * 3,
+        out_specs=hbm,
+        out_shape=jax.ShapeDtypeStruct((gz, gy, 2, rows, ka), F32),
         scratch_shapes=[
             pltpu.VMEM((blocks, ny, width), BF16),
             pltpu.VMEM((4 * n, 2 * n), BF16),
             pltpu.VMEM((2, YR - 1, n, LANES), F32),
-            pltpu.VMEM((gy, 2, rows, ka), F32),
+            pltpu.VMEM((gz, gy, 2, rows, ka), F32),
             pltpu.VMEM((ny, LANES), F32),
             pltpu.VMEM((ny, LANES), F32),
             pltpu.VMEM((YR, 2 * n, LANES), F32),
             pltpu.SemaphoreType.DMA((2 + blocks // 2,)),
-            pltpu.SemaphoreType.DMA((1,)),
+            pltpu.SemaphoreType.DMA((blocks // 2 * gz,)),
         ],
         compiler_params=pltpu.CompilerParams(vmem_limit_bytes=Y_GRANT),
         name="y_inverse",
-    )(edge, data, y_matrix(ny, False, -1.0), y_twiddle(ny))
-    return whole, others
-
-
-def merge_kernel(gz, edge_ref, *refs):
-    pieces, (_, out_hbm, sems) = refs[: gz - 1], refs[gz - 1 :]
-    copies = [
-        pltpu.make_async_copy(piece, out_hbm.at[:, core_on(edge_ref, gz, -r - 1)], sems.at[r])
-        for r, piece in enumerate(pieces)
-    ]
-    for copy in copies:
-        copy.start()
-    for copy in copies:
-        copy.wait()
-
-
-def merge(edge, whole, pieces):
-    gz = whole.shape[1]
-    hbm = pl.BlockSpec(memory_space=pltpu.HBM)
-    return pl.pallas_call(
-        functools.partial(merge_kernel, gz),
-        in_specs=[pl.BlockSpec(memory_space=pltpu.SMEM)]
-        + [pl.BlockSpec(memory_space=pl.ANY)] * (gz - 1)
-        + [hbm],
-        out_specs=hbm,
-        out_shape=jax.ShapeDtypeStruct(whole.shape, F32),
-        scratch_shapes=[pltpu.SemaphoreType.DMA((gz - 1,))],
-        input_output_aliases={gz: 0},
-        compiler_params=pltpu.CompilerParams(vmem_limit_bytes=Y_GRANT),
-        name="merge",
-    )(edge, *pieces, whole)
+    )(data, y_matrix(ny, False, -1.0), y_twiddle(ny))
 
 
 def y_forward_kernel(
@@ -324,7 +292,7 @@
 ):
     blocks, ny, _ = data_ref.shape
     n = ny // YR
-    gy, gz, _, rows, _ = spec_ref.shape
+    gz, gy, _, rows, _ = spec_ref.shape
     pairs = blocks // 2
     half = n // 2
 
@@ -356,8 +324,8 @@
         def unpack(i, carry):
             for core in range(gz):
                 part = pl.ds(pl.multiple_of((i * gz + core) * rows, rows), rows)
-                re_s[part, :] = spec_ref[i, core, 0, :, lanes]
-                im_s[part, :] = spec_ref[i, core, 1, :, lanes]
+                re_s[part, :] = spec_ref[core, i, 0, :, lanes]
+                im_s[part, :] = spec_ref[core, i, 1, :, lanes]
             return carry
 
         lax.fori_loop(0, gy, unpack, 0)
@@ -547,11 +515,10 @@
 
 
 def middle_kernel(
-    gz, edge_ref, spec_hbm, coef_ref, tw_ref, inverse_ref, forward_ref,
-    d0_ref, nd0_ref, head_ref, tail_ref, sums_ref, *refs,
+    edge_ref, spec_hbm, coef_ref, tw_ref, inverse_ref, forward_ref,
+    d0_ref, nd0_ref, head_ref, tail_ref, sums_ref, spec_ref, re_s, im_s, sems,
 ):
-    give_hbm, (spec_s, re_s, im_s, sems, out_sems) = refs[:gz], refs[gz:]
-    kb, _, _, rows, ka = spec_s.shape
+    gz, kb, _, rows, ka = spec_ref.shape
     planes = gz * kb
     lane_parts = [slice(start, start + LANES) for start in range(0, ka, LANES)]
     cuts = sems.shape[0]
@@ -560,7 +527,7 @@
     def fetch(i):
         part = pl.ds(i * cut, cut)
         return pltpu.make_async_copy(
-            spec_hbm.at[:, :, :, part], spec_s.at[:, :, :, part], sems.at[i]
+            spec_hbm.at[:, :, :, part], spec_ref.at[:, :, :, part], sems.at[i]
         )
 
     for i in range(cuts):
@@ -572,7 +539,7 @@
             part = pl.ds(pl.multiple_of(i * cut + j * 8, 8), 8)
             for lanes in lane_parts:
                 spectra = [
-                    [(spec_s[k, z, 0, part, lanes], spec_s[k, z, 1, part, lanes]) for k in range(kb)]
+                    [(spec_ref[z, k, 0, part, lanes], spec_ref[z, k, 1, part, lanes]) for k in range(kb)]
                     for z in range(gz)
                 ]
                 inverse_columns(gz, kb, spectra, coef_ref, tw_ref, lanes, part, re_s, im_s)
@@ -602,19 +569,12 @@
                 for k in range(kb):
                     for p in range(2):
                         value = spectra[z][k][p]
-                        spec_s[k, z, p, part, lanes] = value
+                        spec_ref[z, k, p, part, lanes] = value
                         total = total + value * value
             inverse_columns(gz, kb, spectra, coef_ref, tw_ref, lanes, part, re_s, im_s)
         return total
 
     projected = lax.fori_loop(0, rows // 8, second_columns, jnp.zeros((8, LANES), F32))
-    gives = [
-        pltpu.make_async_copy(spec_s.at[:, core_on(edge_ref, gz, r)], give_hbm[r], out_sems.at[r])
-        for r in range(gz)
-    ]
-    for give in gives:
-        give.start()
-
     def back(i, carry):
         part = pl.ds(i * step, step)
         field = inverse_product(re_s[part].reshape(shape2), im_s[part].reshape(shape2), inverse_ref)
@@ -645,34 +605,30 @@
     sums_ref[0] = square
     sums_ref[1] = projected
     sums_ref[2] = slope
-    for give in gives:
-        give.wait()
 
 
 def middle(edge, spec, coef, nx):
-    kb, gz, _, rows, ka = spec.shape
+    gz, kb, _, rows, ka = spec.shape
     planes = gz * kb
     vmem = pl.BlockSpec(memory_space=pltpu.VMEM)
-    hbm = pl.BlockSpec(memory_space=pltpu.HBM)
     field = jax.ShapeDtypeStruct((planes, rows, ka), F32)
-    d0, nd0, head, tail, sums, *pieces = pl.pallas_call(
-        functools.partial(middle_kernel, gz),
-        in_specs=[pl.BlockSpec(memory_space=pltpu.SMEM), hbm] + [vmem] * 4,
-        out_specs=[vmem] * 5 + [hbm] * gz,
+    return pl.pallas_call(
+        middle_kernel,
+        in_specs=[pl.BlockSpec(memory_space=pltpu.SMEM), pl.BlockSpec(memory_space=pltpu.HBM)]
+        + [vmem] * 4,
+        out_specs=[vmem] * 6,
         out_shape=[
             field,
             field,
             jax.ShapeDtypeStruct((3, planes, ka), F32),
             jax.ShapeDtypeStruct((planes, ka), F32),
             jax.ShapeDtypeStruct((3, 8, LANES), F32),
-        ]
-        + [jax.ShapeDtypeStruct((kb, 2, rows, ka), F32)] * gz,
+            jax.ShapeDtypeStruct(spec.shape, F32),
+        ],
         scratch_shapes=[
-            pltpu.VMEM((kb, gz, 2, rows, ka), F32),
             pltpu.VMEM((planes, rows, ka), F32),
             pltpu.VMEM((planes, rows, ka), F32),
             pltpu.SemaphoreType.DMA((2 if rows % 16 == 0 else 1,)),
-            pltpu.SemaphoreType.DMA((gz,)),
         ],
         compiler_params=pltpu.CompilerParams(vmem_limit_bytes=X_GRANT),
         name="middle",
@@ -680,7 +636,6 @@
         edge, spec, coef, x_twiddle(nx, ka), jnp.asarray(x_inverse_matrix(nx, ka)),
         x_forward_matrix(nx, ka),
     )
-    return d0, nd0, head, tail, sums, pieces
 
 
 def border_kernel(edge_ref, sums_ref, tail_ref, next_ref, prev_ref, out_ref):
@@ -705,8 +660,8 @@
     gz, edge_ref, d0_ref, nd0_ref, tail_ref, prev_ref, next_ref,
     coef_ref, tw_ref, table_ref, *refs,
 ):
-    sums_refs, (d1_ref, eta_ref, out_ref, *refs) = refs[:gz], refs[gz:]
-    piece_refs, (sum_s, re_s, im_s, row_s) = refs[:gz], refs[gz:]
+    sums_refs, refs = refs[:gz], refs[gz:]
+    d1_ref, eta_ref, out_ref, spec_ref, re_s, im_s, row_s = refs
     planes, rows, ka = d0_ref.shape
     kb = planes // gz
     eta_here = step_of(sums_refs)
@@ -780,43 +735,37 @@
 
     lax.fori_loop(0, planes // step, multiply, 0)
 
-    def transform(core):
-        def columns(j, total):
-            part = pl.ds(pl.multiple_of(j * 8, 8), 8)
-            for start in range(0, ka, LANES):
-                lanes = slice(start, start + LANES)
-                spectra = forward_columns(gz, kb, coef_ref, tw_ref, lanes, part, re_s, im_s)
-                for z in range(gz):
-                    for k in range(kb):
-                        for p in range(2):
-                            value = spectra[z][k][p]
-                            piece_refs[(z - core) % gz][k, p, part, lanes] = value
-                            total = total + value * value
-            return total
-
-        sum_s[...] = lax.fori_loop(0, rows // 8, columns, jnp.zeros((8, LANES), F32))
-
-    for core in range(gz):
-        pl.when(edge_ref[2] == core)(functools.partial(transform, core))
-    put_sums(out_ref, [square, sum_s[...], slope])
+    def columns(j, total):
+        part = pl.ds(pl.multiple_of(j * 8, 8), 8)
+        for start in range(0, ka, LANES):
+            lanes = slice(start, start + LANES)
+            spectra = forward_columns(gz, kb, coef_ref, tw_ref, lanes, part, re_s, im_s)
+            for z in range(gz):
+                for k in range(kb):
+                    for p in range(2):
+                        value = spectra[z][k][p]
+                        spec_ref[z, k, p, part, lanes] = value
+                        total = total + value * value
+        return total
+
+    projected = lax.fori_loop(0, rows // 8, columns, jnp.zeros((8, LANES), F32))
+    put_sums(out_ref, [square, projected, slope])
 
 
 def second_descent(edge, sums, d0, nd0, tail, prev_tail, next_head, coef, gz, nx):
     planes, rows, ka = d0.shape
     vmem = pl.BlockSpec(memory_space=pltpu.VMEM)
-    piece = jax.ShapeDtypeStruct((planes // gz, 2, rows, ka), F32)
-    d1, eta, out, *pieces = pl.pallas_call(
+    return pl.pallas_call(
         functools.partial(second_kernel, gz),
         in_specs=[pl.BlockSpec(memory_space=pltpu.SMEM)] + [vmem] * (8 + gz),
-        out_specs=[vmem] * (3 + gz),
+        out_specs=[vmem] * 4,
         out_shape=[
             jax.ShapeDtypeStruct((planes, rows, ka), F32),
             jax.ShapeDtypeStruct((8, LANES), F32),
             jax.ShapeDtypeStruct(sums[0].shape, F32),
-        ]
-        + [piece] * gz,
+            jax.ShapeDtypeStruct((gz, planes // gz, 2, rows, ka), F32),
+        ],
         scratch_shapes=[
-            pltpu.VMEM((8, LANES), F32),
             pltpu.VMEM((planes, rows, ka), F32),
             pltpu.VMEM((planes, rows, ka), F32),
             pltpu.VMEM((planes, ka), F32),
@@ -827,44 +776,40 @@
         edge, d0, nd0, tail, prev_tail, next_head, coef,
         x_twiddle(nx, ka), x_forward_matrix(nx, ka), *sums,
     )
-    return d1, pieces, eta, out
-
-
-def combine_kernel(gz, edge_ref, eta_ref, *refs):
-    sums_refs, refs = refs[:gz], refs[gz:]
-    first_refs, second_refs, (out_ref, steps_ref) = refs[:gz], refs[gz : 2 * gz], refs[2 * gz :]
+
+
+def combine_kernel(gz, eta_ref, *refs):
+    sums_refs, (first_ref, second_ref, out_ref, steps_ref) = refs[:gz], refs[gz:]
     eta0 = jnp.max(eta_ref[...])
     eta1 = jnp.max(step_of(sums_refs))
     steps_ref[0] = eta_ref[...]
     steps_ref[1] = jnp.full((8, LANES), eta1, F32)
     count = out_ref.shape[0]
     start = pl.program_id(0) * count
-    for r in range(gz):
-        core = core_on(edge_ref, gz, -r)
-        for i in range(count):
-            out_ref[i, core] = -(eta0 * first_refs[r][start + i] + eta1 * second_refs[r][start + i])
-
-
-def combine_spectra(edge, eta, sums, first, second):
+    for i in range(count):
+        out_ref[i] = -(eta0 * first_ref[start + i] + eta1 * second_ref[start + i])
+
+
+def combine_spectra(eta, sums, first, second):
     gz = len(sums)
-    kb, *rest = first[0].shape
-    count = 4 if kb % 4 == 0 else 1
+    planes, *rest = first.shape
+    count = 4 if planes % 4 == 0 else 1
     vmem = pl.BlockSpec(memory_space=pltpu.VMEM)
     return pl.pallas_call(
         functools.partial(combine_kernel, gz),
-        grid=(kb // count,),
-        in_specs=[pl.BlockSpec(memory_space=pltpu.SMEM)] + [vmem] * (1 + 3 * gz),
+        grid=(planes // count,),
+        in_specs=[vmem] * (3 + gz),
         out_specs=[
-            pl.BlockSpec((count, gz, *rest), lambda i: (i, 0, 0, 0, 0)),
+            pl.BlockSpec((count, *rest), lambda i: (i, 0, 0, 0)),
             pl.BlockSpec((2, 8, LANES), lambda i: (0, 0, 0)),
         ],
         out_shape=[
-            jax.ShapeDtypeStruct((kb, gz, *rest), F32),
+            jax.ShapeDtypeStruct(first.shape, F32),
             jax.ShapeDtypeStruct((2, 8, LANES), F32),
         ],
         compiler_params=pltpu.CompilerParams(vmem_limit_bytes=6 * MIB),
         name="combine_spectra",
-    )(edge, eta, *sums, *first, *second)
+    )(eta, *sums, first, second)
 
 
 def to_core(piece, r):
@@ -872,12 +817,14 @@
     return lax.ppermute(piece, "gz", [(i, (i + r) % gz) for i in range(gz)]) if r else piece
 
 
-def from_cores(pieces):
-    return [to_core(piece, r + 1) for r, piece in enumerate(pieces)]
-
-
 def to_chips(parts):
     return lax.all_to_all(parts, "gy", 0, 0, tiled=True)
+
+
+def to_devices(parts):
+    gz, gy, *rest = parts.shape
+    parts = lax.all_to_all(parts.reshape(gz * gy, *rest), ("gz", "gy"), 0, 0, tiled=True)
+    return parts.reshape(gz, gy, *rest)
 
 
 def everywhere(sums):
@@ -897,7 +844,7 @@
 
     core = lax.axis_index("gz")
     flat = lax.axis_index("gy") * gz + core
-    edge = jnp.stack([flat == 0, flat == devices - 1, core]).astype(jnp.int32)
+    edge = jnp.stack([flat == 0, flat == devices - 1]).astype(jnp.int32)
     order = [(i % gz) * gy + i // gz for i in range(devices)]
     up = [(order[i + 1], order[i]) for i in range(devices - 1)]
     down = [(order[i], order[i + 1]) for i in range(devices - 1)]
@@ -913,20 +860,18 @@
     ).reshape(3, gy, 1, ka)
     coef = jnp.broadcast_to(coef, (3, gy, 8, ka))
 
-    whole, others = y_inverse(edge, data, rows, gz, gy)
-    spec = to_chips(merge(edge, whole, from_cores(others)))
+    spec = to_devices(y_inverse(data, rows, gz, gy))
     d0, nd0, head, tail, sums, first = middle(edge, spec, coef, nx)
     next_head = lax.ppermute(head, ("gz", "gy"), up)
     prev_tail = lax.ppermute(tail, ("gz", "gy"), down)
     sums = everywhere(border_sums(edge, sums, tail, next_head, prev_tail, gy))
-    first = first[:1] + from_cores(first[1:])
-    d1, second, eta, sums = second_descent(
+    d1, eta, sums, second = second_descent(
         edge, sums, d0, nd0, tail, prev_tail, next_head, coef, gz, nx
     )
     sums = everywhere(sums)
-    second = second[:1] + from_cores(second[1:])
-    spec, etas = combine_spectra(edge, eta, sums, first, second)
-    residual = y_forward(to_chips(spec), data)
+    flat_shape = (devices, 2, rows, ka)
+    spec, etas = combine_spectra(eta, sums, first.reshape(flat_shape), second.reshape(flat_shape))
+    residual = y_forward(to_devices(spec.reshape(gz, gy, 2, rows, ka)), data)
 
     volume = -(etas[0, 0, 0] * d0 + etas[1, 0, 0] * d1)
     volume = volume.reshape(gz, gy, rows, ka).transpose(0, 2, 3, 1).reshape(gz, rows, nx)

time: 364 us -> 286 us (0.79)
  the two profiles are of different devices: /device:TPU:14 before, /device:TPU:0 now
where the time goes in v7:
time: 286 us
  waiting for transfers between devices  177 us (62%)
  Pallas kernels  47.9 us (17%)
  blocking collectives  23.9 us (8%)
  local copies, waits for them, and re-layouts  16.6 us (6%)
  starting transfers between devices  15.4 us (5%)
  other arithmetic  4.58 us (2%)
    all_to_all x2, waiting for transfers between devices, to_devices(): lax.all_to_all(parts.reshape(gz * gy, *rest), ('gz', 'gy'), 0, 0, tiled=T...  171 us
    all_to_all x2, blocking collectives, to_chips(): return lax.all_to_all(parts, 'gy', 0, 0, tiled=True)  23.9 us
    pallas_call x1, Pallas kernels, middle(): pl.pallas_call(middle_kernel, in_specs=[pl.BlockSpec(memory_space=pltpu.S...  18.4 us
    pallas_call x1, Pallas kernels, y_forward(): pl.pallas_call(y_forward_kernel, in_specs=[hbm] * 4, out_specs=hbm, out_s...  11.1 us
    all_to_all x2, starting transfers between devices, to_devices(): lax.all_to_all(parts.reshape(gz * gy, *rest), ('gz', 'gy'), 0, 0, tiled=T...  11 us
    pallas_call x1, Pallas kernels, y_inverse(): pl.pallas_call(y_inverse_kernel, in_specs=[hbm] * 3, out_specs=hbm, out_s...  8.11 us
    pallas_call x1, Pallas kernels, second_descent(): pl.pallas_call(functools.partial(second_kernel, gz), in_specs=[pl.BlockSp...  7.87 us
    dynamic_slice x3, local copies, waits for them, and re-layouts, shards(): lax.dynamic_index_in_dim(volume, lax.rem(core + r, gz), 0, False)  7.54 us
  transfers between devices with their start and end apart: 7, of which 6 were waited for; matrix products, arithmetic and copies ran while one was open for 7% of the time, Pallas kernels for 0%

profile of v7, /device:TPU:0, one launch (start us, length us, event | category | flops | bytes accessed | tf_op | source)
XLA Modules:
  0.0 285.9 jit_solution(17136341171539994500)
XLA Ops:
  0.6 8.1 %y_inverse.1 = f32[2,16,2,64,256]{4,3,2,1,0:T(8,128)} custom-call(bf16[4,2048,128]{2,1,0:T(8,128)(2,1)} %bitcast.28, bf16[1024,512]{1,0:T(8,128)(2,1)} %constant.55.clone.table_hbm, f32[2,7,256,128]{3,2,1,0:T(8,128)} %constant.56.clone.tw_hbm), custom_call_target="tpu_custom_call" | custom-call | tf_op jit(solution)/shard_map/y_inverse/pallas_call | solution.py:268
  8.8 0.0 copy-start.1
  8.8 0.0 copy-start.3
  8.8 7.4 %all-to-all-start = ((f32[32,2,64,256]{3,2,1,0:T(8,128)}), f32[32,2,64,256]{3,2,1,0:T(8,128)}, u32[]{:S(2)}, u32[]{:S(2)}) async-start(f32[32,2,64,256]{3,2,1,0:T(8,128)} %bitcast.25), calls=%async_computation | async-start | bytes 8388608 | tf_op jit(solution)/shard_map/all_to_all | solution.py:826
  16.4 0.1 add_convert_fusion.edge_ref
  16.5 96.0 %all-to-all-done = f32[32,2,64,256]{3,2,1,0:T(8,128)} async-done(((f32[32,2,64,256]{3,2,1,0:T(8,128)}), f32[32,2,64,256]{3,2,1,0:T(8,128)}, u32[]{:S(2)}, u32[]{:S(2)}) %all-to-all-start) | async-done | bytes 4194336 | tf_op jit(solution)/shard_map/all_to_all | solution.py:826
  112.5 18.4 %middle.1 = (f32[32,64,256]{2,1,0:T(8,128)S(1)}, f32[32,64,256]{2,1,0:T(8,128)S(1)}, f32[3,32,256]{2,1,0:T(8,128)S(1)}, f32[32,256]{1,0:T(8,128)S(1)}, f32[3,8,1...) custom-call(s32[2]{0:T(128)S(1)} %add_convert_fusion.edge_ref, f32[2,16,2,64,256]{4,3,2,1,0:T(8,128)} %bitcast.4.spec_hbm, ...), custom_call_target="tpu_custom_call" | custom-call | tf_op jit(solution)/shard_map/middle/pallas_call | solution.py:615
  130.9 1.3 collective-permute-start.1
  132.2 3.0 %collective-permute-start = (f32[32,256]{1,0:T(8,128)S(1)}, f32[32,256]{1,0:T(8,128)S(1)}, u32[]{:S(2)}, u32[]{:S(2)}) collective-permute-start(f32[32,256]{1,0:T(8,128)S(1)} %get-tuple-element.16.tail_ref), channel_id=1, source_target_pairs={{0,16},{16,1},{1,17},{17,2},{2,18},{18,3},{3,19},{19,4},{4,20},{20... | collective-permute-start | bytes 98312 | tf_op jit(solution)/shard_map/ppermute | solution.py:866
  135.2 0.8 collective-permute-done.prev_ref
  136.1 0.6 border_sums.1
  136.7 13.8 %all_to_all.20.refs_0_ = f32[16,8,128]{2,1,0:T(8,128)S(1)} all-to-all(f32[16,8,128]{2,1,0:T(8,128)S(1)} %border_sums.1), channel_id=1, replica_groups=mesh['gz'=2,'gy'=16] {'gy'}, dimensions={0} | all-to-all | bytes 131072 | tf_op jit(solution)/shard_map/all_to_all | solution.py:821
  150.4 1.3 collective-permute-done.2.refs_1_
  151.7 7.9 %second_descent.1 = (f32[32,64,256]{2,1,0:T(8,128)S(1)}, f32[8,128]{1,0:T(8,128)S(1)}, f32[16,8,128]{2,1,0:T(8,128)S(1)}, f32[2,16,2,64,256]{4,3,2,1,0:T(8,128)S(1)}) custom-call(s32[2]{0:T(128)S(1)} %add_convert_fusion.edge_ref, f32[32,64,256]{2,1,0:T(8,128)S(1)} %get-tuple-element.14.d0_ref, f32[32,64,256]{2,1,0:T(8,128)S(1)} %get-tuple-element.15.nd0_ref, ...), custom_call_target="tpu_custom_call" | custom-call | tf_op jit(solution)/shard_map/second_descent/pallas_call | solution.py:758
  159.6 10.1 %all_to_all.21.refs_0_ = f32[16,8,128]{2,1,0:T(8,128)S(1)} all-to-all(f32[16,8,128]{2,1,0:T(8,128)S(1)} %get-tuple-element.20), channel_id=1, replica_groups=mesh['gz'=2,'gy'=16] {'gy'}, dimensions={0} | all-to-all | bytes 131072 | tf_op jit(solution)/shard_map/all_to_all | solution.py:821
  169.7 1.3 collective-permute-done.3.refs_1_
  170.9 1.9 combine_spectra.1
  172.8 2.0 copy-done
  174.8 3.6 %all-to-all-start.3 = ((f32[32,2,64,256]{3,2,1,0:T(8,128)}), f32[32,2,64,256]{3,2,1,0:T(8,128)}, u32[]{:S(2)}, u32[]{:S(2)}) async-start(f32[32,2,64,256]{3,2,1,0:T(8,128)} %copy-done), calls=%async_computation.3 | async-start | bytes 8388608 | tf_op jit(solution)/shard_map/all_to_all | solution.py:826
  178.4 0.5 fusion.2
  178.9 4.5 %add_negate_fusion = f32[32,64,256]{2,1,0:T(8,128)} fusion(f32[32,64,256]{2,1,0:T(8,128)} %copy-done.2, f32[32,64,256]{2,1,0:T(8,128)S(1)} %get-tuple-element.14.d0_ref, f32[]{:T(128)} %bitcast.11, f32[]{:T(128)} %bitcast.10), kind=kLoop, calls=%fused_computation | loop fusion | flops 2097152 | bytes 6291464 | tf_op jit(solution)/shard_map/neg | solution.py:876
  183.4 4.9 %copy.18 = f32[2,16,64,256]{2,1,3,0:T(8,128)} copy(f32[2,16,64,256]{3,2,1,0:T(8,128)} %bitcast.27) | data formatting | bytes 4194304 | tf_op jit(solution)/shard_map/reshape | solution.py:877
  188.3 3.8 %constant_dynamic-slice_fusion = (f32[1,64,4096]{1,2,0:T(8,128)}, f32[1,64,4096]{1,2,0:T(8,128)S(1)}) fusion(f32[2,64,4096]{1,2,0:T(8,128)} %bitcast.26, s32[]{:T(128)S(6)} %select_n.29, s32[]{:T(128)S(6)} %select_n.27), kind=kLoop, calls=%fused_computation.7 | loop fusion | bytes 4194312 | tf_op jit(solution)/shard_map/jit(dynamic_index_in_dim)/dynamic_slice | solution.py:879
  192.1 3.1 %copy.20 = f32[1,64,4096]{2,1,0:T(8,128)} copy(f32[1,64,4096]{1,2,0:T(8,128)} %get-tuple-element.28) | data formatting | bytes 2097152 | tf_op jit(solution)/shard_map/jit(dynamic_index_in_dim)/dynamic_slice | solution.py:879
  195.2 0.0 collective-permute-start.4
  195.3 0.6 copy.19
  195.8 0.2 broadcast_in_dim.21
  196.0 0.1 constant_dynamic-update-slice_fusion
  196.1 2.1 collective-permute-done.4
  198.2 1.3 bitcast_dynamic-update-slice_fusion
  199.5 75.1 %all-to-all-done.3 = f32[32,2,64,256]{3,2,1,0:T(8,128)} async-done(((f32[32,2,64,256]{3,2,1,0:T(8,128)}), f32[32,2,64,256]{3,2,1,0:T(8,128)}, u32[]{:S(2)}, u32[]{:S(2)}) %all-to-all-start.3) | async-done | bytes 4194336 | tf_op jit(solution)/shard_map/all_to_all | solution.py:826
  274.6 11.1 %y_forward.1 = f32[4,8,256,128]{3,2,1,0:T(8,128)} custom-call(f32[2,16,2,64,256]{4,3,2,1,0:T(8,128)} %bitcast.19.spec_hbm, bf16[4,2048,128]{2,1,0:T(8,128)(2,1)} %bitcast.29, bf16[1024,512]{1,0:T(8,128)(2,1)} %constant.60.clone.table_hbm, f32[2,7,256,128]{3,2,1,0:T(8,128)} %constant.56.clone.tw_hbm), custom_call_target="tpu_custom_call" | custom-call | tf_op jit(solution)/shard_map/y_forward/pallas_call | solution.py:384
  (24 shorter events, 0.1 us)
Async XLA Ops:
  8.7 7.5 %copy-start.6 = (f32[2,4096]{1,0:T(2,128)S(1)}, f32[2,4096]{1,0:T(2,128)}, u32[]{:S(2)}) copy-start(f32[2,4096]{1,0:T(2,128)} %param.14) | copy-start | bytes 98308
  8.8 7.5 %copy-start.7 = (s32[4096]{0:T(1024)S(1)}, s32[4096]{0:T(1024)}, u32[]{:S(2)}) copy-start(s32[4096]{0:T(1024)} %param.13) | copy-start | bytes 49156
  8.8 103.7 %copy-start.1 = (bf16[256,1024]{1,0:T(8,128)(2,1)S(1)}, bf16[256,1024]{1,0:T(8,128)(2,1)}, u32[]{:S(2)}) copy-start(bf16[256,1024]{1,0:T(8,128)(2,1)} %constant.59.clone.forward_ref.table_ref) | copy-start | bytes 1572868
  8.8 103.7 %copy-start.3 = (f32[2,16,8,256]{3,2,1,0:T(8,128)S(1)}, f32[2,16,8,256]{3,2,1,0:T(8,128)}, u32[]{:S(2)}) copy-start(f32[2,16,8,256]{3,2,1,0:T(8,128)} %constant.57.clone.tw_ref) | copy-start | bytes 786436
  8.8 103.7 %copy-start.4 = (bf16[512,512]{1,0:T(8,128)(2,1)S(1)}, bf16[512,512]{1,0:T(8,128)(2,1)}, u32[]{:S(2)}) copy-start(bf16[512,512]{1,0:T(8,128)(2,1)} %constant.58.clone.inverse_ref) | copy-start | bytes 1572868
  8.8 103.7 %all-to-all-start = ((f32[32,2,64,256]{3,2,1,0:T(8,128)}), f32[32,2,64,256]{3,2,1,0:T(8,128)}, u32[]{:S(2)}, u32[]{:S(2)}) async-start(f32[32,2,64,256]{3,2,1,0:T(8,128)} %bitcast.25), calls=%async_computation | async-start | bytes 8388608 | tf_op jit(solution)/shard_map/all_to_all | solution.py:826
  130.9 5.2 %collective-permute-start.1 = (f32[3,32,256]{2,1,0:T(8,128)S(1)}, f32[3,32,256]{2,1,0:T(8,128)S(1)}, u32[]{:S(2)}, u32[]{:S(2)}) collective-permute-start(f32[3,32,256]{2,1,0:T(8,128)S(1)} %get-tuple-element.17), channel_id=1, source_target_pairs={{16,0},{1,16},{17,1},{2,17},{18,2},{3,18},{19,3},{4,19},{20,4},{5,... | collective-permute-start | bytes 294920 | tf_op jit(solution)/shard_map/ppermute | solution.py:865
  132.2 3.9 %collective-permute-start = (f32[32,256]{1,0:T(8,128)S(1)}, f32[32,256]{1,0:T(8,128)S(1)}, u32[]{:S(2)}, u32[]{:S(2)}) collective-permute-start(f32[32,256]{1,0:T(8,128)S(1)} %get-tuple-element.16.tail_ref), channel_id=1, source_target_pairs={{0,16},{16,1},{1,17},{17,2},{2,18},{18,3},{3,19},{19,4},{4,20},{20... | collective-permute-start | bytes 98312 | tf_op jit(solution)/shard_map/ppermute | solution.py:866
  150.4 1.3 collective-permute-start.2
  159.5 13.3 %copy-start.2 = (f32[32,64,256]{2,1,0:T(8,128)}, f32[32,64,256]{2,1,0:T(8,128)S(1)}, u32[]{:S(2)}) copy-start(f32[32,64,256]{2,1,0:T(8,128)S(1)} %get-tuple-element.24) | copy-start | bytes 6291460
  169.7 1.3 collective-permute-start.3
  172.8 2.0 copy-start
  174.8 99.8 %all-to-all-start.3 = ((f32[32,2,64,256]{3,2,1,0:T(8,128)}), f32[32,2,64,256]{3,2,1,0:T(8,128)}, u32[]{:S(2)}, u32[]{:S(2)}) async-start(f32[32,2,64,256]{3,2,1,0:T(8,128)} %copy-done), calls=%async_computation.3 | async-start | bytes 8388608 | tf_op jit(solution)/shard_map/all_to_all | solution.py:826
  195.2 3.0 %collective-permute-start.4 = (f32[64,4096]{1,0:T(8,128)}, f32[64,4096]{1,0:T(8,128)}, u32[]{:S(2)}, u32[]{:S(2)}) collective-permute-start(f32[64,4096]{1,0:T(8,128)} %bitcast.16), channel_id=1, source_target_pairs={{0,16},{16,0},{1,17},{17,1},{2,18},{18,2},{3,19},{19,3},{4,20},{20... | collective-permute-start | bytes 3145736 | tf_op jit(solution)/shard_map/ppermute | solution.py:817
  199.5 86.2 %copy-start.5 = (f32[2,64,4096]{2,1,0:T(8,128)}, f32[2,64,4096]{2,1,0:T(8,128)S(1)}, u32[]{:S(2)}) copy-start(f32[2,64,4096]{2,1,0:T(8,128)S(1)} %bitcast_dynamic-update-slice_fusion) | copy-start | bytes 6291460

commit v8 on v7

--- a/solution.py
+++ b/solution.py
@@ -19,6 +19,7 @@
 MIB = 1024 * 1024
 Y_GRANT = 56 * MIB
 X_GRANT = 20 * MIB
+COMBINE_GRANT = 53 * MIB
 
 
 def dft_parts(length, scale):
@@ -139,12 +140,16 @@
     return parts[0:1] / (parts[1:2] + PENALTY * parts[2:3])
 
 
-def put_sums(out_ref, values):
+def sums_block(values):
     rows = [jnp.sum(v, axis=0, keepdims=True) for v in values]
     index = lax.broadcasted_iota(jnp.int32, (8, LANES), 0)
     block = jnp.zeros((8, LANES), F32)
     for i, row in enumerate(rows):
         block = jnp.where(index == i, jnp.broadcast_to(row, (8, LANES)), block)
+    return block
+
+
+def put_copies(out_ref, block):
     for i in range(out_ref.shape[0]):
         out_ref[i] = block
 
@@ -288,18 +293,18 @@
 
 def y_forward_kernel(
     spec_hbm, data_hbm, table_hbm, tw_hbm, out_hbm,
-    spec_ref, data_ref, table_ref, tw_ref, out_ref, re_s, im_s, mix_s, sems, spec_sems, out_sems,
+    spec_ref, data_ref, table_ref, tw_ref, out_ref, mix_s, sems, spec_sems, out_sems,
 ):
     blocks, ny, _ = data_ref.shape
     n = ny // YR
-    gz, gy, _, rows, _ = spec_ref.shape
+    _, gz, gy, _, rows, _ = spec_ref.shape
     pairs = blocks // 2
     half = n // 2
 
     def fetch(chunk):
         lanes = pl.ds(chunk * LANES, LANES)
         return pltpu.make_async_copy(
-            spec_hbm.at[:, :, :, :, lanes], spec_ref.at[:, :, :, :, lanes], spec_sems.at[chunk]
+            spec_hbm.at[:, :, :, :, lanes], spec_ref.at[chunk], spec_sems.at[chunk]
         )
 
     def give(chunk, part):
@@ -316,26 +321,24 @@
     for chunk in range(1, pairs):
         fetch(chunk).start()
 
+    def rows_of(chunk, p, k):
+        part = pl.ds(k, rows // YR, stride=YR)
+        return jnp.concatenate(
+            [spec_ref[chunk, core, i, p, part, :] for i in range(gy) for core in range(gz)], axis=0
+        )
+
     lane = lax.broadcasted_iota(jnp.int32, (16, LANES), 1)
     for chunk in range(pairs):
         lanes = slice(chunk * LANES, (chunk + 1) * LANES)
         fetch(chunk).wait()
 
-        def unpack(i, carry):
-            for core in range(gz):
-                part = pl.ds(pl.multiple_of((i * gz + core) * rows, rows), rows)
-                re_s[part, :] = spec_ref[core, i, 0, :, lanes]
-                im_s[part, :] = spec_ref[core, i, 1, :, lanes]
-            return carry
-
-        lax.fori_loop(0, gy, unpack, 0)
         if chunk == 0:
             fetch_table.wait()
 
         for k in range(0, YR, 2):
             pieces = [
-                jnp.concatenate([s[pl.ds(k + d, n, stride=YR), :] for d in range(2)], axis=1)
-                for s in (re_s, im_s)
+                jnp.concatenate([rows_of(chunk, p, k + d) for d in range(2)], axis=1)
+                for p in range(2)
             ]
             high, low = split2(jnp.concatenate(pieces, axis=0))
             both = dot(table_ref[...], high)
@@ -387,13 +390,11 @@
         out_specs=hbm,
         out_shape=jax.ShapeDtypeStruct((blocks, YR, n, width), F32),
         scratch_shapes=[
-            pltpu.VMEM(spec.shape, F32),
+            pltpu.VMEM((blocks // 2, *spec.shape[:-1], LANES), F32),
             pltpu.VMEM((blocks, ny, width), BF16),
             pltpu.VMEM((4 * n, 2 * n), BF16),
             pltpu.VMEM((2, YR - 1, n, LANES), F32),
             pltpu.VMEM((blocks, YR, n, width), F32),
-            pltpu.VMEM((ny, LANES), F32),
-            pltpu.VMEM((ny, LANES), F32),
             pltpu.VMEM((YR, 2 * n, LANES), F32),
             pltpu.SemaphoreType.DMA((3,)),
             pltpu.SemaphoreType.DMA((blocks // 2,)),
@@ -515,8 +516,8 @@
 
 
 def middle_kernel(
-    edge_ref, spec_hbm, coef_ref, tw_ref, inverse_ref, forward_ref,
-    d0_ref, nd0_ref, head_ref, tail_ref, sums_ref, spec_ref, re_s, im_s, sems,
+    spec_hbm, coef_ref, tw_ref, inverse_ref, forward_ref,
+    d0_ref, nd0_ref, head_ref, tail_ref, spec_ref, re_s, im_s, sems,
 ):
     gz, kb, _, rows, ka = spec_ref.shape
     planes = gz * kb
@@ -530,22 +531,21 @@
             spec_hbm.at[:, :, :, part], spec_ref.at[:, :, :, part], sems.at[i]
         )
 
+    def columns_back(j, carry):
+        part = pl.ds(pl.multiple_of(j * 8, 8), 8)
+        for lanes in lane_parts:
+            spectra = [
+                [(spec_ref[z, k, 0, part, lanes], spec_ref[z, k, 1, part, lanes]) for k in range(kb)]
+                for z in range(gz)
+            ]
+            inverse_columns(gz, kb, spectra, coef_ref, tw_ref, lanes, part, re_s, im_s)
+        return carry
+
     for i in range(cuts):
         fetch(i).start()
     for i in range(cuts):
         fetch(i).wait()
-
-        def first_columns(j, carry):
-            part = pl.ds(pl.multiple_of(i * cut + j * 8, 8), 8)
-            for lanes in lane_parts:
-                spectra = [
-                    [(spec_ref[z, k, 0, part, lanes], spec_ref[z, k, 1, part, lanes]) for k in range(kb)]
-                    for z in range(gz)
-                ]
-                inverse_columns(gz, kb, spectra, coef_ref, tw_ref, lanes, part, re_s, im_s)
-            return carry
-
-        lax.fori_loop(0, cut // 8, first_columns, 0)
+        lax.fori_loop(i * cut // 8, (i + 1) * cut // 8, columns_back, 0)
 
     step = plane_chunk(planes, rows)
     shape2, shape3 = (step * rows, ka), (step, rows, ka)
@@ -571,10 +571,10 @@
                         value = spectra[z][k][p]
                         spec_ref[z, k, p, part, lanes] = value
                         total = total + value * value
-            inverse_columns(gz, kb, spectra, coef_ref, tw_ref, lanes, part, re_s, im_s)
         return total
 
     projected = lax.fori_loop(0, rows // 8, second_columns, jnp.zeros((8, LANES), F32))
+    lax.fori_loop(0, rows // 8, columns_back, 0)
     def back(i, carry):
         part = pl.ds(i * step, step)
         field = inverse_product(re_s[part].reshape(shape2), im_s[part].reshape(shape2), inverse_ref)
@@ -584,9 +584,9 @@
     lax.fori_loop(0, planes // step, back, 0)
 
     for p in range(planes):
-        head_ref[0, p : p + 1, :] = d0_ref[p, :1, :]
-        head_ref[1, p : p + 1, :] = d0_ref[p, 1:2, :]
-        head_ref[2, p : p + 1, :] = nd0_ref[p, :1, :]
+        head_ref[p : p + 1, :] = d0_ref[p, :1, :]
+        head_ref[planes + p : planes + p + 1, :] = d0_ref[p, 1:2, :]
+        head_ref[2 * planes + p : 2 * planes + p + 1, :] = nd0_ref[p, :1, :]
         tail_ref[p : p + 1, :] = d0_ref[p, rows - 1 : rows, :]
 
     row = lax.broadcasted_iota(jnp.int32, (rows, ka), 0)
@@ -602,49 +602,61 @@
             along_z = d0_ref[p + kb] - here
             terms = terms + along_z * along_z
         slope = slope + fold(terms)
-    sums_ref[0] = square
-    sums_ref[1] = projected
-    sums_ref[2] = slope
-
-
-def middle(edge, spec, coef, nx):
+    block = sums_block([square, projected, slope])
+    for ref in (head_ref, tail_ref):
+        at = ref.shape[0] - 8
+        ref[at:, :] = jnp.zeros((8, ka), F32)
+        ref[at:, :LANES] = block
+
+
+def middle(spec, coef, nx):
     gz, kb, _, rows, ka = spec.shape
     planes = gz * kb
     vmem = pl.BlockSpec(memory_space=pltpu.VMEM)
     field = jax.ShapeDtypeStruct((planes, rows, ka), F32)
     return pl.pallas_call(
         middle_kernel,
-        in_specs=[pl.BlockSpec(memory_space=pltpu.SMEM), pl.BlockSpec(memory_space=pltpu.HBM)]
-        + [vmem] * 4,
-        out_specs=[vmem] * 6,
+        in_specs=[pl.BlockSpec(memory_space=pltpu.HBM)] + [vmem] * 4,
+        out_specs=[vmem] * 5,
         out_shape=[
             field,
             field,
-            jax.ShapeDtypeStruct((3, planes, ka), F32),
-            jax.ShapeDtypeStruct((planes, ka), F32),
-            jax.ShapeDtypeStruct((3, 8, LANES), F32),
+            jax.ShapeDtypeStruct((3 * planes + 8, ka), F32),
+            jax.ShapeDtypeStruct((planes + 8, ka), F32),
             jax.ShapeDtypeStruct(spec.shape, F32),
         ],
         scratch_shapes=[
             pltpu.VMEM((planes, rows, ka), F32),
             pltpu.VMEM((planes, rows, ka), F32),
-            pltpu.SemaphoreType.DMA((2 if rows % 16 == 0 else 1,)),
+            pltpu.SemaphoreType.DMA((4 if rows % 32 == 0 else 1,)),
         ],
         compiler_params=pltpu.CompilerParams(vmem_limit_bytes=X_GRANT),
         name="middle",
     )(
-        edge, spec, coef, x_twiddle(nx, ka), jnp.asarray(x_inverse_matrix(nx, ka)),
+        spec, coef, x_twiddle(nx, ka), jnp.asarray(x_inverse_matrix(nx, ka)),
         x_forward_matrix(nx, ka),
     )
 
 
-def border_kernel(edge_ref, sums_ref, tail_ref, next_ref, prev_ref, out_ref):
-    del prev_ref
-    step = (next_ref[0] - tail_ref[...]) * jnp.where(edge_ref[1] > 0, 0.0, 1.0)
-    put_sums(out_ref, [sums_ref[0], sums_ref[1], sums_ref[2] + fold(step * step)])
-
-
-def border_sums(edge, sums, tail, next_head, prev_tail, copies):
+def border_kernel(edge_ref, head_ref, tail_ref, next_ref, prev_ref, out_ref):
+    planes = tail_ref.shape[0] - 8
+
+    def sums_of(ref):
+        return ref[ref.shape[0] - 8 :, :LANES]
+
+    def border(after, before):
+        step = after[:planes, :] - before[:planes, :]
+        return fold(step * step)
+
+    second = edge_ref[2] > 0
+    below = border(head_ref, prev_ref) * jnp.where(edge_ref[0] > 0, 0.0, 1.0)
+    above = border(next_ref, tail_ref) * jnp.where(edge_ref[1] > 0, 0.0, 1.0)
+    other = jnp.where(second, sums_of(prev_ref), sums_of(next_ref))
+    none = jnp.zeros((8, LANES), F32)
+    put_copies(out_ref, sums_of(tail_ref) + other + sums_block([none, none, below + above]))
+
+
+def border_sums(edge, head, tail, next_head, prev_tail, copies):
     vmem = pl.BlockSpec(memory_space=pltpu.VMEM)
     return pl.pallas_call(
         border_kernel,
@@ -653,14 +665,14 @@
         out_shape=jax.ShapeDtypeStruct((copies, 8, LANES), F32),
         compiler_params=pltpu.CompilerParams(vmem_limit_bytes=2 * MIB),
         name="border_sums",
-    )(edge, sums, tail, next_head, prev_tail)
+    )(edge, head, tail, next_head, prev_tail)
 
 
 def second_kernel(
     gz, edge_ref, d0_ref, nd0_ref, tail_ref, prev_ref, next_ref,
     coef_ref, tw_ref, table_ref, *refs,
 ):
-    sums_refs, refs = refs[:gz], refs[gz:]
+    sums_refs, refs = refs[:1], refs[1:]
     d1_ref, eta_ref, out_ref, spec_ref, re_s, im_s, row_s = refs
     planes, rows, ka = d0_ref.shape
     kb = planes // gz
@@ -677,8 +689,8 @@
     row2 = lax.broadcasted_iota(jnp.int32, (kb, ka), 0)
     for z in range(gz):
         part = slice(z * kb, (z + 1) * kb)
-        here = next_ref[0, part, :]
-        value = here - eta * next_ref[2, part, :]
+        here = next_ref[part, :]
+        value = here - eta * next_ref[2 * planes + z * kb : 2 * planes + (z + 1) * kb, :]
         up = pltpu.roll(here, kb - 1, 0)
         up = jnp.where(
             row2 == kb - 1, jnp.where(lane2 == ka - 1, here, pltpu.roll(up, ka - 1, 1)), up
@@ -686,11 +698,11 @@
         down = pltpu.roll(here, 1, 0)
         down = jnp.where(row2 == 0, jnp.where(lane2 == 0, here, pltpu.roll(down, 1, 1)), down)
         value = value + shrink(here - down) - shrink(up - here)
-        value = value + shrink(here - tail_ref[part, :]) - shrink(next_ref[1, part, :] - here)
+        value = value + shrink(here - tail_ref[part, :]) - shrink(next_ref[planes + z * kb : planes + (z + 1) * kb, :] - here)
         if z > 0:
-            value = value + shrink(here - next_ref[0, (z - 1) * kb : z * kb, :])
+            value = value + shrink(here - next_ref[(z - 1) * kb : z * kb, :])
         if z + 1 < gz:
-            value = value - shrink(next_ref[0, (z + 1) * kb : (z + 2) * kb, :] - here)
+            value = value - shrink(next_ref[(z + 1) * kb : (z + 2) * kb, :] - here)
         row_s[part, :] = value
 
     row = lax.broadcasted_iota(jnp.int32, (rows, ka), 0)
@@ -700,7 +712,7 @@
         value = here - eta * nd0_ref[p]
         value = value + shrink(here - prev_plane(d0_ref, p, kb))
         value = value - shrink(next_plane(d0_ref, p, kb) - here)
-        below = jnp.where(last, here[rows - 1 :, :], next_ref[0, p : p + 1, :])
+        below = jnp.where(last, here[rows - 1 :, :], next_ref[p : p + 1, :])
         above = jnp.where(first, here[:1, :], prev_ref[p : p + 1, :])
         upper = shrink(jnp.where(row == rows - 1, below, pltpu.roll(here, rows - 1, 0)) - here)
         lower = jnp.where(row == 0, shrink(here[:1, :] - above), pltpu.roll(upper, 1, 0))
@@ -749,7 +761,7 @@
         return total
 
     projected = lax.fori_loop(0, rows // 8, columns, jnp.zeros((8, LANES), F32))
-    put_sums(out_ref, [square, projected, slope])
+    put_copies(out_ref, sums_block([square, projected, slope]))
 
 
 def second_descent(edge, sums, d0, nd0, tail, prev_tail, next_head, coef, gz, nx):
@@ -757,12 +769,12 @@
     vmem = pl.BlockSpec(memory_space=pltpu.VMEM)
     return pl.pallas_call(
         functools.partial(second_kernel, gz),
-        in_specs=[pl.BlockSpec(memory_space=pltpu.SMEM)] + [vmem] * (8 + gz),
+        in_specs=[pl.BlockSpec(memory_space=pltpu.SMEM)] + [vmem] * 9,
         out_specs=[vmem] * 4,
         out_shape=[
             jax.ShapeDtypeStruct((planes, rows, ka), F32),
             jax.ShapeDtypeStruct((8, LANES), F32),
-            jax.ShapeDtypeStruct(sums[0].shape, F32),
+            jax.ShapeDtypeStruct(sums.shape, F32),
             jax.ShapeDtypeStruct((gz, planes // gz, 2, rows, ka), F32),
         ],
         scratch_shapes=[
@@ -774,7 +786,7 @@
         name="second_descent",
     )(
         edge, d0, nd0, tail, prev_tail, next_head, coef,
-        x_twiddle(nx, ka), x_forward_matrix(nx, ka), *sums,
+        x_twiddle(nx, ka), x_forward_matrix(nx, ka), sums,
     )
 
 
@@ -807,7 +819,7 @@
             jax.ShapeDtypeStruct(first.shape, F32),
             jax.ShapeDtypeStruct((2, 8, LANES), F32),
         ],
-        compiler_params=pltpu.CompilerParams(vmem_limit_bytes=6 * MIB),
+        compiler_params=pltpu.CompilerParams(vmem_limit_bytes=COMBINE_GRANT),
         name="combine_spectra",
     )(eta, *sums, first, second)
 
@@ -844,7 +856,7 @@
 
     core = lax.axis_index("gz")
     flat = lax.axis_index("gy") * gz + core
-    edge = jnp.stack([flat == 0, flat == devices - 1]).astype(jnp.int32)
+    edge = jnp.stack([flat == 0, flat == devices - 1, core]).astype(jnp.int32)
     order = [(i % gz) * gy + i // gz for i in range(devices)]
     up = [(order[i + 1], order[i]) for i in range(devices - 1)]
     down = [(order[i], order[i + 1]) for i in range(devices - 1)]
@@ -861,10 +873,10 @@
     coef = jnp.broadcast_to(coef, (3, gy, 8, ka))
 
     spec = to_devices(y_inverse(data, rows, gz, gy))
-    d0, nd0, head, tail, sums, first = middle(edge, spec, coef, nx)
+    d0, nd0, head, tail, first = middle(spec, coef, nx)
     next_head = lax.ppermute(head, ("gz", "gy"), up)
     prev_tail = lax.ppermute(tail, ("gz", "gy"), down)
-    sums = everywhere(border_sums(edge, sums, tail, next_head, prev_tail, gy))
+    sums = to_chips(border_sums(edge, head, tail, next_head, prev_tail, gy))
     d1, eta, sums, second = second_descent(
         edge, sums, d0, nd0, tail, prev_tail, next_head, coef, gz, nx
     )
@@ -1129,7 +1141,7 @@
 
 def tiles_fit(mesh, ny, blocks):
     rows = ny // (mesh.shape["gz"] * mesh.shape["gy"])
-    return rows % 16 == 0 and mesh.shape["gy"] % YR == 0 and blocks // mesh.shape["gy"] % 2 == 0
+    return mesh.shape["gz"] == 2 and rows % 16 == 0 and mesh.shape["gy"] % YR == 0 and blocks // mesh.shape["gy"] % 2 == 0
 
 
 def solution(mesh):

time: 286 us -> 294 us (1.028)
  Pallas kernels: 47.9 us -> 53 us
  local copies, waits for them, and re-layouts: 16.6 us -> 19.9 us
    pallas_call x1, Pallas kernels: 1.86 us -> 7.81 us  [combine_spectra(): pl.pallas_call(functools.partial(combine_kernel, gz), grid=(planes // cou...]
    unnamed x16 -> x18, local copies, waits for them, and re-layouts: 2.04 us -> 5.35 us
  transfers between devices with their start and end apart: 7 -> 6, of which waited for: 6 -> 5; matrix products, arithmetic and copies ran while one was open for 7% -> 7% of each run, Pallas kernels for 0% -> 0%
where the time goes in v8:
time: 294 us
  waiting for transfers between devices  176 us (60%)
  Pallas kernels  53 us (18%)
  blocking collectives  24.8 us (8%)
  local copies, waits for them, and re-layouts  19.9 us (7%)
  starting transfers between devices  14.3 us (5%)
  other arithmetic  4.58 us (2%)
    all_to_all x2, waiting for transfers between devices, to_devices(): lax.all_to_all(parts.reshape(gz * gy, *rest), ('gz', 'gy'), 0, 0, tiled=T...  171 us
    all_to_all x2, blocking collectives, to_chips(): return lax.all_to_all(parts, 'gy', 0, 0, tiled=True)  24.8 us
    pallas_call x1, Pallas kernels, middle(): pl.pallas_call(middle_kernel, in_specs=[pl.BlockSpec(memory_space=pltpu.H...  17.7 us
    all_to_all x2, starting transfers between devices, to_devices(): lax.all_to_all(parts.reshape(gz * gy, *rest), ('gz', 'gy'), 0, 0, tiled=T...  11 us
    pallas_call x1, Pallas kernels, y_forward(): pl.pallas_call(y_forward_kernel, in_specs=[hbm] * 4, out_specs=hbm, out_s...  10.8 us
    pallas_call x1, Pallas kernels, y_inverse(): pl.pallas_call(y_inverse_kernel, in_specs=[hbm] * 3, out_specs=hbm, out_s...  8.11 us
    pallas_call x1, Pallas kernels, second_descent(): pl.pallas_call(functools.partial(second_kernel, gz), in_specs=[pl.BlockSp...  7.98 us
    pallas_call x1, Pallas kernels, combine_spectra(): pl.pallas_call(functools.partial(combine_kernel, gz), grid=(planes // cou...  7.81 us
  transfers between devices with their start and end apart: 6, of which 5 were waited for; matrix products, arithmetic and copies ran while one was open for 7% of the time, Pallas kernels for 0%

profile of v8, /device:TPU:0, one launch (start us, length us, event | category | flops | bytes accessed | tf_op | source)
XLA Modules:
  0.0 293.8 jit_solution(15799424122471177725)
XLA Ops:
  0.6 8.1 %y_inverse.1 = f32[2,16,2,64,256]{4,3,2,1,0:T(8,128)} custom-call(bf16[4,2048,128]{2,1,0:T(8,128)(2,1)} %bitcast.29, bf16[1024,512]{1,0:T(8,128)(2,1)} %constant.55.clone.table_hbm, f32[2,7,256,128]{3,2,1,0:T(8,128)} %constant.56.clone.tw_hbm), custom_call_target="tpu_custom_call" | custom-call | tf_op jit(solution)/shard_map/y_inverse/pallas_call | solution.py:273
  8.8 7.4 %all-to-all-start = ((f32[32,2,64,256]{3,2,1,0:T(8,128)}), f32[32,2,64,256]{3,2,1,0:T(8,128)}, u32[]{:S(2)}, u32[]{:S(2)}) async-start(f32[32,2,64,256]{3,2,1,0:T(8,128)} %bitcast.26), calls=%async_computation | async-start | bytes 8388608 | tf_op jit(solution)/shard_map/all_to_all | solution.py:838
  16.4 96.1 %all-to-all-done = f32[32,2,64,256]{3,2,1,0:T(8,128)} async-done(((f32[32,2,64,256]{3,2,1,0:T(8,128)}), f32[32,2,64,256]{3,2,1,0:T(8,128)}, u32[]{:S(2)}, u32[]{:S(2)}) %all-to-all-start) | async-done | bytes 4194336 | tf_op jit(solution)/shard_map/all_to_all | solution.py:838
  112.5 17.7 %middle.1 = (f32[32,64,256]{2,1,0:T(8,128)S(1)}, f32[32,64,256]{2,1,0:T(8,128)S(1)}, f32[104,256]{1,0:T(8,128)S(1)}, f32[40,256]{1,0:T(8,128)S(1)}, f32[2,16,2,64,256]{4,3,2,1,0:T(8,128)S(1)}) custom-call(f32[2,16,2,64,256]{4,3,2,1,0:T(8,128)} %bitcast.5.spec_hbm, f32[3,16,8,256]{3,2,1,0:T(8,128)S(1)} %broadcast_in_dim.24.coef_ref, ...), custom_call_target="tpu_custom_call" | custom-call | tf_op jit(solution)/shard_map/middle/pallas_call | solution.py:617
  130.2 2.0 copy-done
  132.2 1.8 collective-permute-start
  134.0 1.3 collective-permute-start.1
  135.3 0.1 pad_add_fusion.edge_ref
  135.4 1.8 collective-permute-done.1.next_ref
  137.2 0.6 border_sums.1
  137.8 14.6 %all_to_all.20.refs_0_ = f32[16,8,128]{2,1,0:T(8,128)S(1)} all-to-all(f32[16,8,128]{2,1,0:T(8,128)S(1)} %border_sums.1), channel_id=1, replica_groups=mesh['gz'=2,'gy'=16] {'gy'}, dimensions={0} | all-to-all | bytes 131072 | tf_op jit(solution)/shard_map/all_to_all | solution.py:833
  152.4 8.0 %second_descent.1 = (f32[32,64,256]{2,1,0:T(8,128)S(1)}, f32[8,128]{1,0:T(8,128)S(1)}, f32[16,8,128]{2,1,0:T(8,128)S(1)}, f32[2,16,2,64,256]{4,3,2,1,0:T(8,128)S(1)}) custom-call(s32[3]{0:T(128)S(1)} %pad_add_fusion.edge_ref, f32[32,64,256]{2,1,0:T(8,128)S(1)} %get-tuple-element.13.d0_ref, f32[32,64,256]{2,1,0:T(8,128)S(1)} %get-tuple-element.14.nd0_ref, ...), custom_call_target="tpu_custom_call" | custom-call | tf_op jit(solution)/shard_map/second_descent/pallas_call | solution.py:770
  160.4 2.0 copy-done.1
  162.4 1.3 copy-done.3
  163.7 10.2 %all_to_all.21.refs_0_ = f32[16,8,128]{2,1,0:T(8,128)S(1)} all-to-all(f32[16,8,128]{2,1,0:T(8,128)S(1)} %get-tuple-element.18), channel_id=1, replica_groups=mesh['gz'=2,'gy'=16] {'gy'}, dimensions={0} | all-to-all | bytes 131072 | tf_op jit(solution)/shard_map/all_to_all | solution.py:833
  173.9 0.2 collective-permute-start.2
  174.1 1.1 collective-permute-done.2.refs_1_
  175.2 7.8 %combine_spectra.1 = (f32[32,2,64,256]{3,2,1,0:T(8,128)}, f32[2,8,128]{2,1,0:T(8,128)S(1)}) custom-call(f32[8,128]{1,0:T(8,128)S(1)} %get-tuple-element.17.eta_ref, f32[16,8,128]{2,1,0:T(8,128)S(1)} %all_to_all.21.refs_0_, f32[16,8,128]{2,1,0:T(8,128)S(1)} %collective-permute-done.2.refs_1_, f32[32,2,64,256]{3,2,1,0:T(8,128)} %bitcast.24, ...), custom_call_target="tpu_custom_call" | custom-call | tf_op jit(solution)/shard_map/combine_spectra/pallas_call | solution.py:810
  183.0 3.6 %all-to-all-start.3 = ((f32[32,2,64,256]{3,2,1,0:T(8,128)}), f32[32,2,64,256]{3,2,1,0:T(8,128)}, u32[]{:S(2)}, u32[]{:S(2)}) async-start(f32[32,2,64,256]{3,2,1,0:T(8,128)} %get-tuple-element.23), calls=%async_computation.3 | async-start | bytes 8388608 | tf_op jit(solution)/shard_map/all_to_all | solution.py:838
  186.6 0.5 fusion.2
  187.1 4.5 %add_negate_fusion = f32[32,64,256]{2,1,0:T(8,128)} fusion(f32[32,64,256]{2,1,0:T(8,128)} %copy-done.3, f32[32,64,256]{2,1,0:T(8,128)S(1)} %get-tuple-element.13.d0_ref, f32[]{:T(128)} %bitcast.12, f32[]{:T(128)} %bitcast.11), kind=kLoop, calls=%fused_computation | loop fusion | flops 2097152 | bytes 6291464 | tf_op jit(solution)/shard_map/neg | solution.py:888
  191.6 4.9 %copy.18 = f32[2,16,64,256]{2,1,3,0:T(8,128)} copy(f32[2,16,64,256]{3,2,1,0:T(8,128)} %bitcast.28) | data formatting | bytes 4194304 | tf_op jit(solution)/shard_map/reshape | solution.py:889
  196.5 3.8 %constant_dynamic-slice_fusion = (f32[1,64,4096]{1,2,0:T(8,128)}, f32[1,64,4096]{1,2,0:T(8,128)S(1)}) fusion(f32[2,64,4096]{1,2,0:T(8,128)} %bitcast.27, s32[]{:T(128)S(6)} %select_n.29, s32[]{:T(128)S(6)} %select_n.27), kind=kLoop, calls=%fused_computation.6 | loop fusion | bytes 4194312 | tf_op jit(solution)/shard_map/jit(dynamic_index_in_dim)/dynamic_slice | solution.py:891
  200.3 3.1 %copy.20 = f32[1,64,4096]{2,1,0:T(8,128)} copy(f32[1,64,4096]{1,2,0:T(8,128)} %get-tuple-element.26) | data formatting | bytes 2097152 | tf_op jit(solution)/shard_map/jit(dynamic_index_in_dim)/dynamic_slice | solution.py:891
  203.4 0.0 collective-permute-start.3
  203.5 0.6 copy.19
  204.0 0.2 broadcast_in_dim.21
  204.2 0.1 constant_dynamic-update-slice_fusion
  204.3 2.1 collective-permute-done.3
  206.4 1.3 bitcast_dynamic-update-slice_fusion
  207.7 75.1 %all-to-all-done.3 = f32[32,2,64,256]{3,2,1,0:T(8,128)} async-done(((f32[32,2,64,256]{3,2,1,0:T(8,128)}), f32[32,2,64,256]{3,2,1,0:T(8,128)}, u32[]{:S(2)}, u32[]{:S(2)}) %all-to-all-start.3) | async-done | bytes 4194336 | tf_op jit(solution)/shard_map/all_to_all | solution.py:838
  282.8 10.8 %y_forward.1 = f32[4,8,256,128]{3,2,1,0:T(8,128)} custom-call(f32[2,16,2,64,256]{4,3,2,1,0:T(8,128)} %bitcast.20.spec_hbm, bf16[4,2048,128]{2,1,0:T(8,128)(2,1)} %bitcast.30, bf16[1024,512]{1,0:T(8,128)(2,1)} %constant.60.clone.table_hbm, f32[2,7,256,128]{3,2,1,0:T(8,128)} %constant.56.clone.tw_hbm), custom_call_target="tpu_custom_call" | custom-call | tf_op jit(solution)/shard_map/y_forward/pallas_call | solution.py:387
  (24 shorter events, 0.1 us)
Async XLA Ops:
  8.7 7.5 %copy-start.7 = (f32[2,4096]{1,0:T(2,128)S(1)}, f32[2,4096]{1,0:T(2,128)}, u32[]{:S(2)}) copy-start(f32[2,4096]{1,0:T(2,128)} %param.14) | copy-start | bytes 98308
  8.8 7.5 %copy-start.8 = (s32[4096]{0:T(1024)S(1)}, s32[4096]{0:T(1024)}, u32[]{:S(2)}) copy-start(s32[4096]{0:T(1024)} %param.13) | copy-start | bytes 49156
  8.8 103.7 %copy-start.2 = (bf16[256,1024]{1,0:T(8,128)(2,1)S(1)}, bf16[256,1024]{1,0:T(8,128)(2,1)}, u32[]{:S(2)}) copy-start(bf16[256,1024]{1,0:T(8,128)(2,1)} %constant.59.clone.forward_ref.table_ref) | copy-start | bytes 1572868
  8.8 103.7 %copy-start.4 = (f32[2,16,8,256]{3,2,1,0:T(8,128)S(1)}, f32[2,16,8,256]{3,2,1,0:T(8,128)}, u32[]{:S(2)}) copy-start(f32[2,16,8,256]{3,2,1,0:T(8,128)} %constant.57.clone.tw_ref) | copy-start | bytes 786436
  8.8 103.7 %copy-start.5 = (bf16[512,512]{1,0:T(8,128)(2,1)S(1)}, bf16[512,512]{1,0:T(8,128)(2,1)}, u32[]{:S(2)}) copy-start(bf16[512,512]{1,0:T(8,128)(2,1)} %constant.58.clone.inverse_ref) | copy-start | bytes 1572868
  8.8 103.7 %all-to-all-start = ((f32[32,2,64,256]{3,2,1,0:T(8,128)}), f32[32,2,64,256]{3,2,1,0:T(8,128)}, u32[]{:S(2)}, u32[]{:S(2)}) async-start(f32[32,2,64,256]{3,2,1,0:T(8,128)} %bitcast.26), calls=%async_computation | async-start | bytes 8388608 | tf_op jit(solution)/shard_map/all_to_all | solution.py:838
  130.2 2.0 copy-start
  132.2 3.2 %collective-permute-start = (f32[40,256]{1,0:T(8,128)S(1)}, f32[40,256]{1,0:T(8,128)S(1)}, u32[]{:S(2)}, u32[]{:S(2)}) collective-permute-start(f32[40,256]{1,0:T(8,128)S(1)} %get-tuple-element.15.tail_ref), channel_id=1, source_target_pairs={{0,16},{16,1},{1,17},{17,2},{2,18},{18,3},{3,19},{19,4},{4,20},{20... | collective-permute-start | bytes 122888 | tf_op jit(solution)/shard_map/ppermute | solution.py:878
  134.0 3.2 %collective-permute-start.1 = (f32[104,256]{1,0:T(8,128)S(1)}, f32[104,256]{1,0:T(8,128)S(1)}, u32[]{:S(2)}, u32[]{:S(2)}) collective-permute-start(f32[104,256]{1,0:T(8,128)S(1)} %get-tuple-element.16.head_ref), channel_id=1, source_target_pairs={{16,0},{1,16},{17,1},{2,17},{18,2},{3,18},{19,3},{4,19},{20,4},{5,... | collective-permute-start | bytes 319496 | tf_op jit(solution)/shard_map/ppermute | solution.py:877
  160.4 2.0 copy-start.1
  162.4 1.3 copy-start.3
  173.9 1.3 collective-permute-start.2
  183.0 99.8 %all-to-all-start.3 = ((f32[32,2,64,256]{3,2,1,0:T(8,128)}), f32[32,2,64,256]{3,2,1,0:T(8,128)}, u32[]{:S(2)}, u32[]{:S(2)}) async-start(f32[32,2,64,256]{3,2,1,0:T(8,128)} %get-tuple-element.23), calls=%async_computation.3 | async-start | bytes 8388608 | tf_op jit(solution)/shard_map/all_to_all | solution.py:838
  203.4 3.0 %collective-permute-start.3 = (f32[64,4096]{1,0:T(8,128)}, f32[64,4096]{1,0:T(8,128)}, u32[]{:S(2)}, u32[]{:S(2)}) collective-permute-start(f32[64,4096]{1,0:T(8,128)} %bitcast.17), channel_id=1, source_target_pairs={{0,16},{16,0},{1,17},{17,1},{2,18},{18,2},{3,19},{19,3},{4,20},{20... | collective-permute-start | bytes 3145736 | tf_op jit(solution)/shard_map/ppermute | solution.py:829
  207.7 85.9 %copy-start.6 = (f32[2,64,4096]{2,1,0:T(8,128)}, f32[2,64,4096]{2,1,0:T(8,128)S(1)}, u32[]{:S(2)}) copy-start(f32[2,64,4096]{2,1,0:T(8,128)S(1)} %bitcast_dynamic-update-slice_fusion) | copy-start | bytes 6291460

commit v9 on v8

--- a/solution.py
+++ b/solution.py
@@ -19,7 +19,6 @@
 MIB = 1024 * 1024
 Y_GRANT = 56 * MIB
 X_GRANT = 20 * MIB
-COMBINE_GRANT = 53 * MIB
 
 
 def dft_parts(length, scale):
@@ -517,7 +516,7 @@
 
 def middle_kernel(
     spec_hbm, coef_ref, tw_ref, inverse_ref, forward_ref,
-    d0_ref, nd0_ref, head_ref, tail_ref, spec_ref, re_s, im_s, sems,
+    d0_ref, head_ref, tail_ref, spec_ref, re_s, im_s, sems,
 ):
     gz, kb, _, rows, ka = spec_ref.shape
     planes = gz * kb
@@ -574,19 +573,12 @@
         return total
 
     projected = lax.fori_loop(0, rows // 8, second_columns, jnp.zeros((8, LANES), F32))
-    lax.fori_loop(0, rows // 8, columns_back, 0)
-    def back(i, carry):
-        part = pl.ds(i * step, step)
-        field = inverse_product(re_s[part].reshape(shape2), im_s[part].reshape(shape2), inverse_ref)
-        nd0_ref[part] = field.reshape(shape3)
-        return carry
-
-    lax.fori_loop(0, planes // step, back, 0)
-
     for p in range(planes):
         head_ref[p : p + 1, :] = d0_ref[p, :1, :]
         head_ref[planes + p : planes + p + 1, :] = d0_ref[p, 1:2, :]
-        head_ref[2 * planes + p : 2 * planes + p + 1, :] = nd0_ref[p, :1, :]
+        for part in range(2):
+            at = 2 * planes + 2 * p + part
+            head_ref[at : at + 1, :] = spec_ref[p // kb, p % kb, part, :1, :]
         tail_ref[p : p + 1, :] = d0_ref[p, rows - 1 : rows, :]
 
     row = lax.broadcasted_iota(jnp.int32, (rows, ka), 0)
@@ -617,11 +609,10 @@
     return pl.pallas_call(
         middle_kernel,
         in_specs=[pl.BlockSpec(memory_space=pltpu.HBM)] + [vmem] * 4,
-        out_specs=[vmem] * 5,
+        out_specs=[vmem] * 4,
         out_shape=[
             field,
-            field,
-            jax.ShapeDtypeStruct((3 * planes + 8, ka), F32),
+            jax.ShapeDtypeStruct((4 * planes + 8, ka), F32),
             jax.ShapeDtypeStruct((planes + 8, ka), F32),
             jax.ShapeDtypeStruct(spec.shape, F32),
         ],
@@ -638,6 +629,65 @@
     )
 
 
+def normal_kernel(spec_ref, next_ref, coef_ref, tw_ref, table_ref, out_ref, row_ref, re_s, im_s):
+    gz, kb, _, rows, ka = spec_ref.shape
+    planes = gz * kb
+    lane_parts = [slice(start, start + LANES) for start in range(0, ka, LANES)]
+
+    def columns(j, carry):
+        part = pl.ds(pl.multiple_of(j * 8, 8), 8)
+        for lanes in lane_parts:
+            spectra = [
+                [(spec_ref[z, k, 0, part, lanes], spec_ref[z, k, 1, part, lanes]) for k in range(kb)]
+                for z in range(gz)
+            ]
+            inverse_columns(gz, kb, spectra, coef_ref, tw_ref, lanes, part, re_s, im_s)
+        return carry
+
+    lax.fori_loop(0, rows // 8, columns, 0)
+
+    for lanes in lane_parts:
+
+        def row_of(z, k, part):
+            at = 2 * planes + 2 * (z * kb + k) + part
+            return jnp.broadcast_to(next_ref[at : at + 1, lanes], (8, LANES))
+
+        spectra = [[(row_of(z, k, 0), row_of(z, k, 1)) for k in range(kb)] for z in range(gz)]
+        inverse_columns(gz, kb, spectra, coef_ref, tw_ref, lanes, slice(rows, rows + 8), re_s, im_s)
+
+    step = plane_chunk(planes, rows)
+    high_rows = rows + 8
+    for start in range(0, planes, step):
+        part = slice(start, start + step)
+        shape = (step * high_rows, ka)
+        field = inverse_product(re_s[part].reshape(shape), im_s[part].reshape(shape), table_ref)
+        field = field.reshape(step, high_rows, ka)
+        out_ref[part] = field[:, :rows]
+        for p in range(step):
+            row_ref[start + p : start + p + 1, :] = field[p, rows : rows + 1, :]
+
+
+def normal_product(spec, next_head, coef, nx):
+    gz, kb, _, rows, ka = spec.shape
+    planes = gz * kb
+    vmem = pl.BlockSpec(memory_space=pltpu.VMEM)
+    return pl.pallas_call(
+        normal_kernel,
+        in_specs=[vmem] * 5,
+        out_specs=[vmem] * 2,
+        out_shape=[
+            jax.ShapeDtypeStruct((planes, rows, ka), F32),
+            jax.ShapeDtypeStruct((planes, ka), F32),
+        ],
+        scratch_shapes=[pltpu.VMEM((planes, rows + 8, ka), F32)] * 2,
+        compiler_params=pltpu.CompilerParams(vmem_limit_bytes=X_GRANT),
+        cost_estimate=pl.CostEstimate(
+            flops=12 * planes * rows * ka * ka, bytes_accessed=12 * planes * rows * ka, transcendentals=0
+        ),
+        name="normal_product",
+    )(spec, next_head, coef, x_twiddle(nx, ka), jnp.asarray(x_inverse_matrix(nx, ka)))
+
+
 def border_kernel(edge_ref, head_ref, tail_ref, next_ref, prev_ref, out_ref):
     planes = tail_ref.shape[0] - 8
 
@@ -669,7 +719,7 @@
 
 
 def second_kernel(
-    gz, edge_ref, d0_ref, nd0_ref, tail_ref, prev_ref, next_ref,
+    gz, edge_ref, d0_ref, nd0_ref, nrow_ref, tail_ref, prev_ref, next_ref,
     coef_ref, tw_ref, table_ref, *refs,
 ):
     sums_refs, refs = refs[:1], refs[1:]
@@ -690,7 +740,7 @@
     for z in range(gz):
         part = slice(z * kb, (z + 1) * kb)
         here = next_ref[part, :]
-        value = here - eta * next_ref[2 * planes + z * kb : 2 * planes + (z + 1) * kb, :]
+        value = here - eta * nrow_ref[part, :]
         up = pltpu.roll(here, kb - 1, 0)
         up = jnp.where(
             row2 == kb - 1, jnp.where(lane2 == ka - 1, here, pltpu.roll(up, ka - 1, 1)), up
@@ -764,12 +814,12 @@
     put_copies(out_ref, sums_block([square, projected, slope]))
 
 
-def second_descent(edge, sums, d0, nd0, tail, prev_tail, next_head, coef, gz, nx):
+def second_descent(edge, sums, d0, nd0, nrow, tail, prev_tail, next_head, coef, gz, nx):
     planes, rows, ka = d0.shape
     vmem = pl.BlockSpec(memory_space=pltpu.VMEM)
     return pl.pallas_call(
         functools.partial(second_kernel, gz),
-        in_specs=[pl.BlockSpec(memory_space=pltpu.SMEM)] + [vmem] * 9,
+        in_specs=[pl.BlockSpec(memory_space=pltpu.SMEM)] + [vmem] * 10,
         out_specs=[vmem] * 4,
         out_shape=[
             jax.ShapeDtypeStruct((planes, rows, ka), F32),
@@ -785,7 +835,7 @@
         compiler_params=pltpu.CompilerParams(vmem_limit_bytes=X_GRANT),
         name="second_descent",
     )(
-        edge, d0, nd0, tail, prev_tail, next_head, coef,
+        edge, d0, nd0, nrow, tail, prev_tail, next_head, coef,
         x_twiddle(nx, ka), x_forward_matrix(nx, ka), sums,
     )
 
@@ -819,7 +869,7 @@
             jax.ShapeDtypeStruct(first.shape, F32),
             jax.ShapeDtypeStruct((2, 8, LANES), F32),
         ],
-        compiler_params=pltpu.CompilerParams(vmem_limit_bytes=COMBINE_GRANT),
+        compiler_params=pltpu.CompilerParams(vmem_limit_bytes=6 * MIB),
         name="combine_spectra",
     )(eta, *sums, first, second)
 
@@ -873,12 +923,13 @@
     coef = jnp.broadcast_to(coef, (3, gy, 8, ka))
 
     spec = to_devices(y_inverse(data, rows, gz, gy))
-    d0, nd0, head, tail, first = middle(spec, coef, nx)
+    d0, head, tail, first = middle(spec, coef, nx)
     next_head = lax.ppermute(head, ("gz", "gy"), up)
     prev_tail = lax.ppermute(tail, ("gz", "gy"), down)
     sums = to_chips(border_sums(edge, head, tail, next_head, prev_tail, gy))
+    nd0, nrow = normal_product(first, next_head, coef, nx)
     d1, eta, sums, second = second_descent(
-        edge, sums, d0, nd0, tail, prev_tail, next_head, coef, gz, nx
+        edge, sums, d0, nd0, nrow, tail, prev_tail, next_head, coef, gz, nx
     )
     sums = everywhere(sums)
     flat_shape = (devices, 2, rows, ka)

time: 294 us -> 294 us (level)
  blocking collectives: 24.8 us -> 14.2 us
  starting transfers between devices: 14.3 us -> 22 us
  local copies, waits for them, and re-layouts: 19.9 us -> 27.2 us
  Pallas kernels: 53 us -> 48.7 us
    all_to_all x2 -> x1, blocking collectives: 24.8 us -> 14.2 us  [to_chips(): return lax.all_to_all(parts, 'gy', 0, 0, tiled=True)]
    unnamed x18 -> x36, local copies, waits for them, and re-layouts: 5.35 us -> 12.7 us
    all_to_all x0 -> x1, starting transfers between devices: none -> 6.5 us  [to_chips(): return lax.all_to_all(parts, 'gy', 0, 0, tiled=True)]
    pallas_call x1, Pallas kernels: 7.81 us -> 1.85 us  [combine_spectra(): pl.pallas_call(functools.partial(combine_kernel, gz), grid=(planes // cou...]
    pallas_call x0 -> x1, Pallas kernels: none -> 4.35 us  [normal_product(): pl.pallas_call(normal_kernel, in_specs=[vmem] * 5, out_specs=[vmem] * 2,...]
    pallas_call x1, Pallas kernels: 17.7 us -> 14.1 us  [middle(): pl.pallas_call(middle_kernel, in_specs=[pl.BlockSpec(memory_space=pltpu.H...]
  transfers between devices with their start and end apart: 6 -> 7, of which waited for: 5 -> 5; matrix products, arithmetic and copies ran while one was open for 7% -> 7% of each run, Pallas kernels for 0% -> 1%
where the time goes in v9:
time: 294 us; the launch traced here: 293 us
  waiting for transfers between devices  175 us (60%)
  Pallas kernels  48.7 us (17%)
  local copies, waits for them, and re-layouts  27.2 us (9%)
  starting transfers between devices  22 us (7%)
  blocking collectives  14.2 us (5%)
  other arithmetic  4.57 us (2%)
    all_to_all x2, waiting for transfers between devices, to_devices(): lax.all_to_all(parts.reshape(gz * gy, *rest), ('gz', 'gy'), 0, 0, tiled=T...  171 us
    all_to_all x1, blocking collectives, to_chips(): return lax.all_to_all(parts, 'gy', 0, 0, tiled=True)  14.2 us
    pallas_call x1, Pallas kernels, middle(): pl.pallas_call(middle_kernel, in_specs=[pl.BlockSpec(memory_space=pltpu.H...  14.1 us
    unnamed x36, local copies, waits for them, and re-layouts  12.7 us
    all_to_all x2, starting transfers between devices, to_devices(): lax.all_to_all(parts.reshape(gz * gy, *rest), ('gz', 'gy'), 0, 0, tiled=T...  11.2 us
    pallas_call x1, Pallas kernels, y_forward(): pl.pallas_call(y_forward_kernel, in_specs=[hbm] * 4, out_specs=hbm, out_s...  10.8 us
    pallas_call x1, Pallas kernels, y_inverse(): pl.pallas_call(y_inverse_kernel, in_specs=[hbm] * 3, out_specs=hbm, out_s...  8.11 us
    pallas_call x1, Pallas kernels, second_descent(): pl.pallas_call(functools.partial(second_kernel, gz), in_specs=[pl.BlockSp...  7.89 us
  transfers between devices with their start and end apart: 7, of which 5 were waited for; matrix products, arithmetic and copies ran while one was open for 7% of the time, Pallas kernels for 1%

profile of v9, /device:TPU:0, one launch (start us, length us, event | category | flops | bytes accessed | tf_op | source)
XLA Modules:
  0.0 293.0 jit_solution(14484910096732342709)
XLA Ops:
  0.6 8.1 %y_inverse.1 = f32[2,16,2,64,256]{4,3,2,1,0:T(8,128)} custom-call(bf16[4,2048,128]{2,1,0:T(8,128)(2,1)} %bitcast.29, bf16[1024,512]{1,0:T(8,128)(2,1)} %constant.55.clone.table_hbm, f32[2,7,256,128]{3,2,1,0:T(8,128)} %constant.56.clone.tw_hbm), custom_call_target="tpu_custom_call" | custom-call | tf_op jit(solution)/shard_map/y_inverse/pallas_call | solution.py:272
  8.8 7.4 %all-to-all-start = ((f32[32,2,64,256]{3,2,1,0:T(8,128)}), f32[32,2,64,256]{3,2,1,0:T(8,128)}, u32[]{:S(2)}, u32[]{:S(2)}) async-start(f32[32,2,64,256]{3,2,1,0:T(8,128)} %bitcast.26), calls=%async_computation | async-start | bytes 8388608 | tf_op jit(solution)/shard_map/all_to_all | solution.py:888
  16.4 96.1 %all-to-all-done = f32[32,2,64,256]{3,2,1,0:T(8,128)} async-done(((f32[32,2,64,256]{3,2,1,0:T(8,128)}), f32[32,2,64,256]{3,2,1,0:T(8,128)}, u32[]{:S(2)}, u32[]{:S(2)}) %all-to-all-start) | async-done | bytes 4194336 | tf_op jit(solution)/shard_map/all_to_all | solution.py:888
  112.5 1.0 copy-done.9
  113.6 14.1 %middle.1 = (f32[32,64,256]{2,1,0:T(8,128)S(1)}, f32[136,256]{1,0:T(8,128)}, f32[40,256]{1,0:T(8,128)S(1)}, f32[2,16,2,64,256]{4,3,2,1,0:T(8,128)S(1)}) custom-call(f32[2,16,2,64,256]{4,3,2,1,0:T(8,128)} %bitcast.5.spec_hbm, f32[3,16,8,256]{3,2,1,0:T(8,128)S(1)} %broadcast_in_dim.24.coef_ref, f32[2,16,8,256]{3,2,1,0:T(8,128)S(1)} %copy-done.8, ...), custom_call_target="tpu_custom_call" | custom-call | tf_op jit(solution)/shard_map/middle/pallas_call | solution.py:609
  127.7 2.0 copy-done.1
  129.7 1.3 collective-permute-start
  131.0 3.0 %collective-permute-start.1 = (f32[40,256]{1,0:T(8,128)S(1)}, f32[40,256]{1,0:T(8,128)S(1)}, u32[]{:S(2)}, u32[]{:S(2)}) collective-permute-start(f32[40,256]{1,0:T(8,128)S(1)} %get-tuple-element.19.tail_ref), channel_id=1, source_target_pairs={{0,16},{16,1},{1,17},{17,2},{2,18},{18,3},{3,19},{19,4},{4,20},{20... | collective-permute-start | bytes 122888 | tf_op jit(solution)/shard_map/ppermute | solution.py:928
  134.1 0.8 collective-permute-done.1.prev_ref
  134.9 1.6 border_sums.1
  136.5 6.5 %all-to-all-start.1 = ((f32[16,8,128]{2,1,0:T(8,128)}), f32[16,8,128]{2,1,0:T(8,128)S(1)}, u32[]{:S(2)}, u32[]{:S(2)}) async-start(f32[16,8,128]{2,1,0:T(8,128)} %border_sums.1), calls=%async_computation.1 | async-start | bytes 131072 | tf_op jit(solution)/shard_map/all_to_all | solution.py:883
  143.0 2.2 copy-done.2
  145.2 1.0 copy-done.10
  146.2 4.4 %normal_product.1 = (f32[32,64,256]{2,1,0:T(8,128)S(1)}, f32[32,256]{1,0:T(8,128)S(1)}) custom-call(f32[2,16,2,64,256]{4,3,2,1,0:T(8,128)S(1)} %copy-done.2, f32[136,256]{1,0:T(8,128)S(1)} %collective-permute-done.next_ref, f32[3,16,8,256]{3,2,1,0:T(8,128)S(1)} %broadcast_in_dim.24.coef_ref, f32[2,16,8,256]{3,2,1,0:T(8,128)S(1)} %copy-done.8, ...), custom_call_target="tpu_custom_call" | custom-call | flops 1610612736 | bytes 6291456 | tf_op jit(solution)/shard_map/normal_product/pallas_call | solution.py:674
  150.6 1.3 copy-done.6
  151.9 1.6 copy-done.7
  153.5 0.8 copy-done.12
  154.3 0.6 copy-done.14
  154.9 7.9 %second_descent.1 = (f32[32,64,256]{2,1,0:T(8,128)S(1)}, f32[8,128]{1,0:T(8,128)S(1)}, f32[16,8,128]{2,1,0:T(8,128)S(1)}, f32[2,16,2,64,256]{4,3,2,1,0:T(8,128)S(1)}) custom-call(s32[3]{0:T(128)S(1)} %copy-done.14, f32[32,64,256]{2,1,0:T(8,128)S(1)} %get-tuple-element.14.d0_ref, f32[32,64,256]{2,1,0:T(8,128)S(1)} %copy-done.7, ...), custom_call_target="tpu_custom_call" | custom-call | tf_op jit(solution)/shard_map/second_descent/pallas_call | solution.py:820
  162.9 14.2 %all_to_all.20.refs_0_ = f32[16,8,128]{2,1,0:T(8,128)S(1)} all-to-all(f32[16,8,128]{2,1,0:T(8,128)S(1)} %get-tuple-element.21), channel_id=1, replica_groups=mesh['gz'=2,'gy'=16] {'gy'}, dimensions={0} | all-to-all | bytes 131072 | tf_op jit(solution)/shard_map/all_to_all | solution.py:883
  177.1 1.3 collective-permute-done.2.refs_1_
  178.3 1.9 combine_spectra.1
  180.2 2.0 copy-done
  182.2 3.8 %all-to-all-start.3 = ((f32[32,2,64,256]{3,2,1,0:T(8,128)}), f32[32,2,64,256]{3,2,1,0:T(8,128)}, u32[]{:S(2)}, u32[]{:S(2)}) async-start(f32[32,2,64,256]{3,2,1,0:T(8,128)} %copy-done), calls=%async_computation.3 | async-start | bytes 8388608 | tf_op jit(solution)/shard_map/all_to_all | solution.py:888
  186.6 4.5 %add_negate_fusion = f32[32,64,256]{2,1,0:T(8,128)} fusion(f32[32,64,256]{2,1,0:T(8,128)} %copy-done.5, f32[32,64,256]{2,1,0:T(8,128)S(1)} %get-tuple-element.14.d0_ref, f32[]{:T(128)} %bitcast.12, f32[]{:T(128)} %bitcast.11), kind=kLoop, calls=%fused_computation | loop fusion | flops 2097152 | bytes 6291464 | tf_op jit(solution)/shard_map/neg | solution.py:939
  191.1 4.9 %copy.20 = f32[2,16,64,256]{2,1,3,0:T(8,128)} copy(f32[2,16,64,256]{3,2,1,0:T(8,128)} %bitcast.28) | data formatting | bytes 4194304 | tf_op jit(solution)/shard_map/reshape | solution.py:940
  195.9 3.8 %constant_dynamic-slice_fusion = (f32[1,64,4096]{1,2,0:T(8,128)}, f32[1,64,4096]{1,2,0:T(8,128)S(1)}) fusion(f32[2,64,4096]{1,2,0:T(8,128)} %bitcast.27, s32[]{:T(128)S(6)} %select_n.29, s32[]{:T(128)S(6)} %select_n.27), kind=kLoop, calls=%fused_computation.6 | loop fusion | bytes 4194312 | tf_op jit(solution)/shard_map/jit(dynamic_index_in_dim)/dynamic_slice | solution.py:942
  199.7 3.1 %copy.22 = f32[1,64,4096]{2,1,0:T(8,128)} copy(f32[1,64,4096]{1,2,0:T(8,128)} %get-tuple-element.28) | data formatting | bytes 2097152 | tf_op jit(solution)/shard_map/jit(dynamic_index_in_dim)/dynamic_slice | solution.py:942
  203.7 2.1 collective-permute-done.3
  205.9 1.3 bitcast_dynamic-update-slice_fusion
  207.2 74.9 %all-to-all-done.3 = f32[32,2,64,256]{3,2,1,0:T(8,128)} async-done(((f32[32,2,64,256]{3,2,1,0:T(8,128)}), f32[32,2,64,256]{3,2,1,0:T(8,128)}, u32[]{:S(2)}, u32[]{:S(2)}) %all-to-all-start.3) | async-done | bytes 4194336 | tf_op jit(solution)/shard_map/all_to_all | solution.py:888
  282.0 10.8 %y_forward.1 = f32[4,8,256,128]{3,2,1,0:T(8,128)} custom-call(f32[2,16,2,64,256]{4,3,2,1,0:T(8,128)} %bitcast.20.spec_hbm, bf16[4,2048,128]{2,1,0:T(8,128)(2,1)} %bitcast.30, bf16[1024,512]{1,0:T(8,128)(2,1)} %constant.60.clone.table_hbm, f32[2,7,256,128]{3,2,1,0:T(8,128)} %constant.56.clone.tw_hbm), custom_call_target="tpu_custom_call" | custom-call | tf_op jit(solution)/shard_map/y_forward/pallas_call | solution.py:386
  (44 shorter events, 1.6 us)
Async XLA Ops:
  8.7 7.5 %copy-start.16 = (f32[2,4096]{1,0:T(2,128)S(1)}, f32[2,4096]{1,0:T(2,128)}, u32[]{:S(2)}) copy-start(f32[2,4096]{1,0:T(2,128)} %param.16) | copy-start | bytes 98308
  8.8 7.5 %copy-start.17 = (s32[4096]{0:T(1024)S(1)}, s32[4096]{0:T(1024)}, u32[]{:S(2)}) copy-start(s32[4096]{0:T(1024)} %param.15) | copy-start | bytes 49156
  8.8 103.7 %copy-start.4 = (bf16[256,1024]{1,0:T(8,128)(2,1)S(1)}, bf16[256,1024]{1,0:T(8,128)(2,1)}, u32[]{:S(2)}) copy-start(bf16[256,1024]{1,0:T(8,128)(2,1)} %constant.59.clone.forward_ref.table_ref) | copy-start | bytes 1572868
  8.8 103.7 %copy-start.8 = (f32[2,16,8,256]{3,2,1,0:T(8,128)S(1)}, f32[2,16,8,256]{3,2,1,0:T(8,128)}, u32[]{:S(2)}) copy-start(f32[2,16,8,256]{3,2,1,0:T(8,128)} %constant.57.clone.tw_ref) | copy-start | bytes 786436
  8.8 103.7 %all-to-all-start = ((f32[32,2,64,256]{3,2,1,0:T(8,128)}), f32[32,2,64,256]{3,2,1,0:T(8,128)}, u32[]{:S(2)}, u32[]{:S(2)}) async-start(f32[32,2,64,256]{3,2,1,0:T(8,128)} %bitcast.26), calls=%async_computation | async-start | bytes 8388608 | tf_op jit(solution)/shard_map/all_to_all | solution.py:888
  112.5 1.0 copy-start.9
  127.7 2.0 copy-start.1
  129.7 5.2 %collective-permute-start = (f32[136,256]{1,0:T(8,128)}, f32[136,256]{1,0:T(8,128)S(1)}, u32[]{:S(2)}, u32[]{:S(2)}) collective-permute-start(f32[136,256]{1,0:T(8,128)} %get-tuple-element.16.head_ref), channel_id=1, source_target_pairs={{16,0},{1,16},{17,1},{2,17},{18,2},{3,18},{19,3},{4,19},{20,4},{5,... | collective-permute-start | bytes 417800 | tf_op jit(solution)/shard_map/ppermute | solution.py:927
  131.0 3.9 %collective-permute-start.1 = (f32[40,256]{1,0:T(8,128)S(1)}, f32[40,256]{1,0:T(8,128)S(1)}, u32[]{:S(2)}, u32[]{:S(2)}) collective-permute-start(f32[40,256]{1,0:T(8,128)S(1)} %get-tuple-element.19.tail_ref), channel_id=1, source_target_pairs={{0,16},{16,1},{1,17},{17,2},{2,18},{18,3},{3,19},{19,4},{4,20},{20... | collective-permute-start | bytes 122888 | tf_op jit(solution)/shard_map/ppermute | solution.py:928
  134.1 2.4 copy-start.13
  134.9 1.6 copy-start.11
  136.5 15.4 %all-to-all-start.1 = ((f32[16,8,128]{2,1,0:T(8,128)}), f32[16,8,128]{2,1,0:T(8,128)S(1)}, u32[]{:S(2)}, u32[]{:S(2)}) async-start(f32[16,8,128]{2,1,0:T(8,128)} %border_sums.1), calls=%async_computation.1 | async-start | bytes 131072 | tf_op jit(solution)/shard_map/all_to_all | solution.py:883
  143.0 2.2 copy-start.2
  145.2 1.0 copy-start.10
  150.6 1.3 copy-start.6
  151.9 1.6 copy-start.7
  153.5 0.8 copy-start.12
  154.3 0.6 copy-start.14
  154.9 23.4 %copy-start.3 = (f32[2,16,2,64,256]{4,3,2,1,0:T(8,128)S(1)}, f32[2,16,2,64,256]{4,3,2,1,0:T(8,128)}, u32[]{:S(2)}) copy-start(f32[2,16,2,64,256]{4,3,2,1,0:T(8,128)} %copy-done.1) | copy-start | bytes 12582916
  162.8 17.4 %copy-start.5 = (f32[32,64,256]{2,1,0:T(8,128)}, f32[32,64,256]{2,1,0:T(8,128)S(1)}, u32[]{:S(2)}) copy-start(f32[32,64,256]{2,1,0:T(8,128)S(1)} %get-tuple-element.24) | copy-start | bytes 6291460
  177.1 1.3 collective-permute-start.2
  180.2 2.0 copy-start
  182.2 99.8 %all-to-all-start.3 = ((f32[32,2,64,256]{3,2,1,0:T(8,128)}), f32[32,2,64,256]{3,2,1,0:T(8,128)}, u32[]{:S(2)}, u32[]{:S(2)}) async-start(f32[32,2,64,256]{3,2,1,0:T(8,128)} %copy-done), calls=%async_computation.3 | async-start | bytes 8388608 | tf_op jit(solution)/shard_map/all_to_all | solution.py:888
  202.9 3.0 %collective-permute-start.3 = (f32[64,4096]{1,0:T(8,128)}, f32[64,4096]{1,0:T(8,128)}, u32[]{:S(2)}, u32[]{:S(2)}) collective-permute-start(f32[64,4096]{1,0:T(8,128)} %bitcast.17), channel_id=1, source_target_pairs={{0,16},{16,0},{1,17},{17,1},{2,18},{18,2},{3,19},{19,3},{4,20},{20... | collective-permute-start | bytes 3145736 | tf_op jit(solution)/shard_map/ppermute | solution.py:879
  207.2 85.7 %copy-start.15 = (f32[2,64,4096]{2,1,0:T(8,128)}, f32[2,64,4096]{2,1,0:T(8,128)S(1)}, u32[]{:S(2)}) copy-start(f32[2,64,4096]{2,1,0:T(8,128)S(1)} %bitcast_dynamic-update-slice_fusion) | copy-start | bytes 6291460

commit v10 on v8

--- a/solution.py
+++ b/solution.py
@@ -19,20 +19,12 @@
 MIB = 1024 * 1024
 Y_GRANT = 56 * MIB
 X_GRANT = 20 * MIB
-COMBINE_GRANT = 53 * MIB
 
 
 def dft_parts(length, scale):
     index = np.arange(length)
     angles = 2.0 * np.pi / length * (index[:, None] * index[None, :] % length)
     return np.cos(angles) * scale, np.sin(angles) * scale
-
-
-def two_parts(table):
-    table = jnp.asarray(table.astype(np.float32))
-    high = table.astype(BF16)
-    low = (table - high.astype(F32)).astype(BF16)
-    return high, low
 
 
 def host_parts(table):
@@ -49,7 +41,8 @@
         table = np.block([[cos, sin], [-sin, cos]])
     else:
         table = np.block([[cos, -sin], [sin, cos]])
-    return jnp.asarray(np.concatenate(host_parts(table), axis=0))
+    high, low = host_parts(table)
+    return jnp.asarray(np.concatenate([high, high, low] if forward else [high, low], axis=1))
 
 
 def y_twiddle(ny):
@@ -61,12 +54,14 @@
 
 def x_inverse_matrix(nx, ka):
     cos, sin = dft_parts(ka, nx**-0.5)
-    return np.concatenate(host_parts(np.concatenate([cos, -sin], axis=0)), axis=1)
+    high, low = host_parts(np.concatenate([cos, -sin], axis=0))
+    return jnp.asarray(np.concatenate([high, high, low], axis=0))
 
 
 def x_forward_matrix(nx, ka):
     cos, sin = dft_parts(ka, nx**-0.5)
-    return jnp.asarray(np.concatenate(host_parts(np.concatenate([cos, -sin], axis=1)), axis=1))
+    high, low = host_parts(np.concatenate([cos, -sin], axis=1))
+    return jnp.asarray(np.concatenate([high, high, low], axis=0))
 
 
 def x_twiddle(nx, ka):
@@ -227,8 +222,8 @@
                 jnp.concatenate([s[pl.ds(k + d, n, stride=YR), :] for d in range(2)], axis=1)
                 for s in (re_s, im_s)
             ]
-            both = dot(table_ref[...], jnp.concatenate(pieces, axis=0).astype(BF16))
-            both = both[: 2 * n] + both[2 * n :]
+            piece = jnp.concatenate(pieces, axis=0).astype(BF16)
+            both = dot(table_ref[...], jnp.concatenate([piece, piece], axis=0))
             for d in range(2):
                 mix_s[k + d] = both[:, d * LANES : (d + 1) * LANES]
 
@@ -277,7 +272,7 @@
         out_shape=jax.ShapeDtypeStruct((gz, gy, 2, rows, ka), F32),
         scratch_shapes=[
             pltpu.VMEM((blocks, ny, width), BF16),
-            pltpu.VMEM((4 * n, 2 * n), BF16),
+            pltpu.VMEM((2 * n, 4 * n), BF16),
             pltpu.VMEM((2, YR - 1, n, LANES), F32),
             pltpu.VMEM((gz, gy, 2, rows, ka), F32),
             pltpu.VMEM((ny, LANES), F32),
@@ -341,8 +336,7 @@
                 for p in range(2)
             ]
             high, low = split2(jnp.concatenate(pieces, axis=0))
-            both = dot(table_ref[...], high)
-            both = both[: 2 * n] + both[2 * n :] + dot(table_ref[: 2 * n], low)
+            both = dot(table_ref[...], jnp.concatenate([high, low, high], axis=0))
             for d in range(2):
                 mix_s[k + d] = both[:, d * LANES : (d + 1) * LANES]
         if chunk == 0:
@@ -392,7 +386,7 @@
         scratch_shapes=[
             pltpu.VMEM((blocks // 2, *spec.shape[:-1], LANES), F32),
             pltpu.VMEM((blocks, ny, width), BF16),
-            pltpu.VMEM((4 * n, 2 * n), BF16),
+            pltpu.VMEM((2 * n, 6 * n), BF16),
             pltpu.VMEM((2, YR - 1, n, LANES), F32),
             pltpu.VMEM((blocks, YR, n, width), F32),
             pltpu.VMEM((YR, 2 * n, LANES), F32),
@@ -459,17 +453,14 @@
 
 
 def inverse_product(re, im, table_ref):
-    ka = re.shape[1]
     high, low = split2(jnp.concatenate([re, im], axis=1))
-    value = dot(high, table_ref[...])
-    return value[:, :ka] + value[:, ka:] + dot(low, table_ref[:, :ka])
+    return dot(jnp.concatenate([high, low, high], axis=1), table_ref[...])
 
 
 def forward_product(field, table_ref):
     ka = field.shape[1]
     high, low = split2(field)
-    value = dot(high, table_ref[...])
-    value = value[:, : 2 * ka] + value[:, 2 * ka :] + dot(low, table_ref[:, : 2 * ka])
+    value = dot(jnp.concatenate([high, low, high], axis=1), table_ref[...])
     return value[:, :ka], value[:, ka:]
 
 
@@ -633,7 +624,7 @@
         compiler_params=pltpu.CompilerParams(vmem_limit_bytes=X_GRANT),
         name="middle",
     )(
-        spec, coef, x_twiddle(nx, ka), jnp.asarray(x_inverse_matrix(nx, ka)),
+        spec, coef, x_twiddle(nx, ka), x_inverse_matrix(nx, ka),
         x_forward_matrix(nx, ka),
     )
 
@@ -819,7 +810,7 @@
             jax.ShapeDtypeStruct(first.shape, F32),
             jax.ShapeDtypeStruct((2, 8, LANES), F32),
         ],
-        compiler_params=pltpu.CompilerParams(vmem_limit_bytes=COMBINE_GRANT),
+        compiler_params=pltpu.CompilerParams(vmem_limit_bytes=6 * MIB),
         name="combine_spectra",
     )(eta, *sums, first, second)
 

time: 294 us -> 286 us (0.973)
  Pallas kernels: 53 us -> 47.3 us
    pallas_call x1, Pallas kernels: 7.81 us -> 1.85 us  [combine_spectra(): pl.pallas_call(functools.partial(combine_kernel, gz), grid=(planes // cou...]
where the time goes in v10:
time: 286 us
  waiting for transfers between devices  176 us (62%)
  Pallas kernels  47.3 us (17%)
  blocking collectives  24.8 us (9%)
  local copies, waits for them, and re-layouts  17.7 us (6%)
  starting transfers between devices  14.3 us (5%)
  other arithmetic  4.66 us (2%)
    all_to_all x2, waiting for transfers between devices, to_devices(): lax.all_to_all(parts.reshape(gz * gy, *rest), ('gz', 'gy'), 0, 0, tiled=T...  171 us
    all_to_all x2, blocking collectives, to_chips(): return lax.all_to_all(parts, 'gy', 0, 0, tiled=True)  24.8 us
    pallas_call x1, Pallas kernels, middle(): pl.pallas_call(middle_kernel, in_specs=[pl.BlockSpec(memory_space=pltpu.H...  17.7 us
    pallas_call x1, Pallas kernels, y_forward(): pl.pallas_call(y_forward_kernel, in_specs=[hbm] * 4, out_specs=hbm, out_s...  11.1 us
    all_to_all x2, starting transfers between devices, to_devices(): lax.all_to_all(parts.reshape(gz * gy, *rest), ('gz', 'gy'), 0, 0, tiled=T...  11 us
    pallas_call x1, Pallas kernels, y_inverse(): pl.pallas_call(y_inverse_kernel, in_specs=[hbm] * 3, out_specs=hbm, out_s...  8.21 us
    pallas_call x1, Pallas kernels, second_descent(): pl.pallas_call(functools.partial(second_kernel, gz), in_specs=[pl.BlockSp...  7.87 us
    dynamic_slice x3, local copies, waits for them, and re-layouts, shards(): lax.dynamic_index_in_dim(volume, lax.rem(core + r, gz), 0, False)  7.54 us
  transfers between devices with their start and end apart: 6, of which 5 were waited for; matrix products, arithmetic and copies ran while one was open for 7% of the time, Pallas kernels for 0%

profile of v10, /device:TPU:0, one launch (start us, length us, event | category | flops | bytes accessed | tf_op | source)
XLA Modules:
  0.0 286.0 jit_solution(12709989630800078717)
XLA Ops:
  0.6 8.2 %y_inverse.1 = f32[2,16,2,64,256]{4,3,2,1,0:T(8,128)} custom-call(bf16[4,2048,128]{2,1,0:T(8,128)(2,1)} %bitcast.29, bf16[512,1024]{1,0:T(8,128)(2,1)} %constant.55.clone.table_hbm, f32[2,7,256,128]{3,2,1,0:T(8,128)} %constant.56.clone.tw_hbm), custom_call_target="tpu_custom_call" | custom-call | tf_op jit(solution)/shard_map/y_inverse/pallas_call | solution.py:268
  8.9 0.0 copy-start.1
  8.9 7.4 %all-to-all-start = ((f32[32,2,64,256]{3,2,1,0:T(8,128)}), f32[32,2,64,256]{3,2,1,0:T(8,128)}, u32[]{:S(2)}, u32[]{:S(2)}) async-start(f32[32,2,64,256]{3,2,1,0:T(8,128)} %bitcast.26), calls=%async_computation | async-start | bytes 8388608 | tf_op jit(solution)/shard_map/all_to_all | solution.py:829
  16.5 96.1 %all-to-all-done = f32[32,2,64,256]{3,2,1,0:T(8,128)} async-done(((f32[32,2,64,256]{3,2,1,0:T(8,128)}), f32[32,2,64,256]{3,2,1,0:T(8,128)}, u32[]{:S(2)}, u32[]{:S(2)}) %all-to-all-start) | async-done | bytes 4194336 | tf_op jit(solution)/shard_map/all_to_all | solution.py:829
  112.6 1.1 copy-done.4
  113.8 17.7 %middle.1 = (f32[32,64,256]{2,1,0:T(8,128)S(1)}, f32[32,64,256]{2,1,0:T(8,128)S(1)}, f32[104,256]{1,0:T(8,128)S(1)}, f32[40,256]{1,0:T(8,128)S(1)}, f32[2,16,2,64,256]{4,3,2,1,0:T(8,128)S(1)}) custom-call(f32[2,16,2,64,256]{4,3,2,1,0:T(8,128)} %bitcast.5.spec_hbm, f32[3,16,8,256]{3,2,1,0:T(8,128)S(1)} %broadcast_in_dim.24.coef_ref, ...), custom_call_target="tpu_custom_call" | custom-call | tf_op jit(solution)/shard_map/middle/pallas_call | solution.py:608
  131.5 1.8 collective-permute-start
  133.3 1.3 collective-permute-start.1
  134.6 0.1 pad_add_fusion.edge_ref
  134.7 1.8 collective-permute-done.1.next_ref
  136.5 0.6 border_sums.1
  137.0 14.6 %all_to_all.20.refs_0_ = f32[16,8,128]{2,1,0:T(8,128)S(1)} all-to-all(f32[16,8,128]{2,1,0:T(8,128)S(1)} %border_sums.1), channel_id=1, replica_groups=mesh['gz'=2,'gy'=16] {'gy'}, dimensions={0} | all-to-all | bytes 131072 | tf_op jit(solution)/shard_map/all_to_all | solution.py:824
  151.7 7.9 %second_descent.1 = (f32[32,64,256]{2,1,0:T(8,128)S(1)}, f32[8,128]{1,0:T(8,128)S(1)}, f32[16,8,128]{2,1,0:T(8,128)S(1)}, f32[2,16,2,64,256]{4,3,2,1,0:T(8,128)S(1)}) custom-call(s32[3]{0:T(128)S(1)} %pad_add_fusion.edge_ref, f32[32,64,256]{2,1,0:T(8,128)S(1)} %get-tuple-element.13.d0_ref, f32[32,64,256]{2,1,0:T(8,128)S(1)} %get-tuple-element.14.nd0_ref, ...), custom_call_target="tpu_custom_call" | custom-call | tf_op jit(solution)/shard_map/second_descent/pallas_call | solution.py:761
  159.6 10.2 %all_to_all.21.refs_0_ = f32[16,8,128]{2,1,0:T(8,128)S(1)} all-to-all(f32[16,8,128]{2,1,0:T(8,128)S(1)} %get-tuple-element.18), channel_id=1, replica_groups=mesh['gz'=2,'gy'=16] {'gy'}, dimensions={0} | all-to-all | bytes 131072 | tf_op jit(solution)/shard_map/all_to_all | solution.py:824
  169.8 0.2 collective-permute-start.2
  169.9 1.1 collective-permute-done.2.refs_1_
  171.0 1.9 combine_spectra.1
  172.9 2.0 copy-done
  174.9 3.6 %all-to-all-start.3 = ((f32[32,2,64,256]{3,2,1,0:T(8,128)}), f32[32,2,64,256]{3,2,1,0:T(8,128)}, u32[]{:S(2)}, u32[]{:S(2)}) async-start(f32[32,2,64,256]{3,2,1,0:T(8,128)} %copy-done), calls=%async_computation.3 | async-start | bytes 8388608 | tf_op jit(solution)/shard_map/all_to_all | solution.py:829
  178.5 0.5 fusion.2
  179.0 4.6 %add_negate_fusion = f32[32,64,256]{2,1,0:T(8,128)} fusion(f32[32,64,256]{2,1,0:T(8,128)} %copy-done.2, f32[32,64,256]{2,1,0:T(8,128)S(1)} %get-tuple-element.13.d0_ref, f32[]{:T(128)} %bitcast.12, f32[]{:T(128)} %bitcast.11), kind=kLoop, calls=%fused_computation | loop fusion | flops 2097152 | bytes 6291464 | tf_op jit(solution)/shard_map/neg | solution.py:879
  183.6 4.9 %copy.18 = f32[2,16,64,256]{2,1,3,0:T(8,128)} copy(f32[2,16,64,256]{3,2,1,0:T(8,128)} %bitcast.28) | data formatting | bytes 4194304 | tf_op jit(solution)/shard_map/reshape | solution.py:880
  188.4 3.8 %constant_dynamic-slice_fusion = (f32[1,64,4096]{1,2,0:T(8,128)}, f32[1,64,4096]{1,2,0:T(8,128)S(1)}) fusion(f32[2,64,4096]{1,2,0:T(8,128)} %bitcast.27, s32[]{:T(128)S(6)} %select_n.29, s32[]{:T(128)S(6)} %select_n.27), kind=kLoop, calls=%fused_computation.6 | loop fusion | bytes 4194312 | tf_op jit(solution)/shard_map/jit(dynamic_index_in_dim)/dynamic_slice | solution.py:882
  192.3 3.1 %copy.20 = f32[1,64,4096]{2,1,0:T(8,128)} copy(f32[1,64,4096]{1,2,0:T(8,128)} %get-tuple-element.26) | data formatting | bytes 2097152 | tf_op jit(solution)/shard_map/jit(dynamic_index_in_dim)/dynamic_slice | solution.py:882
  195.4 0.0 collective-permute-start.3
  195.4 0.6 copy.19
  196.0 0.2 broadcast_in_dim.21
  196.2 0.1 constant_dynamic-update-slice_fusion
  196.3 2.1 collective-permute-done.3
  198.4 1.3 bitcast_dynamic-update-slice_fusion
  199.7 75.0 %all-to-all-done.3 = f32[32,2,64,256]{3,2,1,0:T(8,128)} async-done(((f32[32,2,64,256]{3,2,1,0:T(8,128)}), f32[32,2,64,256]{3,2,1,0:T(8,128)}, u32[]{:S(2)}, u32[]{:S(2)}) %all-to-all-start.3) | async-done | bytes 4194336 | tf_op jit(solution)/shard_map/all_to_all | solution.py:829
  274.7 11.1 %y_forward.1 = f32[4,8,256,128]{3,2,1,0:T(8,128)} custom-call(f32[2,16,2,64,256]{4,3,2,1,0:T(8,128)} %bitcast.20.spec_hbm, bf16[4,2048,128]{2,1,0:T(8,128)(2,1)} %bitcast.30, bf16[512,1536]{1,0:T(8,128)(2,1)} %constant.60.clone.table_hbm, f32[2,7,256,128]{3,2,1,0:T(8,128)} %constant.56.clone.tw_hbm), custom_call_target="tpu_custom_call" | custom-call | tf_op jit(solution)/shard_map/y_forward/pallas_call | solution.py:381
  (22 shorter events, 0.1 us)
Async XLA Ops:
  8.8 7.5 %copy-start.6 = (f32[2,4096]{1,0:T(2,128)S(1)}, f32[2,4096]{1,0:T(2,128)}, u32[]{:S(2)}) copy-start(f32[2,4096]{1,0:T(2,128)} %param.14) | copy-start | bytes 98308
  8.9 7.5 %copy-start.7 = (s32[4096]{0:T(1024)S(1)}, s32[4096]{0:T(1024)}, u32[]{:S(2)}) copy-start(s32[4096]{0:T(1024)} %param.13) | copy-start | bytes 49156
  8.9 103.7 %copy-start.1 = (bf16[768,512]{1,0:T(8,128)(2,1)S(1)}, bf16[768,512]{1,0:T(8,128)(2,1)}, u32[]{:S(2)}) copy-start(bf16[768,512]{1,0:T(8,128)(2,1)} %constant.59.clone.forward_ref.table_ref) | copy-start | bytes 2359300
  8.9 103.7 %copy-start.3 = (f32[2,16,8,256]{3,2,1,0:T(8,128)S(1)}, f32[2,16,8,256]{3,2,1,0:T(8,128)}, u32[]{:S(2)}) copy-start(f32[2,16,8,256]{3,2,1,0:T(8,128)} %constant.57.clone.tw_ref) | copy-start | bytes 786436
  8.9 103.7 %all-to-all-start = ((f32[32,2,64,256]{3,2,1,0:T(8,128)}), f32[32,2,64,256]{3,2,1,0:T(8,128)}, u32[]{:S(2)}, u32[]{:S(2)}) async-start(f32[32,2,64,256]{3,2,1,0:T(8,128)} %bitcast.26), calls=%async_computation | async-start | bytes 8388608 | tf_op jit(solution)/shard_map/all_to_all | solution.py:829
  112.6 1.1 copy-start.4
  131.5 3.2 %collective-permute-start = (f32[40,256]{1,0:T(8,128)S(1)}, f32[40,256]{1,0:T(8,128)S(1)}, u32[]{:S(2)}, u32[]{:S(2)}) collective-permute-start(f32[40,256]{1,0:T(8,128)S(1)} %get-tuple-element.15.tail_ref), channel_id=1, source_target_pairs={{0,16},{16,1},{1,17},{17,2},{2,18},{18,3},{3,19},{19,4},{4,20},{20... | collective-permute-start | bytes 122888 | tf_op jit(solution)/shard_map/ppermute | solution.py:869
  133.3 3.2 %collective-permute-start.1 = (f32[104,256]{1,0:T(8,128)S(1)}, f32[104,256]{1,0:T(8,128)S(1)}, u32[]{:S(2)}, u32[]{:S(2)}) collective-permute-start(f32[104,256]{1,0:T(8,128)S(1)} %get-tuple-element.16.head_ref), channel_id=1, source_target_pairs={{16,0},{1,16},{17,1},{2,17},{18,2},{3,18},{19,3},{4,19},{20,4},{5,... | collective-permute-start | bytes 319496 | tf_op jit(solution)/shard_map/ppermute | solution.py:868
  159.5 13.3 %copy-start.2 = (f32[32,64,256]{2,1,0:T(8,128)}, f32[32,64,256]{2,1,0:T(8,128)S(1)}, u32[]{:S(2)}) copy-start(f32[32,64,256]{2,1,0:T(8,128)S(1)} %get-tuple-element.22) | copy-start | bytes 6291460
  169.8 1.3 collective-permute-start.2
  172.9 2.0 copy-start
  174.9 99.8 %all-to-all-start.3 = ((f32[32,2,64,256]{3,2,1,0:T(8,128)}), f32[32,2,64,256]{3,2,1,0:T(8,128)}, u32[]{:S(2)}, u32[]{:S(2)}) async-start(f32[32,2,64,256]{3,2,1,0:T(8,128)} %copy-done), calls=%async_computation.3 | async-start | bytes 8388608 | tf_op jit(solution)/shard_map/all_to_all | solution.py:829
  195.4 3.0 %collective-permute-start.3 = (f32[64,4096]{1,0:T(8,128)}, f32[64,4096]{1,0:T(8,128)}, u32[]{:S(2)}, u32[]{:S(2)}) collective-permute-start(f32[64,4096]{1,0:T(8,128)} %bitcast.17), channel_id=1, source_target_pairs={{0,16},{16,0},{1,17},{17,1},{2,18},{18,2},{3,19},{19,3},{4,20},{20... | collective-permute-start | bytes 3145736 | tf_op jit(solution)/shard_map/ppermute | solution.py:820
  199.7 86.1 %copy-start.5 = (f32[2,64,4096]{2,1,0:T(8,128)}, f32[2,64,4096]{2,1,0:T(8,128)S(1)}, u32[]{:S(2)}) copy-start(f32[2,64,4096]{2,1,0:T(8,128)S(1)} %bitcast_dynamic-update-slice_fusion) | copy-start | bytes 6291460

commit v11 on v9

--- a/solution.py
+++ b/solution.py
@@ -25,13 +25,6 @@
     index = np.arange(length)
     angles = 2.0 * np.pi / length * (index[:, None] * index[None, :] % length)
     return np.cos(angles) * scale, np.sin(angles) * scale
-
-
-def two_parts(table):
-    table = jnp.asarray(table.astype(np.float32))
-    high = table.astype(BF16)
-    low = (table - high.astype(F32)).astype(BF16)
-    return high, low
 
 
 def host_parts(table):
@@ -200,14 +193,12 @@
     fetch_table = pltpu.make_async_copy(table_hbm, table_ref, sems.at[0])
     fetch_tw = pltpu.make_async_copy(tw_hbm, tw_ref, sems.at[1])
     fetch(0).start()
-    fetch_table.start()
-    fetch_tw.start()
-    for chunk in range(1, pairs):
-        fetch(chunk).start()
 
     for chunk in range(pairs):
         lanes = slice(chunk * LANES, (chunk + 1) * LANES)
         fetch(chunk).wait()
+        if chunk == 0:
+            fetch_table.start()
 
         def unpack(i, carry):
             part = pl.ds(pl.multiple_of(i * n, n), n)
@@ -220,6 +211,9 @@
         lax.fori_loop(0, YR, unpack, 0)
         if chunk == 0:
             fetch_table.wait()
+            fetch_tw.start()
+        if chunk + 1 < pairs:
+            fetch(chunk + 1).start()
 
         for k in range(0, YR, 2):
             pieces = [
@@ -315,10 +309,6 @@
     fetch_data = pltpu.make_async_copy(data_hbm, data_ref, sems.at[2])
     fetch(0).start()
     fetch_table.start()
-    fetch_tw.start()
-    fetch_data.start()
-    for chunk in range(1, pairs):
-        fetch(chunk).start()
 
     def rows_of(chunk, p, k):
         part = pl.ds(k, rows // YR, stride=YR)
@@ -333,6 +323,8 @@
 
         if chunk == 0:
             fetch_table.wait()
+            fetch_tw.start()
+            fetch_data.start()
 
         for k in range(0, YR, 2):
             pieces = [
@@ -347,6 +339,8 @@
         if chunk == 0:
             fetch_tw.wait()
             fetch_data.wait()
+        if chunk + 1 < pairs:
+            fetch(chunk + 1).start()
 
         def combine(i, carry):
             start = pl.multiple_of(i * 16, 16)
@@ -540,10 +534,11 @@
             inverse_columns(gz, kb, spectra, coef_ref, tw_ref, lanes, part, re_s, im_s)
         return carry
 
-    for i in range(cuts):
-        fetch(i).start()
+    fetch(0).start()
     for i in range(cuts):
         fetch(i).wait()
+        if i + 1 < cuts:
+            fetch(i + 1).start()
         lax.fori_loop(i * cut // 8, (i + 1) * cut // 8, columns_back, 0)
 
     step = plane_chunk(planes, rows)
@@ -629,7 +624,7 @@
     )
 
 
-def normal_kernel(spec_ref, next_ref, coef_ref, tw_ref, table_ref, out_ref, row_ref, re_s, im_s):
+def normal_kernel(spec_ref, coef_ref, tw_ref, table_ref, out_ref, re_s, im_s):
     gz, kb, _, rows, ka = spec_ref.shape
     planes = gz * kb
     lane_parts = [slice(start, start + LANES) for start in range(0, ka, LANES)]
@@ -646,49 +641,52 @@
 
     lax.fori_loop(0, rows // 8, columns, 0)
 
-    for lanes in lane_parts:
-
-        def row_of(z, k, part):
-            at = 2 * planes + 2 * (z * kb + k) + part
-            return jnp.broadcast_to(next_ref[at : at + 1, lanes], (8, LANES))
-
-        spectra = [[(row_of(z, k, 0), row_of(z, k, 1)) for k in range(kb)] for z in range(gz)]
-        inverse_columns(gz, kb, spectra, coef_ref, tw_ref, lanes, slice(rows, rows + 8), re_s, im_s)
-
     step = plane_chunk(planes, rows)
-    high_rows = rows + 8
+    shape = (step * rows, ka)
     for start in range(0, planes, step):
         part = slice(start, start + step)
-        shape = (step * high_rows, ka)
         field = inverse_product(re_s[part].reshape(shape), im_s[part].reshape(shape), table_ref)
-        field = field.reshape(step, high_rows, ka)
-        out_ref[part] = field[:, :rows]
-        for p in range(step):
-            row_ref[start + p : start + p + 1, :] = field[p, rows : rows + 1, :]
-
-
-def normal_product(spec, next_head, coef, nx):
+        out_ref[part] = field.reshape(step, rows, ka)
+
+
+def normal_product(spec, coef, nx):
     gz, kb, _, rows, ka = spec.shape
     planes = gz * kb
     vmem = pl.BlockSpec(memory_space=pltpu.VMEM)
     return pl.pallas_call(
         normal_kernel,
-        in_specs=[vmem] * 5,
-        out_specs=[vmem] * 2,
-        out_shape=[
-            jax.ShapeDtypeStruct((planes, rows, ka), F32),
-            jax.ShapeDtypeStruct((planes, ka), F32),
-        ],
-        scratch_shapes=[pltpu.VMEM((planes, rows + 8, ka), F32)] * 2,
+        in_specs=[vmem] * 4,
+        out_specs=vmem,
+        out_shape=jax.ShapeDtypeStruct((planes, rows, ka), F32),
+        scratch_shapes=[pltpu.VMEM((planes, rows, ka), F32)] * 2,
         compiler_params=pltpu.CompilerParams(vmem_limit_bytes=X_GRANT),
         cost_estimate=pl.CostEstimate(
             flops=12 * planes * rows * ka * ka, bytes_accessed=12 * planes * rows * ka, transcendentals=0
         ),
         name="normal_product",
-    )(spec, next_head, coef, x_twiddle(nx, ka), jnp.asarray(x_inverse_matrix(nx, ka)))
-
-
-def border_kernel(edge_ref, head_ref, tail_ref, next_ref, prev_ref, out_ref):
+    )(spec, coef, x_twiddle(nx, ka), jnp.asarray(x_inverse_matrix(nx, ka)))
+
+
+def next_normal_row(gz, next_ref, coef_ref, tw_ref, table_ref, row_s, re_s, im_s):
+    planes, ka = row_s.shape
+    kb = planes // gz
+    for start in range(0, ka, LANES):
+        lanes = slice(start, start + LANES)
+
+        def row_of(z, k, part):
+            at = 2 * planes + 2 * (z * kb + k) + part
+            return jnp.broadcast_to(next_ref[at : at + 1, lanes], (8, LANES))
+
+        spectra = [[(row_of(z, k, 0), row_of(z, k, 1)) for k in range(kb)] for z in range(gz)]
+        inverse_columns(gz, kb, spectra, coef_ref, tw_ref, lanes, slice(0, 8), re_s, im_s)
+    shape = (planes * 8, ka)
+    field = inverse_product(re_s[...].reshape(shape), im_s[...].reshape(shape), table_ref)
+    for p in range(planes):
+        row_s[p : p + 1, :] = field[8 * p : 8 * p + 1, :]
+
+
+def border_kernel(edge_ref, head_ref, tail_ref, next_ref, prev_ref, after_ref, out_ref):
+    del after_ref
     planes = tail_ref.shape[0] - 8
 
     def sums_of(ref):
@@ -706,24 +704,27 @@
     put_copies(out_ref, sums_of(tail_ref) + other + sums_block([none, none, below + above]))
 
 
-def border_sums(edge, head, tail, next_head, prev_tail, copies):
+def border_sums(edge, head, tail, next_head, prev_tail, after, copies):
     vmem = pl.BlockSpec(memory_space=pltpu.VMEM)
     return pl.pallas_call(
         border_kernel,
-        in_specs=[pl.BlockSpec(memory_space=pltpu.SMEM)] + [vmem] * 4,
+        in_specs=[pl.BlockSpec(memory_space=pltpu.SMEM)]
+        + [vmem] * 4
+        + [pl.BlockSpec(memory_space=pl.ANY)],
         out_specs=vmem,
         out_shape=jax.ShapeDtypeStruct((copies, 8, LANES), F32),
         compiler_params=pltpu.CompilerParams(vmem_limit_bytes=2 * MIB),
         name="border_sums",
-    )(edge, head, tail, next_head, prev_tail)
+    )(edge, head, tail, next_head, prev_tail, after)
 
 
 def second_kernel(
-    gz, edge_ref, d0_ref, nd0_ref, nrow_ref, tail_ref, prev_ref, next_ref,
-    coef_ref, tw_ref, table_ref, *refs,
+    gz, edge_ref, d0_ref, nd0_ref, tail_ref, prev_ref, next_ref,
+    coef_ref, tw_ref, table_ref, inverse_ref, *refs,
 ):
     sums_refs, refs = refs[:1], refs[1:]
-    d1_ref, eta_ref, out_ref, spec_ref, re_s, im_s, row_s = refs
+    d1_ref, eta_ref, out_ref, spec_ref, re_s, im_s, row_s, nrow_s, re8_s, im8_s = refs
+    next_normal_row(gz, next_ref, coef_ref, tw_ref, inverse_ref, nrow_s, re8_s, im8_s)
     planes, rows, ka = d0_ref.shape
     kb = planes // gz
     eta_here = step_of(sums_refs)
@@ -740,7 +741,7 @@
     for z in range(gz):
         part = slice(z * kb, (z + 1) * kb)
         here = next_ref[part, :]
-        value = here - eta * nrow_ref[part, :]
+        value = here - eta * nrow_s[part, :]
         up = pltpu.roll(here, kb - 1, 0)
         up = jnp.where(
             row2 == kb - 1, jnp.where(lane2 == ka - 1, here, pltpu.roll(up, ka - 1, 1)), up
@@ -814,7 +815,7 @@
     put_copies(out_ref, sums_block([square, projected, slope]))
 
 
-def second_descent(edge, sums, d0, nd0, nrow, tail, prev_tail, next_head, coef, gz, nx):
+def second_descent(edge, sums, d0, nd0, tail, prev_tail, next_head, coef, gz, nx):
     planes, rows, ka = d0.shape
     vmem = pl.BlockSpec(memory_space=pltpu.VMEM)
     return pl.pallas_call(
@@ -831,12 +832,15 @@
             pltpu.VMEM((planes, rows, ka), F32),
             pltpu.VMEM((planes, rows, ka), F32),
             pltpu.VMEM((planes, ka), F32),
+            pltpu.VMEM((planes, ka), F32),
+            pltpu.VMEM((planes, 8, ka), F32),
+            pltpu.VMEM((planes, 8, ka), F32),
         ],
         compiler_params=pltpu.CompilerParams(vmem_limit_bytes=X_GRANT),
         name="second_descent",
     )(
-        edge, d0, nd0, nrow, tail, prev_tail, next_head, coef,
-        x_twiddle(nx, ka), x_forward_matrix(nx, ka), sums,
+        edge, d0, nd0, tail, prev_tail, next_head, coef,
+        x_twiddle(nx, ka), x_forward_matrix(nx, ka), jnp.asarray(x_inverse_matrix(nx, ka)), sums,
     )
 
 
@@ -926,10 +930,10 @@
     d0, head, tail, first = middle(spec, coef, nx)
     next_head = lax.ppermute(head, ("gz", "gy"), up)
     prev_tail = lax.ppermute(tail, ("gz", "gy"), down)
-    sums = to_chips(border_sums(edge, head, tail, next_head, prev_tail, gy))
-    nd0, nrow = normal_product(first, next_head, coef, nx)
+    nd0 = normal_product(first, coef, nx)
+    sums = to_chips(border_sums(edge, head, tail, next_head, prev_tail, nd0, gy))
     d1, eta, sums, second = second_descent(
-        edge, sums, d0, nd0, nrow, tail, prev_tail, next_head, coef, gz, nx
+        edge, sums, d0, nd0, tail, prev_tail, next_head, coef, gz, nx
     )
     sums = everywhere(sums)
     flat_shape = (devices, 2, rows, ka)

time: 294 us -> 286 us (0.973)
  local copies, waits for them, and re-layouts: 27.2 us -> 16.6 us
  blocking collectives: 14.2 us -> 24.6 us
  starting transfers between devices: 22 us -> 14.1 us
    unnamed x36 -> x16, local copies, waits for them, and re-layouts: 12.7 us -> 2.04 us
    all_to_all x1 -> x2, blocking collectives: 14.2 us -> 24.6 us  [to_chips(): return lax.all_to_all(parts, 'gy', 0, 0, tiled=True)]
    all_to_all x1 -> x0, starting transfers between devices: 6.5 us -> none  [to_chips(): return lax.all_to_all(parts, 'gy', 0, 0, tiled=True)]
  transfers between devices with their start and end apart: 7 -> 6, of which waited for: 5 -> 4; matrix products, arithmetic and copies ran while one was open for 7% -> 7% of each run, Pallas kernels for 1% -> 1%
where the time goes in v11:
time: 286 us
  waiting for transfers between devices  174 us (61%)
  Pallas kernels  50.1 us (18%)
  blocking collectives  24.6 us (9%)
  local copies, waits for them, and re-layouts  16.6 us (6%)
  starting transfers between devices  14.1 us (5%)
  other arithmetic  4.65 us (2%)
    all_to_all x2, waiting for transfers between devices, to_devices(): lax.all_to_all(parts.reshape(gz * gy, *rest), ('gz', 'gy'), 0, 0, tiled=T...  171 us
    all_to_all x2, blocking collectives, to_chips(): return lax.all_to_all(parts, 'gy', 0, 0, tiled=True)  24.6 us
    pallas_call x1, Pallas kernels, middle(): pl.pallas_call(middle_kernel, in_specs=[pl.BlockSpec(memory_space=pltpu.H...  15.4 us
    all_to_all x2, starting transfers between devices, to_devices(): lax.all_to_all(parts.reshape(gz * gy, *rest), ('gz', 'gy'), 0, 0, tiled=T...  11 us
    pallas_call x1, Pallas kernels, y_forward(): pl.pallas_call(y_forward_kernel, in_specs=[hbm] * 4, out_specs=hbm, out_s...  11 us
    pallas_call x1, Pallas kernels, y_inverse(): pl.pallas_call(y_inverse_kernel, in_specs=[hbm] * 3, out_specs=hbm, out_s...  8.77 us
    pallas_call x1, Pallas kernels, second_descent(): pl.pallas_call(functools.partial(second_kernel, gz), in_specs=[pl.BlockSp...  8.41 us
    dynamic_slice x3, local copies, waits for them, and re-layouts, shards(): lax.dynamic_index_in_dim(volume, lax.rem(core + r, gz), 0, False)  7.54 us
  transfers between devices with their start and end apart: 6, of which 4 were waited for; matrix products, arithmetic and copies ran while one was open for 7% of the time, Pallas kernels for 1%

profile of v11, /device:TPU:0, one launch (start us, length us, event | category | flops | bytes accessed | tf_op | source)
XLA Modules:
  0.0 285.6 jit_solution(9408072606203770800)
XLA Ops:
  0.6 8.8 %y_inverse.1 = f32[2,16,2,64,256]{4,3,2,1,0:T(8,128)} custom-call(bf16[4,2048,128]{2,1,0:T(8,128)(2,1)} %bitcast.29, bf16[1024,512]{1,0:T(8,128)(2,1)} %constant.55.clone.table_hbm, f32[2,7,256,128]{3,2,1,0:T(8,128)} %constant.56.clone.tw_hbm), custom_call_target="tpu_custom_call" | custom-call | tf_op jit(solution)/shard_map/y_inverse/pallas_call | solution.py:266
  9.4 0.0 copy-start
  9.4 0.0 copy-start.2
  9.5 0.0 copy-start.3
  9.5 7.4 %all-to-all-start = ((f32[32,2,64,256]{3,2,1,0:T(8,128)}), f32[32,2,64,256]{3,2,1,0:T(8,128)}, u32[]{:S(2)}, u32[]{:S(2)}) async-start(f32[32,2,64,256]{3,2,1,0:T(8,128)} %bitcast.26), calls=%async_computation | async-start | bytes 8388608 | tf_op jit(solution)/shard_map/all_to_all | solution.py:892
  17.1 0.1 pad_add_fusion.edge_ref
  17.1 96.0 %all-to-all-done = f32[32,2,64,256]{3,2,1,0:T(8,128)} async-done(((f32[32,2,64,256]{3,2,1,0:T(8,128)}), f32[32,2,64,256]{3,2,1,0:T(8,128)}, u32[]{:S(2)}, u32[]{:S(2)}) %all-to-all-start) | async-done | bytes 4194336 | tf_op jit(solution)/shard_map/all_to_all | solution.py:892
  113.2 15.4 %middle.1 = (f32[32,64,256]{2,1,0:T(8,128)S(1)}, f32[136,256]{1,0:T(8,128)S(1)}, f32[40,256]{1,0:T(8,128)S(1)}, f32[2,16,2,64,256]{4,3,2,1,0:T(8,128)S(1)}) custom-call(f32[2,16,2,64,256]{4,3,2,1,0:T(8,128)} %bitcast.5.spec_hbm, f32[3,16,8,256]{3,2,1,0:T(8,128)S(1)} %broadcast_in_dim.24.coef_ref, f32[2,16,8,256]{3,2,1,0:T(8,128)S(1)} %copy-done.2, ...), custom_call_target="tpu_custom_call" | custom-call | tf_op jit(solution)/shard_map/middle/pallas_call | solution.py:604
  128.6 1.8 collective-permute-start
  130.4 1.3 collective-permute-start.1
  131.7 4.0 %normal_product.1.after_ref.nd0_ref = f32[32,64,256]{2,1,0:T(8,128)S(1)} custom-call(f32[2,16,2,64,256]{4,3,2,1,0:T(8,128)S(1)} %get-tuple-element.13.spec_ref, f32[3,16,8,256]{3,2,1,0:T(8,128)S(1)} %broadcast_in_dim.24.coef_ref, f32[2,16,8,256]{3,2,1,0:T(8,128)S(1)} %copy-done.2, bf16[512,512]{1,0:T(8,128)(2,1)S(1)} %copy-done), custom_call_target="tpu_custom_call" | custom-call | flops 1610612736 | bytes 6291456 | tf_op jit(solution)/shard_map/normal_product/pallas_call | solution.py:656
  135.8 0.6 border_sums.1
  136.4 14.5 %all_to_all.20.refs_0_ = f32[16,8,128]{2,1,0:T(8,128)S(1)} all-to-all(f32[16,8,128]{2,1,0:T(8,128)S(1)} %border_sums.1), channel_id=1, replica_groups=mesh['gz'=2,'gy'=16] {'gy'}, dimensions={0} | all-to-all | bytes 131072 | tf_op jit(solution)/shard_map/all_to_all | solution.py:887
  150.9 8.4 %second_descent.1 = (f32[32,64,256]{2,1,0:T(8,128)S(1)}, f32[8,128]{1,0:T(8,128)S(1)}, f32[16,8,128]{2,1,0:T(8,128)S(1)}, f32[2,16,2,64,256]{4,3,2,1,0:T(8,128)S(1)}) custom-call(s32[3]{0:T(128)S(1)} %pad_add_fusion.edge_ref, f32[32,64,256]{2,1,0:T(8,128)S(1)} %get-tuple-element.12.d0_ref, f32[32,64,256]{2,1,0:T(8,128)S(1)} %normal_product.1.after_ref.nd0_ref, ...), custom_call_target="tpu_custom_call" | custom-call | tf_op jit(solution)/shard_map/second_descent/pallas_call | solution.py:821
  159.3 10.1 %all_to_all.21.refs_0_ = f32[16,8,128]{2,1,0:T(8,128)S(1)} all-to-all(f32[16,8,128]{2,1,0:T(8,128)S(1)} %get-tuple-element.17), channel_id=1, replica_groups=mesh['gz'=2,'gy'=16] {'gy'}, dimensions={0} | all-to-all | bytes 131072 | tf_op jit(solution)/shard_map/all_to_all | solution.py:887
  169.4 1.3 collective-permute-done.2.refs_1_
  170.7 1.9 combine_spectra.1
  172.6 2.0 copy-done.1
  174.6 3.6 %all-to-all-start.3 = ((f32[32,2,64,256]{3,2,1,0:T(8,128)}), f32[32,2,64,256]{3,2,1,0:T(8,128)}, u32[]{:S(2)}, u32[]{:S(2)}) async-start(f32[32,2,64,256]{3,2,1,0:T(8,128)} %copy-done.1), calls=%async_computation.3 | async-start | bytes 8388608 | tf_op jit(solution)/shard_map/all_to_all | solution.py:892
  178.2 0.5 fusion.2
  178.7 4.6 %add_negate_fusion = f32[32,64,256]{2,1,0:T(8,128)} fusion(f32[32,64,256]{2,1,0:T(8,128)} %copy-done.4, f32[32,64,256]{2,1,0:T(8,128)S(1)} %get-tuple-element.12.d0_ref, f32[]{:T(128)} %bitcast.12, f32[]{:T(128)} %bitcast.11), kind=kLoop, calls=%fused_computation | loop fusion | flops 2097152 | bytes 6291464 | tf_op jit(solution)/shard_map/neg | solution.py:943
  183.3 4.9 %copy.21 = f32[2,16,64,256]{2,1,3,0:T(8,128)} copy(f32[2,16,64,256]{3,2,1,0:T(8,128)} %bitcast.28) | data formatting | bytes 4194304 | tf_op jit(solution)/shard_map/reshape | solution.py:944
  188.1 3.8 %constant_dynamic-slice_fusion = (f32[1,64,4096]{1,2,0:T(8,128)}, f32[1,64,4096]{1,2,0:T(8,128)S(1)}) fusion(f32[2,64,4096]{1,2,0:T(8,128)} %bitcast.27, s32[]{:T(128)S(6)} %select_n.29, s32[]{:T(128)S(6)} %select_n.27), kind=kLoop, calls=%fused_computation.6 | loop fusion | bytes 4194312 | tf_op jit(solution)/shard_map/jit(dynamic_index_in_dim)/dynamic_slice | solution.py:946
  191.9 3.1 %copy.23 = f32[1,64,4096]{2,1,0:T(8,128)} copy(f32[1,64,4096]{1,2,0:T(8,128)} %get-tuple-element.24) | data formatting | bytes 2097152 | tf_op jit(solution)/shard_map/jit(dynamic_index_in_dim)/dynamic_slice | solution.py:946
  195.1 0.0 collective-permute-start.3
  195.1 0.6 copy.22
  195.7 0.2 broadcast_in_dim.21
  195.9 0.1 constant_dynamic-update-slice_fusion
  196.0 2.1 collective-permute-done.3
  198.1 1.3 bitcast_dynamic-update-slice_fusion
  199.4 75.0 %all-to-all-done.3 = f32[32,2,64,256]{3,2,1,0:T(8,128)} async-done(((f32[32,2,64,256]{3,2,1,0:T(8,128)}), f32[32,2,64,256]{3,2,1,0:T(8,128)}, u32[]{:S(2)}, u32[]{:S(2)}) %all-to-all-start.3) | async-done | bytes 4194336 | tf_op jit(solution)/shard_map/all_to_all | solution.py:892
  274.4 11.0 %y_forward.1 = f32[4,8,256,128]{3,2,1,0:T(8,128)} custom-call(f32[2,16,2,64,256]{4,3,2,1,0:T(8,128)} %bitcast.20.spec_hbm, bf16[4,2048,128]{2,1,0:T(8,128)(2,1)} %bitcast.30, bf16[1024,512]{1,0:T(8,128)(2,1)} %constant.60.clone.table_hbm, f32[2,7,256,128]{3,2,1,0:T(8,128)} %constant.56.clone.tw_hbm), custom_call_target="tpu_custom_call" | custom-call | tf_op jit(solution)/shard_map/y_forward/pallas_call | solution.py:380
  (23 shorter events, 0.1 us)
Async XLA Ops:
  9.4 7.5 %copy-start.6 = (f32[2,4096]{1,0:T(2,128)S(1)}, f32[2,4096]{1,0:T(2,128)}, u32[]{:S(2)}) copy-start(f32[2,4096]{1,0:T(2,128)} %param.17) | copy-start | bytes 98308
  9.4 7.5 %copy-start.7 = (s32[4096]{0:T(1024)S(1)}, s32[4096]{0:T(1024)}, u32[]{:S(2)}) copy-start(s32[4096]{0:T(1024)} %param.16) | copy-start | bytes 49156
  9.4 103.7 %copy-start = (bf16[512,512]{1,0:T(8,128)(2,1)S(1)}, bf16[512,512]{1,0:T(8,128)(2,1)}, u32[]{:S(2)}) copy-start(bf16[512,512]{1,0:T(8,128)(2,1)} %constant.58.clone.inverse_ref.table_ref) | copy-start | bytes 1572868
  9.4 103.7 %copy-start.2 = (f32[2,16,8,256]{3,2,1,0:T(8,128)S(1)}, f32[2,16,8,256]{3,2,1,0:T(8,128)}, u32[]{:S(2)}) copy-start(f32[2,16,8,256]{3,2,1,0:T(8,128)} %constant.57.clone.tw_ref) | copy-start | bytes 786436
  9.5 103.7 %copy-start.3 = (bf16[256,1024]{1,0:T(8,128)(2,1)S(1)}, bf16[256,1024]{1,0:T(8,128)(2,1)}, u32[]{:S(2)}) copy-start(bf16[256,1024]{1,0:T(8,128)(2,1)} %constant.59.clone.forward_ref.table_ref) | copy-start | bytes 1572868
  9.5 103.7 %all-to-all-start = ((f32[32,2,64,256]{3,2,1,0:T(8,128)}), f32[32,2,64,256]{3,2,1,0:T(8,128)}, u32[]{:S(2)}, u32[]{:S(2)}) async-start(f32[32,2,64,256]{3,2,1,0:T(8,128)} %bitcast.26), calls=%async_computation | async-start | bytes 8388608 | tf_op jit(solution)/shard_map/all_to_all | solution.py:892
  128.6 7.1 %collective-permute-start = (f32[40,256]{1,0:T(8,128)S(1)}, f32[40,256]{1,0:T(8,128)S(1)}, u32[]{:S(2)}, u32[]{:S(2)}) collective-permute-start(f32[40,256]{1,0:T(8,128)S(1)} %get-tuple-element.14.tail_ref), channel_id=1, source_target_pairs={{0,16},{16,1},{1,17},{17,2},{2,18},{18,3},{3,19},{19,4},{4,20},{20... | collective-permute-start | bytes 122888 | tf_op jit(solution)/shard_map/ppermute | solution.py:932
  130.4 5.4 %collective-permute-start.1 = (f32[136,256]{1,0:T(8,128)S(1)}, f32[136,256]{1,0:T(8,128)S(1)}, u32[]{:S(2)}, u32[]{:S(2)}) collective-permute-start(f32[136,256]{1,0:T(8,128)S(1)} %get-tuple-element.15.head_ref), channel_id=1, source_target_pairs={{16,0},{1,16},{17,1},{2,17},{18,2},{3,18},{19,3},{4,19},{20,4},{5,... | collective-permute-start | bytes 417800 | tf_op jit(solution)/shard_map/ppermute | solution.py:931
  159.3 13.3 %copy-start.4 = (f32[32,64,256]{2,1,0:T(8,128)}, f32[32,64,256]{2,1,0:T(8,128)S(1)}, u32[]{:S(2)}) copy-start(f32[32,64,256]{2,1,0:T(8,128)S(1)} %get-tuple-element.20) | copy-start | bytes 6291460
  169.4 1.3 collective-permute-start.2
  172.6 2.0 copy-start.1
  174.6 99.8 %all-to-all-start.3 = ((f32[32,2,64,256]{3,2,1,0:T(8,128)}), f32[32,2,64,256]{3,2,1,0:T(8,128)}, u32[]{:S(2)}, u32[]{:S(2)}) async-start(f32[32,2,64,256]{3,2,1,0:T(8,128)} %copy-done.1), calls=%async_computation.3 | async-start | bytes 8388608 | tf_op jit(solution)/shard_map/all_to_all | solution.py:892
  195.1 3.0 %collective-permute-start.3 = (f32[64,4096]{1,0:T(8,128)}, f32[64,4096]{1,0:T(8,128)}, u32[]{:S(2)}, u32[]{:S(2)}) collective-permute-start(f32[64,4096]{1,0:T(8,128)} %bitcast.17), channel_id=1, source_target_pairs={{0,16},{16,0},{1,17},{17,1},{2,18},{18,2},{3,19},{19,3},{4,20},{20... | collective-permute-start | bytes 3145736 | tf_op jit(solution)/shard_map/ppermute | solution.py:883
  199.4 86.0 %copy-start.5 = (f32[2,64,4096]{2,1,0:T(8,128)}, f32[2,64,4096]{2,1,0:T(8,128)S(1)}, u32[]{:S(2)}) copy-start(f32[2,64,4096]{2,1,0:T(8,128)S(1)} %bitcast_dynamic-update-slice_fusion) | copy-start | bytes 6291460

commit v12 on v11

--- a/solution.py
+++ b/solution.py
@@ -178,7 +178,7 @@
 ):
     blocks, ny, _ = data_ref.shape
     n = ny // YR
-    gz, _, _, rows, _ = out_ref.shape
+    gz, _, _, _, rows, _ = out_ref.shape
     lane = lax.broadcasted_iota(jnp.int32, (n, LANES), 1)
     pairs = blocks // 2
 
@@ -187,18 +187,19 @@
         return pltpu.make_async_copy(data_hbm.at[part], data_ref.at[part], sems.at[2 + chunk])
 
     def give(chunk, core):
-        at = (core, slice(None), slice(None), slice(None), pl.ds(chunk * LANES, LANES))
+        at = (core, slice(None), chunk)
         return pltpu.make_async_copy(out_ref.at[at], out_hbm.at[at], out_sems.at[chunk * gz + core])
 
     fetch_table = pltpu.make_async_copy(table_hbm, table_ref, sems.at[0])
     fetch_tw = pltpu.make_async_copy(tw_hbm, tw_ref, sems.at[1])
     fetch(0).start()
+    fetch_table.start()
+    fetch_tw.start()
+    for chunk in range(1, pairs):
+        fetch(chunk).start()
 
     for chunk in range(pairs):
-        lanes = slice(chunk * LANES, (chunk + 1) * LANES)
         fetch(chunk).wait()
-        if chunk == 0:
-            fetch_table.start()
 
         def unpack(i, carry):
             part = pl.ds(pl.multiple_of(i * n, n), n)
@@ -211,9 +212,6 @@
         lax.fori_loop(0, YR, unpack, 0)
         if chunk == 0:
             fetch_table.wait()
-            fetch_tw.start()
-        if chunk + 1 < pairs:
-            fetch(chunk + 1).start()
 
         for k in range(0, YR, 2):
             pieces = [
@@ -246,8 +244,8 @@
                 at = pl.ds(pl.multiple_of(lax.rem(i, tiles) * 8, 8), 8)
                 for k, (re, im) in enumerate(short_fft(planes, 1)):
                     to = k * (n // (gz * rows)) + i // tiles
-                    out_ref[core, to, 0, at, lanes] = re
-                    out_ref[core, to, 1, at, lanes] = im
+                    out_ref[core, to, chunk, 0, at, :] = re
+                    out_ref[core, to, chunk, 1, at, :] = im
                 return carry
 
             lax.fori_loop(0, n // gz // 8, combine, 0, unroll=2)
@@ -261,18 +259,18 @@
 def y_inverse(data, rows, gz, gy):
     blocks, ny, width = data.shape
     n = ny // YR
-    ka = blocks * HALF
+    shape = (gz, gy, blocks // 2, 2, rows, LANES)
     hbm = pl.BlockSpec(memory_space=pltpu.HBM)
     return pl.pallas_call(
         y_inverse_kernel,
         in_specs=[hbm] * 3,
         out_specs=hbm,
-        out_shape=jax.ShapeDtypeStruct((gz, gy, 2, rows, ka), F32),
+        out_shape=jax.ShapeDtypeStruct(shape, F32),
         scratch_shapes=[
             pltpu.VMEM((blocks, ny, width), BF16),
             pltpu.VMEM((4 * n, 2 * n), BF16),
             pltpu.VMEM((2, YR - 1, n, LANES), F32),
-            pltpu.VMEM((gz, gy, 2, rows, ka), F32),
+            pltpu.VMEM(shape, F32),
             pltpu.VMEM((ny, LANES), F32),
             pltpu.VMEM((ny, LANES), F32),
             pltpu.VMEM((YR, 2 * n, LANES), F32),
@@ -295,9 +293,8 @@
     half = n // 2
 
     def fetch(chunk):
-        lanes = pl.ds(chunk * LANES, LANES)
         return pltpu.make_async_copy(
-            spec_hbm.at[:, :, :, :, lanes], spec_ref.at[chunk], spec_sems.at[chunk]
+            spec_hbm.at[:, :, chunk], spec_ref.at[chunk], spec_sems.at[chunk]
         )
 
     def give(chunk, part):
@@ -309,6 +306,10 @@
     fetch_data = pltpu.make_async_copy(data_hbm, data_ref, sems.at[2])
     fetch(0).start()
     fetch_table.start()
+    fetch_tw.start()
+    fetch_data.start()
+    for chunk in range(1, pairs):
+        fetch(chunk).start()
 
     def rows_of(chunk, p, k):
         part = pl.ds(k, rows // YR, stride=YR)
@@ -318,13 +319,10 @@
 
     lane = lax.broadcasted_iota(jnp.int32, (16, LANES), 1)
     for chunk in range(pairs):
-        lanes = slice(chunk * LANES, (chunk + 1) * LANES)
         fetch(chunk).wait()
 
         if chunk == 0:
             fetch_table.wait()
-            fetch_tw.start()
-            fetch_data.start()
 
         for k in range(0, YR, 2):
             pieces = [
@@ -339,8 +337,6 @@
         if chunk == 0:
             fetch_tw.wait()
             fetch_data.wait()
-        if chunk + 1 < pairs:
-            fetch(chunk + 1).start()
 
         def combine(i, carry):
             start = pl.multiple_of(i * 16, 16)
@@ -383,7 +379,7 @@
         out_specs=hbm,
         out_shape=jax.ShapeDtypeStruct((blocks, YR, n, width), F32),
         scratch_shapes=[
-            pltpu.VMEM((blocks // 2, *spec.shape[:-1], LANES), F32),
+            pltpu.VMEM((blocks // 2, *spec.shape[:2], *spec.shape[3:]), F32),
             pltpu.VMEM((blocks, ny, width), BF16),
             pltpu.VMEM((4 * n, 2 * n), BF16),
             pltpu.VMEM((2, YR - 1, n, LANES), F32),
@@ -508,38 +504,39 @@
     sums_ref[2] = slope
 
 
+def columns_back(spec_ref, chunk, coef_ref, tw_ref, re_s, im_s, j, carry):
+    gz, kb = spec_ref.shape[:2]
+    lanes = slice(chunk * LANES, (chunk + 1) * LANES)
+    part = pl.ds(pl.multiple_of(j * 8, 8), 8)
+    spectra = [
+        [(spec_ref[z, k, chunk, 0, part, :], spec_ref[z, k, chunk, 1, part, :]) for k in range(kb)]
+        for z in range(gz)
+    ]
+    inverse_columns(gz, kb, spectra, coef_ref, tw_ref, lanes, part, re_s, im_s)
+    return carry
+
+
 def middle_kernel(
     spec_hbm, coef_ref, tw_ref, inverse_ref, forward_ref,
     d0_ref, head_ref, tail_ref, spec_ref, re_s, im_s, sems,
 ):
-    gz, kb, _, rows, ka = spec_ref.shape
+    gz, kb, chunks, _, rows, _ = spec_ref.shape
+    ka = chunks * LANES
     planes = gz * kb
-    lane_parts = [slice(start, start + LANES) for start in range(0, ka, LANES)]
-    cuts = sems.shape[0]
-    cut = rows // cuts
-
-    def fetch(i):
-        part = pl.ds(i * cut, cut)
+
+    def fetch(chunk):
         return pltpu.make_async_copy(
-            spec_hbm.at[:, :, :, part], spec_ref.at[:, :, :, part], sems.at[i]
+            spec_hbm.at[:, :, chunk], spec_ref.at[:, :, chunk], sems.at[chunk]
         )
 
-    def columns_back(j, carry):
-        part = pl.ds(pl.multiple_of(j * 8, 8), 8)
-        for lanes in lane_parts:
-            spectra = [
-                [(spec_ref[z, k, 0, part, lanes], spec_ref[z, k, 1, part, lanes]) for k in range(kb)]
-                for z in range(gz)
-            ]
-            inverse_columns(gz, kb, spectra, coef_ref, tw_ref, lanes, part, re_s, im_s)
-        return carry
-
-    fetch(0).start()
-    for i in range(cuts):
-        fetch(i).wait()
-        if i + 1 < cuts:
-            fetch(i + 1).start()
-        lax.fori_loop(i * cut // 8, (i + 1) * cut // 8, columns_back, 0)
+    for chunk in range(chunks):
+        fetch(chunk).start()
+    for chunk in range(chunks):
+        fetch(chunk).wait()
+        lax.fori_loop(
+            0, rows // 8,
+            functools.partial(columns_back, spec_ref, chunk, coef_ref, tw_ref, re_s, im_s), 0,
+        )
 
     step = plane_chunk(planes, rows)
     shape2, shape3 = (step * rows, ka), (step, rows, ka)
@@ -557,13 +554,14 @@
 
     def second_columns(j, total):
         part = pl.ds(pl.multiple_of(j * 8, 8), 8)
-        for lanes in lane_parts:
+        for chunk in range(chunks):
+            lanes = slice(chunk * LANES, (chunk + 1) * LANES)
             spectra = forward_columns(gz, kb, coef_ref, tw_ref, lanes, part, re_s, im_s)
             for z in range(gz):
                 for k in range(kb):
                     for p in range(2):
                         value = spectra[z][k][p]
-                        spec_ref[z, k, p, part, lanes] = value
+                        spec_ref[z, k, chunk, p, part, :] = value
                         total = total + value * value
         return total
 
@@ -573,7 +571,9 @@
         head_ref[planes + p : planes + p + 1, :] = d0_ref[p, 1:2, :]
         for part in range(2):
             at = 2 * planes + 2 * p + part
-            head_ref[at : at + 1, :] = spec_ref[p // kb, p % kb, part, :1, :]
+            for chunk in range(chunks):
+                lanes = slice(chunk * LANES, (chunk + 1) * LANES)
+                head_ref[at : at + 1, lanes] = spec_ref[p // kb, p % kb, chunk, part, :1, :]
         tail_ref[p : p + 1, :] = d0_ref[p, rows - 1 : rows, :]
 
     row = lax.broadcasted_iota(jnp.int32, (rows, ka), 0)
@@ -597,7 +597,8 @@
 
 
 def middle(spec, coef, nx):
-    gz, kb, _, rows, ka = spec.shape
+    gz, kb, chunks, _, rows, _ = spec.shape
+    ka = chunks * LANES
     planes = gz * kb
     vmem = pl.BlockSpec(memory_space=pltpu.VMEM)
     field = jax.ShapeDtypeStruct((planes, rows, ka), F32)
@@ -614,7 +615,7 @@
         scratch_shapes=[
             pltpu.VMEM((planes, rows, ka), F32),
             pltpu.VMEM((planes, rows, ka), F32),
-            pltpu.SemaphoreType.DMA((4 if rows % 32 == 0 else 1,)),
+            pltpu.SemaphoreType.DMA((chunks,)),
         ],
         compiler_params=pltpu.CompilerParams(vmem_limit_bytes=X_GRANT),
         name="middle",
@@ -625,21 +626,14 @@
 
 
 def normal_kernel(spec_ref, coef_ref, tw_ref, table_ref, out_ref, re_s, im_s):
-    gz, kb, _, rows, ka = spec_ref.shape
-    planes = gz * kb
-    lane_parts = [slice(start, start + LANES) for start in range(0, ka, LANES)]
-
-    def columns(j, carry):
-        part = pl.ds(pl.multiple_of(j * 8, 8), 8)
-        for lanes in lane_parts:
-            spectra = [
-                [(spec_ref[z, k, 0, part, lanes], spec_ref[z, k, 1, part, lanes]) for k in range(kb)]
-                for z in range(gz)
-            ]
-            inverse_columns(gz, kb, spectra, coef_ref, tw_ref, lanes, part, re_s, im_s)
-        return carry
-
-    lax.fori_loop(0, rows // 8, columns, 0)
+    gz, kb, chunks, _, rows, _ = spec_ref.shape
+    planes, ka = gz * kb, chunks * LANES
+
+    for chunk in range(chunks):
+        lax.fori_loop(
+            0, rows // 8,
+            functools.partial(columns_back, spec_ref, chunk, coef_ref, tw_ref, re_s, im_s), 0,
+        )
 
     step = plane_chunk(planes, rows)
     shape = (step * rows, ka)
@@ -650,8 +644,8 @@
 
 
 def normal_product(spec, coef, nx):
-    gz, kb, _, rows, ka = spec.shape
-    planes = gz * kb
+    gz, kb, chunks, _, rows, _ = spec.shape
+    planes, ka = gz * kb, chunks * LANES
     vmem = pl.BlockSpec(memory_space=pltpu.VMEM)
     return pl.pallas_call(
         normal_kernel,
@@ -800,14 +794,14 @@
 
     def columns(j, total):
         part = pl.ds(pl.multiple_of(j * 8, 8), 8)
-        for start in range(0, ka, LANES):
-            lanes = slice(start, start + LANES)
+        for chunk in range(ka // LANES):
+            lanes = slice(chunk * LANES, (chunk + 1) * LANES)
             spectra = forward_columns(gz, kb, coef_ref, tw_ref, lanes, part, re_s, im_s)
             for z in range(gz):
                 for k in range(kb):
                     for p in range(2):
                         value = spectra[z][k][p]
-                        spec_ref[z, k, p, part, lanes] = value
+                        spec_ref[z, k, chunk, p, part, :] = value
                         total = total + value * value
         return total
 
@@ -826,7 +820,7 @@
             jax.ShapeDtypeStruct((planes, rows, ka), F32),
             jax.ShapeDtypeStruct((8, LANES), F32),
             jax.ShapeDtypeStruct(sums.shape, F32),
-            jax.ShapeDtypeStruct((gz, planes // gz, 2, rows, ka), F32),
+            jax.ShapeDtypeStruct((gz, planes // gz, ka // LANES, 2, rows, LANES), F32),
         ],
         scratch_shapes=[
             pltpu.VMEM((planes, rows, ka), F32),
@@ -866,7 +860,7 @@
         grid=(planes // count,),
         in_specs=[vmem] * (3 + gz),
         out_specs=[
-            pl.BlockSpec((count, *rest), lambda i: (i, 0, 0, 0)),
+            pl.BlockSpec((count, *rest), lambda i: (i, 0, 0, 0, 0)),
             pl.BlockSpec((2, 8, LANES), lambda i: (0, 0, 0)),
         ],
         out_shape=[
@@ -936,9 +930,9 @@
         edge, sums, d0, nd0, tail, prev_tail, next_head, coef, gz, nx
     )
     sums = everywhere(sums)
-    flat_shape = (devices, 2, rows, ka)
+    flat_shape = (devices, ka // LANES, 2, rows, LANES)
     spec, etas = combine_spectra(eta, sums, first.reshape(flat_shape), second.reshape(flat_shape))
-    residual = y_forward(to_devices(spec.reshape(gz, gy, 2, rows, ka)), data)
+    residual = y_forward(to_devices(spec.reshape(first.shape)), data)
 
     volume = -(etas[0, 0, 0] * d0 + etas[1, 0, 0] * d1)
     volume = volume.reshape(gz, gy, rows, ka).transpose(0, 2, 3, 1).reshape(gz, rows, nx)

time: 286 us -> 283 us (0.990)
  no operation moved by 1% of the time
where the time goes in v12:
time: 283 us
  waiting for transfers between devices  174 us (61%)
  Pallas kernels  47.6 us (17%)
  blocking collectives  24.6 us (9%)
  local copies, waits for them, and re-layouts  16.6 us (6%)
  starting transfers between devices  14.1 us (5%)
  other arithmetic  4.65 us (2%)
    all_to_all x2, waiting for transfers between devices, to_devices(): lax.all_to_all(parts.reshape(gz * gy, *rest), ('gz', 'gy'), 0, 0, tiled=T...  171 us
    all_to_all x2, blocking collectives, to_chips(): return lax.all_to_all(parts, 'gy', 0, 0, tiled=True)  24.6 us
    pallas_call x1, Pallas kernels, middle(): pl.pallas_call(middle_kernel, in_specs=[pl.BlockSpec(memory_space=pltpu.H...  13.8 us
    all_to_all x2, starting transfers between devices, to_devices(): lax.all_to_all(parts.reshape(gz * gy, *rest), ('gz', 'gy'), 0, 0, tiled=T...  11 us
    pallas_call x1, Pallas kernels, y_forward(): pl.pallas_call(y_forward_kernel, in_specs=[hbm] * 4, out_specs=hbm, out_s...  10.8 us
    pallas_call x1, Pallas kernels, second_descent(): pl.pallas_call(functools.partial(second_kernel, gz), in_specs=[pl.BlockSp...  8.41 us
    pallas_call x1, Pallas kernels, y_inverse(): pl.pallas_call(y_inverse_kernel, in_specs=[hbm] * 3, out_specs=hbm, out_s...  8.1 us
    dynamic_slice x3, local copies, waits for them, and re-layouts, shards(): lax.dynamic_index_in_dim(volume, lax.rem(core + r, gz), 0, False)  7.54 us
  transfers between devices with their start and end apart: 6, of which 4 were waited for; matrix products, arithmetic and copies ran while one was open for 7% of the time, Pallas kernels for 1%

profile of v12, /device:TPU:0, one launch (start us, length us, event | category | flops | bytes accessed | tf_op | source)
XLA Modules:
  0.0 283.0 jit_solution(11655262648919341558)
XLA Ops:
  0.6 8.1 %y_inverse.1 = f32[2,16,2,2,64,128]{5,4,3,2,1,0:T(8,128)} custom-call(bf16[4,2048,128]{2,1,0:T(8,128)(2,1)} %bitcast.29, bf16[1024,512]{1,0:T(8,128)(2,1)} %constant.55.clone.table_hbm, f32[2,7,256,128]{3,2,1,0:T(8,128)} %constant.56.clone.tw_hbm), custom_call_target="tpu_custom_call" | custom-call | tf_op jit(solution)/shard_map/y_inverse/pallas_call | solution.py:264
  8.8 0.0 copy-start
  8.8 0.0 copy-start.2
  8.8 0.0 copy-start.3
  8.8 7.4 %all-to-all-start = ((f32[32,2,2,64,128]{4,3,2,1,0:T(8,128)}), f32[32,2,2,64,128]{4,3,2,1,0:T(8,128)}, u32[]{:S(2)}, u32[]{:S(2)}) async-start(f32[32,2,2,64,128]{4,3,2,1,0:T(8,128)} %bitcast.26), calls=%async_computation | async-start | bytes 8388608 | tf_op jit(solution)/shard_map/all_to_all | solution.py:886
  16.4 0.1 pad_add_fusion.edge_ref
  16.5 96.0 %all-to-all-done = f32[32,2,2,64,128]{4,3,2,1,0:T(8,128)} async-done(((f32[32,2,2,64,128]{4,3,2,1,0:T(8,128)}), f32[32,2,2,64,128]{4,3,2,1,0:T(8,128)}, u32[]{:S(2)}, u32[]{:S(2)}) %all-to-all-start) | async-done | bytes 4194336 | tf_op jit(solution)/shard_map/all_to_all | solution.py:886
  112.5 13.8 %middle.1 = (f32[32,64,256]{2,1,0:T(8,128)S(1)}, f32[136,256]{1,0:T(8,128)S(1)}, f32[40,256]{1,0:T(8,128)S(1)}, f32[2,16,2,2,64,128]{5,4,3,2,1,0:T(8,128)S(1)}) custom-call(f32[2,16,2,2,64,128]{5,4,3,2,1,0:T(8,128)} %bitcast.5.spec_hbm, f32[3,16,8,256]{3,2,1,0:T(8,128)S(1)} %broadcast_in_dim.24.coef_ref, f32[2,16,8,256]{3,2,1,0:T(8,128)S(1)} %copy-done.2, ...), custom_call_target="tpu_custom_call" | custom-call | tf_op jit(solution)/shard_map/middle/pallas_call | solution.py:605
  126.4 1.8 collective-permute-start
  128.1 1.3 collective-permute-start.1
  129.4 4.0 %normal_product.1.after_ref.nd0_ref = f32[32,64,256]{2,1,0:T(8,128)S(1)} custom-call(f32[2,16,2,2,64,128]{5,4,3,2,1,0:T(8,128)S(1)} %get-tuple-element.13.spec_ref, f32[3,16,8,256]{3,2,1,0:T(8,128)S(1)} %broadcast_in_dim.24.coef_ref, f32[2,16,8,256]{3,2,1,0:T(8,128)S(1)} %copy-done.2, bf16[512,512]{1,0:T(8,128)(2,1)S(1)} %copy-done), custom_call_target="tpu_custom_call" | custom-call | flops 1610612736 | bytes 6291456 | tf_op jit(solution)/shard_map/normal_product/pallas_call | solution.py:650
  133.5 0.6 border_sums.1
  134.1 14.5 %all_to_all.20.refs_0_ = f32[16,8,128]{2,1,0:T(8,128)S(1)} all-to-all(f32[16,8,128]{2,1,0:T(8,128)S(1)} %border_sums.1), channel_id=1, replica_groups=mesh['gz'=2,'gy'=16] {'gy'}, dimensions={0} | all-to-all | bytes 131072 | tf_op jit(solution)/shard_map/all_to_all | solution.py:881
  148.6 8.4 %second_descent.1 = (f32[32,64,256]{2,1,0:T(8,128)S(1)}, f32[8,128]{1,0:T(8,128)S(1)}, f32[16,8,128]{2,1,0:T(8,128)S(1)}, f32[2,16,2,2,64,128]{5,4,3,2,1,0:T(8,128)S(1)}) custom-call(s32[3]{0:T(128)S(1)} %pad_add_fusion.edge_ref, f32[32,64,256]{2,1,0:T(8,128)S(1)} %get-tuple-element.12.d0_ref, f32[32,64,256]{2,1,0:T(8,128)S(1)} %normal_product.1.after_ref.nd0_ref, ...), custom_call_target="tpu_custom_call" | custom-call | tf_op jit(solution)/shard_map/second_descent/pallas_call | solution.py:815
  157.0 10.1 %all_to_all.21.refs_0_ = f32[16,8,128]{2,1,0:T(8,128)S(1)} all-to-all(f32[16,8,128]{2,1,0:T(8,128)S(1)} %get-tuple-element.17), channel_id=1, replica_groups=mesh['gz'=2,'gy'=16] {'gy'}, dimensions={0} | all-to-all | bytes 131072 | tf_op jit(solution)/shard_map/all_to_all | solution.py:881
  167.1 1.3 collective-permute-done.2.refs_1_
  168.4 1.9 combine_spectra.1
  170.3 2.0 copy-done.1
  172.3 3.6 %all-to-all-start.3 = ((f32[32,2,2,64,128]{4,3,2,1,0:T(8,128)}), f32[32,2,2,64,128]{4,3,2,1,0:T(8,128)}, u32[]{:S(2)}, u32[]{:S(2)}) async-start(f32[32,2,2,64,128]{4,3,2,1,0:T(8,128)} %copy-done.1), calls=%async_computation.3 | async-start | bytes 8388608 | tf_op jit(solution)/shard_map/all_to_all | solution.py:886
  175.9 0.5 fusion.2
  176.4 4.6 %add_negate_fusion = f32[32,64,256]{2,1,0:T(8,128)} fusion(f32[32,64,256]{2,1,0:T(8,128)} %copy-done.4, f32[32,64,256]{2,1,0:T(8,128)S(1)} %get-tuple-element.12.d0_ref, f32[]{:T(128)} %bitcast.12, f32[]{:T(128)} %bitcast.11), kind=kLoop, calls=%fused_computation | loop fusion | flops 2097152 | bytes 6291464 | tf_op jit(solution)/shard_map/neg | solution.py:937
  180.9 4.9 %copy.21 = f32[2,16,64,256]{2,1,3,0:T(8,128)} copy(f32[2,16,64,256]{3,2,1,0:T(8,128)} %bitcast.28) | data formatting | bytes 4194304 | tf_op jit(solution)/shard_map/reshape | solution.py:938
  185.8 3.8 %constant_dynamic-slice_fusion = (f32[1,64,4096]{1,2,0:T(8,128)}, f32[1,64,4096]{1,2,0:T(8,128)S(1)}) fusion(f32[2,64,4096]{1,2,0:T(8,128)} %bitcast.27, s32[]{:T(128)S(6)} %select_n.29, s32[]{:T(128)S(6)} %select_n.27), kind=kLoop, calls=%fused_computation.6 | loop fusion | bytes 4194312 | tf_op jit(solution)/shard_map/jit(dynamic_index_in_dim)/dynamic_slice | solution.py:940
  189.6 3.1 %copy.23 = f32[1,64,4096]{2,1,0:T(8,128)} copy(f32[1,64,4096]{1,2,0:T(8,128)} %get-tuple-element.24) | data formatting | bytes 2097152 | tf_op jit(solution)/shard_map/jit(dynamic_index_in_dim)/dynamic_slice | solution.py:940
  192.8 0.0 collective-permute-start.3
  192.8 0.6 copy.22
  193.4 0.2 broadcast_in_dim.21
  193.6 0.1 constant_dynamic-update-slice_fusion
  193.7 2.1 collective-permute-done.3
  195.8 1.3 bitcast_dynamic-update-slice_fusion
  197.1 75.0 %all-to-all-done.3 = f32[32,2,2,64,128]{4,3,2,1,0:T(8,128)} async-done(((f32[32,2,2,64,128]{4,3,2,1,0:T(8,128)}), f32[32,2,2,64,128]{4,3,2,1,0:T(8,128)}, u32[]{:S(2)}, u32[]{:S(2)}) %all-to-all-start.3) | async-done | bytes 4194336 | tf_op jit(solution)/shard_map/all_to_all | solution.py:886
  272.1 10.8 %y_forward.1 = f32[4,8,256,128]{3,2,1,0:T(8,128)} custom-call(f32[2,16,2,2,64,128]{5,4,3,2,1,0:T(8,128)} %bitcast.20.spec_hbm, bf16[4,2048,128]{2,1,0:T(8,128)(2,1)} %bitcast.30, bf16[1024,512]{1,0:T(8,128)(2,1)} %constant.60.clone.table_hbm, f32[2,7,256,128]{3,2,1,0:T(8,128)} %constant.56.clone.tw_hbm), custom_call_target="tpu_custom_call" | custom-call | tf_op jit(solution)/shard_map/y_forward/pallas_call | solution.py:376
  (23 shorter events, 0.1 us)
Async XLA Ops:
  8.7 7.5 %copy-start.6 = (f32[2,4096]{1,0:T(2,128)S(1)}, f32[2,4096]{1,0:T(2,128)}, u32[]{:S(2)}) copy-start(f32[2,4096]{1,0:T(2,128)} %param.17) | copy-start | bytes 98308
  8.8 7.5 %copy-start.7 = (s32[4096]{0:T(1024)S(1)}, s32[4096]{0:T(1024)}, u32[]{:S(2)}) copy-start(s32[4096]{0:T(1024)} %param.16) | copy-start | bytes 49156
  8.8 103.7 %copy-start = (bf16[512,512]{1,0:T(8,128)(2,1)S(1)}, bf16[512,512]{1,0:T(8,128)(2,1)}, u32[]{:S(2)}) copy-start(bf16[512,512]{1,0:T(8,128)(2,1)} %constant.58.clone.inverse_ref.table_ref) | copy-start | bytes 1572868
  8.8 103.7 %copy-start.2 = (f32[2,16,8,256]{3,2,1,0:T(8,128)S(1)}, f32[2,16,8,256]{3,2,1,0:T(8,128)}, u32[]{:S(2)}) copy-start(f32[2,16,8,256]{3,2,1,0:T(8,128)} %constant.57.clone.tw_ref) | copy-start | bytes 786436
  8.8 103.7 %copy-start.3 = (bf16[256,1024]{1,0:T(8,128)(2,1)S(1)}, bf16[256,1024]{1,0:T(8,128)(2,1)}, u32[]{:S(2)}) copy-start(bf16[256,1024]{1,0:T(8,128)(2,1)} %constant.59.clone.forward_ref.table_ref) | copy-start | bytes 1572868
  8.8 103.7 %all-to-all-start = ((f32[32,2,2,64,128]{4,3,2,1,0:T(8,128)}), f32[32,2,2,64,128]{4,3,2,1,0:T(8,128)}, u32[]{:S(2)}, u32[]{:S(2)}) async-start(f32[32,2,2,64,128]{4,3,2,1,0:T(8,128)} %bitcast.26), calls=%async_computation | async-start | bytes 8388608 | tf_op jit(solution)/shard_map/all_to_all | solution.py:886
  126.4 7.1 %collective-permute-start = (f32[40,256]{1,0:T(8,128)S(1)}, f32[40,256]{1,0:T(8,128)S(1)}, u32[]{:S(2)}, u32[]{:S(2)}) collective-permute-start(f32[40,256]{1,0:T(8,128)S(1)} %get-tuple-element.14.tail_ref), channel_id=1, source_target_pairs={{0,16},{16,1},{1,17},{17,2},{2,18},{18,3},{3,19},{19,4},{4,20},{20... | collective-permute-start | bytes 122888 | tf_op jit(solution)/shard_map/ppermute | solution.py:926
  128.1 5.3 %collective-permute-start.1 = (f32[136,256]{1,0:T(8,128)S(1)}, f32[136,256]{1,0:T(8,128)S(1)}, u32[]{:S(2)}, u32[]{:S(2)}) collective-permute-start(f32[136,256]{1,0:T(8,128)S(1)} %get-tuple-element.15.head_ref), channel_id=1, source_target_pairs={{16,0},{1,16},{17,1},{2,17},{18,2},{3,18},{19,3},{4,19},{20,4},{5,... | collective-permute-start | bytes 417800 | tf_op jit(solution)/shard_map/ppermute | solution.py:925
  157.0 13.3 %copy-start.4 = (f32[32,64,256]{2,1,0:T(8,128)}, f32[32,64,256]{2,1,0:T(8,128)S(1)}, u32[]{:S(2)}) copy-start(f32[32,64,256]{2,1,0:T(8,128)S(1)} %get-tuple-element.20) | copy-start | bytes 6291460
  167.1 1.3 collective-permute-start.2
  170.2 2.0 copy-start.1
  172.3 99.8 %all-to-all-start.3 = ((f32[32,2,2,64,128]{4,3,2,1,0:T(8,128)}), f32[32,2,2,64,128]{4,3,2,1,0:T(8,128)}, u32[]{:S(2)}, u32[]{:S(2)}) async-start(f32[32,2,2,64,128]{4,3,2,1,0:T(8,128)} %copy-done.1), calls=%async_computation.3 | async-start | bytes 8388608 | tf_op jit(solution)/shard_map/all_to_all | solution.py:886
  192.8 3.0 %collective-permute-start.3 = (f32[64,4096]{1,0:T(8,128)}, f32[64,4096]{1,0:T(8,128)}, u32[]{:S(2)}, u32[]{:S(2)}) collective-permute-start(f32[64,4096]{1,0:T(8,128)} %bitcast.17), channel_id=1, source_target_pairs={{0,16},{16,0},{1,17},{17,1},{2,18},{18,2},{3,19},{19,3},{4,20},{20... | collective-permute-start | bytes 3145736 | tf_op jit(solution)/shard_map/ppermute | solution.py:877
  197.1 85.8 %copy-start.5 = (f32[2,64,4096]{2,1,0:T(8,128)}, f32[2,64,4096]{2,1,0:T(8,128)S(1)}, u32[]{:S(2)}) copy-start(f32[2,64,4096]{2,1,0:T(8,128)S(1)} %bitcast_dynamic-update-slice_fusion) | copy-start | bytes 6291460

commit v13 on v12

--- a/solution.py
+++ b/solution.py
@@ -126,8 +126,8 @@
     return jnp.sum(jnp.sum(x, axis=0, keepdims=True), axis=1, keepdims=True)
 
 
-def step_of(sums_refs):
-    total = sum(jnp.sum(sums_ref[...], axis=0) for sums_ref in sums_refs)
+def step_of(sums_ref):
+    total = jnp.sum(sums_ref[...], axis=0)
     parts = jnp.sum(total, axis=1, keepdims=True)
     return parts[0:1] / (parts[1:2] + PENALTY * parts[2:3])
 
@@ -716,12 +716,11 @@
     gz, edge_ref, d0_ref, nd0_ref, tail_ref, prev_ref, next_ref,
     coef_ref, tw_ref, table_ref, inverse_ref, *refs,
 ):
-    sums_refs, refs = refs[:1], refs[1:]
-    d1_ref, eta_ref, out_ref, spec_ref, re_s, im_s, row_s, nrow_s, re8_s, im8_s = refs
+    sums_ref, d1_ref, eta_ref, out_ref, spec_ref, re_s, im_s, row_s, nrow_s, re8_s, im8_s = refs
     next_normal_row(gz, next_ref, coef_ref, tw_ref, inverse_ref, nrow_s, re8_s, im8_s)
     planes, rows, ka = d0_ref.shape
     kb = planes // gz
-    eta_here = step_of(sums_refs)
+    eta_here = step_of(sums_ref)
     eta_ref[...] = jnp.broadcast_to(eta_here, (8, LANES))
     eta = jnp.max(eta_here)
     first = edge_ref[0] > 0
@@ -809,7 +808,7 @@
     put_copies(out_ref, sums_block([square, projected, slope]))
 
 
-def second_descent(edge, sums, d0, nd0, tail, prev_tail, next_head, coef, gz, nx):
+def second_descent(edge, sums, d0, nd0, tail, prev_tail, next_head, coef, gz, nx, copies):
     planes, rows, ka = d0.shape
     vmem = pl.BlockSpec(memory_space=pltpu.VMEM)
     return pl.pallas_call(
@@ -819,7 +818,7 @@
         out_shape=[
             jax.ShapeDtypeStruct((planes, rows, ka), F32),
             jax.ShapeDtypeStruct((8, LANES), F32),
-            jax.ShapeDtypeStruct(sums.shape, F32),
+            jax.ShapeDtypeStruct((copies, 8, LANES), F32),
             jax.ShapeDtypeStruct((gz, planes // gz, ka // LANES, 2, rows, LANES), F32),
         ],
         scratch_shapes=[
@@ -838,10 +837,9 @@
     )
 
 
-def combine_kernel(gz, eta_ref, *refs):
-    sums_refs, (first_ref, second_ref, out_ref, steps_ref) = refs[:gz], refs[gz:]
+def combine_kernel(eta_ref, sums_ref, first_ref, second_ref, out_ref, steps_ref):
     eta0 = jnp.max(eta_ref[...])
-    eta1 = jnp.max(step_of(sums_refs))
+    eta1 = jnp.max(step_of(sums_ref))
     steps_ref[0] = eta_ref[...]
     steps_ref[1] = jnp.full((8, LANES), eta1, F32)
     count = out_ref.shape[0]
@@ -851,14 +849,13 @@
 
 
 def combine_spectra(eta, sums, first, second):
-    gz = len(sums)
     planes, *rest = first.shape
     count = 4 if planes % 4 == 0 else 1
     vmem = pl.BlockSpec(memory_space=pltpu.VMEM)
     return pl.pallas_call(
-        functools.partial(combine_kernel, gz),
+        combine_kernel,
         grid=(planes // count,),
-        in_specs=[vmem] * (3 + gz),
+        in_specs=[vmem] * 4,
         out_specs=[
             pl.BlockSpec((count, *rest), lambda i: (i, 0, 0, 0, 0)),
             pl.BlockSpec((2, 8, LANES), lambda i: (0, 0, 0)),
@@ -869,7 +866,7 @@
         ],
         compiler_params=pltpu.CompilerParams(vmem_limit_bytes=6 * MIB),
         name="combine_spectra",
-    )(eta, *sums, first, second)
+    )(eta, sums, first, second)
 
 
 def to_core(piece, r):
@@ -877,19 +874,42 @@
     return lax.ppermute(piece, "gz", [(i, (i + r) % gz) for i in range(gz)]) if r else piece
 
 
-def to_chips(parts):
-    return lax.all_to_all(parts, "gy", 0, 0, tiled=True)
+def near_chips(gy):
+    near = 1
+    while near * near < gy:
+        near *= 2
+    return near
+
+
+def resum_kernel(in_ref, out_ref):
+    put_copies(out_ref, jnp.sum(in_ref[...], axis=0))
+
+
+def everywhere(sums, both_cores):
+    gz, gy = lax.axis_size("gz"), lax.axis_size("gy")
+    near = near_chips(gy)
+    far = gy // near
+    cores = range(gz) if both_cores else range(1)
+    groups = [[g * gy + k * near + j for g in cores for j in range(near)] for k in range(far)]
+    axes = ("gz", "gy") if both_cores else "gy"
+    sums = lax.all_to_all(sums, axes, 0, 0, tiled=True, axis_index_groups=groups)
+    vmem = pl.BlockSpec(memory_space=pltpu.VMEM)
+    sums = pl.pallas_call(
+        resum_kernel,
+        in_specs=[vmem],
+        out_specs=vmem,
+        out_shape=jax.ShapeDtypeStruct((far, 8, LANES), F32),
+        compiler_params=pltpu.CompilerParams(vmem_limit_bytes=2 * MIB),
+        name="resum",
+    )(sums)
+    groups = [[j + k * near for k in range(far)] for j in range(near)]
+    return lax.all_to_all(sums, "gy", 0, 0, tiled=True, axis_index_groups=groups)
 
 
 def to_devices(parts):
     gz, gy, *rest = parts.shape
     parts = lax.all_to_all(parts.reshape(gz * gy, *rest), ("gz", "gy"), 0, 0, tiled=True)
     return parts.reshape(gz, gy, *rest)
-
-
-def everywhere(sums):
-    sums = to_chips(sums)
-    return [to_core(sums, r) for r in range(lax.axis_size("gz"))]
 
 
 def shards(data, band_offset, interp_weight):
@@ -925,11 +945,12 @@
     next_head = lax.ppermute(head, ("gz", "gy"), up)
     prev_tail = lax.ppermute(tail, ("gz", "gy"), down)
     nd0 = normal_product(first, coef, nx)
-    sums = to_chips(border_sums(edge, head, tail, next_head, prev_tail, nd0, gy))
+    near = near_chips(gy)
+    sums = everywhere(border_sums(edge, head, tail, next_head, prev_tail, nd0, near), False)
     d1, eta, sums, second = second_descent(
-        edge, sums, d0, nd0, tail, prev_tail, next_head, coef, gz, nx
+        edge, sums, d0, nd0, tail, prev_tail, next_head, coef, gz, nx, gz * near
     )
-    sums = everywhere(sums)
+    sums = everywhere(sums, True)
     flat_shape = (devices, ka // LANES, 2, rows, LANES)
     spec, etas = combine_spectra(eta, sums, first.reshape(flat_shape), second.reshape(flat_shape))
     residual = y_forward(to_devices(spec.reshape(first.shape)), data)

time: 283 us -> 292 us (1.032)
  blocking collectives: 24.6 us -> 34.4 us
    all_to_all x2 -> x4, blocking collectives: 24.6 us -> 34.4 us  [the longest x2 18.9 us: everywhere(): lax.all_to_all(sums, 'gy', 0, 0, tiled=True, axis_index_groups=groups)]
  transfers between devices with their start and end apart: 6 -> 5, of which waited for: 4 -> 3; matrix products, arithmetic and copies ran while one was open for 7% -> 7% of each run, Pallas kernels for 1% -> 1%
where the time goes in v13:
time: 292 us; the launch traced here: 291 us
  waiting for transfers between devices  173 us (59%)
  Pallas kernels  47.3 us (16%)
  blocking collectives  34.4 us (12%)
  local copies, waits for them, and re-layouts  16.6 us (6%)
  starting transfers between devices  14.1 us (5%)
  other arithmetic  4.58 us (2%)
    all_to_all x2, waiting for transfers between devices, to_devices(): lax.all_to_all(parts.reshape(gz * gy, *rest), ('gz', 'gy'), 0, 0, tiled=T...  171 us
    all_to_all x2, blocking collectives, everywhere(): lax.all_to_all(sums, 'gy', 0, 0, tiled=True, axis_index_groups=groups)  18.9 us
    all_to_all x2, blocking collectives, everywhere(): lax.all_to_all(sums, axes, 0, 0, tiled=True, axis_index_groups=groups)  15.5 us
    pallas_call x1, Pallas kernels, middle(): pl.pallas_call(middle_kernel, in_specs=[pl.BlockSpec(memory_space=pltpu.H...  13.8 us
    all_to_all x2, starting transfers between devices, to_devices(): lax.all_to_all(parts.reshape(gz * gy, *rest), ('gz', 'gy'), 0, 0, tiled=T...  11 us
    pallas_call x1, Pallas kernels, y_forward(): pl.pallas_call(y_forward_kernel, in_specs=[hbm] * 4, out_specs=hbm, out_s...  10.8 us
    pallas_call x1, Pallas kernels, second_descent(): pl.pallas_call(functools.partial(second_kernel, gz), in_specs=[pl.BlockSp...  8.23 us
    pallas_call x1, Pallas kernels, y_inverse(): pl.pallas_call(y_inverse_kernel, in_specs=[hbm] * 3, out_specs=hbm, out_s...  8.1 us
  transfers between devices with their start and end apart: 5, of which 3 were waited for; matrix products, arithmetic and copies ran while one was open for 7% of the time, Pallas kernels for 1%

profile of v13, /device:TPU:0, one launch (start us, length us, event | category | flops | bytes accessed | tf_op | source)
XLA Modules:
  0.0 291.2 jit_solution(1506652317299924939)
XLA Ops:
  0.6 8.1 %y_inverse.1 = f32[2,16,2,2,64,128]{5,4,3,2,1,0:T(8,128)} custom-call(bf16[4,2048,128]{2,1,0:T(8,128)(2,1)} %bitcast.29, bf16[1024,512]{1,0:T(8,128)(2,1)} %constant.55.clone.table_hbm, f32[2,7,256,128]{3,2,1,0:T(8,128)} %constant.56.clone.tw_hbm), custom_call_target="tpu_custom_call" | custom-call | tf_op jit(solution)/shard_map/y_inverse/pallas_call | solution.py:264
  8.8 0.0 copy-start
  8.8 0.0 copy-start.2
  8.8 7.4 %all-to-all-start = ((f32[32,2,2,64,128]{4,3,2,1,0:T(8,128)}), f32[32,2,2,64,128]{4,3,2,1,0:T(8,128)}, u32[]{:S(2)}, u32[]{:S(2)}) async-start(f32[32,2,2,64,128]{4,3,2,1,0:T(8,128)} %bitcast.26), calls=%async_computation | async-start | bytes 8388608 | tf_op jit(solution)/shard_map/all_to_all | solution.py:911
  16.4 0.1 pad_add_fusion.edge_ref
  16.5 96.0 %all-to-all-done = f32[32,2,2,64,128]{4,3,2,1,0:T(8,128)} async-done(((f32[32,2,2,64,128]{4,3,2,1,0:T(8,128)}), f32[32,2,2,64,128]{4,3,2,1,0:T(8,128)}, u32[]{:S(2)}, u32[]{:S(2)}) %all-to-all-start) | async-done | bytes 4194336 | tf_op jit(solution)/shard_map/all_to_all | solution.py:911
  112.5 13.8 %middle.1 = (f32[32,64,256]{2,1,0:T(8,128)S(1)}, f32[136,256]{1,0:T(8,128)S(1)}, f32[40,256]{1,0:T(8,128)S(1)}, f32[2,16,2,2,64,128]{5,4,3,2,1,0:T(8,128)S(1)}) custom-call(f32[2,16,2,2,64,128]{5,4,3,2,1,0:T(8,128)} %bitcast.5.spec_hbm, f32[3,16,8,256]{3,2,1,0:T(8,128)S(1)} %broadcast_in_dim.24.coef_ref, f32[2,16,8,256]{3,2,1,0:T(8,128)S(1)} %copy-done.2, ...), custom_call_target="tpu_custom_call" | custom-call | tf_op jit(solution)/shard_map/middle/pallas_call | solution.py:605
  126.4 1.8 collective-permute-start
  128.1 1.3 collective-permute-start.1
  129.4 4.0 %normal_product.1.after_ref.nd0_ref = f32[32,64,256]{2,1,0:T(8,128)S(1)} custom-call(f32[2,16,2,2,64,128]{5,4,3,2,1,0:T(8,128)S(1)} %get-tuple-element.13.spec_ref, f32[3,16,8,256]{3,2,1,0:T(8,128)S(1)} %broadcast_in_dim.24.coef_ref, f32[2,16,8,256]{3,2,1,0:T(8,128)S(1)} %copy-done.2, bf16[512,512]{1,0:T(8,128)(2,1)S(1)} %copy-done), custom_call_target="tpu_custom_call" | custom-call | flops 1610612736 | bytes 6291456 | tf_op jit(solution)/shard_map/normal_product/pallas_call | solution.py:650
  133.5 0.6 border_sums.1
  134.0 8.3 %all_to_all.30.in_ref = f32[4,8,128]{2,1,0:T(8,128)S(1)} all-to-all(f32[4,8,128]{2,1,0:T(8,128)S(1)} %border_sums.1), channel_id=1, replica_groups={{0,1,2,3},{4,5,6,7},{8,9,10,11},{12,13,14,15},{16,17,18,19},{20,21,22,2..., dimensions={0} | all-to-all | bytes 32768 | tf_op jit(solution)/shard_map/all_to_all | solution.py:895
  142.4 11.0 %all_to_all.31.refs_0_ = f32[4,8,128]{2,1,0:T(8,128)S(1)} all-to-all(f32[4,8,128]{2,1,0:T(8,128)S(1)} %resum.2), channel_id=1, replica_groups={{0,4,8,12},{1,5,9,13},{2,6,10,14},{3,7,11,15},{16,20,24,28},{17,21,25,2..., dimensions={0} | all-to-all | bytes 32768 | tf_op jit(solution)/shard_map/all_to_all | solution.py:906
  153.3 8.2 %second_descent.1 = (f32[32,64,256]{2,1,0:T(8,128)S(1)}, f32[8,128]{1,0:T(8,128)S(1)}, f32[8,8,128]{2,1,0:T(8,128)S(1)}, f32[2,16,2,2,64,128]{5,4,3,2,1,0:T(8,128)S(1)}) custom-call(s32[3]{0:T(128)S(1)} %pad_add_fusion.edge_ref, f32[32,64,256]{2,1,0:T(8,128)S(1)} %get-tuple-element.12.d0_ref, f32[32,64,256]{2,1,0:T(8,128)S(1)} %normal_product.1.after_ref.nd0_ref, ...), custom_call_target="tpu_custom_call" | custom-call | tf_op jit(solution)/shard_map/second_descent/pallas_call | solution.py:814
  161.6 7.2 %all_to_all.32.in_ref = f32[8,8,128]{2,1,0:T(8,128)S(1)} all-to-all(f32[8,8,128]{2,1,0:T(8,128)S(1)} %get-tuple-element.17), channel_id=1, replica_groups={{0,1,2,3,16,17,18,19},{4,5,6,7,20,21,22,23},{8,9,10,11,24,25,26,27},{12..., dimensions={0} | all-to-all | bytes 65536 | tf_op jit(solution)/shard_map/all_to_all | solution.py:895
  168.8 8.0 %all_to_all.33.sums_ref = f32[4,8,128]{2,1,0:T(8,128)S(1)} all-to-all(f32[4,8,128]{2,1,0:T(8,128)S(1)} %resum.3), channel_id=1, replica_groups={{0,4,8,12},{1,5,9,13},{2,6,10,14},{3,7,11,15},{16,20,24,28},{17,21,25,2..., dimensions={0} | all-to-all | bytes 32768 | tf_op jit(solution)/shard_map/all_to_all | solution.py:906
  176.7 1.7 combine_spectra.1
  178.5 2.0 copy-done.1
  180.5 3.6 %all-to-all-start.5 = ((f32[32,2,2,64,128]{4,3,2,1,0:T(8,128)}), f32[32,2,2,64,128]{4,3,2,1,0:T(8,128)}, u32[]{:S(2)}, u32[]{:S(2)}) async-start(f32[32,2,2,64,128]{4,3,2,1,0:T(8,128)} %copy-done.1), calls=%async_computation.5 | async-start | bytes 8388608 | tf_op jit(solution)/shard_map/all_to_all | solution.py:911
  184.1 0.5 fusion.2
  184.6 4.5 %add_negate_fusion = f32[32,64,256]{2,1,0:T(8,128)} fusion(f32[32,64,256]{2,1,0:T(8,128)} %copy-done.4, f32[32,64,256]{2,1,0:T(8,128)S(1)} %get-tuple-element.12.d0_ref, f32[]{:T(128)} %bitcast.12, f32[]{:T(128)} %bitcast.11), kind=kLoop, calls=%fused_computation | loop fusion | flops 2097152 | bytes 6291464 | tf_op jit(solution)/shard_map/neg | solution.py:958
  189.1 4.9 %copy.21 = f32[2,16,64,256]{2,1,3,0:T(8,128)} copy(f32[2,16,64,256]{3,2,1,0:T(8,128)} %bitcast.28) | data formatting | bytes 4194304 | tf_op jit(solution)/shard_map/reshape | solution.py:959
  193.9 3.8 %constant_dynamic-slice_fusion = (f32[1,64,4096]{1,2,0:T(8,128)}, f32[1,64,4096]{1,2,0:T(8,128)S(1)}) fusion(f32[2,64,4096]{1,2,0:T(8,128)} %bitcast.27, s32[]{:T(128)S(6)} %select_n.29, s32[]{:T(128)S(6)} %select_n.27), kind=kLoop, calls=%fused_computation.6 | loop fusion | bytes 4194312 | tf_op jit(solution)/shard_map/jit(dynamic_index_in_dim)/dynamic_slice | solution.py:961
  197.7 3.1 %copy.23 = f32[1,64,4096]{2,1,0:T(8,128)} copy(f32[1,64,4096]{1,2,0:T(8,128)} %get-tuple-element.24) | data formatting | bytes 2097152 | tf_op jit(solution)/shard_map/jit(dynamic_index_in_dim)/dynamic_slice | solution.py:961
  200.9 0.0 collective-permute-start.2
  200.9 0.6 copy.22
  201.5 0.2 broadcast_in_dim.21
  201.7 0.1 constant_dynamic-update-slice_fusion
  201.8 2.1 collective-permute-done.2
  203.9 1.3 bitcast_dynamic-update-slice_fusion
  205.2 75.1 %all-to-all-done.5 = f32[32,2,2,64,128]{4,3,2,1,0:T(8,128)} async-done(((f32[32,2,2,64,128]{4,3,2,1,0:T(8,128)}), f32[32,2,2,64,128]{4,3,2,1,0:T(8,128)}, u32[]{:S(2)}, u32[]{:S(2)}) %all-to-all-start.5) | async-done | bytes 4194336 | tf_op jit(solution)/shard_map/all_to_all | solution.py:911
  280.3 10.8 %y_forward.1 = f32[4,8,256,128]{3,2,1,0:T(8,128)} custom-call(f32[2,16,2,2,64,128]{5,4,3,2,1,0:T(8,128)} %bitcast.20.spec_hbm, bf16[4,2048,128]{2,1,0:T(8,128)(2,1)} %bitcast.30, bf16[1024,512]{1,0:T(8,128)(2,1)} %constant.60.clone.table_hbm, f32[2,7,256,128]{3,2,1,0:T(8,128)} %constant.56.clone.tw_hbm), custom_call_target="tpu_custom_call" | custom-call | tf_op jit(solution)/shard_map/y_forward/pallas_call | solution.py:376
  (25 shorter events, 0.2 us)
Async XLA Ops:
  8.7 7.5 %copy-start.6 = (f32[2,4096]{1,0:T(2,128)S(1)}, f32[2,4096]{1,0:T(2,128)}, u32[]{:S(2)}) copy-start(f32[2,4096]{1,0:T(2,128)} %param.17) | copy-start | bytes 98308
  8.8 7.5 %copy-start.7 = (s32[4096]{0:T(1024)S(1)}, s32[4096]{0:T(1024)}, u32[]{:S(2)}) copy-start(s32[4096]{0:T(1024)} %param.16) | copy-start | bytes 49156
  8.8 103.7 %copy-start = (bf16[512,512]{1,0:T(8,128)(2,1)S(1)}, bf16[512,512]{1,0:T(8,128)(2,1)}, u32[]{:S(2)}) copy-start(bf16[512,512]{1,0:T(8,128)(2,1)} %constant.58.clone.inverse_ref.table_ref) | copy-start | bytes 1572868
  8.8 103.7 %copy-start.2 = (f32[2,16,8,256]{3,2,1,0:T(8,128)S(1)}, f32[2,16,8,256]{3,2,1,0:T(8,128)}, u32[]{:S(2)}) copy-start(f32[2,16,8,256]{3,2,1,0:T(8,128)} %constant.57.clone.tw_ref) | copy-start | bytes 786436
  8.8 103.7 %copy-start.3 = (bf16[256,1024]{1,0:T(8,128)(2,1)S(1)}, bf16[256,1024]{1,0:T(8,128)(2,1)}, u32[]{:S(2)}) copy-start(bf16[256,1024]{1,0:T(8,128)(2,1)} %constant.59.clone.forward_ref.table_ref) | copy-start | bytes 1572868
  8.8 103.7 %all-to-all-start = ((f32[32,2,2,64,128]{4,3,2,1,0:T(8,128)}), f32[32,2,2,64,128]{4,3,2,1,0:T(8,128)}, u32[]{:S(2)}, u32[]{:S(2)}) async-start(f32[32,2,2,64,128]{4,3,2,1,0:T(8,128)} %bitcast.26), calls=%async_computation | async-start | bytes 8388608 | tf_op jit(solution)/shard_map/all_to_all | solution.py:911
  126.4 7.1 %collective-permute-start = (f32[40,256]{1,0:T(8,128)S(1)}, f32[40,256]{1,0:T(8,128)S(1)}, u32[]{:S(2)}, u32[]{:S(2)}) collective-permute-start(f32[40,256]{1,0:T(8,128)S(1)} %get-tuple-element.14.tail_ref), channel_id=1, source_target_pairs={{0,16},{16,1},{1,17},{17,2},{2,18},{18,3},{3,19},{19,4},{4,20},{20... | collective-permute-start | bytes 122888 | tf_op jit(solution)/shard_map/ppermute | solution.py:946
  128.1 5.3 %collective-permute-start.1 = (f32[136,256]{1,0:T(8,128)S(1)}, f32[136,256]{1,0:T(8,128)S(1)}, u32[]{:S(2)}, u32[]{:S(2)}) collective-permute-start(f32[136,256]{1,0:T(8,128)S(1)} %get-tuple-element.15.head_ref), channel_id=1, source_target_pairs={{16,0},{1,16},{17,1},{2,17},{18,2},{3,18},{19,3},{4,19},{20,4},{5,... | collective-permute-start | bytes 417800 | tf_op jit(solution)/shard_map/ppermute | solution.py:945
  161.6 16.9 %copy-start.4 = (f32[32,64,256]{2,1,0:T(8,128)}, f32[32,64,256]{2,1,0:T(8,128)S(1)}, u32[]{:S(2)}) copy-start(f32[32,64,256]{2,1,0:T(8,128)S(1)} %get-tuple-element.20) | copy-start | bytes 6291460
  178.5 2.0 copy-start.1
  180.5 99.8 %all-to-all-start.5 = ((f32[32,2,2,64,128]{4,3,2,1,0:T(8,128)}), f32[32,2,2,64,128]{4,3,2,1,0:T(8,128)}, u32[]{:S(2)}, u32[]{:S(2)}) async-start(f32[32,2,2,64,128]{4,3,2,1,0:T(8,128)} %copy-done.1), calls=%async_computation.5 | async-start | bytes 8388608 | tf_op jit(solution)/shard_map/all_to_all | solution.py:911
  200.9 3.0 %collective-permute-start.2 = (f32[64,4096]{1,0:T(8,128)}, f32[64,4096]{1,0:T(8,128)}, u32[]{:S(2)}, u32[]{:S(2)}) collective-permute-start(f32[64,4096]{1,0:T(8,128)} %bitcast.17), channel_id=1, source_target_pairs={{0,16},{16,0},{1,17},{17,1},{2,18},{18,2},{3,19},{19,3},{4,20},{20... | collective-permute-start | bytes 3145736 | tf_op jit(solution)/shard_map/ppermute | solution.py:874
  205.2 85.9 %copy-start.5 = (f32[2,64,4096]{2,1,0:T(8,128)}, f32[2,64,4096]{2,1,0:T(8,128)S(1)}, u32[]{:S(2)}) copy-start(f32[2,64,4096]{2,1,0:T(8,128)S(1)} %bitcast_dynamic-update-slice_fusion) | copy-start | bytes 6291460

commit v14 on v12

--- a/solution.py
+++ b/solution.py
@@ -755,8 +755,11 @@
     for p in range(planes):
         here = d0_ref[p]
         value = here - eta * nd0_ref[p]
-        value = value + shrink(here - prev_plane(d0_ref, p, kb))
-        value = value - shrink(next_plane(d0_ref, p, kb) - here)
+        if p % kb == 0:
+            clipped_x = shrink(here - prev_plane(d0_ref, p, kb))
+        value = value + clipped_x
+        clipped_x = shrink(next_plane(d0_ref, p, kb) - here)
+        value = value - clipped_x
         below = jnp.where(last, here[rows - 1 :, :], next_ref[p : p + 1, :])
         above = jnp.where(first, here[:1, :], prev_ref[p : p + 1, :])
         upper = shrink(jnp.where(row == rows - 1, below, pltpu.roll(here, rows - 1, 0)) - here)
@@ -867,7 +870,7 @@
             jax.ShapeDtypeStruct(first.shape, F32),
             jax.ShapeDtypeStruct((2, 8, LANES), F32),
         ],
-        compiler_params=pltpu.CompilerParams(vmem_limit_bytes=6 * MIB),
+        compiler_params=pltpu.CompilerParams(vmem_limit_bytes=50 * MIB),
         name="combine_spectra",
     )(eta, *sums, first, second)
 

time: 283 us -> 291 us (1.028)
  Pallas kernels: 47.6 us -> 53.4 us
    pallas_call x1, Pallas kernels: 1.85 us -> 7.81 us  [combine_spectra(): pl.pallas_call(functools.partial(combine_kernel, gz), grid=(planes // cou...]
where the time goes in v14:
time: 291 us; the launch traced here: 290 us
  waiting for transfers between devices  174 us (60%)
  Pallas kernels  53.4 us (18%)
  blocking collectives  24.6 us (8%)
  local copies, waits for them, and re-layouts  17.9 us (6%)
  starting transfers between devices  14.1 us (5%)
  other arithmetic  4.58 us (2%)
    all_to_all x2, waiting for transfers between devices, to_devices(): lax.all_to_all(parts.reshape(gz * gy, *rest), ('gz', 'gy'), 0, 0, tiled=T...  171 us
    all_to_all x2, blocking collectives, to_chips(): return lax.all_to_all(parts, 'gy', 0, 0, tiled=True)  24.6 us
    pallas_call x1, Pallas kernels, middle(): pl.pallas_call(middle_kernel, in_specs=[pl.BlockSpec(memory_space=pltpu.H...  13.8 us
    all_to_all x2, starting transfers between devices, to_devices(): lax.all_to_all(parts.reshape(gz * gy, *rest), ('gz', 'gy'), 0, 0, tiled=T...  11 us
    pallas_call x1, Pallas kernels, y_forward(): pl.pallas_call(y_forward_kernel, in_specs=[hbm] * 4, out_specs=hbm, out_s...  10.8 us
    pallas_call x1, Pallas kernels, second_descent(): pl.pallas_call(functools.partial(second_kernel, gz), in_specs=[pl.BlockSp...  8.28 us
    pallas_call x1, Pallas kernels, y_inverse(): pl.pallas_call(y_inverse_kernel, in_specs=[hbm] * 3, out_specs=hbm, out_s...  8.1 us
    pallas_call x1, Pallas kernels, combine_spectra(): pl.pallas_call(functools.partial(combine_kernel, gz), grid=(planes // cou...  7.81 us
  transfers between devices with their start and end apart: 6, of which 4 were waited for; matrix products, arithmetic and copies ran while one was open for 7% of the time, Pallas kernels for 1%

profile of v14, /device:TPU:0, one launch (start us, length us, event | category | flops | bytes accessed | tf_op | source)
XLA Modules:
  0.0 290.2 jit_solution(14737479891741874051)
XLA Ops:
  0.6 8.1 %y_inverse.1 = f32[2,16,2,2,64,128]{5,4,3,2,1,0:T(8,128)} custom-call(bf16[4,2048,128]{2,1,0:T(8,128)(2,1)} %bitcast.29, bf16[1024,512]{1,0:T(8,128)(2,1)} %constant.55.clone.table_hbm, f32[2,7,256,128]{3,2,1,0:T(8,128)} %constant.56.clone.tw_hbm), custom_call_target="tpu_custom_call" | custom-call | tf_op jit(solution)/shard_map/y_inverse/pallas_call | solution.py:264
  8.8 0.0 copy-start.1
  8.8 0.0 copy-start.3
  8.8 7.4 %all-to-all-start = ((f32[32,2,2,64,128]{4,3,2,1,0:T(8,128)}), f32[32,2,2,64,128]{4,3,2,1,0:T(8,128)}, u32[]{:S(2)}, u32[]{:S(2)}) async-start(f32[32,2,2,64,128]{4,3,2,1,0:T(8,128)} %bitcast.26), calls=%async_computation | async-start | bytes 8388608 | tf_op jit(solution)/shard_map/all_to_all | solution.py:889
  16.4 0.1 pad_add_fusion.edge_ref
  16.5 96.0 %all-to-all-done = f32[32,2,2,64,128]{4,3,2,1,0:T(8,128)} async-done(((f32[32,2,2,64,128]{4,3,2,1,0:T(8,128)}), f32[32,2,2,64,128]{4,3,2,1,0:T(8,128)}, u32[]{:S(2)}, u32[]{:S(2)}) %all-to-all-start) | async-done | bytes 4194336 | tf_op jit(solution)/shard_map/all_to_all | solution.py:889
  112.5 13.8 %middle.1 = (f32[32,64,256]{2,1,0:T(8,128)S(1)}, f32[136,256]{1,0:T(8,128)S(1)}, f32[40,256]{1,0:T(8,128)S(1)}, f32[2,16,2,2,64,128]{5,4,3,2,1,0:T(8,128)S(1)}) custom-call(f32[2,16,2,2,64,128]{5,4,3,2,1,0:T(8,128)} %bitcast.5.spec_hbm, f32[3,16,8,256]{3,2,1,0:T(8,128)S(1)} %broadcast_in_dim.24.coef_ref, f32[2,16,8,256]{3,2,1,0:T(8,128)S(1)} %copy-done.3, ...), custom_call_target="tpu_custom_call" | custom-call | tf_op jit(solution)/shard_map/middle/pallas_call | solution.py:605
  126.4 1.8 collective-permute-start
  128.2 1.3 collective-permute-start.1
  129.5 4.0 %normal_product.1.after_ref.nd0_ref = f32[32,64,256]{2,1,0:T(8,128)S(1)} custom-call(f32[2,16,2,2,64,128]{5,4,3,2,1,0:T(8,128)S(1)} %get-tuple-element.13.spec_ref, f32[3,16,8,256]{3,2,1,0:T(8,128)S(1)} %broadcast_in_dim.24.coef_ref, f32[2,16,8,256]{3,2,1,0:T(8,128)S(1)} %copy-done.3, bf16[512,512]{1,0:T(8,128)(2,1)S(1)} %copy-done.1), custom_call_target="tpu_custom_call" | custom-call | flops 1610612736 | bytes 6291456 | tf_op jit(solution)/shard_map/normal_product/pallas_call | solution.py:650
  133.5 0.6 border_sums.1
  134.1 14.5 %all_to_all.20.refs_0_ = f32[16,8,128]{2,1,0:T(8,128)S(1)} all-to-all(f32[16,8,128]{2,1,0:T(8,128)S(1)} %border_sums.1), channel_id=1, replica_groups=mesh['gz'=2,'gy'=16] {'gy'}, dimensions={0} | all-to-all | bytes 131072 | tf_op jit(solution)/shard_map/all_to_all | solution.py:884
  148.6 8.3 %second_descent.1 = (f32[32,64,256]{2,1,0:T(8,128)S(1)}, f32[8,128]{1,0:T(8,128)S(1)}, f32[16,8,128]{2,1,0:T(8,128)S(1)}, f32[2,16,2,2,64,128]{5,4,3,2,1,0:T(8,128)S(1)}) custom-call(s32[3]{0:T(128)S(1)} %pad_add_fusion.edge_ref, f32[32,64,256]{2,1,0:T(8,128)S(1)} %get-tuple-element.12.d0_ref, f32[32,64,256]{2,1,0:T(8,128)S(1)} %normal_product.1.after_ref.nd0_ref, ...), custom_call_target="tpu_custom_call" | custom-call | tf_op jit(solution)/shard_map/second_descent/pallas_call | solution.py:818
  156.9 2.0 copy-done.2
  158.9 1.3 copy-done.5
  160.2 10.1 %all_to_all.21.refs_0_ = f32[16,8,128]{2,1,0:T(8,128)S(1)} all-to-all(f32[16,8,128]{2,1,0:T(8,128)S(1)} %get-tuple-element.17), channel_id=1, replica_groups=mesh['gz'=2,'gy'=16] {'gy'}, dimensions={0} | all-to-all | bytes 131072 | tf_op jit(solution)/shard_map/all_to_all | solution.py:884
  170.3 1.3 collective-permute-done.2.refs_1_
  171.6 7.8 %combine_spectra.1 = (f32[32,2,2,64,128]{4,3,2,1,0:T(8,128)}, f32[2,8,128]{2,1,0:T(8,128)S(1)}) custom-call(f32[8,128]{1,0:T(8,128)S(1)} %get-tuple-element.16.eta_ref, f32[16,8,128]{2,1,0:T(8,128)S(1)} %all_to_all.21.refs_0_, f32[16,8,128]{2,1,0:T(8,128)S(1)} %collective-permute-done.2.refs_1_, f32[32,2,2,64,128]{4,3,2,1,0:T(8,128)} %bitcast.24, ...), custom_call_target="tpu_custom_call" | custom-call | tf_op jit(solution)/shard_map/combine_spectra/pallas_call | solution.py:861
  179.4 3.6 %all-to-all-start.3 = ((f32[32,2,2,64,128]{4,3,2,1,0:T(8,128)}), f32[32,2,2,64,128]{4,3,2,1,0:T(8,128)}, u32[]{:S(2)}, u32[]{:S(2)}) async-start(f32[32,2,2,64,128]{4,3,2,1,0:T(8,128)} %get-tuple-element.21), calls=%async_computation.3 | async-start | bytes 8388608 | tf_op jit(solution)/shard_map/all_to_all | solution.py:889
  183.0 0.5 fusion.2
  183.5 4.5 %add_negate_fusion = f32[32,64,256]{2,1,0:T(8,128)} fusion(f32[32,64,256]{2,1,0:T(8,128)} %copy-done.5, f32[32,64,256]{2,1,0:T(8,128)S(1)} %get-tuple-element.12.d0_ref, f32[]{:T(128)} %bitcast.12, f32[]{:T(128)} %bitcast.11), kind=kLoop, calls=%fused_computation | loop fusion | flops 2097152 | bytes 6291464 | tf_op jit(solution)/shard_map/neg | solution.py:940
  188.0 4.9 %copy.21 = f32[2,16,64,256]{2,1,3,0:T(8,128)} copy(f32[2,16,64,256]{3,2,1,0:T(8,128)} %bitcast.28) | data formatting | bytes 4194304 | tf_op jit(solution)/shard_map/reshape | solution.py:941
  192.9 3.8 %constant_dynamic-slice_fusion = (f32[1,64,4096]{1,2,0:T(8,128)}, f32[1,64,4096]{1,2,0:T(8,128)S(1)}) fusion(f32[2,64,4096]{1,2,0:T(8,128)} %bitcast.27, s32[]{:T(128)S(6)} %select_n.29, s32[]{:T(128)S(6)} %select_n.27), kind=kLoop, calls=%fused_computation.6 | loop fusion | bytes 4194312 | tf_op jit(solution)/shard_map/jit(dynamic_index_in_dim)/dynamic_slice | solution.py:943
  196.7 3.1 %copy.23 = f32[1,64,4096]{2,1,0:T(8,128)} copy(f32[1,64,4096]{1,2,0:T(8,128)} %get-tuple-element.24) | data formatting | bytes 2097152 | tf_op jit(solution)/shard_map/jit(dynamic_index_in_dim)/dynamic_slice | solution.py:943
  199.8 0.0 collective-permute-start.3
  199.9 0.6 copy.22
  200.4 0.2 broadcast_in_dim.21
  200.6 0.1 constant_dynamic-update-slice_fusion
  200.7 2.1 collective-permute-done.3
  202.8 1.3 bitcast_dynamic-update-slice_fusion
  204.1 75.1 %all-to-all-done.3 = f32[32,2,2,64,128]{4,3,2,1,0:T(8,128)} async-done(((f32[32,2,2,64,128]{4,3,2,1,0:T(8,128)}), f32[32,2,2,64,128]{4,3,2,1,0:T(8,128)}, u32[]{:S(2)}, u32[]{:S(2)}) %all-to-all-start.3) | async-done | bytes 4194336 | tf_op jit(solution)/shard_map/all_to_all | solution.py:889
  279.2 10.8 %y_forward.1 = f32[4,8,256,128]{3,2,1,0:T(8,128)} custom-call(f32[2,16,2,2,64,128]{5,4,3,2,1,0:T(8,128)} %bitcast.20.spec_hbm, bf16[4,2048,128]{2,1,0:T(8,128)(2,1)} %bitcast.30, bf16[1024,512]{1,0:T(8,128)(2,1)} %constant.60.clone.table_hbm, f32[2,7,256,128]{3,2,1,0:T(8,128)} %constant.56.clone.tw_hbm), custom_call_target="tpu_custom_call" | custom-call | tf_op jit(solution)/shard_map/y_forward/pallas_call | solution.py:376
  (25 shorter events, 0.1 us)
Async XLA Ops:
  8.7 7.5 %copy-start.7 = (f32[2,4096]{1,0:T(2,128)S(1)}, f32[2,4096]{1,0:T(2,128)}, u32[]{:S(2)}) copy-start(f32[2,4096]{1,0:T(2,128)} %param.17) | copy-start | bytes 98308
  8.8 7.5 %copy-start.8 = (s32[4096]{0:T(1024)S(1)}, s32[4096]{0:T(1024)}, u32[]{:S(2)}) copy-start(s32[4096]{0:T(1024)} %param.16) | copy-start | bytes 49156
  8.8 103.7 %copy-start.1 = (bf16[512,512]{1,0:T(8,128)(2,1)S(1)}, bf16[512,512]{1,0:T(8,128)(2,1)}, u32[]{:S(2)}) copy-start(bf16[512,512]{1,0:T(8,128)(2,1)} %constant.58.clone.inverse_ref.table_ref) | copy-start | bytes 1572868
  8.8 103.7 %copy-start.3 = (f32[2,16,8,256]{3,2,1,0:T(8,128)S(1)}, f32[2,16,8,256]{3,2,1,0:T(8,128)}, u32[]{:S(2)}) copy-start(f32[2,16,8,256]{3,2,1,0:T(8,128)} %constant.57.clone.tw_ref) | copy-start | bytes 786436
  8.8 103.7 %copy-start.4 = (bf16[256,1024]{1,0:T(8,128)(2,1)S(1)}, bf16[256,1024]{1,0:T(8,128)(2,1)}, u32[]{:S(2)}) copy-start(bf16[256,1024]{1,0:T(8,128)(2,1)} %constant.59.clone.forward_ref.table_ref) | copy-start | bytes 1572868
  8.8 103.7 %all-to-all-start = ((f32[32,2,2,64,128]{4,3,2,1,0:T(8,128)}), f32[32,2,2,64,128]{4,3,2,1,0:T(8,128)}, u32[]{:S(2)}, u32[]{:S(2)}) async-start(f32[32,2,2,64,128]{4,3,2,1,0:T(8,128)} %bitcast.26), calls=%async_computation | async-start | bytes 8388608 | tf_op jit(solution)/shard_map/all_to_all | solution.py:889
  126.4 7.1 %copy-start = (f32[2,16,2,2,64,128]{5,4,3,2,1,0:T(8,128)}, f32[2,16,2,2,64,128]{5,4,3,2,1,0:T(8,128)S(1)}, u32[]{:S(2)}) copy-start(f32[2,16,2,2,64,128]{5,4,3,2,1,0:T(8,128)S(1)} %get-tuple-element.13.spec_ref) | copy-start | bytes 12582916
  126.4 7.1 %collective-permute-start = (f32[40,256]{1,0:T(8,128)S(1)}, f32[40,256]{1,0:T(8,128)S(1)}, u32[]{:S(2)}, u32[]{:S(2)}) collective-permute-start(f32[40,256]{1,0:T(8,128)S(1)} %get-tuple-element.14.tail_ref), channel_id=1, source_target_pairs={{0,16},{16,1},{1,17},{17,2},{2,18},{18,3},{3,19},{19,4},{4,20},{20... | collective-permute-start | bytes 122888 | tf_op jit(solution)/shard_map/ppermute | solution.py:929
  128.2 5.3 %collective-permute-start.1 = (f32[136,256]{1,0:T(8,128)S(1)}, f32[136,256]{1,0:T(8,128)S(1)}, u32[]{:S(2)}, u32[]{:S(2)}) collective-permute-start(f32[136,256]{1,0:T(8,128)S(1)} %get-tuple-element.15.head_ref), channel_id=1, source_target_pairs={{16,0},{1,16},{17,1},{2,17},{18,2},{3,18},{19,3},{4,19},{20,4},{5,... | collective-permute-start | bytes 417800 | tf_op jit(solution)/shard_map/ppermute | solution.py:928
  156.9 2.0 copy-start.2
  158.9 1.3 copy-start.5
  170.3 1.3 collective-permute-start.2
  179.4 99.8 %all-to-all-start.3 = ((f32[32,2,2,64,128]{4,3,2,1,0:T(8,128)}), f32[32,2,2,64,128]{4,3,2,1,0:T(8,128)}, u32[]{:S(2)}, u32[]{:S(2)}) async-start(f32[32,2,2,64,128]{4,3,2,1,0:T(8,128)} %get-tuple-element.21), calls=%async_computation.3 | async-start | bytes 8388608 | tf_op jit(solution)/shard_map/all_to_all | solution.py:889
  199.8 3.0 %collective-permute-start.3 = (f32[64,4096]{1,0:T(8,128)}, f32[64,4096]{1,0:T(8,128)}, u32[]{:S(2)}, u32[]{:S(2)}) collective-permute-start(f32[64,4096]{1,0:T(8,128)} %bitcast.17), channel_id=1, source_target_pairs={{0,16},{16,0},{1,17},{17,1},{2,18},{18,2},{3,19},{19,3},{4,20},{20... | collective-permute-start | bytes 3145736 | tf_op jit(solution)/shard_map/ppermute | solution.py:880
  204.1 85.9 %copy-start.6 = (f32[2,64,4096]{2,1,0:T(8,128)}, f32[2,64,4096]{2,1,0:T(8,128)S(1)}, u32[]{:S(2)}) copy-start(f32[2,64,4096]{2,1,0:T(8,128)S(1)} %bitcast_dynamic-update-slice_fusion) | copy-start | bytes 6291460

commit v15 on v14

--- a/solution.py
+++ b/solution.py
@@ -524,15 +524,17 @@
     ka = chunks * LANES
     planes = gz * kb
 
-    def fetch(chunk):
+    def fetch(chunk, z):
         return pltpu.make_async_copy(
-            spec_hbm.at[:, :, chunk], spec_ref.at[:, :, chunk], sems.at[chunk]
+            spec_hbm.at[z, :, chunk], spec_ref.at[z, :, chunk], sems.at[chunk * gz + z]
         )
 
     for chunk in range(chunks):
-        fetch(chunk).start()
+        for z in range(gz):
+            fetch(chunk, z).start()
     for chunk in range(chunks):
-        fetch(chunk).wait()
+        for z in range(gz):
+            fetch(chunk, z).wait()
         lax.fori_loop(
             0, rows // 8,
             functools.partial(columns_back, spec_ref, chunk, coef_ref, tw_ref, re_s, im_s), 0,
@@ -615,7 +617,7 @@
         scratch_shapes=[
             pltpu.VMEM((planes, rows, ka), F32),
             pltpu.VMEM((planes, rows, ka), F32),
-            pltpu.SemaphoreType.DMA((chunks,)),
+            pltpu.SemaphoreType.DMA((chunks * gz,)),
         ],
         compiler_params=pltpu.CompilerParams(vmem_limit_bytes=X_GRANT),
         name="middle",
@@ -870,7 +872,7 @@
             jax.ShapeDtypeStruct(first.shape, F32),
             jax.ShapeDtypeStruct((2, 8, LANES), F32),
         ],
-        compiler_params=pltpu.CompilerParams(vmem_limit_bytes=50 * MIB),
+        compiler_params=pltpu.CompilerParams(vmem_limit_bytes=6 * MIB),
         name="combine_spectra",
     )(eta, *sums, first, second)
 

time: 291 us -> 283 us (0.973)
  Pallas kernels: 53.4 us -> 47.4 us
    pallas_call x1, Pallas kernels: 7.81 us -> 1.85 us  [combine_spectra(): pl.pallas_call(functools.partial(combine_kernel, gz), grid=(planes // cou...]
where the time goes in v15:
time: 283 us
  waiting for transfers between devices  174 us (61%)
  Pallas kernels  47.4 us (17%)
  blocking collectives  24.6 us (9%)
  local copies, waits for them, and re-layouts  16.6 us (6%)
  starting transfers between devices  14.1 us (5%)
  other arithmetic  4.65 us (2%)
    all_to_all x2, waiting for transfers between devices, to_devices(): lax.all_to_all(parts.reshape(gz * gy, *rest), ('gz', 'gy'), 0, 0, tiled=T...  171 us
    all_to_all x2, blocking collectives, to_chips(): return lax.all_to_all(parts, 'gy', 0, 0, tiled=True)  24.6 us
    pallas_call x1, Pallas kernels, middle(): pl.pallas_call(middle_kernel, in_specs=[pl.BlockSpec(memory_space=pltpu.H...  13.8 us
    all_to_all x2, starting transfers between devices, to_devices(): lax.all_to_all(parts.reshape(gz * gy, *rest), ('gz', 'gy'), 0, 0, tiled=T...  11 us
    pallas_call x1, Pallas kernels, y_forward(): pl.pallas_call(y_forward_kernel, in_specs=[hbm] * 4, out_specs=hbm, out_s...  10.8 us
    pallas_call x1, Pallas kernels, second_descent(): pl.pallas_call(functools.partial(second_kernel, gz), in_specs=[pl.BlockSp...  8.24 us
    pallas_call x1, Pallas kernels, y_inverse(): pl.pallas_call(y_inverse_kernel, in_specs=[hbm] * 3, out_specs=hbm, out_s...  8.1 us
    dynamic_slice x3, local copies, waits for them, and re-layouts, shards(): lax.dynamic_index_in_dim(volume, lax.rem(core + r, gz), 0, False)  7.54 us
  transfers between devices with their start and end apart: 6, of which 4 were waited for; matrix products, arithmetic and copies ran while one was open for 7% of the time, Pallas kernels for 1%

profile of v15, /device:TPU:0, one launch (start us, length us, event | category | flops | bytes accessed | tf_op | source)
XLA Modules:
  0.0 282.8 jit_solution(14794661644647990180)
XLA Ops:
  0.6 8.1 %y_inverse.1 = f32[2,16,2,2,64,128]{5,4,3,2,1,0:T(8,128)} custom-call(bf16[4,2048,128]{2,1,0:T(8,128)(2,1)} %bitcast.29, bf16[1024,512]{1,0:T(8,128)(2,1)} %constant.55.clone.table_hbm, f32[2,7,256,128]{3,2,1,0:T(8,128)} %constant.56.clone.tw_hbm), custom_call_target="tpu_custom_call" | custom-call | tf_op jit(solution)/shard_map/y_inverse/pallas_call | solution.py:264
  8.8 0.0 copy-start
  8.8 0.0 copy-start.2
  8.8 0.0 copy-start.3
  8.8 7.4 %all-to-all-start = ((f32[32,2,2,64,128]{4,3,2,1,0:T(8,128)}), f32[32,2,2,64,128]{4,3,2,1,0:T(8,128)}, u32[]{:S(2)}, u32[]{:S(2)}) async-start(f32[32,2,2,64,128]{4,3,2,1,0:T(8,128)} %bitcast.26), calls=%async_computation | async-start | bytes 8388608 | tf_op jit(solution)/shard_map/all_to_all | solution.py:891
  16.4 0.1 pad_add_fusion.edge_ref
  16.5 96.0 %all-to-all-done = f32[32,2,2,64,128]{4,3,2,1,0:T(8,128)} async-done(((f32[32,2,2,64,128]{4,3,2,1,0:T(8,128)}), f32[32,2,2,64,128]{4,3,2,1,0:T(8,128)}, u32[]{:S(2)}, u32[]{:S(2)}) %all-to-all-start) | async-done | bytes 4194336 | tf_op jit(solution)/shard_map/all_to_all | solution.py:891
  112.5 13.8 %middle.1 = (f32[32,64,256]{2,1,0:T(8,128)S(1)}, f32[136,256]{1,0:T(8,128)S(1)}, f32[40,256]{1,0:T(8,128)S(1)}, f32[2,16,2,2,64,128]{5,4,3,2,1,0:T(8,128)S(1)}) custom-call(f32[2,16,2,2,64,128]{5,4,3,2,1,0:T(8,128)} %bitcast.5.spec_hbm, f32[3,16,8,256]{3,2,1,0:T(8,128)S(1)} %broadcast_in_dim.24.coef_ref, f32[2,16,8,256]{3,2,1,0:T(8,128)S(1)} %copy-done.2, ...), custom_call_target="tpu_custom_call" | custom-call | tf_op jit(solution)/shard_map/middle/pallas_call | solution.py:607
  126.3 1.8 collective-permute-start
  128.1 1.3 collective-permute-start.1
  129.4 4.0 %normal_product.1.after_ref.nd0_ref = f32[32,64,256]{2,1,0:T(8,128)S(1)} custom-call(f32[2,16,2,2,64,128]{5,4,3,2,1,0:T(8,128)S(1)} %get-tuple-element.13.spec_ref, f32[3,16,8,256]{3,2,1,0:T(8,128)S(1)} %broadcast_in_dim.24.coef_ref, f32[2,16,8,256]{3,2,1,0:T(8,128)S(1)} %copy-done.2, bf16[512,512]{1,0:T(8,128)(2,1)S(1)} %copy-done), custom_call_target="tpu_custom_call" | custom-call | flops 1610612736 | bytes 6291456 | tf_op jit(solution)/shard_map/normal_product/pallas_call | solution.py:652
  133.5 0.6 border_sums.1
  134.0 14.5 %all_to_all.20.refs_0_ = f32[16,8,128]{2,1,0:T(8,128)S(1)} all-to-all(f32[16,8,128]{2,1,0:T(8,128)S(1)} %border_sums.1), channel_id=1, replica_groups=mesh['gz'=2,'gy'=16] {'gy'}, dimensions={0} | all-to-all | bytes 131072 | tf_op jit(solution)/shard_map/all_to_all | solution.py:886
  148.5 8.2 %second_descent.1 = (f32[32,64,256]{2,1,0:T(8,128)S(1)}, f32[8,128]{1,0:T(8,128)S(1)}, f32[16,8,128]{2,1,0:T(8,128)S(1)}, f32[2,16,2,2,64,128]{5,4,3,2,1,0:T(8,128)S(1)}) custom-call(s32[3]{0:T(128)S(1)} %pad_add_fusion.edge_ref, f32[32,64,256]{2,1,0:T(8,128)S(1)} %get-tuple-element.12.d0_ref, f32[32,64,256]{2,1,0:T(8,128)S(1)} %normal_product.1.after_ref.nd0_ref, ...), custom_call_target="tpu_custom_call" | custom-call | tf_op jit(solution)/shard_map/second_descent/pallas_call | solution.py:820
  156.8 10.1 %all_to_all.21.refs_0_ = f32[16,8,128]{2,1,0:T(8,128)S(1)} all-to-all(f32[16,8,128]{2,1,0:T(8,128)S(1)} %get-tuple-element.17), channel_id=1, replica_groups=mesh['gz'=2,'gy'=16] {'gy'}, dimensions={0} | all-to-all | bytes 131072 | tf_op jit(solution)/shard_map/all_to_all | solution.py:886
  166.9 1.3 collective-permute-done.2.refs_1_
  168.2 1.9 combine_spectra.1
  170.1 2.0 copy-done.1
  172.1 3.6 %all-to-all-start.3 = ((f32[32,2,2,64,128]{4,3,2,1,0:T(8,128)}), f32[32,2,2,64,128]{4,3,2,1,0:T(8,128)}, u32[]{:S(2)}, u32[]{:S(2)}) async-start(f32[32,2,2,64,128]{4,3,2,1,0:T(8,128)} %copy-done.1), calls=%async_computation.3 | async-start | bytes 8388608 | tf_op jit(solution)/shard_map/all_to_all | solution.py:891
  175.7 0.5 fusion.2
  176.2 4.6 %add_negate_fusion = f32[32,64,256]{2,1,0:T(8,128)} fusion(f32[32,64,256]{2,1,0:T(8,128)} %copy-done.4, f32[32,64,256]{2,1,0:T(8,128)S(1)} %get-tuple-element.12.d0_ref, f32[]{:T(128)} %bitcast.12, f32[]{:T(128)} %bitcast.11), kind=kLoop, calls=%fused_computation | loop fusion | flops 2097152 | bytes 6291464 | tf_op jit(solution)/shard_map/neg | solution.py:942
  180.8 4.9 %copy.21 = f32[2,16,64,256]{2,1,3,0:T(8,128)} copy(f32[2,16,64,256]{3,2,1,0:T(8,128)} %bitcast.28) | data formatting | bytes 4194304 | tf_op jit(solution)/shard_map/reshape | solution.py:943
  185.6 3.8 %constant_dynamic-slice_fusion = (f32[1,64,4096]{1,2,0:T(8,128)}, f32[1,64,4096]{1,2,0:T(8,128)S(1)}) fusion(f32[2,64,4096]{1,2,0:T(8,128)} %bitcast.27, s32[]{:T(128)S(6)} %select_n.29, s32[]{:T(128)S(6)} %select_n.27), kind=kLoop, calls=%fused_computation.6 | loop fusion | bytes 4194312 | tf_op jit(solution)/shard_map/jit(dynamic_index_in_dim)/dynamic_slice | solution.py:945
  189.4 3.1 %copy.23 = f32[1,64,4096]{2,1,0:T(8,128)} copy(f32[1,64,4096]{1,2,0:T(8,128)} %get-tuple-element.24) | data formatting | bytes 2097152 | tf_op jit(solution)/shard_map/jit(dynamic_index_in_dim)/dynamic_slice | solution.py:945
  192.6 0.0 collective-permute-start.3
  192.6 0.6 copy.22
  193.2 0.2 broadcast_in_dim.21
  193.4 0.1 constant_dynamic-update-slice_fusion
  193.5 2.1 collective-permute-done.3
  195.6 1.3 bitcast_dynamic-update-slice_fusion
  196.9 75.0 %all-to-all-done.3 = f32[32,2,2,64,128]{4,3,2,1,0:T(8,128)} async-done(((f32[32,2,2,64,128]{4,3,2,1,0:T(8,128)}), f32[32,2,2,64,128]{4,3,2,1,0:T(8,128)}, u32[]{:S(2)}, u32[]{:S(2)}) %all-to-all-start.3) | async-done | bytes 4194336 | tf_op jit(solution)/shard_map/all_to_all | solution.py:891
  271.9 10.8 %y_forward.1 = f32[4,8,256,128]{3,2,1,0:T(8,128)} custom-call(f32[2,16,2,2,64,128]{5,4,3,2,1,0:T(8,128)} %bitcast.20.spec_hbm, bf16[4,2048,128]{2,1,0:T(8,128)(2,1)} %bitcast.30, bf16[1024,512]{1,0:T(8,128)(2,1)} %constant.60.clone.table_hbm, f32[2,7,256,128]{3,2,1,0:T(8,128)} %constant.56.clone.tw_hbm), custom_call_target="tpu_custom_call" | custom-call | tf_op jit(solution)/shard_map/y_forward/pallas_call | solution.py:376
  (23 shorter events, 0.1 us)
Async XLA Ops:
  8.7 7.5 %copy-start.6 = (f32[2,4096]{1,0:T(2,128)S(1)}, f32[2,4096]{1,0:T(2,128)}, u32[]{:S(2)}) copy-start(f32[2,4096]{1,0:T(2,128)} %param.17) | copy-start | bytes 98308
  8.8 7.5 %copy-start.7 = (s32[4096]{0:T(1024)S(1)}, s32[4096]{0:T(1024)}, u32[]{:S(2)}) copy-start(s32[4096]{0:T(1024)} %param.16) | copy-start | bytes 49156
  8.8 103.7 %copy-start = (bf16[512,512]{1,0:T(8,128)(2,1)S(1)}, bf16[512,512]{1,0:T(8,128)(2,1)}, u32[]{:S(2)}) copy-start(bf16[512,512]{1,0:T(8,128)(2,1)} %constant.58.clone.inverse_ref.table_ref) | copy-start | bytes 1572868
  8.8 103.7 %copy-start.2 = (f32[2,16,8,256]{3,2,1,0:T(8,128)S(1)}, f32[2,16,8,256]{3,2,1,0:T(8,128)}, u32[]{:S(2)}) copy-start(f32[2,16,8,256]{3,2,1,0:T(8,128)} %constant.57.clone.tw_ref) | copy-start | bytes 786436
  8.8 103.7 %copy-start.3 = (bf16[256,1024]{1,0:T(8,128)(2,1)S(1)}, bf16[256,1024]{1,0:T(8,128)(2,1)}, u32[]{:S(2)}) copy-start(bf16[256,1024]{1,0:T(8,128)(2,1)} %constant.59.clone.forward_ref.table_ref) | copy-start | bytes 1572868
  8.8 103.7 %all-to-all-start = ((f32[32,2,2,64,128]{4,3,2,1,0:T(8,128)}), f32[32,2,2,64,128]{4,3,2,1,0:T(8,128)}, u32[]{:S(2)}, u32[]{:S(2)}) async-start(f32[32,2,2,64,128]{4,3,2,1,0:T(8,128)} %bitcast.26), calls=%async_computation | async-start | bytes 8388608 | tf_op jit(solution)/shard_map/all_to_all | solution.py:891
  126.3 7.1 %collective-permute-start = (f32[40,256]{1,0:T(8,128)S(1)}, f32[40,256]{1,0:T(8,128)S(1)}, u32[]{:S(2)}, u32[]{:S(2)}) collective-permute-start(f32[40,256]{1,0:T(8,128)S(1)} %get-tuple-element.14.tail_ref), channel_id=1, source_target_pairs={{0,16},{16,1},{1,17},{17,2},{2,18},{18,3},{3,19},{19,4},{4,20},{20... | collective-permute-start | bytes 122888 | tf_op jit(solution)/shard_map/ppermute | solution.py:931
  128.1 5.3 %collective-permute-start.1 = (f32[136,256]{1,0:T(8,128)S(1)}, f32[136,256]{1,0:T(8,128)S(1)}, u32[]{:S(2)}, u32[]{:S(2)}) collective-permute-start(f32[136,256]{1,0:T(8,128)S(1)} %get-tuple-element.15.head_ref), channel_id=1, source_target_pairs={{16,0},{1,16},{17,1},{2,17},{18,2},{3,18},{19,3},{4,19},{20,4},{5,... | collective-permute-start | bytes 417800 | tf_op jit(solution)/shard_map/ppermute | solution.py:930
  156.8 13.3 %copy-start.4 = (f32[32,64,256]{2,1,0:T(8,128)}, f32[32,64,256]{2,1,0:T(8,128)S(1)}, u32[]{:S(2)}) copy-start(f32[32,64,256]{2,1,0:T(8,128)S(1)} %get-tuple-element.20) | copy-start | bytes 6291460
  166.9 1.3 collective-permute-start.2
  170.1 2.0 copy-start.1
  172.1 99.8 %all-to-all-start.3 = ((f32[32,2,2,64,128]{4,3,2,1,0:T(8,128)}), f32[32,2,2,64,128]{4,3,2,1,0:T(8,128)}, u32[]{:S(2)}, u32[]{:S(2)}) async-start(f32[32,2,2,64,128]{4,3,2,1,0:T(8,128)} %copy-done.1), calls=%async_computation.3 | async-start | bytes 8388608 | tf_op jit(solution)/shard_map/all_to_all | solution.py:891
  192.6 3.0 %collective-permute-start.3 = (f32[64,4096]{1,0:T(8,128)}, f32[64,4096]{1,0:T(8,128)}, u32[]{:S(2)}, u32[]{:S(2)}) collective-permute-start(f32[64,4096]{1,0:T(8,128)} %bitcast.17), channel_id=1, source_target_pairs={{0,16},{16,0},{1,17},{17,1},{2,18},{18,2},{3,19},{19,3},{4,20},{20... | collective-permute-start | bytes 3145736 | tf_op jit(solution)/shard_map/ppermute | solution.py:882
  196.9 85.8 %copy-start.5 = (f32[2,64,4096]{2,1,0:T(8,128)}, f32[2,64,4096]{2,1,0:T(8,128)S(1)}, u32[]{:S(2)}) copy-start(f32[2,64,4096]{2,1,0:T(8,128)S(1)} %bitcast_dynamic-update-slice_fusion) | copy-start | bytes 6291460
